TPU v7x, 32 devices: a whole 2x2x4 slice. The times are simulated.
32 devices in a mesh: dp: 2 (over x), seq: 16 (over z, y, core).
Axes of the slice: x: 2, y: 2, z: 4, core: 2. Of those that a mesh axis runs over, the one named last changes fastest.
Arguments:
- tokens: bfloat16 [2, 4096, 1280], P('dp', 'seq'), may hold values from -80 to 80
- cotangent: bfloat16 [2, 4096, 1280], P('dp', 'seq'), may hold values from -16 to 16
- router: bfloat16 [1280, 64], replicated, may hold values from -1 to 1
- slot_outputs: bfloat16 [2, 64, 1280], P('dp'), may hold values from -6 to 6
- base_in: bfloat16 [1280, 5120], P(None, 'seq'), may hold values from -0.15625 to 0.15625
- base_out: bfloat16 [5120, 1280], P('seq'), may hold values from -0.078125 to 0.078125
- delta_in_left: bfloat16 [64, 1280, 64], P('seq', 'dp'), may hold values from -0.15625 to 0.15625
- delta_in_right: bfloat16 [64, 64, 5120], P('dp', None, 'seq'), may hold values from -0.75 to 0.75
- delta_out_left: bfloat16 [64, 5120, 64], P('dp', 'seq'), may hold values from -0.078125 to 0.078125
- delta_out_right: bfloat16 [64, 64, 1280], P('seq', None, 'dp'), may hold values from -0.75 to 0.75
Outputs:
- token_grad: bfloat16 [2, 4096, 1280], P('dp', 'seq')
- grad_in_left: bfloat16 [64, 1280, 64], P('seq', 'dp')
- grad_in_right: bfloat16 [64, 64, 5120], P('dp', None, 'seq')
- grad_out_left: bfloat16 [64, 5120, 64], P('dp', 'seq')
- grad_out_right: bfloat16 [64, 64, 1280], P('seq', None, 'dp')
All inputs are finite; a program needn't handle non-finite values.
Results may differ from a plain program's by a relative error of at most 0.015.
Values may be sent and summed in bfloat16 or wider, within the bound.
No kernel may reach another device: no remote copies, remote signals or barrier semaphores. Data moves between devices by JAX's collectives and lax.ppermute only.
A program may use at most 64 MiB of HBM per device.

v0:
```python
import jax
import jax.numpy as jnp
from jax import lax
from jax.sharding import PartitionSpec as P


def gelu_backward(preact, upstream):
    return jax.vjp(jax.nn.gelu, preact)[1](upstream)[0]


def dot_first(left, right):
    return lax.dot_general(
        left, right, (((0,), (0,)), ((), ())), preferred_element_type=jnp.float32
    )


def dot_last(left, right):
    return lax.dot_general(
        left, right, (((1,), (1,)), ((), ())), preferred_element_type=jnp.float32
    )


def local(
    tokens,
    cotangent,
    router,
    slot_outputs,
    base_in,
    base_out,
    delta_in_left,
    delta_in_right,
    delta_out_left,
    delta_out_right,
):
    image_rows = tokens[0]
    cot_rows = cotangent[0]
    saved_outputs = slot_outputs[0]
    in_left, in_right, out_left, out_right = (
        lax.all_gather(delta_in_left, "dp", axis=1, tiled=True),
        lax.all_gather(delta_in_right, "dp", axis=0, tiled=True),
        lax.all_gather(delta_out_left, "dp", axis=0, tiled=True),
        lax.all_gather(delta_out_right, "dp", axis=2, tiled=True),
    )
    owned_count = in_left.shape[0]
    rank_width = in_left.shape[2]
    logits = jnp.dot(image_rows, router, preferred_element_type=jnp.float32)
    slot_peak = lax.pmax(jnp.max(logits, axis=0), "seq")
    slot_total = lax.psum(jnp.sum(jnp.exp(logits - slot_peak), axis=0), "seq")
    dispatch = jnp.exp(logits - slot_peak) / slot_total
    dispatch_low = dispatch.astype(jnp.bfloat16)
    combine = jax.nn.softmax(logits, axis=1)
    combine_low = combine.astype(jnp.bfloat16)
    slot_start = lax.axis_index("seq") * owned_count
    stacked = jnp.stack(
        [dot_first(dispatch_low, image_rows), dot_first(combine_low, cot_rows)], axis=1
    )
    summed = lax.psum(stacked, "seq")
    slots_low = summed.astype(jnp.bfloat16)
    owned_low = lax.dynamic_slice_in_dim(slots_low, slot_start, owned_count, 0)
    inputs_low = slots_low[:, 0]
    grads_low = slots_low[:, 1]
    up_owned = jnp.einsum(
        "jd,jdr->jr", owned_low[:, 0], in_left, preferred_element_type=jnp.float32
    ).astype(jnp.bfloat16)
    back_owned = jnp.einsum(
        "jd,jrd->jr", owned_low[:, 1], out_right, preferred_element_type=jnp.float32
    ).astype(jnp.bfloat16)
    factors = lax.all_gather(
        jnp.concatenate([up_owned, back_owned], axis=1), "seq", axis=0, tiled=True
    )
    up_low = factors[:, :rank_width]
    back_low = factors[:, rank_width:]
    preact = jnp.dot(inputs_low, base_in, preferred_element_type=jnp.float32) + jnp.einsum(
        "jr,jrf->jf", up_low, in_right, preferred_element_type=jnp.float32
    )
    hidden_low = jax.nn.gelu(preact).astype(jnp.bfloat16)
    hidden_grad = dot_last(grads_low, base_out) + jnp.einsum(
        "jr,jfr->jf", back_low, out_left, preferred_element_type=jnp.float32
    )
    preact_grad = gelu_backward(preact, hidden_grad).astype(jnp.bfloat16)
    slot_term = dot_last(preact_grad, base_in)
    down_term = jnp.einsum("jf,jrf->jr", preact_grad, in_right, preferred_element_type=jnp.float32)
    value_term = jnp.einsum("jf,jfr->jr", hidden_low, out_left, preferred_element_type=jnp.float32)
    owned_slot, owned_rank = (
        lax.psum_scatter(slot_term, "seq", scatter_dimension=0, tiled=True),
        lax.psum_scatter(
            jnp.concatenate([down_term, value_term], axis=1), "seq", scatter_dimension=0, tiled=True
        ),
    )
    owned_rank_low = owned_rank.astype(jnp.bfloat16)
    down_owned = owned_rank_low[:, :rank_width]
    owned_grad = (
        owned_slot
        + jnp.einsum("jr,jdr->jd", down_owned, in_left, preferred_element_type=jnp.float32)
    ).astype(jnp.bfloat16)
    slot_grads = lax.all_gather(owned_grad, "seq", axis=0, tiled=True)
    weight_grad = dot_last(image_rows, slot_grads)
    shift_back = lax.psum(jnp.sum(dispatch_low.astype(jnp.float32) * weight_grad, axis=0), "seq")
    dispatch_logit = dispatch * (weight_grad - shift_back)
    mixing_grad = dot_last(cot_rows, saved_outputs)
    combine_logit = combine * (mixing_grad - jnp.sum(combine * mixing_grad, axis=1, keepdims=True))
    logit_grad = (dispatch_logit + combine_logit).astype(jnp.bfloat16)
    token_grad = (
        jnp.dot(dispatch_low, slot_grads, preferred_element_type=jnp.float32)
        + dot_last(logit_grad, router)
    ).astype(jnp.bfloat16)
    hidden_pair = jnp.stack([preact_grad, hidden_low], axis=1)
    all_factors, all_hidden, all_owned, all_owned_rank = (
        lax.all_gather(factors[None], "dp", axis=0, tiled=True),
        lax.all_gather(hidden_pair[None], "dp", axis=0, tiled=True),
        lax.all_gather(owned_low[None], "dp", axis=0, tiled=True),
        lax.all_gather(owned_rank_low[None], "dp", axis=0, tiled=True),
    )
    block_rows = delta_in_right.shape[0]
    block_start = lax.axis_index("dp") * block_rows
    chosen_factors = lax.dynamic_slice_in_dim(all_factors, block_start, block_rows, 1)
    chosen_hidden = lax.dynamic_slice_in_dim(all_hidden, block_start, block_rows, 1)
    grad_in_right = jnp.einsum(
        "gjr,gjf->jrf",
        chosen_factors[:, :, :rank_width],
        chosen_hidden[:, :, 0],
        preferred_element_type=jnp.float32,
    ).astype(jnp.bfloat16)
    grad_out_left = jnp.einsum(
        "gjf,gjr->jfr",
        chosen_hidden[:, :, 1],
        chosen_factors[:, :, rank_width:],
        preferred_element_type=jnp.float32,
    ).astype(jnp.bfloat16)
    feature_rows = delta_in_left.shape[1]
    feature_start = lax.axis_index("dp") * feature_rows
    owned_slice = lax.dynamic_slice_in_dim(all_owned, feature_start, feature_rows, 3)
    grad_in_left = jnp.einsum(
        "gjd,gjr->jdr",
        owned_slice[:, :, 0],
        all_owned_rank[:, :, :rank_width],
        preferred_element_type=jnp.float32,
    ).astype(jnp.bfloat16)
    grad_out_right = jnp.einsum(
        "gjr,gjd->jrd",
        all_owned_rank[:, :, rank_width:],
        owned_slice[:, :, 1],
        preferred_element_type=jnp.float32,
    ).astype(jnp.bfloat16)
    return (token_grad[None], grad_in_left, grad_in_right, grad_out_left, grad_out_right)


def solution(mesh):
    in_specs = (
        P("dp", "seq", None),
        P("dp", "seq", None),
        P(),
        P("dp", None, None),
        P(None, "seq"),
        P("seq", None),
        P("seq", "dp", None),
        P("dp", None, "seq"),
        P("dp", "seq", None),
        P("seq", None, "dp"),
    )
    out_specs = (
        P("dp", "seq", None),
        P("seq", "dp", None),
        P("dp", None, "seq"),
        P("dp", "seq", None),
        P("seq", None, "dp"),
    )
    return jax.shard_map(local, mesh=mesh, in_specs=in_specs, out_specs=out_specs, check_vma=False)
```

profile of v0, /device:TPU:1, one launch (start us, length us, event | category | flops | bytes accessed | tf_op | source)
XLA Modules:
  0.0 405.4 jit_solution(10892588238444750715)
XLA Ops:
  7.2 0.0 copy-start
  7.2 0.0 copy-start.4
  7.2 0.0 copy-start.3
  7.2 0.0 copy-start.2
  7.2 0.0 all-gather.12.cloned.1.call-start
  7.3 0.7 all-gather.12.cloned.1.call-update
  7.9 0.0 all-gather.10.cloned.1.call-start
  8.0 0.7 all-gather.10.cloned.1.call-update
  8.7 0.0 all-reduce.5.cloned.1.call-start
  8.8 0.0 copy-done.4
  8.8 0.0 copy-done.3
  8.8 0.4 fusion.54
  9.2 30.6 %pmax.7 = f32[64]{0:T(128)S(1)} all-reduce(f32[64]{0:T(128)S(1)} %get-tuple-element.9), channel_id=1, replica_groups=mesh['dp'=2,'seq'=16] {'seq'}, use_global_device_ids=true, to_apply=%region_1.0 | all-reduce | flops 64 | bytes 512 | tf_op jit(solution)/shard_map/pmax | solution.py:47
  39.8 0.2 fusion.22
  40.0 33.2 %psum.21 = f32[64]{0:T(128)S(1)} all-reduce(f32[64]{0:T(128)S(1)} %get-tuple-element.7), channel_id=1, replica_groups=mesh['dp'=2,'seq'=16] {'seq'}, use_global_device_ids=true, to_apply=%region_3.0 | all-reduce | flops 64 | bytes 512 | tf_op jit(solution)/shard_map/psum | solution.py:48
  73.2 0.3 convolution_bitcast_fusion.1
  73.5 0.0 copy-done.2
  73.5 0.2 convolution_bitcast_fusion
  73.8 60.1 %all-reduce.6 = bf16[64,2,1280]{2,0,1:T(8,128)(2,1)S(1)} all-reduce(f32[64,2,1280]{2,0,1:T(8,128)S(1)} %pad_maximum_fusion), channel_id=1, replica_groups=mesh['dp'=2,'seq'=16] {'seq'}, use_global_device_ids=true, to_apply=%region_6.0 | all-reduce | flops 163840 | bytes 983040 | tf_op jit(solution)/shard_map/psum | solution.py:57
  133.9 6.8 %all_gather.31 = bf16[4,64,1280]{2,1,0:T(8,128)(2,1)S(1)} all-gather(bf16[4,64,640]{2,1,0:T(8,128)(2,1)} %param.19), channel_id=1, replica_groups=mesh['dp'=2,'seq'=16] {'dp'}, dimensions={2}, use_global_device_ids=true | all-gather | bytes 983040 | tf_op jit(solution)/shard_map/all_gather | solution.py:42
  140.7 0.3 fusion.33
  141.0 8.9 %all_gather.30 = bf16[4,1280,64]{1,2,0:T(8,128)(2,1)S(1)} all-gather(bf16[4,640,64]{1,2,0:T(8,128)(2,1)} %param.16), channel_id=1, replica_groups=mesh['dp'=2,'seq'=16] {'dp'}, dimensions={1}, use_global_device_ids=true | all-gather | bytes 983040 | tf_op jit(solution)/shard_map/all_gather | solution.py:39
  149.9 0.3 fusion.35
  150.3 0.0 copy-done.6
  150.3 0.6 dynamic-slice
  151.5 0.1 maximum_bitcast_fusion
  151.6 27.7 %all-gather.4 = bf16[16,4,128]{2,1,0:T(4,128)(2,1)S(1)} all-gather(bf16[1,4,128]{2,1,0:T(4,128)(2,1)S(1)} %maximum_bitcast_fusion), channel_id=1, replica_groups=mesh['dp'=2,'seq'=16] {'seq'}, dimensions={0}, use_global_device_ids=true | all-gather | bytes 17408 | tf_op jit(solution)/shard_map/all_gather | solution.py:68
  179.3 3.3 all-gather.2
  182.6 3.3 all-gather
  185.9 0.1 constant_dynamic-slice_fusion.4
  185.9 0.1 constant_dynamic-slice_fusion.5
  186.0 0.1 slice_bitcast_fusion.7
  186.1 1.2 fusion.2
  187.3 0.0 all-gather.12.cloned.1.call-done
  187.4 2.5 fusion.25
  189.9 0.0 copy-done
  189.9 0.4 convolution_add_fusion.1
  190.4 0.0 all-gather.10.cloned.1.call-done
  190.4 0.0 copy-start.5
  190.4 2.6 fusion.27
  193.0 0.0 copy-done.5
  193.0 0.4 fusion.16
  193.4 1.0 fusion.56
  194.4 3.2 fusion.17
  197.6 0.0 copy-done.1
  197.6 1.2 fusion.19
  198.8 0.1 pad_maximum_fusion.2
  198.9 55.1 %all-reduce.1 = bf16[64,128]{1,0:T(8,128)(2,1)S(1)} all-reduce(f32[64,128]{1,0:T(8,128)S(1)} %pad_maximum_fusion.2), channel_id=7, replica_groups=mesh['dp'=2,'seq'=16] {'seq'}, use_global_device_ids=true, to_apply=%region_8.0.clone | all-reduce | flops 8192 | bytes 49152
  254.0 0.2 fusion.42
  254.2 0.0 all-reduce.5.cloned.1.call-update
  254.3 3.4 all-gather.6
  257.6 0.1 fusion.55
  257.7 4.1 %all-gather.3 = bf16[128,2,320]{2,0,1:T(8,128)(2,1)S(1)} all-gather(bf16[64,2,320]{2,0,1:T(8,128)(2,1)S(1)} %pad_maximum_fusion.1), channel_id=5, replica_groups=mesh['dp'=2,'seq'=16] {'dp'}, dimensions={0}, use_global_device_ids=true | all-gather | bytes 245760 | tf_op jit(solution)/shard_map/all_gather | solution.py:110
  261.9 1.0 convolution_convert_fusion.3
  262.9 1.8 convolution_convert_fusion.1
  264.7 1.8 convolution_convert_fusion
  266.4 1.0 convolution_convert_fusion.2
  267.4 77.6 %all-reduce.5.cloned.1.call-done = f32[64,1280]{1,0:T(8,128)} async-done(((f32[64,1280]{1,0:T(8,128)}), f32[64,1280]{1,0:T(8,128)}) %all-reduce.5.cloned.1.call-update) | async-done | bytes 327696
  345.0 0.8 fusion.39
  345.8 21.8 %all-gather.5 = bf16[16,4,1280]{2,1,0:T(4,128)(2,1)S(1)} all-gather(bf16[1,4,1280]{2,1,0:T(4,128)(2,1)S(1)} %fusion.39), channel_id=1, replica_groups=mesh['dp'=2,'seq'=16] {'seq'}, dimensions={0}, use_global_device_ids=true | all-gather | bytes 174080 | tf_op jit(solution)/shard_map/all_gather | solution.py:96
  367.6 0.4 fusion.44
  368.1 0.5 multiply_reduce_fusion.1
  368.5 29.0 %psum.23 = f32[64]{0:T(128)S(1)} all-reduce(f32[64]{0:T(128)S(1)} %get-tuple-element.5), channel_id=1, replica_groups=mesh['dp'=2,'seq'=16] {'seq'}, use_global_device_ids=true, to_apply=%region_10.0 | all-reduce | flops 64 | bytes 512 | tf_op jit(solution)/shard_map/psum | solution.py:98
  397.5 1.3 fusion.1
  (15 shorter events, 0.3 us)
Async XLA Ops:
  7.2 182.8 %copy-start = (bf16[1280,320]{0,1:T(8,128)(2,1)S(1)}, bf16[1280,320]{0,1:T(8,128)(2,1)}, u32[]{:S(2)}) copy-start(bf16[1280,320]{0,1:T(8,128)(2,1)} %param.14) | copy-start | bytes 2457604
  7.2 1.6 copy-start.4
  7.2 1.6 copy-start.3
  7.2 66.3 %copy-start.2 = (bf16[1,256,1280]{2,1,0:T(8,128)(2,1)S(1)}, bf16[1,256,1280]{2,1,0:T(8,128)(2,1)}, u32[]{:S(2)}) copy-start(bf16[1,256,1280]{2,1,0:T(8,128)(2,1)} %param.11) | copy-start | bytes 1966084
  7.2 180.2 %all-gather.12.cloned.1.call-start = ((), (), s32[]{:S(2)}) async-start(), calls=%async_computation.1 | async-start | bytes 4718592 | tf_op jit(solution)/shard_map/all_gather | solution.py:40
  7.9 182.4 %all-gather.10.cloned.1.call-start = ((), (), s32[]{:S(2)}) async-start(), calls=%async_computation | async-start | bytes 4718592 | tf_op jit(solution)/shard_map/all_gather | solution.py:41
  8.7 336.3 %all-reduce.5.cloned.1.call-start = ((), (), s32[]{:S(2)}) async-start(), calls=%async_computation.2 | async-start | bytes 655360
  73.8 76.5 %copy-start.6 = (u32[32]{0:T(128)S(1)}, u32[32]{0:T(128)}, u32[]{:S(2)}) copy-start(u32[32]{0:T(128)} %constant.45) | copy-start | bytes 388
  190.4 2.6 copy-start.5
  194.4 3.2 copy-start.1
Sparse Core Ops, SparseCore 0:
  9.6 46.9 all-gather.11
  58.2 44.9 all-gather.9
  254.4 90.5 all-reduce.4
where the time goes:
time: 407 us; the launch traced here: 405 us
  blocking collectives  287 us (71%)
  waiting for transfers between devices  79 us (19%)
  matrix products  21.9 us (5%)
  between operations  14.6 us (4%)
    unnamed x4, waiting for transfers between devices  79 us
    psum x1, blocking collectives, local(): summed = lax.psum(stacked, 'seq')  60.1 us
    unnamed x1, blocking collectives  55.1 us
    psum x1, blocking collectives, local(): slot_total = lax.psum(jnp.sum(jnp.exp(logits - slot_peak), axis=0), 'seq')  33.2 us
    pmax x1, blocking collectives, local(): slot_peak = lax.pmax(jnp.max(logits, axis=0), 'seq')  30.6 us
    psum x1, blocking collectives, local(): lax.psum(jnp.sum(dispatch_low.astype(jnp.float32) * weight_grad, axis=0),...  29 us
    all_gather x1, blocking collectives, local(): lax.all_gather(jnp.concatenate([up_owned, back_owned], axis=1), 'seq', ax...  27.7 us
    all_gather x1, blocking collectives, local(): slot_grads = lax.all_gather(owned_grad, 'seq', axis=0, tiled=True)  21.8 us
  transfers between devices with their start and end apart: 3, of which 1 were waited for; matrix products, arithmetic and copies ran while one was open for 3% of the time, Pallas kernels for 0%

commit v1 on v0

v1 whole, which is shorter than its diff:
```python
import jax
import jax.numpy as jnp
from jax import lax
from jax.sharding import PartitionSpec as P

BOTH = ("dp", "seq")
STATS = 128


def gelu_backward(preact, upstream):
    return jax.vjp(jax.nn.gelu, preact)[1](upstream)[0]


def dot_first(left, right):
    return lax.dot_general(
        left, right, (((0,), (0,)), ((), ())), preferred_element_type=jnp.float32
    )


def dot_last(left, right):
    return lax.dot_general(
        left, right, (((1,), (1,)), ((), ())), preferred_element_type=jnp.float32
    )


def split(value):
    high = lax.reduce_precision(value, 8, 7)
    low = lax.reduce_precision(value - high, 8, 7)
    return high.astype(jnp.bfloat16), low.astype(jnp.bfloat16)


def joined(high, low):
    return high.astype(jnp.float32) + low.astype(jnp.float32)


def exchange(blocks):
    flat = blocks.reshape((-1,) + blocks.shape[2:])
    return lax.all_to_all(flat, BOTH, 0, 0, tiled=True).reshape(blocks.shape)


def local(
    tokens,
    cotangent,
    router,
    slot_outputs,
    base_in,
    base_out,
    in_left,
    in_right,
    out_left,
    out_right,
):
    groups, ring = lax.axis_size("dp"), lax.axis_size("seq")
    image_rows = tokens[0]
    cot_rows = cotangent[0]
    saved_outputs = slot_outputs[0]
    width = image_rows.shape[1]
    slots = router.shape[1]
    owned, slice_width, rank = in_left.shape
    members = in_right.shape[0]
    places = members // owned
    group, place = lax.axis_index("dp"), lax.axis_index("seq")

    logits = jnp.dot(image_rows, router, preferred_element_type=jnp.float32)
    peak_high, peak_low = split(jnp.max(logits, axis=0))
    near = jnp.exp(logits - joined(peak_high, peak_low))
    total_high, total_low = split(jnp.sum(near, axis=0))
    combine = jax.nn.softmax(logits, axis=1)
    sums = jnp.stack(
        [
            dot_first(near.astype(jnp.bfloat16), image_rows),
            dot_first(combine.astype(jnp.bfloat16), cot_rows),
        ],
        axis=1,
    ).astype(jnp.bfloat16)
    sums = sums.reshape(ring, owned, 2, groups, slice_width).transpose(3, 0, 1, 2, 4)
    sums = sums.reshape(groups, ring, owned, 2 * slice_width)
    stats = jnp.stack([peak_high, peak_low, total_high, total_low], axis=1)
    stats = jnp.pad(stats, ((0, 0), (0, STATS - 4))).reshape(1, ring, owned, STATS)
    stats = jnp.broadcast_to(stats, (groups, ring, owned, STATS))
    first = exchange(jnp.concatenate([sums, stats], axis=3))

    tail = 2 * slice_width
    peaks = joined(first[..., tail], first[..., tail + 1])
    totals = joined(first[..., tail + 2], first[..., tail + 3])
    peak = jnp.max(peaks, axis=1)
    near_scale = jnp.exp(peaks - peak[:, None])
    total = jnp.sum(near_scale * totals, axis=1)
    near_scale = near_scale / total[:, None]
    parts = first[..., :tail].astype(jnp.float32)
    slot_inputs = jnp.sum(parts[..., :slice_width] * near_scale[..., None], axis=1)
    inputs_own = slot_inputs.astype(jnp.bfloat16)
    grads_own = jnp.sum(parts[..., slice_width:], axis=1).astype(jnp.bfloat16)
    up_part = jnp.einsum("gjd,jdr->gjr", inputs_own, in_left, preferred_element_type=jnp.float32)
    back_part = jnp.einsum("gjd,jrd->gjr", grads_own, out_right, preferred_element_type=jnp.float32)
    second = jnp.concatenate(
        [inputs_own, grads_own, *split(up_part), *split(back_part)], axis=2
    )
    second = exchange(jnp.broadcast_to(second, (groups, ring) + second.shape))
    second = lax.dynamic_slice_in_dim(second, group * places, places, 1)

    def gathered(start):
        piece = second[..., start : start + slice_width]
        return piece.transpose(2, 1, 3, 0, 4).reshape(groups * members, width)

    def ranks(start):
        piece = joined(
            second[..., start : start + rank], second[..., start + rank : start + 2 * rank]
        )
        piece = jnp.sum(piece, axis=0).transpose(1, 0, 2, 3)
        return piece.reshape(groups, members, rank).astype(jnp.bfloat16)

    inputs_low, grads_low = gathered(0), gathered(slice_width)
    up_low, back_low = ranks(tail), ranks(tail + 2 * rank)
    hidden = base_in.shape[1]
    preact = jnp.dot(inputs_low, base_in, preferred_element_type=jnp.float32).reshape(
        groups, members, hidden
    ) + jnp.einsum("gjr,jrf->gjf", up_low, in_right, preferred_element_type=jnp.float32)
    hidden_low = jax.nn.gelu(preact).astype(jnp.bfloat16)
    hidden_grad = dot_last(grads_low, base_out).reshape(groups, members, hidden) + jnp.einsum(
        "gjr,jfr->gjf", back_low, out_left, preferred_element_type=jnp.float32
    )
    preact_grad = gelu_backward(preact, hidden_grad).astype(jnp.bfloat16)
    slot_term = dot_last(preact_grad.reshape(groups * members, hidden), base_in)
    down_term = jnp.einsum(
        "gjf,jrf->gjr", preact_grad, in_right, preferred_element_type=jnp.float32
    )
    value_term = jnp.einsum(
        "gjf,jfr->gjr", hidden_low, out_left, preferred_element_type=jnp.float32
    )
    slot_term = slot_term.astype(jnp.bfloat16).reshape(groups, places, owned, groups, slice_width)
    slot_term = slot_term.transpose(3, 1, 0, 2, 4)
    rank_term = jnp.concatenate([down_term, value_term], axis=2).astype(jnp.bfloat16)
    rank_term = rank_term.reshape(groups, places, owned, 2 * rank).transpose(1, 0, 2, 3)
    rank_term = jnp.broadcast_to(rank_term, (groups,) + rank_term.shape)
    third = jnp.concatenate([slot_term, rank_term], axis=4)
    third = lax.dynamic_update_slice_in_dim(
        jnp.zeros((groups, ring) + third.shape[2:], jnp.bfloat16), third, group * places, 1
    )
    third = exchange(third)
    third = lax.dynamic_index_in_dim(third, place // places, 0, keepdims=False)
    third = jnp.sum(third.astype(jnp.float32), axis=0)
    down_own = third[..., slice_width : slice_width + rank].astype(jnp.bfloat16)
    value_own = third[..., slice_width + rank :].astype(jnp.bfloat16)
    slot_grads_own = (
        third[..., :slice_width]
        + jnp.einsum("gjr,jdr->gjd", down_own, in_left, preferred_element_type=jnp.float32)
    ).astype(jnp.bfloat16)
    shift_part = jnp.sum(slot_grads_own.astype(jnp.float32) * slot_inputs, axis=2)
    stats = jnp.stack([*split(peak), *split(total), *split(shift_part)], axis=2)
    stats = jnp.pad(stats, ((0, 0), (0, 0), (0, STATS - 6)))
    fourth = jnp.concatenate([slot_grads_own, stats], axis=2)[:, None]
    fourth = exchange(jnp.broadcast_to(fourth, (groups, ring) + fourth.shape[2:]))
    slot_grads = fourth[..., :slice_width].transpose(1, 2, 0, 3).reshape(slots, width)
    stats = fourth[..., slice_width:].astype(jnp.float32).reshape(groups, slots, STATS)
    slot_peak = stats[0, :, 0] + stats[0, :, 1]
    slot_total = stats[0, :, 2] + stats[0, :, 3]
    shift_back = jnp.sum(stats[:, :, 4] + stats[:, :, 5], axis=0)

    dispatch = jnp.exp(logits - slot_peak) / slot_total
    dispatch_low = dispatch.astype(jnp.bfloat16)
    weight_grad = dot_last(image_rows, slot_grads)
    dispatch_logit = dispatch * (weight_grad - shift_back)
    mixing_grad = dot_last(cot_rows, saved_outputs)
    combine_logit = combine * (mixing_grad - jnp.sum(combine * mixing_grad, axis=1, keepdims=True))
    logit_grad = (dispatch_logit + combine_logit).astype(jnp.bfloat16)
    token_grad = (
        jnp.dot(dispatch_low, slot_grads, preferred_element_type=jnp.float32)
        + dot_last(logit_grad, router)
    ).astype(jnp.bfloat16)
    grad_in_right = jnp.einsum(
        "gjr,gjf->jrf", up_low, preact_grad, preferred_element_type=jnp.float32
    ).astype(jnp.bfloat16)
    grad_out_left = jnp.einsum(
        "gjf,gjr->jfr", hidden_low, back_low, preferred_element_type=jnp.float32
    ).astype(jnp.bfloat16)
    grad_in_left = jnp.einsum(
        "gjd,gjr->jdr", inputs_own, down_own, preferred_element_type=jnp.float32
    ).astype(jnp.bfloat16)
    grad_out_right = jnp.einsum(
        "gjr,gjd->jrd", value_own, grads_own, preferred_element_type=jnp.float32
    ).astype(jnp.bfloat16)
    return (token_grad[None], grad_in_left, grad_in_right, grad_out_left, grad_out_right)


def solution(mesh):
    in_specs = (
        P("dp", "seq", None),
        P("dp", "seq", None),
        P(),
        P("dp", None, None),
        P(None, "seq"),
        P("seq", None),
        P("seq", "dp", None),
        P("dp", None, "seq"),
        P("dp", "seq", None),
        P("seq", None, "dp"),
    )
    out_specs = (
        P("dp", "seq", None),
        P("seq", "dp", None),
        P("dp", None, "seq"),
        P("dp", "seq", None),
        P("seq", None, "dp"),
    )
    return jax.shard_map(local, mesh=mesh, in_specs=in_specs, out_specs=out_specs, check_vma=False)
```

time: 407 us -> 107 us (0.26)
  blocking collectives: 287 us -> 18.8 us
  waiting for transfers between devices: 79 us -> 37.4 us
  between operations: 14.6 us -> 1.27 us
  local copies, waits for them, and re-layouts: 1.1 us -> 10.7 us
  starting transfers between devices: 0.11 us -> 9.07 us
    psum x3 -> x0, blocking collectives: 122 us -> none  [the longest x1 60.1 us: local(): summed = lax.psum(stacked, 'seq')]
    all_gather x8 -> x0, blocking collectives: 79.3 us -> none  [the longest x1 27.7 us: local(): lax.all_gather(jnp.concatenate([up_owned, back_owned], axis=1), 'seq', ax...]
    unnamed x4 -> x0, waiting for transfers between devices: 79 us -> none
    unnamed x1 -> x0, blocking collectives: 55.1 us -> none
    all_to_all x0 -> x3, waiting for transfers between devices: none -> 37.4 us  [exchange(): return lax.all_to_all(flat, BOTH, 0, 0, tiled=True).reshape(blocks.shape)]
    pmax x1 -> x0, blocking collectives: 30.6 us -> none  [local(): slot_peak = lax.pmax(jnp.max(logits, axis=0), 'seq')]
    all_to_all x0 -> x1, blocking collectives: none -> 18.8 us  [exchange(): return lax.all_to_all(flat, BOTH, 0, 0, tiled=True).reshape(blocks.shape)]
    all_to_all x0 -> x3, starting transfers between devices: none -> 9.07 us  [exchange(): return lax.all_to_all(flat, BOTH, 0, 0, tiled=True).reshape(blocks.shape)]
  transfers between devices with their start and end apart: 3 -> 3, of which waited for: 1 -> 3; matrix products, arithmetic and copies ran while one was open for 3% -> 5% of each run, Pallas kernels for 0% -> 0%
where the time goes in v1:
time: 107 us; the launch traced here: 106 us
  waiting for transfers between devices  37.4 us (35%)
  matrix products  25 us (23%)
  blocking collectives  18.8 us (18%)
  local copies, waits for them, and re-layouts  10.7 us (10%)
  starting transfers between devices  9.07 us (8%)
  other arithmetic  3.97 us (4%)
  between operations  1.27 us (1%)
    all_to_all x3, waiting for transfers between devices, exchange(): return lax.all_to_all(flat, BOTH, 0, 0, tiled=True).reshape(blocks.shape)  37.4 us
    all_to_all x1, blocking collectives, exchange(): return lax.all_to_all(flat, BOTH, 0, 0, tiled=True).reshape(blocks.shape)  18.8 us
    all_to_all x3, starting transfers between devices, exchange(): return lax.all_to_all(flat, BOTH, 0, 0, tiled=True).reshape(blocks.shape)  9.07 us
    dot_general x4, matrix products, dot_last(): lax.dot_general(left, right, (((1,), (1,)), ((), ())), preferred_element_...  6.13 us
    dot_general x2, local copies, waits for them, and re-layouts, dot_first(): lax.dot_general(left, right, (((0,), (0,)), ((), ())), preferred_element_...  2.78 us
    dot_general x2, matrix products, dot_first(): lax.dot_general(left, right, (((0,), (0,)), ((), ())), preferred_element_...  2.2 us
  transfers between devices with their start and end apart: 3, of which 3 were waited for; matrix products, arithmetic and copies ran while one was open for 5% of the time, Pallas kernels for 0%

profile of v1, /device:TPU:1, one launch (start us, length us, event | category | flops | bytes accessed | tf_op | source)
XLA Modules:
  0.0 106.2 jit_solution(7220733094177408109)
XLA Ops:
  0.7 1.6 %fusion.83 = (f32[256]{0:T(256)S(1)}, f32[256,64]{0,1:T(8,128)S(1)}) fusion(bf16[1280,64]{0,1:T(8,128)(2,1)} %param.12, bf16[1,256,1280]{2,1,0:T(8,128)(2,1)} %param.10), kind=kOutput, calls=%fused_computation.154 | convolution fusion | flops 41959168 | bytes 885760 | tf_op jit(solution)/shard_map/dot_general | solution.py:64
  2.3 0.1 fusion.35
  2.5 1.4 %fusion.12 = f32[256,64]{0,1:T(8,128)S(1)} fusion(bf16[1,256,1280]{2,1,0:T(8,128)(2,1)} %param.11, bf16[1,64,1280]{2,1,0:T(8,128)(2,1)} %param.13), kind=kOutput, calls=%fused_computation.28 | convolution fusion | flops 41943040 | bytes 884736 | tf_op jit(solution)/shard_map/dot_general | solution.py:21
  3.9 1.3 %multiply_reduce_fusion = (f32[256]{0:T(256)}, f32[64]{0:T(128)S(1)}, bf16[64,256]{1,0:T(8,128)(2,1)}, bf16[64,256]{1,0:T(8,128)(2,1)}) fusion(f32[256,64]{0,1:T(8,128)S(1)} %fusion.12, f32[256]{0:T(256)S(1)} %get-tuple-element.13, f32[256,64]{0,1:T(8,128)S(1)} %get-tuple-element.32, f32[256]{0:T(256)S(1)} %get-tuple-element.31, f32[64]{0:T(128)S(1)} %fusion.73), kind=kLoop, calls=%fused_computation.60 | loop fusion | flops 130752 | bytes 200192 | tf_op jit(solution)/shard_map/reduce_sum | solution.py:165
  5.3 0.1 copy.251
  5.4 0.2 copy.244
  5.7 1.4 %dot_general.84 = bf16[16,4,256]{2,1,0:T(4,128)(2,1)} reshape(bf16[64,256]{1,0:T(8,128)(2,1)} %get-tuple-element.21) | data formatting | bytes 65536 | tf_op jit(solution)/shard_map/dot_general | solution.py:15
  7.0 0.2 copy.241
  7.3 1.4 %dot_general.80 = bf16[16,4,256]{2,1,0:T(4,128)(2,1)} reshape(bf16[64,256]{1,0:T(8,128)(2,1)} %get-tuple-element.22) | data formatting | bytes 65536 | tf_op jit(solution)/shard_map/dot_general | solution.py:15
  8.7 1.1 %fusion.3 = bf16[16,4,1,2,640]{4,0,3,1,2:T(8,128)(2,1)S(1)} fusion(bf16[2,640,256,1]{2,1,0,3:T(8,128)(2,1)S(1)} %bitcast.176, bf16[16,4,256,1]{2,1,0,3:T(4,128)(2,1)} %bitcast.198), kind=kOutput, calls=%fused_computation.11 | convolution fusion | flops 42024960 | bytes 851968 | tf_op jit(solution)/shard_map/dot_general | solution.py:15
  9.8 1.1 %fusion.2 = bf16[16,4,1,2,640]{4,0,3,1,2:T(8,128)(2,1)S(1)} fusion(bf16[2,640,256,1]{2,1,0,3:T(8,128)(2,1)S(1)} %bitcast.177, bf16[16,4,256,1]{2,1,0,3:T(4,128)(2,1)} %bitcast.199), kind=kOutput, calls=%fused_computation.10 | convolution fusion | flops 42024960 | bytes 851968 | tf_op jit(solution)/shard_map/dot_general | solution.py:15
  10.9 0.3 copy.195
  11.3 0.2 concatenate.28
  11.5 0.2 copy.198
  11.7 18.8 %all_to_all.20 = bf16[32,4,1408]{2,1,0:T(4,128)(2,1)S(1)} all-to-all(bf16[32,4,1408]{2,1,0:T(4,128)(2,1)S(1)} %copy.198), channel_id=1, replica_groups=mesh['dp'=2,'seq'=16] {'dp','seq'}, dimensions={0} | all-to-all | bytes 720896 | tf_op jit(solution)/shard_map/all_to_all | solution.py:38
  30.6 0.1 fusion.82
  30.8 0.1 copy.247
  30.9 0.1 copy.246
  31.0 0.1 copy.249
  31.2 0.1 copy.248
  31.3 0.1 fusion.62
  31.4 0.2 fusion.60
  31.5 0.1 divide_bitcast_fusion
  31.6 0.2 slice_reduce_fusion
  31.9 1.2 %fusion.57 = (bf16[2,4,64]{2,0,1:T(2,128)(2,1)S(1)}, bf16[2,4,64]{2,0,1:T(2,128)(2,1)S(1)}) fusion(bf16[2,4,640]{2,0,1:T(2,128)(2,1)S(1)} %convert_element_type.277, bf16[4,640,64]{1,2,0:T(8,128)(2,1)} %param.16), kind=kOutput, calls=%fused_computation.110 | convolution fusion | flops 657920 | bytes 339968 | tf_op jit(solution)/shard_map/gjd,jdr->gjr/dot_general | solution.py:94
  33.1 0.2 fusion.59
  33.3 0.1 concatenate.31
  33.4 1.1 %reshape.254 = bf16[32,2,4,1536]{3,2,1,0:T(4,128)(2,1)} broadcast(bf16[2,4,1536]{2,1,0:T(4,128)(2,1)S(1)} %copy.208), dimensions={1,2,3} | broadcast | bytes 811008 | tf_op jit(solution)/shard_map/reshape | solution.py:37
  34.5 3.0 %all-to-all-start.1 = ((bf16[32,2,4,1536]{3,2,1,0:T(4,128)(2,1)}), bf16[32,2,4,1536]{3,2,1,0:T(4,128)(2,1)S(1)}, u32[]{:S(2)}, u32[]{:S(2)}) async-start(bf16[32,2,4,1536]{3,2,1,0:T(4,128)(2,1)} %reshape.254), calls=%async_computation.1 | async-start | bytes 1572864 | tf_op jit(solution)/shard_map/all_to_all | solution.py:38
  37.5 21.0 %all-to-all-done.1 = bf16[32,2,4,1536]{3,2,1,0:T(4,128)(2,1)S(1)} async-done(((bf16[32,2,4,1536]{3,2,1,0:T(4,128)(2,1)}), bf16[32,2,4,1536]{3,2,1,0:T(4,128)(2,1)S(1)}, u32[]{:S(2)}, u32[]{:S(2)}) %all-to-all-start.1) | async-done | bytes 786464 | tf_op jit(solution)/shard_map/all_to_all | solution.py:38
  58.5 0.2 copy.209
  58.8 0.7 add_reduce_fusion.1
  59.5 0.1 copy.214
  59.7 0.1 dot_general.93
  59.8 0.7 copy.211
  60.5 1.8 %fusion.51 = f32[32,2,320]{2,1,0:T(2,128)S(1)} fusion(bf16[32,64,320]{2,1,0:T(8,128)(2,1)} %param.17, bf16[2,32,64]{2,1,0:T(8,128)(2,1)S(1)} %bitcast.193), kind=kOutput, calls=%fused_computation.100 | convolution fusion | flops 2621440 | bytes 1400832 | tf_op jit(solution)/shard_map/gjr,jrf->gjf/dot_general | solution.py:118
  62.3 0.4 multiply_convert_fusion
  62.7 1.3 %convolution_convert_fusion.7 = bf16[32,2,64]{2,1,0:T(2,128)(2,1)} fusion(bf16[32,320,64]{1,2,0:T(8,128)(2,1)S(1)} %copy-done, bf16[2,32,320]{2,1,0:T(8,128)(2,1)S(1)} %get-tuple-element.33), kind=kOutput, calls=%fused_computation.19 | convolution fusion | flops 2625536 | bytes 1359872 | tf_op jit(solution)/shard_map/gjf,jfr->gjr/dot_general | solution.py:128
  64.0 1.0 fusion.54
  65.0 0.1 copy.210
  65.1 0.1 dot_general.90
  65.3 1.5 %fusion.26 = bf16[2,32,320]{2,1,0:T(8,128)(2,1)S(1)} fusion(f32[2,32,320]{2,1,0:T(8,128)S(1)} %get-tuple-element.34, f32[32,2,320]{2,1,0:T(2,128)} %fusion.54, bf16[2,32,1280]{2,1,0:T(8,128)(2,1)S(1)} %dot_general.90, bf16[320,1280]{1,0:T(8,128)(2,1)} %param.15), kind=kOutput, calls=%fused_computation.54 | convolution fusion | flops 52858880 | bytes 1187840 | tf_op jit(solution)/shard_map/dot_general | solution.py:21
  66.8 2.0 %convolution_convert_fusion.8 = bf16[32,2,64]{2,1,0:T(2,128)(2,1)S(1)} fusion(bf16[32,64,320]{2,1,0:T(8,128)(2,1)} %param.17, bf16[2,32,320]{2,1,0:T(8,128)(2,1)S(1)} %fusion.26), kind=kOutput, calls=%fused_computation.20 | convolution fusion | flops 2625536 | bytes 1359872 | tf_op jit(solution)/shard_map/gjf,jrf->gjr/dot_general | solution.py:125
  68.9 0.1 maximum_bitcast_fusion.1
  69.0 0.3 convolution_convert_fusion
  69.4 1.1 copy.222
  70.5 3.1 %all-to-all-start.2 = ((bf16[32,2,4,768]{3,2,1,0:T(4,128)(2,1)}), bf16[32,2,4,768]{3,2,1,0:T(4,128)(2,1)S(1)}, u32[]{:S(2)}, u32[]{:S(2)}) async-start(bf16[32,2,4,768]{3,2,1,0:T(4,128)(2,1)} %copy.222), calls=%async_computation.2 | async-start | bytes 786432 | tf_op jit(solution)/shard_map/all_to_all | solution.py:38
  73.6 1.8 %convolution_convert_fusion.2 = bf16[32,64,320]{2,1,0:T(8,128)(2,1)} fusion(bf16[2,32,320]{2,1,0:T(8,128)(2,1)S(1)} %fusion.26, bf16[2,32,64]{2,1,0:T(8,128)(2,1)S(1)} %bitcast.194), kind=kOutput, calls=%fused_computation.5 | convolution fusion | flops 3276800 | bytes 1359872 | tf_op jit(solution)/shard_map/gjr,gjf->jrf/dot_general | solution.py:171
  75.4 1.8 %convolution_convert_fusion.1 = bf16[32,320,64]{1,2,0:T(8,128)(2,1)} fusion(bf16[2,32,320]{2,1,0:T(8,128)(2,1)S(1)} %get-tuple-element.33, bf16[2,32,64]{2,1,0:T(8,128)(2,1)S(1)} %bitcast.196), kind=kOutput, calls=%fused_computation.4 | convolution fusion | flops 3276800 | bytes 1359872 | tf_op jit(solution)/shard_map/gjf,gjr->jfr/dot_general | solution.py:174
  77.1 9.1 %all-to-all-done.2 = bf16[32,2,4,768]{3,2,1,0:T(4,128)(2,1)S(1)} async-done(((bf16[32,2,4,768]{3,2,1,0:T(4,128)(2,1)}), bf16[32,2,4,768]{3,2,1,0:T(4,128)(2,1)S(1)}, u32[]{:S(2)}, u32[]{:S(2)}) %all-to-all-start.2) | async-done | bytes 393248 | tf_op jit(solution)/shard_map/all_to_all | solution.py:38
  86.4 0.3 multiply_reduce_fusion.1
  86.7 0.1 copy.227
  86.8 0.1 copy.252
  87.0 0.7 broadcast_in_dim.16
  87.7 3.0 %all-to-all-start.3 = ((bf16[32,4,768]{2,1,0:T(4,128)(2,1)}), bf16[32,4,768]{2,1,0:T(4,128)(2,1)S(1)}, u32[]{:S(2)}, u32[]{:S(2)}) async-start(bf16[32,4,768]{2,1,0:T(4,128)(2,1)} %bitcast.49), calls=%async_computation.3 | async-start | bytes 393216 | tf_op jit(solution)/shard_map/all_to_all | solution.py:38
  90.8 1.0 convolution_convert_fusion.4
  91.8 1.1 %convolution_convert_fusion.3 = bf16[4,64,640]{2,1,0:T(8,128)(2,1)} fusion(bf16[2,4,640]{2,0,1:T(2,128)(2,1)S(1)} %copy-done.10, bf16[2,4,768]{2,0,1:T(2,128)(2,1)S(1)} %copy.281), kind=kOutput, calls=%fused_computation.6 | convolution fusion | flops 819200 | bytes 339968 | tf_op jit(solution)/shard_map/gjr,gjd->jrd/dot_general | solution.py:180
  92.9 7.3 %all-to-all-done.3 = bf16[32,4,768]{2,1,0:T(4,128)(2,1)S(1)} async-done(((bf16[32,4,768]{2,1,0:T(4,128)(2,1)}), bf16[32,4,768]{2,1,0:T(4,128)(2,1)S(1)}, u32[]{:S(2)}, u32[]{:S(2)}) %all-to-all-start.3) | async-done | bytes 196640 | tf_op jit(solution)/shard_map/all_to_all | solution.py:38
  100.3 0.2 fusion.38
  100.5 0.7 fusion.29
  101.2 0.1 copy.232
  101.4 0.6 copy-done.5
  102.0 1.3 %fusion.43 = f32[256,1280]{1,0:T(8,128)S(1)} fusion(bf16[64,1280]{1,0:T(8,128)(2,1)S(1)} %bitcast.185, f32[256,64]{0,1:T(8,128)} %copy-done.4, f32[64]{0:T(128)S(1)} %get-tuple-element.12, f32[64]{0:T(128)S(1)} %get-tuple-element.11), kind=kOutput, calls=%fused_computation.81 | convolution fusion | flops 41992192 | bytes 1540608 | tf_op jit(solution)/shard_map/dot_general | solution.py:168
  103.3 2.9 %fusion.1 = bf16[1,256,1280]{2,1,0:T(8,128)(2,1)} fusion(f32[256,1280]{1,0:T(8,128)S(1)} %fusion.43, bf16[1280,64]{0,1:T(8,128)(2,1)} %param.12, bf16[64,1280]{1,0:T(8,128)(2,1)} %bitcast.186, bf16[1,256,1280]{2,1,0:T(8,128)(2,1)S(1)} %copy-done.1, f32[256,64]{0,1:T(8,128)} %copy-done.6, f32[256]{0:T(256)} %get-tuple-element.9, f32[64]{0:T(128)} %fusion.29, ...), kind=kOutput, calls=%fused_computation.2 | convolution fusion | flops 84705280 | bytes 3084032 | tf_op jit(solution)/shard_map/dot_general | solution.py:21
  (85 shorter events, 0.9 us)
Async XLA Ops:
  0.6 62.1 %copy-start = (bf16[32,320,64]{1,2,0:T(8,128)(2,1)S(1)}, bf16[32,320,64]{1,2,0:T(8,128)(2,1)}, u32[]{:S(2)}) copy-start(bf16[32,320,64]{1,2,0:T(8,128)(2,1)} %param.18) | copy-start | bytes 3932164
  0.6 6.4 %copy-start.1 = (bf16[1,256,1280]{2,1,0:T(8,128)(2,1)S(1)}, bf16[1,256,1280]{2,1,0:T(8,128)(2,1)}, u32[]{:S(2)}) copy-start(bf16[1,256,1280]{2,1,0:T(8,128)(2,1)} %param.10) | copy-start | bytes 1966084
  0.7 4.7 %copy-start.3 = (bf16[1,256,1280]{2,1,0:T(8,128)(2,1)S(1)}, bf16[1,256,1280]{2,1,0:T(8,128)(2,1)}, u32[]{:S(2)}) copy-start(bf16[1,256,1280]{2,1,0:T(8,128)(2,1)} %param.11) | copy-start | bytes 1966084
  2.3 1.6 %copy-start.4 = (f32[256,64]{0,1:T(8,128)}, f32[256,64]{0,1:T(8,128)S(1)}, u32[]{:S(2)}) copy-start(f32[256,64]{0,1:T(8,128)S(1)} %get-tuple-element.32) | copy-start | bytes 196612
  2.3 2.9 %copy-start.13 = (f32[256]{0:T(256)}, f32[256]{0:T(256)S(1)}, u32[]{:S(2)}) copy-start(f32[256]{0:T(256)S(1)} %get-tuple-element.31) | copy-start | bytes 3076
  2.4 2.8 %copy-start.16 = (f32[256]{0:T(256)}, f32[256]{0:T(256)S(1)}, u32[]{:S(2)}) copy-start(f32[256]{0:T(256)S(1)} %get-tuple-element.13) | copy-start | bytes 3076
  3.9 1.3 %copy-start.6 = (f32[256,64]{0,1:T(8,128)}, f32[256,64]{0,1:T(8,128)S(1)}, u32[]{:S(2)}) copy-start(f32[256,64]{0,1:T(8,128)S(1)} %fusion.12) | copy-start | bytes 196612
  30.6 2.5 %copy-start.22 = (bf16[4,64,640]{2,1,0:T(8,128)(2,1)S(1)}, bf16[4,64,640]{2,1,0:T(8,128)(2,1)}, u32[]{:S(2)}) copy-start(bf16[4,64,640]{2,1,0:T(8,128)(2,1)} %param.19) | copy-start | bytes 983044
  31.5 3.0 %copy-start.18 = (f32[2,4]{1,0:T(2,128)}, f32[2,4]{1,0:T(2,128)S(1)}, u32[]{:S(2)}) copy-start(f32[2,4]{1,0:T(2,128)S(1)} %fusion.60) | copy-start | bytes 100
  31.8 1.5 %copy-start.11 = (f32[2,4,640]{2,0,1:T(2,128)}, f32[2,4,640]{2,0,1:T(2,128)S(1)}, u32[]{:S(2)}) copy-start(f32[2,4,640]{2,0,1:T(2,128)S(1)} %get-tuple-element.8) | copy-start | bytes 61444
  31.8 2.7 %copy-start.9 = (bf16[2,4,640]{2,0,1:T(2,128)(2,1)}, bf16[2,4,640]{2,0,1:T(2,128)(2,1)S(1)}, u32[]{:S(2)}) copy-start(bf16[2,4,640]{2,0,1:T(2,128)(2,1)S(1)} %get-tuple-element.7) | copy-start | bytes 30724
  31.9 2.7 %copy-start.7 = (bf16[2,4,640]{2,0,1:T(2,128)(2,1)}, bf16[2,4,640]{2,0,1:T(2,128)(2,1)S(1)}, u32[]{:S(2)}) copy-start(bf16[2,4,640]{2,0,1:T(2,128)(2,1)S(1)} %convert_element_type.277) | copy-start | bytes 30724
  34.5 24.0 %all-to-all-start.1 = ((bf16[32,2,4,1536]{3,2,1,0:T(4,128)(2,1)}), bf16[32,2,4,1536]{3,2,1,0:T(4,128)(2,1)S(1)}, u32[]{:S(2)}, u32[]{:S(2)}) async-start(bf16[32,2,4,1536]{3,2,1,0:T(4,128)(2,1)} %reshape.254), calls=%async_computation.1 | async-start | bytes 1572864 | tf_op jit(solution)/shard_map/all_to_all | solution.py:38
  37.5 21.2 %copy-start.20 = (bf16[2,4,6]{1,0,2:T(2,128)(2,1)}, bf16[2,4,6]{1,0,2:T(2,128)(2,1)S(1)}, u32[]{:S(2)}) copy-start(bf16[2,4,6]{1,0,2:T(2,128)(2,1)S(1)} %constant_dynamic-update-slice_fusion.4) | copy-start | bytes 292
  59.5 2.8 %copy-start.2 = (bf16[1280,320]{0,1:T(8,128)(2,1)S(1)}, bf16[1280,320]{0,1:T(8,128)(2,1)}, u32[]{:S(2)}) copy-start(bf16[1280,320]{0,1:T(8,128)(2,1)} %param.14) | copy-start | bytes 2457604
  65.2 3.6 %copy-start.15 = (bf16[32,2,64]{2,1,0:T(2,128)(2,1)S(1)}, bf16[32,2,64]{2,1,0:T(2,128)(2,1)}, u32[]{:S(2)}) copy-start(bf16[32,2,64]{2,1,0:T(2,128)(2,1)} %convolution_convert_fusion.7) | copy-start | bytes 24580
  69.3 4.3 %copy-start.19 = (f32[2,4]{1,0:T(2,128)S(1)}, f32[2,4]{1,0:T(2,128)}, u32[]{:S(2)}) copy-start(f32[2,4]{1,0:T(2,128)} %copy-done.18) | copy-start | bytes 100
  69.3 4.3 %copy-start.21 = (bf16[2,4,6]{1,0,2:T(2,128)(2,1)S(1)}, bf16[2,4,6]{1,0,2:T(2,128)(2,1)}, u32[]{:S(2)}) copy-start(bf16[2,4,6]{1,0,2:T(2,128)(2,1)} %copy-done.20) | copy-start | bytes 292
  70.5 15.7 %all-to-all-start.2 = ((bf16[32,2,4,768]{3,2,1,0:T(4,128)(2,1)}), bf16[32,2,4,768]{3,2,1,0:T(4,128)(2,1)S(1)}, u32[]{:S(2)}, u32[]{:S(2)}) async-start(bf16[32,2,4,768]{3,2,1,0:T(4,128)(2,1)} %copy.222), calls=%async_computation.2 | async-start | bytes 786432 | tf_op jit(solution)/shard_map/all_to_all | solution.py:38
  75.4 11.0 %copy-start.12 = (f32[2,4,640]{2,0,1:T(2,128)S(1)}, f32[2,4,640]{2,0,1:T(2,128)}, u32[]{:S(2)}) copy-start(f32[2,4,640]{2,0,1:T(2,128)} %copy-done.11) | copy-start | bytes 61444
  75.4 11.0 %copy-start.23 = (bf16[4,640,64]{1,2,0:T(8,128)(2,1)S(1)}, bf16[4,640,64]{1,2,0:T(8,128)(2,1)}, u32[]{:S(2)}) copy-start(bf16[4,640,64]{1,2,0:T(8,128)(2,1)} %param.16) | copy-start | bytes 983044
  75.4 15.4 %copy-start.8 = (bf16[2,4,640]{2,0,1:T(2,128)(2,1)S(1)}, bf16[2,4,640]{2,0,1:T(2,128)(2,1)}, u32[]{:S(2)}) copy-start(bf16[2,4,640]{2,0,1:T(2,128)(2,1)} %copy-done.7) | copy-start | bytes 30724
  75.4 16.4 %copy-start.10 = (bf16[2,4,640]{2,0,1:T(2,128)(2,1)S(1)}, bf16[2,4,640]{2,0,1:T(2,128)(2,1)}, u32[]{:S(2)}) copy-start(bf16[2,4,640]{2,0,1:T(2,128)(2,1)} %copy-done.9) | copy-start | bytes 30724
  87.7 12.5 %all-to-all-start.3 = ((bf16[32,4,768]{2,1,0:T(4,128)(2,1)}), bf16[32,4,768]{2,1,0:T(4,128)(2,1)S(1)}, u32[]{:S(2)}, u32[]{:S(2)}) async-start(bf16[32,4,768]{2,1,0:T(4,128)(2,1)} %bitcast.49), calls=%async_computation.3 | async-start | bytes 393216 | tf_op jit(solution)/shard_map/all_to_all | solution.py:38
  100.2 3.1 %copy-start.14 = (f32[256]{0:T(256)S(1)}, f32[256]{0:T(256)}, u32[]{:S(2)}) copy-start(f32[256]{0:T(256)} %copy-done.13) | copy-start | bytes 3076
  100.2 3.1 %copy-start.17 = (f32[256]{0:T(256)S(1)}, f32[256]{0:T(256)}, u32[]{:S(2)}) copy-start(f32[256]{0:T(256)} %copy-done.16) | copy-start | bytes 3076
  101.4 0.7 copy-start.5

commit v2 on v1

--- a/solution.py
+++ b/solution.py
@@ -36,6 +36,36 @@
 def exchange(blocks):
     flat = blocks.reshape((-1,) + blocks.shape[2:])
     return lax.all_to_all(flat, BOTH, 0, 0, tiled=True).reshape(blocks.shape)
+
+
+def to_group(block, groups, ring):
+    places = ring // groups
+    here = lax.axis_index("seq")
+    received = []
+    for step in range(ring):
+        pairs = []
+        for group in range(groups):
+            for place in range(ring):
+                sender = place // places * ring + group * places + place % places
+                pairs.append((sender, group * ring + (place ^ step)))
+        received.append(lax.ppermute(block, BOTH, pairs))
+    blocks = jnp.stack(received)
+    bits = ring.bit_length() - 1
+    blocks = blocks.reshape((2,) * bits + block.shape)
+    for bit in range(bits):
+        turned = (here >> (bits - 1 - bit)) & 1
+        blocks = jnp.where(turned == 1, jnp.flip(blocks, bit), blocks)
+    return blocks.reshape((groups, places) + block.shape)
+
+
+def home(block, groups, ring):
+    places = ring // groups
+    pairs = [
+        (group * ring + place, place // places * ring + group * places + place % places)
+        for group in range(groups)
+        for place in range(ring)
+    ]
+    return lax.ppermute(block, BOTH, pairs)
 
 
 def local(
@@ -59,7 +89,6 @@
     owned, slice_width, rank = in_left.shape
     members = in_right.shape[0]
     places = members // owned
-    group, place = lax.axis_index("dp"), lax.axis_index("seq")
 
     logits = jnp.dot(image_rows, router, preferred_element_type=jnp.float32)
     peak_high, peak_low = split(jnp.max(logits, axis=0))
@@ -96,8 +125,7 @@
     second = jnp.concatenate(
         [inputs_own, grads_own, *split(up_part), *split(back_part)], axis=2
     )
-    second = exchange(jnp.broadcast_to(second, (groups, ring) + second.shape))
-    second = lax.dynamic_slice_in_dim(second, group * places, places, 1)
+    second = to_group(second, groups, ring)
 
     def gathered(start):
         piece = second[..., start : start + slice_width]
@@ -134,12 +162,9 @@
     rank_term = rank_term.reshape(groups, places, owned, 2 * rank).transpose(1, 0, 2, 3)
     rank_term = jnp.broadcast_to(rank_term, (groups,) + rank_term.shape)
     third = jnp.concatenate([slot_term, rank_term], axis=4)
-    third = lax.dynamic_update_slice_in_dim(
-        jnp.zeros((groups, ring) + third.shape[2:], jnp.bfloat16), third, group * places, 1
-    )
-    third = exchange(third)
-    third = lax.dynamic_index_in_dim(third, place // places, 0, keepdims=False)
-    third = jnp.sum(third.astype(jnp.float32), axis=0)
+    third = third.reshape((ring,) + third.shape[2:])
+    third = lax.all_to_all(third, "seq", 0, 0, tiled=True)
+    third = home(jnp.sum(third.astype(jnp.float32), axis=0), groups, ring)
     down_own = third[..., slice_width : slice_width + rank].astype(jnp.bfloat16)
     value_own = third[..., slice_width + rank :].astype(jnp.bfloat16)
     slot_grads_own = (

time: 107 us -> 123 us (1.15)
  starting transfers between devices: 9.07 us -> 52.5 us
  blocking collectives: 18.8 us -> 0 us
  waiting for transfers between devices: 37.4 us -> 27.6 us
  other arithmetic: 3.97 us -> 5.54 us
    ppermute x0 -> x17, starting transfers between devices: none -> 32.5 us  [the longest x16 31.8 us: to_group(): received.append(lax.ppermute(block, BOTH, pairs))]
    all_to_all x1 -> x0, blocking collectives: 18.8 us -> none  [exchange(): return lax.all_to_all(flat, BOTH, 0, 0, tiled=True).reshape(blocks.shape)]
    all_to_all x3 -> x2, waiting for transfers between devices: 37.4 us -> 19.1 us  [exchange(): return lax.all_to_all(flat, BOTH, 0, 0, tiled=True).reshape(blocks.shape)]
    all_to_all x0 -> x1, waiting for transfers between devices: none -> 6.5 us  [local(): third = lax.all_to_all(third, 'seq', 0, 0, tiled=True)]
    all_to_all x0 -> x1, starting transfers between devices: none -> 5.72 us  [local(): third = lax.all_to_all(third, 'seq', 0, 0, tiled=True)]
    all_to_all x3 -> x2, starting transfers between devices: 9.07 us -> 14.3 us  [exchange(): return lax.all_to_all(flat, BOTH, 0, 0, tiled=True).reshape(blocks.shape)]
    ppermute x0 -> x17, waiting for transfers between devices: none -> 2.02 us  [the longest x16 2.02 us: to_group(): received.append(lax.ppermute(block, BOTH, pairs))]
    select_n x0 -> x4, other arithmetic: none -> 1.39 us  [to_group(): blocks = jnp.where(turned == 1, jnp.flip(blocks, bit), blocks)]
  transfers between devices with their start and end apart: 3 -> 20, of which waited for: 3 -> 5; matrix products, arithmetic and copies ran while one was open for 5% -> 5% of each run, Pallas kernels for 0% -> 0%
where the time goes in v2:
time: 123 us; the launch traced here: 122 us
  starting transfers between devices  52.5 us (43%)
  waiting for transfers between devices  27.6 us (22%)
  matrix products  23.9 us (19%)
  local copies, waits for them, and re-layouts  11 us (9%)
  other arithmetic  5.54 us (5%)
  between operations  1.39 us (1%)
    ppermute x16, starting transfers between devices, to_group(): received.append(lax.ppermute(block, BOTH, pairs))  31.8 us
    all_to_all x2, waiting for transfers between devices, exchange(): return lax.all_to_all(flat, BOTH, 0, 0, tiled=True).reshape(blocks.shape)  19.1 us
    all_to_all x2, starting transfers between devices, exchange(): return lax.all_to_all(flat, BOTH, 0, 0, tiled=True).reshape(blocks.shape)  14.3 us
    all_to_all x1, waiting for transfers between devices, local(): third = lax.all_to_all(third, 'seq', 0, 0, tiled=True)  6.5 us
    dot_general x4, matrix products, dot_last(): lax.dot_general(left, right, (((1,), (1,)), ((), ())), preferred_element_...  6.21 us
    all_to_all x1, starting transfers between devices, local(): third = lax.all_to_all(third, 'seq', 0, 0, tiled=True)  5.72 us
    dot_general x2, local copies, waits for them, and re-layouts, dot_first(): lax.dot_general(left, right, (((0,), (0,)), ((), ())), preferred_element_...  2.78 us
    unnamed x70, local copies, waits for them, and re-layouts  2.57 us
  transfers between devices with their start and end apart: 20, of which 5 were waited for; matrix products, arithmetic and copies ran while one was open for 5% of the time, Pallas kernels for 0%

profile of v2, /device:TPU:1, one launch (start us, length us, event | category | flops | bytes accessed | tf_op | source)
XLA Modules:
  0.0 121.9 jit_solution(16807059806413592578)
XLA Ops:
  0.7 1.6 %fusion.84 = (f32[256]{0:T(256)S(1)}, f32[256,64]{0,1:T(8,128)S(1)}) fusion(bf16[1280,64]{0,1:T(8,128)(2,1)} %param.12, bf16[1,256,1280]{2,1,0:T(8,128)(2,1)} %param.10), kind=kOutput, calls=%fused_computation.170 | convolution fusion | flops 41959168 | bytes 885760 | tf_op jit(solution)/shard_map/dot_general | solution.py:93
  2.5 1.4 %fusion.10 = f32[256,64]{0,1:T(8,128)S(1)} fusion(bf16[1,256,1280]{2,1,0:T(8,128)(2,1)} %param.11, bf16[1,64,1280]{2,1,0:T(8,128)(2,1)} %param.13), kind=kOutput, calls=%fused_computation.30 | convolution fusion | flops 41943040 | bytes 884736 | tf_op jit(solution)/shard_map/dot_general | solution.py:21
  3.9 1.2 %multiply_reduce_fusion = (f32[256]{0:T(256)}, f32[64]{0:T(128)S(1)}, bf16[64,256]{1,0:T(8,128)(2,1)}, bf16[64,256]{1,0:T(8,128)(2,1)}) fusion(f32[256,64]{0,1:T(8,128)S(1)} %fusion.10, f32[256]{0:T(256)S(1)} %get-tuple-element.13, f32[256,64]{0,1:T(8,128)S(1)} %get-tuple-element.32, f32[256]{0:T(256)S(1)} %get-tuple-element.31, f32[64]{0:T(128)S(1)} %fusion.74), kind=kLoop, calls=%fused_computation.62 | loop fusion | flops 130752 | bytes 200192 | tf_op jit(solution)/shard_map/reduce_sum | solution.py:190
  5.4 0.2 copy.185
  5.6 1.4 %dot_general.84 = bf16[16,4,256]{2,1,0:T(4,128)(2,1)} reshape(bf16[64,256]{1,0:T(8,128)(2,1)} %get-tuple-element.21) | data formatting | bytes 65536 | tf_op jit(solution)/shard_map/dot_general | solution.py:15
  7.0 0.2 copy.182
  7.3 1.4 %dot_general.80 = bf16[16,4,256]{2,1,0:T(4,128)(2,1)} reshape(bf16[64,256]{1,0:T(8,128)(2,1)} %get-tuple-element.22) | data formatting | bytes 65536 | tf_op jit(solution)/shard_map/dot_general | solution.py:15
  8.6 1.1 fusion.3
  9.7 1.1 fusion.2
  10.9 0.3 copy.142
  11.5 0.9 copy.145
  12.4 7.1 %all-to-all-start = ((bf16[32,4,1408]{2,1,0:T(4,128)(2,1)}), bf16[32,4,1408]{2,1,0:T(4,128)(2,1)S(1)}, u32[]{:S(2)}, u32[]{:S(2)}) async-start(bf16[32,4,1408]{2,1,0:T(4,128)(2,1)} %copy.145), calls=%async_computation | async-start | bytes 720896 | tf_op jit(solution)/shard_map/all_to_all | solution.py:38
  19.5 11.9 %all-to-all-done = bf16[32,4,1408]{2,1,0:T(4,128)(2,1)S(1)} async-done(((bf16[32,4,1408]{2,1,0:T(4,128)(2,1)}), bf16[32,4,1408]{2,1,0:T(4,128)(2,1)S(1)}, u32[]{:S(2)}, u32[]{:S(2)}) %all-to-all-start) | async-done | bytes 360480 | tf_op jit(solution)/shard_map/all_to_all | solution.py:38
  32.7 0.6 copy-done.12
  33.4 1.2 fusion.56
  34.9 0.7 collective-permute-start
  35.6 0.8 collective-permute-start.1
  36.3 1.2 %collective-permute-start.2 = (bf16[2,4,1536]{2,0,1:T(2,128)(2,1)S(1)}, bf16[2,4,1536]{2,0,1:T(2,128)(2,1)S(1)}, u32[]{:S(2)}, u32[]{:S(2)}) collective-permute-start(bf16[2,4,1536]{2,0,1:T(2,128)(2,1)S(1)} %concatenate.31), channel_id=1, source_target_pairs={{0,2},{1,3},{2,0},{3,1},{4,6},{5,7},{6,4},{7,5},{16,10},{17,11},{1... | collective-permute-start | bytes 73736 | tf_op jit(solution)/shard_map/ppermute | solution.py:51
  37.6 0.5 collective-permute-start.3
  38.0 0.7 collective-permute-start.4
  38.8 1.1 collective-permute-start.5
  40.0 0.7 collective-permute-start.6
  40.7 2.0 %collective-permute-start.7 = (bf16[2,4,1536]{2,0,1:T(2,128)(2,1)S(1)}, bf16[2,4,1536]{2,0,1:T(2,128)(2,1)S(1)}, u32[]{:S(2)}, u32[]{:S(2)}) collective-permute-start(bf16[2,4,1536]{2,0,1:T(2,128)(2,1)S(1)} %concatenate.31), channel_id=1, source_target_pairs={{0,7},{1,6},{2,5},{3,4},{4,3},{5,2},{6,1},{7,0},{16,15},{17,14},{1... | collective-permute-start | bytes 73736 | tf_op jit(solution)/shard_map/ppermute | solution.py:51
  42.8 9.3 %collective-permute-start.8 = (bf16[2,4,1536]{2,0,1:T(2,128)(2,1)S(1)}, bf16[2,4,1536]{2,0,1:T(2,128)(2,1)S(1)}, u32[]{:S(2)}, u32[]{:S(2)}) collective-permute-start(bf16[2,4,1536]{2,0,1:T(2,128)(2,1)S(1)} %concatenate.31), channel_id=1, source_target_pairs={{0,8},{1,9},{2,10},{3,11},{4,12},{5,13},{6,14},{7,15},{16,0},{17,1... | collective-permute-start | bytes 73736 | tf_op jit(solution)/shard_map/ppermute | solution.py:51
  52.1 0.7 collective-permute-start.9
  52.8 6.8 %collective-permute-start.10 = (bf16[2,4,1536]{2,0,1:T(2,128)(2,1)S(1)}, bf16[2,4,1536]{2,0,1:T(2,128)(2,1)S(1)}, u32[]{:S(2)}, u32[]{:S(2)}) collective-permute-start(bf16[2,4,1536]{2,0,1:T(2,128)(2,1)S(1)} %concatenate.31), channel_id=1, source_target_pairs={{0,10},{1,11},{2,8},{3,9},{4,14},{5,15},{6,12},{7,13},{16,2},{17,3... | collective-permute-start | bytes 73736 | tf_op jit(solution)/shard_map/ppermute | solution.py:51
  59.7 0.8 collective-permute-start.11
  60.6 1.2 collective-permute-start.12
  61.8 1.3 %collective-permute-start.13 = (bf16[2,4,1536]{2,0,1:T(2,128)(2,1)S(1)}, bf16[2,4,1536]{2,0,1:T(2,128)(2,1)S(1)}, u32[]{:S(2)}, u32[]{:S(2)}) collective-permute-start(bf16[2,4,1536]{2,0,1:T(2,128)(2,1)S(1)} %concatenate.31), channel_id=1, source_target_pairs={{0,13},{1,12},{2,15},{3,14},{4,9},{5,8},{6,11},{7,10},{16,5},{17,4... | collective-permute-start | bytes 73736 | tf_op jit(solution)/shard_map/ppermute | solution.py:51
  63.1 0.4 collective-permute-start.14
  63.5 3.6 %collective-permute-start.15 = (bf16[2,4,1536]{2,0,1:T(2,128)(2,1)S(1)}, bf16[2,4,1536]{2,0,1:T(2,128)(2,1)S(1)}, u32[]{:S(2)}, u32[]{:S(2)}) collective-permute-start(bf16[2,4,1536]{2,0,1:T(2,128)(2,1)S(1)} %concatenate.31), channel_id=1, source_target_pairs={{0,15},{1,14},{2,13},{3,12},{4,11},{5,10},{6,9},{7,8},{16,7},{17,6... | collective-permute-start | bytes 73736 | tf_op jit(solution)/shard_map/ppermute | solution.py:51
  67.3 1.5 %collective-permute-done.14 = bf16[2,4,1536]{2,0,1:T(2,128)(2,1)S(1)} collective-permute-done((bf16[2,4,1536]{2,0,1:T(2,128)(2,1)S(1)}, bf16[2,4,1536]{2,0,1:T(2,128)(2,1)S(1)}, u32[]{:S(2)}, u32[]{:S(2)}) %collective-permute-start.14) | collective-permute-done | bytes 24608 | tf_op jit(solution)/shard_map/ppermute | solution.py:51
  68.8 0.5 collective-permute-done.15
  69.3 0.4 broadcast_select_fusion
  69.7 0.4 broadcast_select_fusion.1
  70.0 0.3 broadcast_select_fusion.2
  70.4 0.4 broadcast_select_fusion.3
  70.8 0.4 copy.155
  71.2 0.9 add_reduce_fusion.1
  72.0 0.2 slice_bitcast_fusion.2
  72.4 1.8 %fusion.50 = f32[32,2,320]{2,1,0:T(2,128)S(1)} fusion(bf16[32,64,320]{2,1,0:T(8,128)(2,1)} %param.17, bf16[2,32,64]{2,1,0:T(8,128)(2,1)} %bitcast.223), kind=kOutput, calls=%fused_computation.118 | convolution fusion | flops 2621440 | bytes 1400832 | tf_op jit(solution)/shard_map/gjr,jrf->gjf/dot_general | solution.py:146
  74.2 0.4 multiply_convert_fusion
  74.6 0.6 convolution_convert_fusion.7
  75.2 0.4 fusion.53
  75.6 0.8 dot_general.90
  76.4 1.6 %fusion.24 = bf16[2,32,320]{2,1,0:T(8,128)(2,1)S(1)} fusion(f32[2,32,320]{2,1,0:T(8,128)S(1)} %get-tuple-element.34, f32[32,2,320]{2,1,0:T(2,128)S(1)} %fusion.53, bf16[2,32,1280]{2,1,0:T(8,128)(2,1)} %dot_general.90, bf16[320,1280]{1,0:T(8,128)(2,1)} %param.15), kind=kOutput, calls=%fused_computation.56 | convolution fusion | flops 52858880 | bytes 1187840 | tf_op jit(solution)/shard_map/dot_general | solution.py:21
  78.0 2.0 %convolution_convert_fusion.8 = bf16[32,2,64]{2,1,0:T(2,128)(2,1)S(1)} fusion(bf16[32,64,320]{2,1,0:T(8,128)(2,1)} %param.17, bf16[2,32,320]{2,1,0:T(8,128)(2,1)S(1)} %fusion.24), kind=kOutput, calls=%fused_computation.20 | convolution fusion | flops 2625536 | bytes 1359872 | tf_op jit(solution)/shard_map/gjf,jrf->gjr/dot_general | solution.py:153
  80.2 0.3 convolution_convert_fusion
  80.6 0.8 copy.164
  81.4 5.7 %all-to-all-start.1 = ((bf16[16,2,4,768]{3,2,1,0:T(4,128)(2,1)}), bf16[16,2,4,768]{3,2,1,0:T(4,128)(2,1)S(1)}, u32[]{:S(2)}, u32[]{:S(2)}) async-start(bf16[16,2,4,768]{3,2,1,0:T(4,128)(2,1)} %copy.164), calls=%async_computation.1 | async-start | bytes 393216 | tf_op jit(solution)/shard_map/all_to_all | solution.py:166
  87.2 1.8 %convolution_convert_fusion.2 = bf16[32,64,320]{2,1,0:T(8,128)(2,1)} fusion(bf16[2,32,320]{2,1,0:T(8,128)(2,1)S(1)} %fusion.24, bf16[2,32,64]{2,1,0:T(8,128)(2,1)S(1)} %bitcast.224), kind=kOutput, calls=%fused_computation.5 | convolution fusion | flops 3276800 | bytes 1359872 | tf_op jit(solution)/shard_map/gjr,gjf->jrf/dot_general | solution.py:196
  88.9 6.5 %all-to-all-done.1 = bf16[16,2,4,768]{3,2,1,0:T(4,128)(2,1)S(1)} async-done(((bf16[16,2,4,768]{3,2,1,0:T(4,128)(2,1)}), bf16[16,2,4,768]{3,2,1,0:T(4,128)(2,1)S(1)}, u32[]{:S(2)}, u32[]{:S(2)}) %all-to-all-start.1) | async-done | bytes 196640 | tf_op jit(solution)/shard_map/all_to_all | solution.py:166
  95.6 0.7 collective-permute-start.16
  96.2 1.8 %convolution_convert_fusion.1 = bf16[32,320,64]{1,2,0:T(8,128)(2,1)} fusion(bf16[2,32,320]{2,1,0:T(8,128)(2,1)S(1)} %get-tuple-element.33, bf16[2,32,64]{2,1,0:T(8,128)(2,1)S(1)} %bitcast.222), kind=kOutput, calls=%fused_computation.4 | convolution fusion | flops 3276800 | bytes 1359872 | tf_op jit(solution)/shard_map/gjf,gjr->jfr/dot_general | solution.py:199
  98.0 0.3 multiply_reduce_fusion.1
  98.5 0.7 broadcast_in_dim.13
  99.3 7.2 %all-to-all-start.2 = ((bf16[32,4,768]{2,1,0:T(4,128)(2,1)}), bf16[32,4,768]{2,1,0:T(4,128)(2,1)S(1)}, u32[]{:S(2)}, u32[]{:S(2)}) async-start(bf16[32,4,768]{2,1,0:T(4,128)(2,1)} %bitcast.65), calls=%async_computation.2 | async-start | bytes 393216 | tf_op jit(solution)/shard_map/all_to_all | solution.py:38
  106.5 1.0 convolution_convert_fusion.4
  107.5 1.1 convolution_convert_fusion.3
  108.6 7.2 %all-to-all-done.2 = bf16[32,4,768]{2,1,0:T(4,128)(2,1)S(1)} async-done(((bf16[32,4,768]{2,1,0:T(4,128)(2,1)}), bf16[32,4,768]{2,1,0:T(4,128)(2,1)S(1)}, u32[]{:S(2)}, u32[]{:S(2)}) %all-to-all-start.2) | async-done | bytes 196640 | tf_op jit(solution)/shard_map/all_to_all | solution.py:38
  116.1 0.8 fusion.27
  117.1 0.7 copy-done.5
  117.8 1.3 %fusion.41 = f32[256,1280]{1,0:T(8,128)S(1)} fusion(bf16[64,1280]{1,0:T(8,128)(2,1)S(1)} %bitcast.213, f32[256,64]{0,1:T(8,128)} %copy-done.4, f32[64]{0:T(128)S(1)} %get-tuple-element.12, f32[64]{0:T(128)S(1)} %get-tuple-element.11), kind=kOutput, calls=%fused_computation.105 | convolution fusion | flops 41992192 | bytes 1540608 | tf_op jit(solution)/shard_map/dot_general | solution.py:193
  119.1 2.9 %fusion.1 = bf16[1,256,1280]{2,1,0:T(8,128)(2,1)} fusion(f32[256,1280]{1,0:T(8,128)S(1)} %fusion.41, bf16[1280,64]{0,1:T(8,128)(2,1)} %param.12, bf16[64,1280]{1,0:T(8,128)(2,1)} %bitcast.214, bf16[1,256,1280]{2,1,0:T(8,128)(2,1)S(1)} %copy-done.1, f32[256,64]{0,1:T(8,128)} %copy-done.6, f32[256]{0:T(256)} %get-tuple-element.9, f32[64]{0:T(128)} %fusion.27, ...), kind=kOutput, calls=%fused_computation.2 | convolution fusion | flops 84705280 | bytes 3084032 | tf_op jit(solution)/shard_map/dot_general | solution.py:21
  (130 shorter events, 3.9 us)
Async XLA Ops:
  0.6 74.0 %copy-start = (bf16[32,320,64]{1,2,0:T(8,128)(2,1)S(1)}, bf16[32,320,64]{1,2,0:T(8,128)(2,1)}, u32[]{:S(2)}) copy-start(bf16[32,320,64]{1,2,0:T(8,128)(2,1)} %param.18) | copy-start | bytes 3932164
  0.6 6.4 %copy-start.1 = (bf16[1,256,1280]{2,1,0:T(8,128)(2,1)S(1)}, bf16[1,256,1280]{2,1,0:T(8,128)(2,1)}, u32[]{:S(2)}) copy-start(bf16[1,256,1280]{2,1,0:T(8,128)(2,1)} %param.10) | copy-start | bytes 1966084
  0.7 4.7 %copy-start.3 = (bf16[1,256,1280]{2,1,0:T(8,128)(2,1)S(1)}, bf16[1,256,1280]{2,1,0:T(8,128)(2,1)}, u32[]{:S(2)}) copy-start(bf16[1,256,1280]{2,1,0:T(8,128)(2,1)} %param.11) | copy-start | bytes 1966084
  2.3 1.6 %copy-start.4 = (f32[256,64]{0,1:T(8,128)}, f32[256,64]{0,1:T(8,128)S(1)}, u32[]{:S(2)}) copy-start(f32[256,64]{0,1:T(8,128)S(1)} %get-tuple-element.32) | copy-start | bytes 196612
  2.3 2.9 %copy-start.14 = (f32[256]{0:T(256)}, f32[256]{0:T(256)S(1)}, u32[]{:S(2)}) copy-start(f32[256]{0:T(256)S(1)} %get-tuple-element.31) | copy-start | bytes 3076
  2.4 2.8 %copy-start.16 = (f32[256]{0:T(256)}, f32[256]{0:T(256)S(1)}, u32[]{:S(2)}) copy-start(f32[256]{0:T(256)S(1)} %get-tuple-element.13) | copy-start | bytes 3076
  3.9 1.3 %copy-start.6 = (f32[256,64]{0,1:T(8,128)}, f32[256,64]{0,1:T(8,128)S(1)}, u32[]{:S(2)}) copy-start(f32[256,64]{0,1:T(8,128)S(1)} %fusion.10) | copy-start | bytes 196612
  12.4 19.0 %all-to-all-start = ((bf16[32,4,1408]{2,1,0:T(4,128)(2,1)}), bf16[32,4,1408]{2,1,0:T(4,128)(2,1)S(1)}, u32[]{:S(2)}, u32[]{:S(2)}) async-start(bf16[32,4,1408]{2,1,0:T(4,128)(2,1)} %copy.145), calls=%async_computation | async-start | bytes 720896 | tf_op jit(solution)/shard_map/all_to_all | solution.py:38
  19.5 15.0 %copy-start.22 = (bf16[4,64,640]{2,1,0:T(8,128)(2,1)S(1)}, bf16[4,64,640]{2,1,0:T(8,128)(2,1)}, u32[]{:S(2)}) copy-start(bf16[4,64,640]{2,1,0:T(8,128)(2,1)} %param.19) | copy-start | bytes 983044
  32.4 37.6 %copy-start.18 = (f32[2,4]{1,0:T(2,128)}, f32[2,4]{1,0:T(2,128)S(1)}, u32[]{:S(2)}) copy-start(f32[2,4]{1,0:T(2,128)S(1)} %fusion.59) | copy-start | bytes 100
  32.7 0.6 copy-start.12
  32.7 37.3 %copy-start.10 = (bf16[2,4,640]{2,0,1:T(2,128)(2,1)}, bf16[2,4,640]{2,0,1:T(2,128)(2,1)S(1)}, u32[]{:S(2)}) copy-start(bf16[2,4,640]{2,0,1:T(2,128)(2,1)S(1)} %get-tuple-element.5) | copy-start | bytes 30724
  33.3 37.0 %copy-start.8 = (bf16[2,4,640]{2,0,1:T(2,128)(2,1)}, bf16[2,4,640]{2,0,1:T(2,128)(2,1)S(1)}, u32[]{:S(2)}) copy-start(bf16[2,4,640]{2,0,1:T(2,128)(2,1)S(1)} %convert_element_type.276) | copy-start | bytes 30724
  34.9 3.9 %collective-permute-start = (bf16[2,4,1536]{2,0,1:T(2,128)(2,1)S(1)}, bf16[2,4,1536]{2,0,1:T(2,128)(2,1)S(1)}, u32[]{:S(2)}, u32[]{:S(2)}) collective-permute-start(bf16[2,4,1536]{2,0,1:T(2,128)(2,1)S(1)} %concatenate.31), channel_id=1, source_target_pairs={{0,0},{1,1},{2,2},{3,3},{4,4},{5,5},{6,6},{7,7},{16,8},{17,9},{18,... | collective-permute-start | bytes 73736 | tf_op jit(solution)/shard_map/ppermute | solution.py:51
  35.6 4.4 %collective-permute-start.1 = (bf16[2,4,1536]{2,0,1:T(2,128)(2,1)S(1)}, bf16[2,4,1536]{2,0,1:T(2,128)(2,1)S(1)}, u32[]{:S(2)}, u32[]{:S(2)}) collective-permute-start(bf16[2,4,1536]{2,0,1:T(2,128)(2,1)S(1)} %concatenate.31), channel_id=1, source_target_pairs={{0,1},{1,0},{2,3},{3,2},{4,5},{5,4},{6,7},{7,6},{16,9},{17,8},{18,... | collective-permute-start | bytes 73736 | tf_op jit(solution)/shard_map/ppermute | solution.py:51
  36.3 4.4 %collective-permute-start.2 = (bf16[2,4,1536]{2,0,1:T(2,128)(2,1)S(1)}, bf16[2,4,1536]{2,0,1:T(2,128)(2,1)S(1)}, u32[]{:S(2)}, u32[]{:S(2)}) collective-permute-start(bf16[2,4,1536]{2,0,1:T(2,128)(2,1)S(1)} %concatenate.31), channel_id=1, source_target_pairs={{0,2},{1,3},{2,0},{3,1},{4,6},{5,7},{6,4},{7,5},{16,10},{17,11},{1... | collective-permute-start | bytes 73736 | tf_op jit(solution)/shard_map/ppermute | solution.py:51
  37.6 5.2 %collective-permute-start.3 = (bf16[2,4,1536]{2,0,1:T(2,128)(2,1)S(1)}, bf16[2,4,1536]{2,0,1:T(2,128)(2,1)S(1)}, u32[]{:S(2)}, u32[]{:S(2)}) collective-permute-start(bf16[2,4,1536]{2,0,1:T(2,128)(2,1)S(1)} %concatenate.31), channel_id=1, source_target_pairs={{0,3},{1,2},{2,1},{3,0},{4,7},{5,6},{6,5},{7,4},{16,11},{17,10},{1... | collective-permute-start | bytes 73736 | tf_op jit(solution)/shard_map/ppermute | solution.py:51
  38.0 14.0 %collective-permute-start.4 = (bf16[2,4,1536]{2,0,1:T(2,128)(2,1)S(1)}, bf16[2,4,1536]{2,0,1:T(2,128)(2,1)S(1)}, u32[]{:S(2)}, u32[]{:S(2)}) collective-permute-start(bf16[2,4,1536]{2,0,1:T(2,128)(2,1)S(1)} %concatenate.31), channel_id=1, source_target_pairs={{0,4},{1,5},{2,6},{3,7},{4,0},{5,1},{6,2},{7,3},{16,12},{17,13},{1... | collective-permute-start | bytes 73736 | tf_op jit(solution)/shard_map/ppermute | solution.py:51
  38.8 31.6 %copy-start.20 = (bf16[2,4,6]{1,0,2:T(2,128)(2,1)}, bf16[2,4,6]{1,0,2:T(2,128)(2,1)S(1)}, u32[]{:S(2)}) copy-start(bf16[2,4,6]{1,0,2:T(2,128)(2,1)S(1)} %constant_dynamic-update-slice_fusion.19) | copy-start | bytes 292
  38.8 14.0 %collective-permute-start.5 = (bf16[2,4,1536]{2,0,1:T(2,128)(2,1)S(1)}, bf16[2,4,1536]{2,0,1:T(2,128)(2,1)S(1)}, u32[]{:S(2)}, u32[]{:S(2)}) collective-permute-start(bf16[2,4,1536]{2,0,1:T(2,128)(2,1)S(1)} %concatenate.31), channel_id=1, source_target_pairs={{0,5},{1,4},{2,7},{3,6},{4,1},{5,0},{6,3},{7,2},{16,13},{17,12},{1... | collective-permute-start | bytes 73736 | tf_op jit(solution)/shard_map/ppermute | solution.py:51
  40.0 19.7 %collective-permute-start.6 = (bf16[2,4,1536]{2,0,1:T(2,128)(2,1)S(1)}, bf16[2,4,1536]{2,0,1:T(2,128)(2,1)S(1)}, u32[]{:S(2)}, u32[]{:S(2)}) collective-permute-start(bf16[2,4,1536]{2,0,1:T(2,128)(2,1)S(1)} %concatenate.31), channel_id=1, source_target_pairs={{0,6},{1,7},{2,4},{3,5},{4,2},{5,3},{6,0},{7,1},{16,14},{17,15},{1... | collective-permute-start | bytes 73736 | tf_op jit(solution)/shard_map/ppermute | solution.py:51
  40.7 19.8 %collective-permute-start.7 = (bf16[2,4,1536]{2,0,1:T(2,128)(2,1)S(1)}, bf16[2,4,1536]{2,0,1:T(2,128)(2,1)S(1)}, u32[]{:S(2)}, u32[]{:S(2)}) collective-permute-start(bf16[2,4,1536]{2,0,1:T(2,128)(2,1)S(1)} %concatenate.31), channel_id=1, source_target_pairs={{0,7},{1,6},{2,5},{3,4},{4,3},{5,2},{6,1},{7,0},{16,15},{17,14},{1... | collective-permute-start | bytes 73736 | tf_op jit(solution)/shard_map/ppermute | solution.py:51
  42.8 19.0 %collective-permute-start.8 = (bf16[2,4,1536]{2,0,1:T(2,128)(2,1)S(1)}, bf16[2,4,1536]{2,0,1:T(2,128)(2,1)S(1)}, u32[]{:S(2)}, u32[]{:S(2)}) collective-permute-start(bf16[2,4,1536]{2,0,1:T(2,128)(2,1)S(1)} %concatenate.31), channel_id=1, source_target_pairs={{0,8},{1,9},{2,10},{3,11},{4,12},{5,13},{6,14},{7,15},{16,0},{17,1... | collective-permute-start | bytes 73736 | tf_op jit(solution)/shard_map/ppermute | solution.py:51
  52.1 11.0 %collective-permute-start.9 = (bf16[2,4,1536]{2,0,1:T(2,128)(2,1)S(1)}, bf16[2,4,1536]{2,0,1:T(2,128)(2,1)S(1)}, u32[]{:S(2)}, u32[]{:S(2)}) collective-permute-start(bf16[2,4,1536]{2,0,1:T(2,128)(2,1)S(1)} %concatenate.31), channel_id=1, source_target_pairs={{0,9},{1,8},{2,11},{3,10},{4,13},{5,12},{6,15},{7,14},{16,1},{17,0... | collective-permute-start | bytes 73736 | tf_op jit(solution)/shard_map/ppermute | solution.py:51
  52.8 10.7 %collective-permute-start.10 = (bf16[2,4,1536]{2,0,1:T(2,128)(2,1)S(1)}, bf16[2,4,1536]{2,0,1:T(2,128)(2,1)S(1)}, u32[]{:S(2)}, u32[]{:S(2)}) collective-permute-start(bf16[2,4,1536]{2,0,1:T(2,128)(2,1)S(1)} %concatenate.31), channel_id=1, source_target_pairs={{0,10},{1,11},{2,8},{3,9},{4,14},{5,15},{6,12},{7,13},{16,2},{17,3... | collective-permute-start | bytes 73736 | tf_op jit(solution)/shard_map/ppermute | solution.py:51
  59.7 7.4 %collective-permute-start.11 = (bf16[2,4,1536]{2,0,1:T(2,128)(2,1)S(1)}, bf16[2,4,1536]{2,0,1:T(2,128)(2,1)S(1)}, u32[]{:S(2)}, u32[]{:S(2)}) collective-permute-start(bf16[2,4,1536]{2,0,1:T(2,128)(2,1)S(1)} %concatenate.31), channel_id=1, source_target_pairs={{0,11},{1,10},{2,9},{3,8},{4,15},{5,14},{6,13},{7,12},{16,3},{17,2... | collective-permute-start | bytes 73736 | tf_op jit(solution)/shard_map/ppermute | solution.py:51
  60.6 6.6 %collective-permute-start.12 = (bf16[2,4,1536]{2,0,1:T(2,128)(2,1)S(1)}, bf16[2,4,1536]{2,0,1:T(2,128)(2,1)S(1)}, u32[]{:S(2)}, u32[]{:S(2)}) collective-permute-start(bf16[2,4,1536]{2,0,1:T(2,128)(2,1)S(1)} %concatenate.31), channel_id=1, source_target_pairs={{0,12},{1,13},{2,14},{3,15},{4,8},{5,9},{6,10},{7,11},{16,4},{17,5... | collective-permute-start | bytes 73736 | tf_op jit(solution)/shard_map/ppermute | solution.py:51
  61.8 5.4 %collective-permute-start.13 = (bf16[2,4,1536]{2,0,1:T(2,128)(2,1)S(1)}, bf16[2,4,1536]{2,0,1:T(2,128)(2,1)S(1)}, u32[]{:S(2)}, u32[]{:S(2)}) collective-permute-start(bf16[2,4,1536]{2,0,1:T(2,128)(2,1)S(1)} %concatenate.31), channel_id=1, source_target_pairs={{0,13},{1,12},{2,15},{3,14},{4,9},{5,8},{6,11},{7,10},{16,5},{17,4... | collective-permute-start | bytes 73736 | tf_op jit(solution)/shard_map/ppermute | solution.py:51
  63.1 5.7 %collective-permute-start.14 = (bf16[2,4,1536]{2,0,1:T(2,128)(2,1)S(1)}, bf16[2,4,1536]{2,0,1:T(2,128)(2,1)S(1)}, u32[]{:S(2)}, u32[]{:S(2)}) collective-permute-start(bf16[2,4,1536]{2,0,1:T(2,128)(2,1)S(1)} %concatenate.31), channel_id=1, source_target_pairs={{0,14},{1,15},{2,12},{3,13},{4,10},{5,11},{6,8},{7,9},{16,6},{17,7... | collective-permute-start | bytes 73736 | tf_op jit(solution)/shard_map/ppermute | solution.py:51
  63.5 5.8 %collective-permute-start.15 = (bf16[2,4,1536]{2,0,1:T(2,128)(2,1)S(1)}, bf16[2,4,1536]{2,0,1:T(2,128)(2,1)S(1)}, u32[]{:S(2)}, u32[]{:S(2)}) collective-permute-start(bf16[2,4,1536]{2,0,1:T(2,128)(2,1)S(1)} %concatenate.31), channel_id=1, source_target_pairs={{0,15},{1,14},{2,13},{3,12},{4,11},{5,10},{6,9},{7,8},{16,7},{17,6... | collective-permute-start | bytes 73736 | tf_op jit(solution)/shard_map/ppermute | solution.py:51
  71.2 3.0 %copy-start.2 = (bf16[1280,320]{0,1:T(8,128)(2,1)S(1)}, bf16[1280,320]{0,1:T(8,128)(2,1)}, u32[]{:S(2)}) copy-start(bf16[1280,320]{0,1:T(8,128)(2,1)} %param.14) | copy-start | bytes 2457604
  80.1 7.0 %copy-start.19 = (f32[2,4]{1,0:T(2,128)S(1)}, f32[2,4]{1,0:T(2,128)}, u32[]{:S(2)}) copy-start(f32[2,4]{1,0:T(2,128)} %copy-done.18) | copy-start | bytes 100
  80.1 7.0 %copy-start.21 = (bf16[2,4,6]{1,0,2:T(2,128)(2,1)S(1)}, bf16[2,4,6]{1,0,2:T(2,128)(2,1)}, u32[]{:S(2)}) copy-start(bf16[2,4,6]{1,0,2:T(2,128)(2,1)} %copy-done.20) | copy-start | bytes 292
  80.1 7.1 %copy-start.7 = (bf16[8,2,4,64]{3,2,0,1:T(4,128)(2,1)S(1)}, bf16[8,2,4,64]{3,2,0,1:T(4,128)(2,1)}, u32[]{:S(2)}) copy-start(bf16[8,2,4,64]{3,2,0,1:T(4,128)(2,1)} %get-tuple-element.8) | copy-start | bytes 24580
  81.4 14.0 %all-to-all-start.1 = ((bf16[16,2,4,768]{3,2,1,0:T(4,128)(2,1)}), bf16[16,2,4,768]{3,2,1,0:T(4,128)(2,1)S(1)}, u32[]{:S(2)}, u32[]{:S(2)}) async-start(bf16[16,2,4,768]{3,2,1,0:T(4,128)(2,1)} %copy.164), calls=%async_computation.1 | async-start | bytes 393216 | tf_op jit(solution)/shard_map/all_to_all | solution.py:166
  87.2 10.8 %copy-start.13 = (f32[2,4,640]{2,0,1:T(2,128)S(1)}, f32[2,4,640]{2,0,1:T(2,128)}, u32[]{:S(2)}) copy-start(f32[2,4,640]{2,0,1:T(2,128)} %copy-done.12) | copy-start | bytes 61444
  87.2 10.8 %copy-start.23 = (bf16[4,640,64]{1,2,0:T(8,128)(2,1)S(1)}, bf16[4,640,64]{1,2,0:T(8,128)(2,1)}, u32[]{:S(2)}) copy-start(bf16[4,640,64]{1,2,0:T(8,128)(2,1)} %param.16) | copy-start | bytes 983044
  88.9 17.6 %copy-start.9 = (bf16[2,4,640]{2,0,1:T(2,128)(2,1)S(1)}, bf16[2,4,640]{2,0,1:T(2,128)(2,1)}, u32[]{:S(2)}) copy-start(bf16[2,4,640]{2,0,1:T(2,128)(2,1)} %copy-done.8) | copy-start | bytes 30724
  95.5 12.0 %copy-start.11 = (bf16[2,4,640]{2,0,1:T(2,128)(2,1)S(1)}, bf16[2,4,640]{2,0,1:T(2,128)(2,1)}, u32[]{:S(2)}) copy-start(bf16[2,4,640]{2,0,1:T(2,128)(2,1)} %copy-done.10) | copy-start | bytes 30724
  95.6 2.4 %collective-permute-start.16 = (f32[2,4,768]{2,0,1:T(2,128)S(1)}, f32[2,4,768]{2,0,1:T(2,128)S(1)}, u32[]{:S(2)}, u32[]{:S(2)}) collective-permute-start(f32[2,4,768]{2,0,1:T(2,128)S(1)} %copy.166), channel_id=1, source_target_pairs={{0,0},{1,1},{2,2},{3,3},{4,4},{5,5},{6,6},{7,7},{8,16},{9,17},{10,... | collective-permute-start | bytes 73736 | tf_op jit(solution)/shard_map/ppermute | solution.py:68
  99.3 16.5 %all-to-all-start.2 = ((bf16[32,4,768]{2,1,0:T(4,128)(2,1)}), bf16[32,4,768]{2,1,0:T(4,128)(2,1)S(1)}, u32[]{:S(2)}, u32[]{:S(2)}) async-start(bf16[32,4,768]{2,1,0:T(4,128)(2,1)} %bitcast.65), calls=%async_computation.2 | async-start | bytes 393216 | tf_op jit(solution)/shard_map/all_to_all | solution.py:38
  115.8 3.2 %copy-start.15 = (f32[256]{0:T(256)S(1)}, f32[256]{0:T(256)}, u32[]{:S(2)}) copy-start(f32[256]{0:T(256)} %copy-done.14) | copy-start | bytes 3076
  115.9 3.2 %copy-start.17 = (f32[256]{0:T(256)S(1)}, f32[256]{0:T(256)}, u32[]{:S(2)}) copy-start(f32[256]{0:T(256)} %copy-done.16) | copy-start | bytes 3076
  117.1 0.7 copy-start.5

commit v3 on v1

--- a/solution.py
+++ b/solution.py
@@ -1,6 +1,10 @@
+import functools
+
 import jax
 import jax.numpy as jnp
 from jax import lax
+from jax.experimental import pallas as pl
+from jax.experimental.pallas import tpu as pltpu
 from jax.sharding import PartitionSpec as P
 
 BOTH = ("dp", "seq")
@@ -38,7 +42,7 @@
     return lax.all_to_all(flat, BOTH, 0, 0, tiled=True).reshape(blocks.shape)
 
 
-def local(
+def local_plain(
     tokens,
     cotangent,
     router,
@@ -183,6 +187,364 @@
     return (token_grad[None], grad_in_left, grad_in_right, grad_out_left, grad_out_right)
 
 
+def dot_plain(left, right):
+    return jnp.dot(left, right, preferred_element_type=jnp.float32)
+
+
+def halves(value):
+    high = value.astype(jnp.bfloat16).astype(jnp.float32)
+    low = (value - high).astype(jnp.bfloat16).astype(jnp.float32)
+    return high, low
+
+
+def in_lanes(columns, shape):
+    lane = lax.broadcasted_iota(jnp.int32, shape, len(shape) - 1)
+    out = jnp.zeros(shape, jnp.float32)
+    for number, column in enumerate(columns):
+        out = jnp.where(lane == number, column, out)
+    return out
+
+
+def own_block(value, owned):
+    rows, rank = value.shape
+    wide = jnp.concatenate([value] * owned, axis=1)
+    shape = (rows, owned * rank)
+    block = lax.broadcasted_iota(jnp.int32, shape, 1) // rank
+    expert = lax.broadcasted_iota(jnp.int32, shape, 0) % owned
+    return jnp.where(block == expert, wide, 0.0).astype(jnp.bfloat16)
+
+
+def from_own_block(value, owned):
+    rows, wide = value.shape
+    rank = wide // owned
+    block = lax.broadcasted_iota(jnp.int32, value.shape, 1) // rank
+    expert = lax.broadcasted_iota(jnp.int32, value.shape, 0) % owned
+    kept = jnp.where(block == expert, value, 0.0)
+    out = kept[:, :rank]
+    for number in range(1, owned):
+        out = out + kept[:, number * rank : (number + 1) * rank]
+    return out
+
+
+def sums_kernel(owned, groups, tokens, cotangent, router, first, logits_out, combine_out):
+    ring = first.shape[0] // groups
+    image_rows, cot_rows = tokens[...], cotangent[...]
+    logits = dot_last(router[...], image_rows)
+    high, low = halves(jnp.max(logits, axis=1, keepdims=True))
+    near = jnp.exp(logits - (high + low))
+    total_high, total_low = halves(jnp.sum(near, axis=1, keepdims=True))
+    spread = jnp.exp(logits - jnp.max(logits, axis=0, keepdims=True))
+    combine = spread / jnp.sum(spread, axis=0, keepdims=True)
+    logits_out[...] = logits
+    combine_out[...] = combine
+    stats = in_lanes([high, low, total_high, total_low], (logits.shape[0], STATS))
+    stats = stats.astype(jnp.bfloat16)
+    inputs = dot_plain(near.astype(jnp.bfloat16), image_rows).astype(jnp.bfloat16)
+    grads = dot_plain(combine.astype(jnp.bfloat16), cot_rows).astype(jnp.bfloat16)
+    width = inputs.shape[1] // groups
+    for group in range(groups):
+        columns = slice(group * width, (group + 1) * width)
+        for place in range(ring):
+            rows = slice(place * owned, (place + 1) * owned)
+            block = group * ring + place
+            first[block, :, :width] = inputs[rows, columns]
+            first[block, :, width : 2 * width] = grads[rows, columns]
+            first[block, :, 2 * width :] = stats[rows, :]
+
+
+def mixing_kernel(cotangent, saved, combine, out):
+    mixing = dot_last(saved[...], cotangent[...])
+    weights = combine[...]
+    out[...] = weights * (mixing - jnp.sum(weights * mixing, axis=0, keepdims=True))
+
+
+def owner_kernel(groups, first, in_left, out_right, second, inputs_out, lows_out, stats_out):
+    ring = first.shape[0] // groups
+    owned, rank, width = in_left.shape
+    inputs, grads, stats_rows = [], [], []
+    for group in range(groups):
+        rows = slice(group * ring, (group + 1) * ring)
+        stats = first[rows, :, 2 * width :].astype(jnp.float32)
+        peaks = stats[:, :, 0:1] + stats[:, :, 1:2]
+        totals = stats[:, :, 2:3] + stats[:, :, 3:4]
+        peak = jnp.max(peaks, axis=0)
+        scale = jnp.exp(peaks - peak[None])
+        total = jnp.sum(scale * totals, axis=0)
+        scale = scale / total[None]
+        inputs.append(jnp.sum(first[rows, :, :width].astype(jnp.float32) * scale, axis=0))
+        grads.append(jnp.sum(first[rows, :, width : 2 * width].astype(jnp.float32), axis=0))
+        stats_rows.append(in_lanes([*halves(peak), *halves(total)], (owned, STATS)))
+    inputs, grads = jnp.concatenate(inputs, axis=0), jnp.concatenate(grads, axis=0)
+    inputs_out[...] = inputs
+    stats_out[...] = jnp.concatenate(stats_rows, axis=0)
+    inputs_low, grads_low = inputs.astype(jnp.bfloat16), grads.astype(jnp.bfloat16)
+    lows_out[0] = inputs_low
+    lows_out[1] = grads_low
+    up = dot_last(inputs_low, in_left[...].reshape(owned * rank, width))
+    back = dot_last(grads_low, out_right[...].reshape(owned * rank, width))
+    ranks = [*halves(from_own_block(up, owned)), *halves(from_own_block(back, owned))]
+    ranks = jnp.concatenate(ranks, axis=1).astype(jnp.bfloat16)
+    block = jnp.concatenate([inputs_low, grads_low, ranks], axis=1)
+    for place in range(second.shape[0]):
+        second[place] = block
+
+
+def hidden_kernel(
+    groups, second, base_in, base_out, in_right, out_left, third, pair_out, ranks_out
+):
+    members, rank, hidden = in_right.shape
+    rows = second.shape[1]
+    owned = rows // groups
+    places = members // owned
+    width = base_in.shape[1] // groups
+    ring = third.shape[0] // groups
+    group = lax.axis_index("dp")
+
+    def gathered(columns):
+        taken = [
+            second[pl.ds(half * ring + group * places, places), :, columns].astype(jnp.float32)
+            for half in range(groups)
+        ]
+        return [part.reshape(places * rows, part.shape[2]) for part in taken]
+
+    def low_rank(value, table):
+        value = value.astype(jnp.float32)
+        taken = []
+        for place in range(places):
+            own = own_block(value[place * rows : (place + 1) * rows], owned)
+            part = table[place * owned : (place + 1) * owned].reshape(owned * rank, hidden)
+            taken.append(dot_plain(own, part))
+        return jnp.concatenate(taken, axis=0)
+
+    def to_rank(value, table):
+        taken = []
+        for place in range(places):
+            part = table[place * owned : (place + 1) * owned].reshape(owned * rank, hidden)
+            wide = dot_last(value[place * rows : (place + 1) * rows].astype(jnp.bfloat16), part)
+            taken.append(from_own_block(wide, owned))
+        return jnp.concatenate(taken, axis=0)
+
+    ranks = functools.reduce(jnp.add, gathered(slice(2 * width, 2 * width + 4 * rank)))
+    up = (ranks[:, :rank] + ranks[:, rank : 2 * rank]).astype(jnp.bfloat16)
+    back = (ranks[:, 2 * rank : 3 * rank] + ranks[:, 3 * rank :]).astype(jnp.bfloat16)
+    preact = low_rank(up, in_right)
+    for half, part in enumerate(gathered(slice(0, width))):
+        columns = slice(half * width, (half + 1) * width)
+        preact = preact + dot_last(part.astype(jnp.bfloat16), base_in[:, columns])
+    hidden_grad = low_rank(back, out_left)
+    for half, part in enumerate(gathered(slice(width, 2 * width))):
+        columns = slice(half * width, (half + 1) * width)
+        hidden_grad = hidden_grad + dot_last(part.astype(jnp.bfloat16), base_out[:, columns])
+    root = 0.7978845608028654
+    bent = jnp.tanh(root * (preact + 0.044715 * (preact * preact * preact)))
+    hidden_value = 0.5 * preact * (1.0 + bent)
+    slope = 0.5 * (1.0 + bent) + 0.5 * preact * (1.0 - bent * bent) * (
+        root * (1.0 + 3.0 * 0.044715 * (preact * preact))
+    )
+    hidden_low = hidden_value.astype(jnp.bfloat16).astype(jnp.float32)
+    preact_grad = (hidden_grad * slope).astype(jnp.bfloat16).astype(jnp.float32)
+    pair_out[0] = preact_grad
+    pair_out[1] = hidden_low
+    ranks_out[0] = up.astype(jnp.float32)
+    ranks_out[1] = back.astype(jnp.float32)
+    slot_term = dot_plain(preact_grad.astype(jnp.bfloat16), base_in[...]).astype(jnp.bfloat16)
+    down = to_rank(preact_grad, in_right)
+    value = to_rank(hidden_low, out_left)
+    ranks = jnp.concatenate([down, value], axis=1).astype(jnp.bfloat16)
+    third[...] = jnp.zeros(third.shape, jnp.bfloat16)
+    for half in range(groups):
+        columns = slice(half * width, (half + 1) * width)
+        for place in range(places):
+            taken = slice(place * rows, (place + 1) * rows)
+            block = half * ring + group * places + place
+            third[block, :, :width] = slot_term[taken, columns]
+            third[block, :, width:] = ranks[taken]
+
+
+def outer_kernel(owned, left_rows, right_rows, *outs):
+    rows = left_rows.shape[1] // (outs[0].shape[0] // owned)
+    for number, out in enumerate(outs):
+        for place in range(out.shape[0] // owned):
+            taken = slice(place * rows, (place + 1) * rows)
+            own = own_block(left_rows[number, taken], owned)
+            product = dot_first(own, right_rows[number, taken].astype(jnp.bfloat16))
+            out[place * owned : (place + 1) * owned] = product.astype(jnp.bfloat16).reshape(
+                (owned,) + out.shape[1:]
+            )
+
+
+def finish_kernel(groups, ring, third, in_left, inputs, stats, fourth, ranks_out):
+    owned, rank, width = in_left.shape
+    members = ring // groups
+    sender = lax.axis_index("seq") // members
+    summed = jnp.sum(third[pl.ds(sender * ring, ring)].astype(jnp.float32), axis=0)
+    ranks = summed[:, width:].astype(jnp.bfloat16).astype(jnp.float32)
+    ranks_out[0] = ranks[:, :rank]
+    ranks_out[1] = ranks[:, rank:]
+    down = own_block(ranks[:, :rank], owned)
+    grads = summed[:, :width] + dot_plain(down, in_left[...].reshape(owned * rank, width))
+    grads = grads.astype(jnp.bfloat16).astype(jnp.float32)
+    high, low = halves(jnp.sum(grads * inputs[...], axis=1, keepdims=True))
+    lane = lax.broadcasted_iota(jnp.int32, stats.shape, 1)
+    tail = jnp.where(lane == 4, high, jnp.where(lane == 5, low, stats[...]))
+    block = jnp.concatenate([grads, tail], axis=1).astype(jnp.bfloat16)
+    for group in range(groups):
+        rows = block[group * owned : (group + 1) * owned]
+        for place in range(ring):
+            fourth[group * ring + place] = rows
+
+
+def tokens_kernel(groups, fourth, tokens, router, logits, mixing, out):
+    blocks, owned, _ = fourth.shape
+    ring = blocks // groups
+    width = tokens.shape[1] // groups
+
+    def rows(half, columns):
+        taken = [
+            fourth[half * ring + place, :, columns].astype(jnp.float32) for place in range(ring)
+        ]
+        return jnp.concatenate(taken, axis=0)
+
+    grads = jnp.concatenate([rows(half, slice(0, width)) for half in range(groups)], axis=1)
+    grads = grads.astype(jnp.bfloat16)
+    stats = [rows(half, slice(width, width + STATS)) for half in range(groups)]
+    peak = stats[0][:, 0:1] + stats[0][:, 1:2]
+    total = stats[0][:, 2:3] + stats[0][:, 3:4]
+    shift = functools.reduce(jnp.add, [part[:, 4:5] + part[:, 5:6] for part in stats])
+    dispatch = jnp.exp(logits[...] - peak) / total
+    weight_grad = dot_last(grads, tokens[...])
+    logit_grad = dispatch * (weight_grad - shift) + mixing[...]
+    left = jnp.concatenate([dispatch, logit_grad], axis=0).astype(jnp.bfloat16)
+    right = jnp.concatenate([grads, router[...]], axis=0)
+    out[...] = dot_first(left, right).astype(jnp.bfloat16)
+
+
+def call(kernel, outs, args, flops):
+    size = sum(array.size * array.dtype.itemsize for array in args)
+    size += sum(out.size * out.dtype.itemsize for out in outs)
+    return pl.pallas_call(
+        kernel,
+        out_shape=outs,
+        cost_estimate=pl.CostEstimate(flops=flops, bytes_accessed=size, transcendentals=0),
+        compiler_params=pltpu.CompilerParams(vmem_limit_bytes=24 * 2**20),
+    )(*args)
+
+
+def array(dtype, *shape):
+    return jax.ShapeDtypeStruct(shape, dtype)
+
+
+def local(
+    tokens,
+    cotangent,
+    router,
+    slot_outputs,
+    base_in,
+    base_out,
+    in_left,
+    in_right,
+    out_left,
+    out_right,
+):
+    groups, ring = lax.axis_size("dp"), lax.axis_size("seq")
+    devices = groups * ring
+    _, count, width = tokens.shape
+    slots = router.shape[1]
+    owned, slice_width, rank = in_left.shape
+    members, _, hidden = in_right.shape
+    rows = groups * owned
+    if slice_width % 128 or rows % 8 or members % owned:
+        return local_plain(
+            tokens,
+            cotangent,
+            router,
+            slot_outputs,
+            base_in,
+            base_out,
+            in_left,
+            in_right,
+            out_left,
+            out_right,
+        )
+    low, full = jnp.bfloat16, jnp.float32
+    image_rows, cot_rows, saved = tokens[0], cotangent[0], slot_outputs[0]
+    router, base_in = router.T, base_in.T
+    in_left, out_left = in_left.swapaxes(1, 2), out_left.swapaxes(1, 2)
+    first, logits, combine = call(
+        functools.partial(sums_kernel, owned, groups),
+        [
+            array(low, devices, owned, 2 * slice_width + STATS),
+            array(full, slots, count),
+            array(full, slots, count),
+        ],
+        [image_rows, cot_rows, router],
+        6 * count * slots * width,
+    )
+    first = lax.all_to_all(first, BOTH, 0, 0, tiled=True)
+    (mixing,) = call(
+        mixing_kernel,
+        [array(full, slots, count)],
+        [cot_rows, saved, combine],
+        2 * count * slots * width,
+    )
+    second, inputs, lows, stats = call(
+        functools.partial(owner_kernel, groups),
+        [
+            array(low, devices, rows, 2 * slice_width + 4 * rank),
+            array(full, rows, slice_width),
+            array(low, 2, rows, slice_width),
+            array(full, rows, STATS),
+        ],
+        [first, in_left, out_right],
+        4 * rows * owned * rank * slice_width,
+    )
+    second = lax.all_to_all(second, BOTH, 0, 0, tiled=True)
+    total_rows = groups * members
+    third, pair, ranks = call(
+        functools.partial(hidden_kernel, groups),
+        [
+            array(low, devices, rows, slice_width + 2 * rank),
+            array(full, 2, total_rows, hidden),
+            array(full, 2, total_rows, rank),
+        ],
+        [second, base_in, base_out, in_right, out_left],
+        6 * total_rows * hidden * (width + owned * rank),
+    )
+    third = lax.all_to_all(third, BOTH, 0, 0, tiled=True)
+    grad_in_right, grad_out_left = call(
+        functools.partial(outer_kernel, owned),
+        [array(low, members, rank, hidden)] * 2,
+        [ranks, pair],
+        4 * members * rank * hidden * rows,
+    )
+    fourth, ranks = call(
+        functools.partial(finish_kernel, groups, ring),
+        [array(low, devices, owned, slice_width + STATS), array(full, 2, rows, rank)],
+        [third, in_left, inputs, stats],
+        2 * rows * owned * rank * slice_width,
+    )
+    fourth = lax.all_to_all(fourth, BOTH, 0, 0, tiled=True)
+    grad_in_left, grad_out_right = call(
+        functools.partial(outer_kernel, owned),
+        [array(low, owned, rank, slice_width)] * 2,
+        [ranks, lows],
+        4 * owned * rank * slice_width * rows,
+    )
+    (token_grad,) = call(
+        functools.partial(tokens_kernel, groups),
+        [array(low, count, width)],
+        [fourth, image_rows, router, logits, mixing],
+        6 * count * slots * width,
+    )
+    return (
+        token_grad[None],
+        grad_in_left.swapaxes(1, 2),
+        grad_in_right,
+        grad_out_left.swapaxes(1, 2),
+        grad_out_right,
+    )
+
+
 def solution(mesh):
     in_specs = (
         P("dp", "seq", None),

time: 107 us -> 82.3 us (0.77)
  blocking collectives: 18.8 us -> 57.5 us
  waiting for transfers between devices: 37.4 us -> 5.35 us
  matrix products: 25 us -> 0 us
  Pallas kernels: 0 us -> 11 us
  local copies, waits for them, and re-layouts: 10.7 us -> 4.27 us
  starting transfers between devices: 9.07 us -> 3.04 us
  other arithmetic: 3.97 us -> 0 us
    all_to_all x1 -> x3, blocking collectives: 18.8 us -> 57.5 us  [the longest x1 23.6 us: local(): second = lax.all_to_all(second, BOTH, 0, 0, tiled=True)]
    all_to_all x3 -> x1, waiting for transfers between devices: 37.4 us -> 5.35 us  [local(): fourth = lax.all_to_all(fourth, BOTH, 0, 0, tiled=True)]
    dot_general x20 -> x0, matrix products: 25 us -> none  [the longest x4 6.13 us: dot_last(): lax.dot_general(left, right, (((1,), (1,)), ((), ())), preferred_element_...]
    pallas_call x0 -> x8, Pallas kernels: none -> 11 us  [call(): pl.pallas_call(kernel, out_shape=outs, cost_estimate=pl.CostEstimate(flop...]
    all_to_all x3 -> x1, starting transfers between devices: 9.07 us -> 3.04 us  [local(): fourth = lax.all_to_all(fourth, BOTH, 0, 0, tiled=True)]
    reduce_sum x7 -> x0, other arithmetic: 3.24 us -> none  [the longest x1 1.28 us: local(): jnp.sum(combine * mixing_grad, axis=1, keepdims=True)]
    dot_general x4 -> x0, local copies, waits for them, and re-layouts: 2.99 us -> none  [the longest x2 2.78 us: dot_first(): lax.dot_general(left, right, (((0,), (0,)), ((), ())), preferred_element_...]
    unnamed x55 -> x26, local copies, waits for them, and re-layouts: 1.56 us -> 4.27 us
  transfers between devices with their start and end apart: 3 -> 1, of which waited for: 3 -> 1; matrix products, arithmetic and copies ran while one was open for 5% -> 0% of each run, Pallas kernels for 0% -> 5%
where the time goes in v3:
time: 82.3 us; the launch traced here: 81.9 us
  blocking collectives  57.5 us (70%)
  Pallas kernels  11 us (13%)
  waiting for transfers between devices  5.35 us (7%)
  local copies, waits for them, and re-layouts  4.27 us (5%)
  starting transfers between devices  3.04 us (4%)
    all_to_all x1, blocking collectives, local(): second = lax.all_to_all(second, BOTH, 0, 0, tiled=True)  23.6 us
    all_to_all x1, blocking collectives, local(): first = lax.all_to_all(first, BOTH, 0, 0, tiled=True)  18.8 us
    all_to_all x1, blocking collectives, local(): third = lax.all_to_all(third, BOTH, 0, 0, tiled=True)  15.1 us
    pallas_call x8, Pallas kernels, call(): pl.pallas_call(kernel, out_shape=outs, cost_estimate=pl.CostEstimate(flop...  11 us
    all_to_all x1, waiting for transfers between devices, local(): fourth = lax.all_to_all(fourth, BOTH, 0, 0, tiled=True)  5.35 us
    unnamed x26, local copies, waits for them, and re-layouts  4.27 us
    all_to_all x1, starting transfers between devices, local(): fourth = lax.all_to_all(fourth, BOTH, 0, 0, tiled=True)  3.04 us
  transfers between devices with their start and end apart: 1, of which 1 were waited for; matrix products, arithmetic and copies ran while one was open for 0% of the time, Pallas kernels for 5%

profile of v3, /device:TPU:1, one launch (start us, length us, event | category | flops | bytes accessed | tf_op | source)
XLA Modules:
  0.0 81.9 jit_solution(9932032184183082147)
XLA Ops:
  0.6 0.0 copy-start
  0.6 1.1 %copy-done = bf16[1,256,1280]{2,1,0:T(8,128)(2,1)S(1)} copy-done((bf16[1,256,1280]{2,1,0:T(8,128)(2,1)S(1)}, bf16[1,256,1280]{2,1,0:T(8,128)(2,1)}, u32[]{:S(2)}) %copy-start) | copy-done | bytes 655384
  1.7 0.0 copy-start.2
  1.7 1.1 %copy-done.2 = bf16[1,256,1280]{2,1,0:T(8,128)(2,1)S(1)} copy-done((bf16[1,256,1280]{2,1,0:T(8,128)(2,1)S(1)}, bf16[1,256,1280]{2,1,0:T(8,128)(2,1)}, u32[]{:S(2)}) %copy-start.2) | copy-done | bytes 655384
  2.8 0.0 copy-start.9
  2.8 0.9 %copy-done.9 = bf16[1280,64]{0,1:T(8,128)(2,1)S(1)} copy-done((bf16[1280,64]{0,1:T(8,128)(2,1)S(1)}, bf16[1280,64]{0,1:T(8,128)(2,1)}, u32[]{:S(2)}) %copy-start.9) | copy-done | bytes 163864
  3.7 0.0 copy-start.6
  3.7 0.0 copy-start.11
  3.7 0.0 copy-start.7
  3.7 1.0 %shard_map.137 = (bf16[32,4,1408]{2,1,0:T(4,128)(2,1)S(1)}, f32[64,256]{1,0:T(8,128)S(1)}, f32[64,256]{1,0:T(8,128)S(1)}) custom-call(bf16[256,1280]{1,0:T(8,128)(2,1)S(1)} %bitcast.10, bf16[256,1280]{1,0:T(8,128)(2,1)S(1)} %bitcast.12, bf16[64,1280]{1,0:T(8,128)(2,1)S(1)} %bitcast.18), custom_call_target="tpu_custom_call" | custom-call | flops 125829120 | bytes 1966080 | tf_op jit(solution)/shard_map/pallas_call | solution.py:425
  4.8 0.0 copy-start.4
  4.8 0.0 copy-start.5
  4.8 18.8 %all_to_all.20.first = bf16[32,4,1408]{2,1,0:T(4,128)(2,1)S(1)} all-to-all(bf16[32,4,1408]{2,1,0:T(4,128)(2,1)S(1)} %get-tuple-element.21), channel_id=1, replica_groups=mesh['dp'=2,'seq'=16] {'dp','seq'}, dimensions={0} | all-to-all | bytes 720896 | tf_op jit(solution)/shard_map/all_to_all | solution.py:483
  23.6 0.0 copy-done.6
  23.6 0.0 copy-done.11
  23.6 0.7 shard_map.138
  24.3 23.6 %all_to_all.21.second = bf16[32,8,1536]{2,1,0:T(8,128)(2,1)S(1)} all-to-all(bf16[32,8,1536]{2,1,0:T(8,128)(2,1)S(1)} %get-tuple-element.22), channel_id=1, replica_groups=mesh['dp'=2,'seq'=16] {'dp','seq'}, dimensions={0} | all-to-all | bytes 1572864 | tf_op jit(solution)/shard_map/all_to_all | solution.py:501
  47.9 0.0 copy-done.7
  47.9 0.0 copy-done.4
  47.9 0.0 copy-done.5
  47.9 0.0 copy-start.8
  47.9 1.1 %copy-done.8 = bf16[320,1280]{1,0:T(8,128)(2,1)S(1)} copy-done((bf16[320,1280]{1,0:T(8,128)(2,1)S(1)}, bf16[320,1280]{1,0:T(8,128)(2,1)}, u32[]{:S(2)}) %copy-start.8) | copy-done | bytes 819224
  49.1 2.4 %shard_map.139 = (bf16[32,8,768]{2,1,0:T(8,128)(2,1)S(1)}, f32[2,64,320]{2,1,0:T(8,128)S(1)}, f32[2,64,64]{2,1,0:T(8,128)S(1)}) custom-call(bf16[32,8,1536]{2,1,0:T(8,128)(2,1)S(1)} %all_to_all.21.second, bf16[320,1280]{1,0:T(8,128)(2,1)S(1)} %bitcast.17, bf16[320,1280]{1,0:T(8,128)(2,1)S(1)} %copy-done.8, bf16[32,64,320]{2,1,0:T(8,128)(2,1)S(1)} %copy-done.4, ...), custom_call_target="tpu_custom_call" | custom-call | flops 188743680 | bytes 5636096 | tf_op jit(solution)/shard_map/pallas_call | solution.py:425
  51.5 0.0 copy-start.3
  51.5 0.0 copy-start.12
  51.5 0.0 copy-start.1
  51.5 0.0 copy-start.10
  51.5 15.1 %all_to_all.22.third = bf16[32,8,768]{2,1,0:T(8,128)(2,1)S(1)} all-to-all(bf16[32,8,768]{2,1,0:T(8,128)(2,1)S(1)} %get-tuple-element.23), channel_id=1, replica_groups=mesh['dp'=2,'seq'=16] {'dp','seq'}, dimensions={0} | all-to-all | bytes 786432 | tf_op jit(solution)/shard_map/all_to_all | solution.py:513
  66.6 1.0 %shard_map.140 = (bf16[32,4,768]{2,1,0:T(4,128)(2,1)}, f32[2,8,64]{2,1,0:T(8,128)S(1)}) custom-call(bf16[32,8,768]{2,1,0:T(8,128)(2,1)S(1)} %all_to_all.22.third, bf16[4,64,640]{2,1,0:T(8,128)(2,1)S(1)} %bitcast.16, f32[8,640]{1,0:T(8,128)S(1)} %get-tuple-element.24.inputs, f32[8,128]{1,0:T(8,128)S(1)} %get-tuple-element.25.stats), custom_call_target="tpu_custom_call" | custom-call | flops 2621440 | bytes 946176 | tf_op jit(solution)/shard_map/pallas_call | solution.py:425
  67.6 3.0 %all-to-all-start.3 = ((bf16[32,4,768]{2,1,0:T(4,128)(2,1)}), bf16[32,4,768]{2,1,0:T(4,128)(2,1)S(1)}, u32[]{:S(2)}, u32[]{:S(2)}) async-start(bf16[32,4,768]{2,1,0:T(4,128)(2,1)} %get-tuple-element.26), calls=%async_computation.3 | async-start | bytes 393216 | tf_op jit(solution)/shard_map/all_to_all | solution.py:526
  70.6 0.0 copy-done.3
  70.7 0.0 copy-done.12
  70.7 0.4 shard_map.141.mixing
  71.0 2.5 %shard_map.144 = (bf16[32,64,320]{2,1,0:T(8,128)(2,1)}, bf16[32,64,320]{2,1,0:T(8,128)(2,1)}) custom-call(f32[2,64,64]{2,1,0:T(8,128)S(1)} %get-tuple-element.32.left_rows, f32[2,64,320]{2,1,0:T(8,128)S(1)} %get-tuple-element.33.right_rows), custom_call_target="tpu_custom_call" | custom-call | flops 20971520 | bytes 2818048 | tf_op jit(solution)/shard_map/pallas_call | solution.py:425
  73.5 1.2 %shard_map.143 = (bf16[4,64,640]{2,1,0:T(8,128)(2,1)}, bf16[4,64,640]{2,1,0:T(8,128)(2,1)}) custom-call(f32[2,8,64]{2,1,0:T(8,128)S(1)} %get-tuple-element.29.left_rows, bf16[2,8,640]{2,1,0:T(8,128)(2,1)S(1)} %get-tuple-element.30.right_rows), custom_call_target="tpu_custom_call" | custom-call | flops 5242880 | bytes 679936 | tf_op jit(solution)/shard_map/pallas_call | solution.py:425
  74.7 5.3 %all-to-all-done.3.fourth = bf16[32,4,768]{2,1,0:T(4,128)(2,1)S(1)} async-done(((bf16[32,4,768]{2,1,0:T(4,128)(2,1)}), bf16[32,4,768]{2,1,0:T(4,128)(2,1)S(1)}, u32[]{:S(2)}, u32[]{:S(2)}) %all-to-all-start.3) | async-done | bytes 196640 | tf_op jit(solution)/shard_map/all_to_all | solution.py:526
  80.1 0.0 copy-done.1
  80.1 0.0 copy-done.10
  80.1 1.8 %shard_map.142 = bf16[256,1280]{1,0:T(8,128)(2,1)} custom-call(bf16[32,4,768]{2,1,0:T(4,128)(2,1)S(1)} %all-to-all-done.3.fourth, bf16[256,1280]{1,0:T(8,128)(2,1)S(1)} %bitcast.11, bf16[64,1280]{1,0:T(8,128)(2,1)S(1)} %bitcast.19, f32[64,256]{1,0:T(8,128)S(1)} %get-tuple-element.27.logits, f32[64,256]{1,0:T(8,128)S(1)} %shard_map.141.mixing), custom_call_target="tpu_custom_call" | custom-call | flops 125829120 | bytes 1802240 | tf_op jit(solution)/shard_map/pallas_call | solution.py:425
Async XLA Ops:
  0.6 1.1 %copy-start = (bf16[1,256,1280]{2,1,0:T(8,128)(2,1)S(1)}, bf16[1,256,1280]{2,1,0:T(8,128)(2,1)}, u32[]{:S(2)}) copy-start(bf16[1,256,1280]{2,1,0:T(8,128)(2,1)} %param.10) | copy-start | bytes 1966084
  1.7 1.1 %copy-start.2 = (bf16[1,256,1280]{2,1,0:T(8,128)(2,1)S(1)}, bf16[1,256,1280]{2,1,0:T(8,128)(2,1)}, u32[]{:S(2)}) copy-start(bf16[1,256,1280]{2,1,0:T(8,128)(2,1)} %param.11) | copy-start | bytes 1966084
  2.8 0.9 %copy-start.9 = (bf16[1280,64]{0,1:T(8,128)(2,1)S(1)}, bf16[1280,64]{0,1:T(8,128)(2,1)}, u32[]{:S(2)}) copy-start(bf16[1280,64]{0,1:T(8,128)(2,1)} %param.12) | copy-start | bytes 491524
  3.7 19.9 %copy-start.6 = (bf16[4,640,64]{1,2,0:T(8,128)(2,1)S(1)}, bf16[4,640,64]{1,2,0:T(8,128)(2,1)}, u32[]{:S(2)}) copy-start(bf16[4,640,64]{1,2,0:T(8,128)(2,1)} %param.16) | copy-start | bytes 983044
  3.7 19.9 %copy-start.11 = (bf16[4,64,640]{2,1,0:T(8,128)(2,1)S(1)}, bf16[4,64,640]{2,1,0:T(8,128)(2,1)}, u32[]{:S(2)}) copy-start(bf16[4,64,640]{2,1,0:T(8,128)(2,1)} %out_right.1) | copy-start | bytes 983044
  3.7 44.2 %copy-start.7 = (bf16[1280,320]{0,1:T(8,128)(2,1)S(1)}, bf16[1280,320]{0,1:T(8,128)(2,1)}, u32[]{:S(2)}) copy-start(bf16[1280,320]{0,1:T(8,128)(2,1)} %param.14) | copy-start | bytes 2457604
  4.8 43.2 %copy-start.4 = (bf16[32,64,320]{2,1,0:T(8,128)(2,1)S(1)}, bf16[32,64,320]{2,1,0:T(8,128)(2,1)}, u32[]{:S(2)}) copy-start(bf16[32,64,320]{2,1,0:T(8,128)(2,1)} %in_right.1) | copy-start | bytes 3932164
  4.8 43.2 %copy-start.5 = (bf16[32,320,64]{1,2,0:T(8,128)(2,1)S(1)}, bf16[32,320,64]{1,2,0:T(8,128)(2,1)}, u32[]{:S(2)}) copy-start(bf16[32,320,64]{1,2,0:T(8,128)(2,1)} %param.18) | copy-start | bytes 3932164
  47.9 1.1 %copy-start.8 = (bf16[320,1280]{1,0:T(8,128)(2,1)S(1)}, bf16[320,1280]{1,0:T(8,128)(2,1)}, u32[]{:S(2)}) copy-start(bf16[320,1280]{1,0:T(8,128)(2,1)} %base_out.1) | copy-start | bytes 2457604
  51.5 19.1 %copy-start.3 = (bf16[1,256,1280]{2,1,0:T(8,128)(2,1)S(1)}, bf16[1,256,1280]{2,1,0:T(8,128)(2,1)}, u32[]{:S(2)}) copy-start(bf16[1,256,1280]{2,1,0:T(8,128)(2,1)} %param.11) | copy-start | bytes 1966084
  51.5 19.1 %copy-start.12 = (bf16[1,64,1280]{2,1,0:T(8,128)(2,1)S(1)}, bf16[1,64,1280]{2,1,0:T(8,128)(2,1)}, u32[]{:S(2)}) copy-start(bf16[1,64,1280]{2,1,0:T(8,128)(2,1)} %param.13) | copy-start | bytes 491524
  51.5 28.6 %copy-start.1 = (bf16[1,256,1280]{2,1,0:T(8,128)(2,1)S(1)}, bf16[1,256,1280]{2,1,0:T(8,128)(2,1)}, u32[]{:S(2)}) copy-start(bf16[1,256,1280]{2,1,0:T(8,128)(2,1)} %param.10) | copy-start | bytes 1966084
  51.5 28.6 %copy-start.10 = (bf16[1280,64]{0,1:T(8,128)(2,1)S(1)}, bf16[1280,64]{0,1:T(8,128)(2,1)}, u32[]{:S(2)}) copy-start(bf16[1280,64]{0,1:T(8,128)(2,1)} %param.12) | copy-start | bytes 491524
  67.6 12.5 %all-to-all-start.3 = ((bf16[32,4,768]{2,1,0:T(4,128)(2,1)}), bf16[32,4,768]{2,1,0:T(4,128)(2,1)S(1)}, u32[]{:S(2)}, u32[]{:S(2)}) async-start(bf16[32,4,768]{2,1,0:T(4,128)(2,1)} %get-tuple-element.26), calls=%async_computation.3 | async-start | bytes 393216 | tf_op jit(solution)/shard_map/all_to_all | solution.py:526

commit v4 on v3

--- a/solution.py
+++ b/solution.py
@@ -226,9 +226,32 @@
     return out
 
 
-def sums_kernel(owned, groups, tokens, cotangent, router, first, logits_out, combine_out):
+def sums_kernel(
+    owned,
+    groups,
+    tokens_far,
+    cotangent_far,
+    router_far,
+    first,
+    logits_out,
+    combine_out,
+    tokens,
+    cotangent,
+    router,
+    arrived,
+):
     ring = first.shape[0] // groups
-    image_rows, cot_rows = tokens[...], cotangent[...]
+    copies = [
+        pltpu.make_async_copy(far, near, arrived.at[number])
+        for number, (far, near) in enumerate(
+            [(router_far, router), (tokens_far, tokens), (cotangent_far, cotangent)]
+        )
+    ]
+    for copy in copies:
+        copy.start()
+    copies[0].wait()
+    copies[1].wait()
+    image_rows = tokens[...]
     logits = dot_last(router[...], image_rows)
     high, low = halves(jnp.max(logits, axis=1, keepdims=True))
     near = jnp.exp(logits - (high + low))
@@ -240,7 +263,8 @@
     stats = in_lanes([high, low, total_high, total_low], (logits.shape[0], STATS))
     stats = stats.astype(jnp.bfloat16)
     inputs = dot_plain(near.astype(jnp.bfloat16), image_rows).astype(jnp.bfloat16)
-    grads = dot_plain(combine.astype(jnp.bfloat16), cot_rows).astype(jnp.bfloat16)
+    copies[2].wait()
+    grads = dot_plain(combine.astype(jnp.bfloat16), cotangent[...]).astype(jnp.bfloat16)
     width = inputs.shape[1] // groups
     for group in range(groups):
         columns = slice(group * width, (group + 1) * width)
@@ -285,15 +309,38 @@
     ranks = [*halves(from_own_block(up, owned)), *halves(from_own_block(back, owned))]
     ranks = jnp.concatenate(ranks, axis=1).astype(jnp.bfloat16)
     block = jnp.concatenate([inputs_low, grads_low, ranks], axis=1)
-    for place in range(second.shape[0]):
-        second[place] = block
+    second[...] = block
+
+
+def pack_kernel(groups, own, beside, across, out):
+    places = out.shape[0]
+    group = lax.axis_index("dp")
+    here = group == lax.axis_index("seq") // places
+    near = jnp.where(here, own[...], beside[...])
+    far = jnp.where(here, beside[...], across[...])
+    first, last = jnp.where(group == 0, near, far), jnp.where(group == 0, far, near)
+    for place in range(places):
+        out[place, 0] = first
+        out[place, 1] = last
 
 
 def hidden_kernel(
-    groups, second, base_in, base_out, in_right, out_left, third, pair_out, ranks_out
+    groups,
+    second,
+    base_in,
+    base_out_far,
+    in_right,
+    out_left,
+    third,
+    pair_out,
+    ranks_out,
+    base_out,
+    arrived,
 ):
+    copy = pltpu.make_async_copy(base_out_far, base_out, arrived)
+    copy.start()
     members, rank, hidden = in_right.shape
-    rows = second.shape[1]
+    rows = second.shape[2]
     owned = rows // groups
     places = members // owned
     width = base_in.shape[1] // groups
@@ -302,7 +349,7 @@
 
     def gathered(columns):
         taken = [
-            second[pl.ds(half * ring + group * places, places), :, columns].astype(jnp.float32)
+            second[:, half, :, columns].astype(jnp.float32)
             for half in range(groups)
         ]
         return [part.reshape(places * rows, part.shape[2]) for part in taken]
@@ -332,6 +379,7 @@
         columns = slice(half * width, (half + 1) * width)
         preact = preact + dot_last(part.astype(jnp.bfloat16), base_in[:, columns])
     hidden_grad = low_rank(back, out_left)
+    copy.wait()
     for half, part in enumerate(gathered(slice(width, 2 * width))):
         columns = slice(half * width, (half + 1) * width)
         hidden_grad = hidden_grad + dot_last(part.astype(jnp.bfloat16), base_out[:, columns])
@@ -419,12 +467,40 @@
     out[...] = dot_first(left, right).astype(jnp.bfloat16)
 
 
-def call(kernel, outs, args, flops):
+def to_group(block, ring):
+    places = ring // 2
+
+    def device(group, half, place):
+        return group * ring + half * places + place
+
+    beside, across = [], []
+    for place in range(places):
+        for half in range(2):
+            beside.append((device(half, half, place), device(half, 1 - half, place)))
+            beside.append((device(1 - half, half, place), device(half, half, place)))
+            across.append((device(1 - half, half, place), device(half, 1 - half, place)))
+    beside = lax.ppermute(block, BOTH, beside)
+    across = lax.ppermute(block, BOTH, across)
+    (blocks,) = call(
+        functools.partial(pack_kernel, 2),
+        [array(block.dtype, places, 2, *block.shape)],
+        [block, beside, across],
+        0,
+    )
+    halves = [[half * places + place for place in range(places)] for half in range(2)]
+    return lax.all_to_all(blocks, "seq", 0, 0, axis_index_groups=halves, tiled=True)
+
+
+def call(kernel, outs, args, flops, far=(), scratch=()):
     size = sum(array.size * array.dtype.itemsize for array in args)
     size += sum(out.size * out.dtype.itemsize for out in outs)
+    spaces = [pltpu.HBM if number in far else pltpu.VMEM for number in range(len(args))]
     return pl.pallas_call(
         kernel,
         out_shape=outs,
+        in_specs=[pl.BlockSpec(memory_space=space) for space in spaces],
+        out_specs=[pl.BlockSpec(memory_space=pltpu.VMEM) for _ in outs],
+        scratch_shapes=scratch,
         cost_estimate=pl.CostEstimate(flops=flops, bytes_accessed=size, transcendentals=0),
         compiler_params=pltpu.CompilerParams(vmem_limit_bytes=24 * 2**20),
     )(*args)
@@ -453,7 +529,7 @@
     owned, slice_width, rank = in_left.shape
     members, _, hidden = in_right.shape
     rows = groups * owned
-    if slice_width % 128 or rows % 8 or members % owned:
+    if groups != 2 or ring % 2 or slice_width % 128 or rows % 8 or members % owned:
         return local_plain(
             tokens,
             cotangent,
@@ -479,6 +555,9 @@
         ],
         [image_rows, cot_rows, router],
         6 * count * slots * width,
+        (0, 1, 2),
+        [pltpu.VMEM((count, width), low)] * 2
+        + [pltpu.VMEM((slots, width), low), pltpu.SemaphoreType.DMA((3,))],
     )
     first = lax.all_to_all(first, BOTH, 0, 0, tiled=True)
     (mixing,) = call(
@@ -490,7 +569,7 @@
     second, inputs, lows, stats = call(
         functools.partial(owner_kernel, groups),
         [
-            array(low, devices, rows, 2 * slice_width + 4 * rank),
+            array(low, rows, 2 * slice_width + 4 * rank),
             array(full, rows, slice_width),
             array(low, 2, rows, slice_width),
             array(full, rows, STATS),
@@ -498,7 +577,7 @@
         [first, in_left, out_right],
         4 * rows * owned * rank * slice_width,
     )
-    second = lax.all_to_all(second, BOTH, 0, 0, tiled=True)
+    second = to_group(second, ring)
     total_rows = groups * members
     third, pair, ranks = call(
         functools.partial(hidden_kernel, groups),
@@ -509,6 +588,8 @@
         ],
         [second, base_in, base_out, in_right, out_left],
         6 * total_rows * hidden * (width + owned * rank),
+        (2,),
+        [pltpu.VMEM((hidden, width), low), pltpu.SemaphoreType.DMA],
     )
     third = lax.all_to_all(third, BOTH, 0, 0, tiled=True)
     grad_in_right, grad_out_left = call(

time: 82.3 us -> 79.7 us (0.968)
  blocking collectives: 57.5 us -> 46.7 us
  starting transfers between devices: 3.04 us -> 8.17 us
  Pallas kernels: 11 us -> 12 us
  local copies, waits for them, and re-layouts: 4.27 us -> 5.24 us
  waiting for transfers between devices: 5.35 us -> 6.29 us
    all_to_all x1, blocking collectives: 23.6 us -> 11.1 us  [to_group(): lax.all_to_all(blocks, 'seq', 0, 0, axis_index_groups=halves, tiled=True)]
    ppermute x0 -> x2, starting transfers between devices: none -> 5.13 us  [the longest x1 4.44 us: to_group(): beside = lax.ppermute(block, BOTH, beside)]
    all_to_all x1, blocking collectives: 15.1 us -> 16.8 us  [local(): third = lax.all_to_all(third, BOTH, 0, 0, tiled=True)]
    pallas_call x8 -> x9, Pallas kernels: 11 us -> 12 us  [call(): pl.pallas_call(kernel, out_shape=outs, in_specs=[pl.BlockSpec(memory_spac...]
    unnamed x26, local copies, waits for them, and re-layouts: 4.27 us -> 5.24 us
    ppermute x0 -> x2, waiting for transfers between devices: none -> 0.95 us  [the longest x1 0.94 us: to_group(): beside = lax.ppermute(block, BOTH, beside)]
  transfers between devices with their start and end apart: 1 -> 3, of which waited for: 1 -> 2; matrix products, arithmetic and copies ran while one was open for 0% -> 0% of each run, Pallas kernels for 5% -> 5%
where the time goes in v4:
time: 79.7 us; the launch traced here: 79.2 us
  blocking collectives  46.7 us (59%)
  Pallas kernels  12 us (15%)
  starting transfers between devices  8.17 us (10%)
  waiting for transfers between devices  6.29 us (8%)
  local copies, waits for them, and re-layouts  5.24 us (7%)
    all_to_all x1, blocking collectives, local(): first = lax.all_to_all(first, BOTH, 0, 0, tiled=True)  18.8 us
    all_to_all x1, blocking collectives, local(): third = lax.all_to_all(third, BOTH, 0, 0, tiled=True)  16.8 us
    pallas_call x9, Pallas kernels, call(): pl.pallas_call(kernel, out_shape=outs, in_specs=[pl.BlockSpec(memory_spac...  12 us
    all_to_all x1, blocking collectives, to_group(): lax.all_to_all(blocks, 'seq', 0, 0, axis_index_groups=halves, tiled=True)  11.1 us
    all_to_all x1, waiting for transfers between devices, local(): fourth = lax.all_to_all(fourth, BOTH, 0, 0, tiled=True)  5.34 us
    unnamed x26, local copies, waits for them, and re-layouts  5.24 us
    ppermute x1, starting transfers between devices, to_group(): beside = lax.ppermute(block, BOTH, beside)  4.44 us
    all_to_all x1, starting transfers between devices, local(): fourth = lax.all_to_all(fourth, BOTH, 0, 0, tiled=True)  3.04 us
  transfers between devices with their start and end apart: 3, of which 2 were waited for; matrix products, arithmetic and copies ran while one was open for 0% of the time, Pallas kernels for 5%

profile of v4, /device:TPU:1, one launch (start us, length us, event | category | flops | bytes accessed | tf_op | source)
XLA Modules:
  0.0 79.2 jit_solution(14214933995484702926)
XLA Ops:
  0.6 0.0 copy-start
  0.6 1.1 %copy-done = bf16[1,256,1280]{2,1,0:T(8,128)(2,1)S(1)} copy-done((bf16[1,256,1280]{2,1,0:T(8,128)(2,1)S(1)}, bf16[1,256,1280]{2,1,0:T(8,128)(2,1)}, u32[]{:S(2)}) %copy-start) | copy-done | bytes 655384
  1.7 0.0 copy-start.2
  1.7 1.1 %copy-done.2 = bf16[1,256,1280]{2,1,0:T(8,128)(2,1)S(1)} copy-done((bf16[1,256,1280]{2,1,0:T(8,128)(2,1)S(1)}, bf16[1,256,1280]{2,1,0:T(8,128)(2,1)}, u32[]{:S(2)}) %copy-start.2) | copy-done | bytes 655384
  2.8 0.0 copy-start.9
  2.8 0.9 %copy-done.9 = bf16[1280,64]{0,1:T(8,128)(2,1)S(1)} copy-done((bf16[1280,64]{0,1:T(8,128)(2,1)S(1)}, bf16[1280,64]{0,1:T(8,128)(2,1)}, u32[]{:S(2)}) %copy-start.9) | copy-done | bytes 163864
  3.7 0.0 copy-start.6
  3.7 0.0 copy-start.5
  3.7 1.8 %shard_map.137 = (bf16[32,4,1408]{2,1,0:T(4,128)(2,1)S(1)}, f32[64,256]{1,0:T(8,128)S(1)}, f32[64,256]{1,0:T(8,128)S(1)}) custom-call(bf16[256,1280]{1,0:T(8,128)(2,1)S(1)} %bitcast.10, bf16[256,1280]{1,0:T(8,128)(2,1)S(1)} %bitcast.12, bf16[64,1280]{1,0:T(8,128)(2,1)S(1)} %bitcast.18), custom_call_target="tpu_custom_call" | custom-call | flops 125829120 | bytes 1966080 | tf_op jit(solution)/shard_map/pallas_call | solution.py:498
  5.5 0.0 copy-start.4
  5.5 0.0 copy-start.7
  5.5 18.8 %all_to_all.20.first = bf16[32,4,1408]{2,1,0:T(4,128)(2,1)S(1)} all-to-all(bf16[32,4,1408]{2,1,0:T(4,128)(2,1)S(1)} %get-tuple-element.21), channel_id=1, replica_groups=mesh['dp'=2,'seq'=16] {'dp','seq'}, dimensions={0} | all-to-all | bytes 720896 | tf_op jit(solution)/shard_map/all_to_all | solution.py:562
  24.4 0.0 copy-done.6
  24.4 0.0 copy-start.11
  24.4 1.0 %copy-done.11 = bf16[4,64,640]{2,1,0:T(8,128)(2,1)S(1)} copy-done((bf16[4,64,640]{2,1,0:T(8,128)(2,1)S(1)}, bf16[4,64,640]{2,1,0:T(8,128)(2,1)}, u32[]{:S(2)}) %copy-start.11) | copy-done | bytes 327704
  25.3 0.7 shard_map.138
  26.0 0.7 collective-permute-start.1
  26.7 4.4 %collective-permute-start = (bf16[8,1536]{1,0:T(8,128)(2,1)S(1)}, bf16[8,1536]{1,0:T(8,128)(2,1)S(1)}, u32[]{:S(2)}, u32[]{:S(2)}) collective-permute-start(bf16[8,1536]{1,0:T(8,128)(2,1)S(1)} %get-tuple-element.22.own), channel_id=1, source_target_pairs={{0,8},{16,0},{24,16},{8,24},{1,9},{17,1},{25,17},{9,25},{2,10},{18... | collective-permute-start | bytes 73736 | tf_op jit(solution)/shard_map/ppermute | solution.py:482
  31.1 0.0 collective-permute-done.1.across
  31.1 0.9 %collective-permute-done.beside = bf16[8,1536]{1,0:T(8,128)(2,1)S(1)} collective-permute-done((bf16[8,1536]{1,0:T(8,128)(2,1)S(1)}, bf16[8,1536]{1,0:T(8,128)(2,1)S(1)}, u32[]{:S(2)}, u32[]{:S(2)}) %collective-permute-start) | collective-permute-done | bytes 24608 | tf_op jit(solution)/shard_map/ppermute | solution.py:482
  32.1 11.1 %all_to_all.21.second = bf16[8,2,8,1536]{3,2,1,0:T(8,128)(2,1)S(1)} all-to-all(bf16[8,2,8,1536]{3,2,1,0:T(8,128)(2,1)S(1)} %shard_map.139), channel_id=1, replica_groups={{0,1,2,3,4,5,6,7},{8,9,10,11,12,13,14,15},{16,17,18,19,20,21,22,23},{24..., dimensions={0} | all-to-all | bytes 786432 | tf_op jit(solution)/shard_map/all_to_all | solution.py:491
  43.2 0.0 copy-done.5
  43.2 0.0 copy-done.4
  43.2 0.0 copy-done.7
  43.2 0.0 copy-start.8
  43.2 1.1 %copy-done.8 = bf16[320,1280]{1,0:T(8,128)(2,1)S(1)} copy-done((bf16[320,1280]{1,0:T(8,128)(2,1)S(1)}, bf16[320,1280]{1,0:T(8,128)(2,1)}, u32[]{:S(2)}) %copy-start.8) | copy-done | bytes 819224
  44.4 2.7 %shard_map.140 = (bf16[32,8,768]{2,1,0:T(8,128)(2,1)S(1)}, f32[2,64,320]{2,1,0:T(8,128)S(1)}, f32[2,64,64]{2,1,0:T(8,128)S(1)}) custom-call(bf16[8,2,8,1536]{3,2,1,0:T(8,128)(2,1)S(1)} %all_to_all.21.second, bf16[320,1280]{1,0:T(8,128)(2,1)S(1)} %bitcast.17, bf16[320,1280]{1,0:T(8,128)(2,1)S(1)} %copy-done.8, bf16[32,64,320]{2,1,0:T(8,128)(2,1)S(1)} %copy-done.4, ...), custom_call_target="tpu_custom_call" | custom-call | flops 188743680 | bytes 5242880 | tf_op jit(solution)/shard_map/pallas_call | solution.py:498
  47.0 0.0 copy-start.3
  47.0 0.0 copy-start.12
  47.1 0.0 copy-start.1
  47.1 0.0 copy-start.10
  47.1 16.8 %all_to_all.22.third = bf16[32,8,768]{2,1,0:T(8,128)(2,1)S(1)} all-to-all(bf16[32,8,768]{2,1,0:T(8,128)(2,1)S(1)} %get-tuple-element.23), channel_id=1, replica_groups=mesh['dp'=2,'seq'=16] {'dp','seq'}, dimensions={0} | all-to-all | bytes 786432 | tf_op jit(solution)/shard_map/all_to_all | solution.py:594
  63.9 1.0 %shard_map.141 = (bf16[32,4,768]{2,1,0:T(4,128)(2,1)}, f32[2,8,64]{2,1,0:T(8,128)S(1)}) custom-call(bf16[32,8,768]{2,1,0:T(8,128)(2,1)S(1)} %all_to_all.22.third, bf16[4,64,640]{2,1,0:T(8,128)(2,1)S(1)} %bitcast.16, f32[8,640]{1,0:T(8,128)S(1)} %get-tuple-element.24.inputs, f32[8,128]{1,0:T(8,128)S(1)} %get-tuple-element.25.stats), custom_call_target="tpu_custom_call" | custom-call | flops 2621440 | bytes 946176 | tf_op jit(solution)/shard_map/pallas_call | solution.py:498
  64.9 3.0 %all-to-all-start.3 = ((bf16[32,4,768]{2,1,0:T(4,128)(2,1)}), bf16[32,4,768]{2,1,0:T(4,128)(2,1)S(1)}, u32[]{:S(2)}, u32[]{:S(2)}) async-start(bf16[32,4,768]{2,1,0:T(4,128)(2,1)} %get-tuple-element.26), calls=%async_computation.3 | async-start | bytes 393216 | tf_op jit(solution)/shard_map/all_to_all | solution.py:607
  68.0 0.0 copy-done.3
  68.0 0.0 copy-done.12
  68.0 0.4 shard_map.142.mixing
  68.4 2.5 %shard_map.145 = (bf16[32,64,320]{2,1,0:T(8,128)(2,1)}, bf16[32,64,320]{2,1,0:T(8,128)(2,1)}) custom-call(f32[2,64,64]{2,1,0:T(8,128)S(1)} %get-tuple-element.32.left_rows, f32[2,64,320]{2,1,0:T(8,128)S(1)} %get-tuple-element.33.right_rows), custom_call_target="tpu_custom_call" | custom-call | flops 20971520 | bytes 2818048 | tf_op jit(solution)/shard_map/pallas_call | solution.py:498
  70.9 1.2 %shard_map.144 = (bf16[4,64,640]{2,1,0:T(8,128)(2,1)}, bf16[4,64,640]{2,1,0:T(8,128)(2,1)}) custom-call(f32[2,8,64]{2,1,0:T(8,128)S(1)} %get-tuple-element.29.left_rows, bf16[2,8,640]{2,1,0:T(8,128)(2,1)S(1)} %get-tuple-element.30.right_rows), custom_call_target="tpu_custom_call" | custom-call | flops 5242880 | bytes 679936 | tf_op jit(solution)/shard_map/pallas_call | solution.py:498
  72.1 5.3 %all-to-all-done.3.fourth = bf16[32,4,768]{2,1,0:T(4,128)(2,1)S(1)} async-done(((bf16[32,4,768]{2,1,0:T(4,128)(2,1)}), bf16[32,4,768]{2,1,0:T(4,128)(2,1)S(1)}, u32[]{:S(2)}, u32[]{:S(2)}) %all-to-all-start.3) | async-done | bytes 196640 | tf_op jit(solution)/shard_map/all_to_all | solution.py:607
  77.4 0.0 copy-done.1
  77.4 0.0 copy-done.10
  77.4 1.8 %shard_map.143 = bf16[256,1280]{1,0:T(8,128)(2,1)} custom-call(bf16[32,4,768]{2,1,0:T(4,128)(2,1)S(1)} %all-to-all-done.3.fourth, bf16[256,1280]{1,0:T(8,128)(2,1)S(1)} %bitcast.11, bf16[64,1280]{1,0:T(8,128)(2,1)S(1)} %bitcast.19, f32[64,256]{1,0:T(8,128)S(1)} %get-tuple-element.27.logits, f32[64,256]{1,0:T(8,128)S(1)} %shard_map.142.mixing), custom_call_target="tpu_custom_call" | custom-call | flops 125829120 | bytes 1802240 | tf_op jit(solution)/shard_map/pallas_call | solution.py:498
  (1 shorter events, 0.0 us)
Async XLA Ops:
  0.6 1.1 %copy-start = (bf16[1,256,1280]{2,1,0:T(8,128)(2,1)S(1)}, bf16[1,256,1280]{2,1,0:T(8,128)(2,1)}, u32[]{:S(2)}) copy-start(bf16[1,256,1280]{2,1,0:T(8,128)(2,1)} %param.10) | copy-start | bytes 1966084
  1.7 1.1 %copy-start.2 = (bf16[1,256,1280]{2,1,0:T(8,128)(2,1)S(1)}, bf16[1,256,1280]{2,1,0:T(8,128)(2,1)}, u32[]{:S(2)}) copy-start(bf16[1,256,1280]{2,1,0:T(8,128)(2,1)} %param.11) | copy-start | bytes 1966084
  2.8 0.9 %copy-start.9 = (bf16[1280,64]{0,1:T(8,128)(2,1)S(1)}, bf16[1280,64]{0,1:T(8,128)(2,1)}, u32[]{:S(2)}) copy-start(bf16[1280,64]{0,1:T(8,128)(2,1)} %param.12) | copy-start | bytes 491524
  3.7 20.6 %copy-start.6 = (bf16[4,640,64]{1,2,0:T(8,128)(2,1)S(1)}, bf16[4,640,64]{1,2,0:T(8,128)(2,1)}, u32[]{:S(2)}) copy-start(bf16[4,640,64]{1,2,0:T(8,128)(2,1)} %param.16) | copy-start | bytes 983044
  3.7 39.5 %copy-start.5 = (bf16[32,320,64]{1,2,0:T(8,128)(2,1)S(1)}, bf16[32,320,64]{1,2,0:T(8,128)(2,1)}, u32[]{:S(2)}) copy-start(bf16[32,320,64]{1,2,0:T(8,128)(2,1)} %param.18) | copy-start | bytes 3932164
  5.5 37.7 %copy-start.4 = (bf16[32,64,320]{2,1,0:T(8,128)(2,1)S(1)}, bf16[32,64,320]{2,1,0:T(8,128)(2,1)}, u32[]{:S(2)}) copy-start(bf16[32,64,320]{2,1,0:T(8,128)(2,1)} %in_right.1) | copy-start | bytes 3932164
  5.5 37.7 %copy-start.7 = (bf16[1280,320]{0,1:T(8,128)(2,1)S(1)}, bf16[1280,320]{0,1:T(8,128)(2,1)}, u32[]{:S(2)}) copy-start(bf16[1280,320]{0,1:T(8,128)(2,1)} %param.14) | copy-start | bytes 2457604
  24.4 1.0 %copy-start.11 = (bf16[4,64,640]{2,1,0:T(8,128)(2,1)S(1)}, bf16[4,64,640]{2,1,0:T(8,128)(2,1)}, u32[]{:S(2)}) copy-start(bf16[4,64,640]{2,1,0:T(8,128)(2,1)} %out_right.1) | copy-start | bytes 983044
  26.0 5.1 %collective-permute-start.1 = (bf16[8,1536]{1,0:T(8,128)(2,1)S(1)}, bf16[8,1536]{1,0:T(8,128)(2,1)S(1)}, u32[]{:S(2)}, u32[]{:S(2)}) collective-permute-start(bf16[8,1536]{1,0:T(8,128)(2,1)S(1)} %get-tuple-element.22.own), channel_id=1, source_target_pairs={{16,8},{8,16},{17,9},{9,17},{18,10},{10,18},{19,11},{11,19},{20,12... | collective-permute-start | bytes 73736 | tf_op jit(solution)/shard_map/ppermute | solution.py:483
  26.7 5.4 %collective-permute-start = (bf16[8,1536]{1,0:T(8,128)(2,1)S(1)}, bf16[8,1536]{1,0:T(8,128)(2,1)S(1)}, u32[]{:S(2)}, u32[]{:S(2)}) collective-permute-start(bf16[8,1536]{1,0:T(8,128)(2,1)S(1)} %get-tuple-element.22.own), channel_id=1, source_target_pairs={{0,8},{16,0},{24,16},{8,24},{1,9},{17,1},{25,17},{9,25},{2,10},{18... | collective-permute-start | bytes 73736 | tf_op jit(solution)/shard_map/ppermute | solution.py:482
  43.2 1.1 %copy-start.8 = (bf16[320,1280]{1,0:T(8,128)(2,1)S(1)}, bf16[320,1280]{1,0:T(8,128)(2,1)}, u32[]{:S(2)}) copy-start(bf16[320,1280]{1,0:T(8,128)(2,1)} %base_out_far.1) | copy-start | bytes 2457604
  47.0 20.9 %copy-start.3 = (bf16[1,256,1280]{2,1,0:T(8,128)(2,1)S(1)}, bf16[1,256,1280]{2,1,0:T(8,128)(2,1)}, u32[]{:S(2)}) copy-start(bf16[1,256,1280]{2,1,0:T(8,128)(2,1)} %param.11) | copy-start | bytes 1966084
  47.0 20.9 %copy-start.12 = (bf16[1,64,1280]{2,1,0:T(8,128)(2,1)S(1)}, bf16[1,64,1280]{2,1,0:T(8,128)(2,1)}, u32[]{:S(2)}) copy-start(bf16[1,64,1280]{2,1,0:T(8,128)(2,1)} %param.13) | copy-start | bytes 491524
  47.1 30.4 %copy-start.1 = (bf16[1,256,1280]{2,1,0:T(8,128)(2,1)S(1)}, bf16[1,256,1280]{2,1,0:T(8,128)(2,1)}, u32[]{:S(2)}) copy-start(bf16[1,256,1280]{2,1,0:T(8,128)(2,1)} %param.10) | copy-start | bytes 1966084
  47.1 30.3 %copy-start.10 = (bf16[1280,64]{0,1:T(8,128)(2,1)S(1)}, bf16[1280,64]{0,1:T(8,128)(2,1)}, u32[]{:S(2)}) copy-start(bf16[1280,64]{0,1:T(8,128)(2,1)} %param.12) | copy-start | bytes 491524
  64.9 12.5 %all-to-all-start.3 = ((bf16[32,4,768]{2,1,0:T(4,128)(2,1)}), bf16[32,4,768]{2,1,0:T(4,128)(2,1)S(1)}, u32[]{:S(2)}, u32[]{:S(2)}) async-start(bf16[32,4,768]{2,1,0:T(4,128)(2,1)} %get-tuple-element.26), calls=%async_computation.3 | async-start | bytes 393216 | tf_op jit(solution)/shard_map/all_to_all | solution.py:607

commit v5 on v4

--- a/solution.py
+++ b/solution.py
@@ -7,7 +7,8 @@
 from jax.experimental.pallas import tpu as pltpu
 from jax.sharding import PartitionSpec as P
 
-BOTH = ("dp", "seq")
+SEQ = ("half", "place")
+BOTH = ("dp", *SEQ)
 STATS = 128
 
 
@@ -54,7 +55,7 @@
     out_left,
     out_right,
 ):
-    groups, ring = lax.axis_size("dp"), lax.axis_size("seq")
+    groups, ring = lax.axis_size("dp"), lax.axis_size(SEQ)
     image_rows = tokens[0]
     cot_rows = cotangent[0]
     saved_outputs = slot_outputs[0]
@@ -63,7 +64,7 @@
     owned, slice_width, rank = in_left.shape
     members = in_right.shape[0]
     places = members // owned
-    group, place = lax.axis_index("dp"), lax.axis_index("seq")
+    group, place = lax.axis_index("dp"), lax.axis_index(SEQ)
 
     logits = jnp.dot(image_rows, router, preferred_element_type=jnp.float32)
     peak_high, peak_low = split(jnp.max(logits, axis=0))
@@ -276,7 +277,8 @@
             first[block, :, 2 * width :] = stats[rows, :]
 
 
-def mixing_kernel(cotangent, saved, combine, out):
+def mixing_kernel(cotangent, saved, combine, *rest):
+    *_, out = rest
     mixing = dot_last(saved[...], cotangent[...])
     weights = combine[...]
     out[...] = weights * (mixing - jnp.sum(weights * mixing, axis=0, keepdims=True))
@@ -312,33 +314,31 @@
     second[...] = block
 
 
-def pack_kernel(groups, own, beside, across, out):
-    places = out.shape[0]
+def spread_kernel(block, out):
+    for group in range(2):
+        for half in range(2):
+            out[group, half] = block[...]
+
+
+def pack_kernel(blocks, out):
     group = lax.axis_index("dp")
-    here = group == lax.axis_index("seq") // places
-    near = jnp.where(here, own[...], beside[...])
-    far = jnp.where(here, beside[...], across[...])
-    first, last = jnp.where(group == 0, near, far), jnp.where(group == 0, far, near)
-    for place in range(places):
-        out[place, 0] = first
-        out[place, 1] = last
+    for number in range(2):
+        block = blocks[2 * number + group]
+        for place in range(out.shape[0]):
+            out[place, number] = block
 
 
 def hidden_kernel(
     groups,
     second,
     base_in,
-    base_out_far,
+    base_out,
     in_right,
     out_left,
     third,
     pair_out,
     ranks_out,
-    base_out,
-    arrived,
 ):
-    copy = pltpu.make_async_copy(base_out_far, base_out, arrived)
-    copy.start()
     members, rank, hidden = in_right.shape
     rows = second.shape[2]
     owned = rows // groups
@@ -379,7 +379,6 @@
         columns = slice(half * width, (half + 1) * width)
         preact = preact + dot_last(part.astype(jnp.bfloat16), base_in[:, columns])
     hidden_grad = low_rank(back, out_left)
-    copy.wait()
     for half, part in enumerate(gathered(slice(width, 2 * width))):
         columns = slice(half * width, (half + 1) * width)
         hidden_grad = hidden_grad + dot_last(part.astype(jnp.bfloat16), base_out[:, columns])
@@ -423,8 +422,7 @@
 
 def finish_kernel(groups, ring, third, in_left, inputs, stats, fourth, ranks_out):
     owned, rank, width = in_left.shape
-    members = ring // groups
-    sender = lax.axis_index("seq") // members
+    sender = lax.axis_index("half")
     summed = jnp.sum(third[pl.ds(sender * ring, ring)].astype(jnp.float32), axis=0)
     ranks = summed[:, width:].astype(jnp.bfloat16).astype(jnp.float32)
     ranks_out[0] = ranks[:, :rank]
@@ -467,31 +465,19 @@
     out[...] = dot_first(left, right).astype(jnp.bfloat16)
 
 
-def to_group(block, ring):
-    places = ring // 2
-
-    def device(group, half, place):
-        return group * ring + half * places + place
-
-    beside, across = [], []
-    for place in range(places):
-        for half in range(2):
-            beside.append((device(half, half, place), device(half, 1 - half, place)))
-            beside.append((device(1 - half, half, place), device(half, half, place)))
-            across.append((device(1 - half, half, place), device(half, 1 - half, place)))
-    beside = lax.ppermute(block, BOTH, beside)
-    across = lax.ppermute(block, BOTH, across)
+def to_group(block):
+    places = lax.axis_size("place")
     (blocks,) = call(
-        functools.partial(pack_kernel, 2),
-        [array(block.dtype, places, 2, *block.shape)],
-        [block, beside, across],
-        0,
-    )
-    halves = [[half * places + place for place in range(places)] for half in range(2)]
-    return lax.all_to_all(blocks, "seq", 0, 0, axis_index_groups=halves, tiled=True)
-
-
-def call(kernel, outs, args, flops, far=(), scratch=()):
+        spread_kernel, [array(block.dtype, 2, 2, *block.shape)], [block], 0
+    )
+    blocks = lax.all_to_all(blocks.reshape(4, *block.shape), ("dp", "half"), 0, 0, tiled=True)
+    (blocks,) = call(
+        pack_kernel, [array(block.dtype, places, 2, *block.shape)], [blocks], 0
+    )
+    return lax.all_to_all(blocks, "place", 0, 0, tiled=True)
+
+
+def call(kernel, outs, args, flops, far=(), scratch=(), grant=24):
     size = sum(array.size * array.dtype.itemsize for array in args)
     size += sum(out.size * out.dtype.itemsize for out in outs)
     spaces = [pltpu.HBM if number in far else pltpu.VMEM for number in range(len(args))]
@@ -502,7 +488,7 @@
         out_specs=[pl.BlockSpec(memory_space=pltpu.VMEM) for _ in outs],
         scratch_shapes=scratch,
         cost_estimate=pl.CostEstimate(flops=flops, bytes_accessed=size, transcendentals=0),
-        compiler_params=pltpu.CompilerParams(vmem_limit_bytes=24 * 2**20),
+        compiler_params=pltpu.CompilerParams(vmem_limit_bytes=grant * 2**20),
     )(*args)
 
 
@@ -522,7 +508,7 @@
     out_left,
     out_right,
 ):
-    groups, ring = lax.axis_size("dp"), lax.axis_size("seq")
+    groups, ring = lax.axis_size("dp"), lax.axis_size(SEQ)
     devices = groups * ring
     _, count, width = tokens.shape
     slots = router.shape[1]
@@ -558,14 +544,16 @@
         (0, 1, 2),
         [pltpu.VMEM((count, width), low)] * 2
         + [pltpu.VMEM((slots, width), low), pltpu.SemaphoreType.DMA((3,))],
+        60,
     )
     first = lax.all_to_all(first, BOTH, 0, 0, tiled=True)
     (mixing,) = call(
         mixing_kernel,
         [array(full, slots, count)],
-        [cot_rows, saved, combine],
+        [cot_rows, saved, combine, out_right, base_out],
         2 * count * slots * width,
     )
+    first, mixing = lax.optimization_barrier((first, mixing))
     second, inputs, lows, stats = call(
         functools.partial(owner_kernel, groups),
         [
@@ -577,7 +565,7 @@
         [first, in_left, out_right],
         4 * rows * owned * rank * slice_width,
     )
-    second = to_group(second, ring)
+    second = to_group(second)
     total_rows = groups * members
     third, pair, ranks = call(
         functools.partial(hidden_kernel, groups),
@@ -588,8 +576,6 @@
         ],
         [second, base_in, base_out, in_right, out_left],
         6 * total_rows * hidden * (width + owned * rank),
-        (2,),
-        [pltpu.VMEM((hidden, width), low), pltpu.SemaphoreType.DMA],
     )
     third = lax.all_to_all(third, BOTH, 0, 0, tiled=True)
     grad_in_right, grad_out_left = call(
@@ -627,23 +613,26 @@
 
 
 def solution(mesh):
+    groups, ring = mesh.shape["dp"], mesh.shape["seq"]
+    split = mesh.devices.reshape(groups, groups, ring // groups)
+    mesh = jax.sharding.Mesh(split, BOTH)
     in_specs = (
-        P("dp", "seq", None),
-        P("dp", "seq", None),
+        P("dp", SEQ, None),
+        P("dp", SEQ, None),
         P(),
         P("dp", None, None),
-        P(None, "seq"),
-        P("seq", None),
-        P("seq", "dp", None),
-        P("dp", None, "seq"),
-        P("dp", "seq", None),
-        P("seq", None, "dp"),
+        P(None, SEQ),
+        P(SEQ, None),
+        P(SEQ, "dp", None),
+        P("dp", None, SEQ),
+        P("dp", SEQ, None),
+        P(SEQ, None, "dp"),
     )
     out_specs = (
-        P("dp", "seq", None),
-        P("seq", "dp", None),
-        P("dp", None, "seq"),
-        P("dp", "seq", None),
-        P("seq", None, "dp"),
+        P("dp", SEQ, None),
+        P(SEQ, "dp", None),
+        P("dp", None, SEQ),
+        P("dp", SEQ, None),
+        P(SEQ, None, "dp"),
     )
     return jax.shard_map(local, mesh=mesh, in_specs=in_specs, out_specs=out_specs, check_vma=False)

time: 79.7 us -> 77.2 us (0.969)
  blocking collectives: 46.7 us -> 34 us
  waiting for transfers between devices: 6.29 us -> 16.4 us
  local copies, waits for them, and re-layouts: 5.24 us -> 2.29 us
  starting transfers between devices: 8.17 us -> 10.1 us
  Pallas kernels: 12 us -> 13.2 us
    all_to_all x2, blocking collectives: 29.9 us -> 19 us  [the longest x1 11.6 us: to_group(): return lax.all_to_all(blocks, 'place', 0, 0, tiled=True)]
    all_to_all x0 -> x1, waiting for transfers between devices: none -> 10.7 us  [local(): first = lax.all_to_all(first, BOTH, 0, 0, tiled=True)]
    all_to_all x0 -> x1, starting transfers between devices: none -> 7.1 us  [local(): first = lax.all_to_all(first, BOTH, 0, 0, tiled=True)]
    ppermute x2 -> x0, starting transfers between devices: 5.13 us -> none  [the longest x1 4.44 us: to_group(): beside = lax.ppermute(block, BOTH, beside)]
    unnamed x26 -> x24, local copies, waits for them, and re-layouts: 5.24 us -> 2.29 us
    all_to_all x1, blocking collectives: 16.8 us -> 15 us  [local(): third = lax.all_to_all(third, BOTH, 0, 0, tiled=True)]
    pallas_call x9 -> x10, Pallas kernels: 12 us -> 13.2 us  [call(): pl.pallas_call(kernel, out_shape=outs, in_specs=[pl.BlockSpec(memory_spac...]
    ppermute x2 -> x0, waiting for transfers between devices: 0.95 us -> none  [the longest x1 0.94 us: to_group(): beside = lax.ppermute(block, BOTH, beside)]
  transfers between devices with their start and end apart: 3 -> 2, of which waited for: 2 -> 2; matrix products, arithmetic and copies ran while one was open for 0% -> 0% of each run, Pallas kernels for 5% -> 5%
where the time goes in v5:
time: 77.2 us; the launch traced here: 76.8 us
  blocking collectives  34 us (44%)
  waiting for transfers between devices  16.4 us (21%)
  Pallas kernels  13.2 us (17%)
  starting transfers between devices  10.1 us (13%)
  local copies, waits for them, and re-layouts  2.29 us (3%)
  between operations  0.78 us (1%)
    all_to_all x1, blocking collectives, local(): third = lax.all_to_all(third, BOTH, 0, 0, tiled=True)  15 us
    pallas_call x10, Pallas kernels, call(): pl.pallas_call(kernel, out_shape=outs, in_specs=[pl.BlockSpec(memory_spac...  13.2 us
    all_to_all x1, blocking collectives, to_group(): return lax.all_to_all(blocks, 'place', 0, 0, tiled=True)  11.6 us
    all_to_all x1, waiting for transfers between devices, local(): first = lax.all_to_all(first, BOTH, 0, 0, tiled=True)  10.7 us
    all_to_all x1, blocking collectives, to_group(): lax.all_to_all(blocks.reshape(4, *block.shape), ('dp', 'half'), 0, 0, til...  7.38 us
    all_to_all x1, starting transfers between devices, local(): first = lax.all_to_all(first, BOTH, 0, 0, tiled=True)  7.1 us
    all_to_all x1, waiting for transfers between devices, local(): fourth = lax.all_to_all(fourth, BOTH, 0, 0, tiled=True)  5.73 us
    all_to_all x1, starting transfers between devices, local(): fourth = lax.all_to_all(fourth, BOTH, 0, 0, tiled=True)  3.04 us
  transfers between devices with their start and end apart: 2, of which 2 were waited for; matrix products, arithmetic and copies ran while one was open for 0% of the time, Pallas kernels for 5%

profile of v5, /device:TPU:1, one launch (start us, length us, event | category | flops | bytes accessed | tf_op | source)
XLA Modules:
  0.0 76.8 jit_solution(11944521105467557853)
XLA Ops:
  0.6 0.0 copy-start.2
  0.6 0.0 copy-start.6
  0.7 0.0 copy-start
  0.7 0.0 copy-start.9
  0.7 3.2 %shard_map.137 = (bf16[32,4,1408]{2,1,0:T(4,128)(2,1)}, f32[64,256]{1,0:T(8,128)}, f32[64,256]{1,0:T(8,128)}) custom-call(bf16[256,1280]{1,0:T(8,128)(2,1)} %bitcast.11, bf16[256,1280]{1,0:T(8,128)(2,1)} %bitcast.13, bf16[64,1280]{1,0:T(8,128)(2,1)} %bitcast.19), custom_call_target="tpu_custom_call" | custom-call | flops 125829120 | bytes 1966080 | tf_op jit(solution)/shard_map/pallas_call | solution.py:484
  3.9 0.0 copy-start.5
  3.9 7.1 %all-to-all-start = ((bf16[32,4,1408]{2,1,0:T(4,128)(2,1)}), bf16[32,4,1408]{2,1,0:T(4,128)(2,1)S(1)}, u32[]{:S(2)}, u32[]{:S(2)}) async-start(bf16[32,4,1408]{2,1,0:T(4,128)(2,1)} %get-tuple-element.23), calls=%async_computation | async-start | bytes 720896 | tf_op jit(solution)/shard_map/all_to_all | solution.py:549
  11.0 0.0 copy-done.2
  11.0 0.0 copy-done.6
  11.0 0.0 copy-done
  11.0 0.0 copy-done.9
  11.1 0.0 copy-start.11
  11.1 0.8 %copy-done.11 = f32[64,256]{1,0:T(8,128)S(1)} copy-done((f32[64,256]{1,0:T(8,128)S(1)}, f32[64,256]{1,0:T(8,128)}, u32[]{:S(2)}) %copy-start.11) | copy-done | bytes 65560
  11.9 0.4 shard_map.138.mixing
  12.3 0.0 copy-start.3
  12.3 10.7 %all-to-all-done.first = bf16[32,4,1408]{2,1,0:T(4,128)(2,1)S(1)} async-done(((bf16[32,4,1408]{2,1,0:T(4,128)(2,1)}), bf16[32,4,1408]{2,1,0:T(4,128)(2,1)S(1)}, u32[]{:S(2)}, u32[]{:S(2)}) %all-to-all-start) | async-done | bytes 360480 | tf_op jit(solution)/shard_map/all_to_all | solution.py:549
  22.9 0.0 copy-start.7
  22.9 0.0 copy-done.5
  22.9 0.7 shard_map.139
  23.7 7.4 %all_to_all.25.blocks = bf16[4,8,1536]{2,1,0:T(8,128)(2,1)S(1)} all-to-all(bf16[4,8,1536]{2,1,0:T(8,128)(2,1)S(1)} %bitcast.21), channel_id=1, replica_groups=mesh['dp'=2,'half'=2,'place'=8] {'dp','half'}, dimensions={0} | all-to-all | bytes 196608 | tf_op jit(solution)/shard_map/all_to_all | solution.py:473
  31.1 11.6 %all_to_all.26.second = bf16[8,2,8,1536]{3,2,1,0:T(8,128)(2,1)S(1)} all-to-all(bf16[8,2,8,1536]{3,2,1,0:T(8,128)(2,1)S(1)} %shard_map.141), channel_id=1, replica_groups=mesh['dp'=2,'half'=2,'place'=8] {'place'}, dimensions={0} | all-to-all | bytes 786432 | tf_op jit(solution)/shard_map/all_to_all | solution.py:477
  42.7 0.0 copy-done.3
  42.7 0.0 copy-done.7
  42.7 0.0 copy-start.4
  42.7 1.4 %copy-done.4 = bf16[32,320,64]{1,2,0:T(8,128)(2,1)S(1)} copy-done((bf16[32,320,64]{1,2,0:T(8,128)(2,1)S(1)}, bf16[32,320,64]{1,2,0:T(8,128)(2,1)}, u32[]{:S(2)}) %copy-start.4) | copy-done | bytes 1310744
  44.1 2.4 %shard_map.142 = (bf16[32,8,768]{2,1,0:T(8,128)(2,1)S(1)}, f32[2,64,320]{2,1,0:T(8,128)S(1)}, f32[2,64,64]{2,1,0:T(8,128)S(1)}) custom-call(bf16[8,2,8,1536]{3,2,1,0:T(8,128)(2,1)S(1)} %all_to_all.26.second, bf16[320,1280]{1,0:T(8,128)(2,1)S(1)} %bitcast.18, bf16[320,1280]{1,0:T(8,128)(2,1)S(1)} %copy-done, bf16[32,64,320]{2,1,0:T(8,128)(2,1)S(1)} %copy-done.3, ...), custom_call_target="tpu_custom_call" | custom-call | flops 188743680 | bytes 5242880 | tf_op jit(solution)/shard_map/pallas_call | solution.py:484
  46.5 0.0 copy-start.1
  46.5 0.0 copy-start.8
  46.5 0.0 copy-start.10
  46.5 15.0 %all_to_all.27.third = bf16[32,8,768]{2,1,0:T(8,128)(2,1)S(1)} all-to-all(bf16[32,8,768]{2,1,0:T(8,128)(2,1)S(1)} %get-tuple-element.27), channel_id=1, replica_groups=mesh['dp'=2,'half'=2,'place'=8] {'dp','half','place'}, dimensions={0} | all-to-all | bytes 786432 | tf_op jit(solution)/shard_map/all_to_all | solution.py:580
  61.5 1.0 %shard_map.143 = (bf16[32,4,768]{2,1,0:T(4,128)(2,1)}, f32[2,8,64]{2,1,0:T(8,128)S(1)}) custom-call(bf16[32,8,768]{2,1,0:T(8,128)(2,1)S(1)} %all_to_all.27.third, bf16[4,64,640]{2,1,0:T(8,128)(2,1)S(1)} %bitcast.17, f32[8,640]{1,0:T(8,128)S(1)} %get-tuple-element.28.inputs, f32[8,128]{1,0:T(8,128)S(1)} %get-tuple-element.29.stats), custom_call_target="tpu_custom_call" | custom-call | flops 2621440 | bytes 946176 | tf_op jit(solution)/shard_map/pallas_call | solution.py:484
  62.5 3.0 %all-to-all-start.4 = ((bf16[32,4,768]{2,1,0:T(4,128)(2,1)}), bf16[32,4,768]{2,1,0:T(4,128)(2,1)S(1)}, u32[]{:S(2)}, u32[]{:S(2)}) async-start(bf16[32,4,768]{2,1,0:T(4,128)(2,1)} %get-tuple-element.30), calls=%async_computation.4 | async-start | bytes 393216 | tf_op jit(solution)/shard_map/all_to_all | solution.py:593
  65.5 2.5 %shard_map.146 = (bf16[32,64,320]{2,1,0:T(8,128)(2,1)}, bf16[32,64,320]{2,1,0:T(8,128)(2,1)}) custom-call(f32[2,64,64]{2,1,0:T(8,128)S(1)} %get-tuple-element.36.left_rows, f32[2,64,320]{2,1,0:T(8,128)S(1)} %get-tuple-element.37.right_rows), custom_call_target="tpu_custom_call" | custom-call | flops 20971520 | bytes 2818048 | tf_op jit(solution)/shard_map/pallas_call | solution.py:484
  68.1 1.2 %shard_map.145 = (bf16[4,64,640]{2,1,0:T(8,128)(2,1)}, bf16[4,64,640]{2,1,0:T(8,128)(2,1)}) custom-call(f32[2,8,64]{2,1,0:T(8,128)S(1)} %get-tuple-element.33.left_rows, bf16[2,8,640]{2,1,0:T(8,128)(2,1)S(1)} %get-tuple-element.34.right_rows), custom_call_target="tpu_custom_call" | custom-call | flops 5242880 | bytes 679936 | tf_op jit(solution)/shard_map/pallas_call | solution.py:484
  69.2 5.7 %all-to-all-done.4.fourth = bf16[32,4,768]{2,1,0:T(4,128)(2,1)S(1)} async-done(((bf16[32,4,768]{2,1,0:T(4,128)(2,1)}), bf16[32,4,768]{2,1,0:T(4,128)(2,1)S(1)}, u32[]{:S(2)}, u32[]{:S(2)}) %all-to-all-start.4) | async-done | bytes 196640 | tf_op jit(solution)/shard_map/all_to_all | solution.py:593
  75.0 0.0 copy-done.1
  75.0 0.0 copy-done.8
  75.0 0.0 copy-done.10
  75.0 1.8 %shard_map.144 = bf16[256,1280]{1,0:T(8,128)(2,1)} custom-call(bf16[32,4,768]{2,1,0:T(4,128)(2,1)S(1)} %all-to-all-done.4.fourth, bf16[256,1280]{1,0:T(8,128)(2,1)S(1)} %bitcast.12, bf16[64,1280]{1,0:T(8,128)(2,1)S(1)} %bitcast.20, f32[64,256]{1,0:T(8,128)S(1)} %copy-done.10, f32[64,256]{1,0:T(8,128)S(1)} %shard_map.138.mixing), custom_call_target="tpu_custom_call" | custom-call | flops 125829120 | bytes 1802240 | tf_op jit(solution)/shard_map/pallas_call | solution.py:484
  (2 shorter events, 0.1 us)
Async XLA Ops:
  0.6 10.4 %copy-start.2 = (bf16[1,256,1280]{2,1,0:T(8,128)(2,1)S(1)}, bf16[1,256,1280]{2,1,0:T(8,128)(2,1)}, u32[]{:S(2)}) copy-start(bf16[1,256,1280]{2,1,0:T(8,128)(2,1)} %param.11) | copy-start | bytes 1966084
  0.6 10.4 %copy-start.6 = (bf16[4,64,640]{2,1,0:T(8,128)(2,1)S(1)}, bf16[4,64,640]{2,1,0:T(8,128)(2,1)}, u32[]{:S(2)}) copy-start(bf16[4,64,640]{2,1,0:T(8,128)(2,1)} %out_right.1) | copy-start | bytes 983044
  0.7 10.4 %copy-start = (bf16[320,1280]{1,0:T(8,128)(2,1)S(1)}, bf16[320,1280]{1,0:T(8,128)(2,1)}, u32[]{:S(2)}) copy-start(bf16[320,1280]{1,0:T(8,128)(2,1)} %base_out.1) | copy-start | bytes 2457604
  0.7 10.4 %copy-start.9 = (bf16[1,64,1280]{2,1,0:T(8,128)(2,1)S(1)}, bf16[1,64,1280]{2,1,0:T(8,128)(2,1)}, u32[]{:S(2)}) copy-start(bf16[1,64,1280]{2,1,0:T(8,128)(2,1)} %param.13) | copy-start | bytes 491524
  3.9 19.1 %copy-start.5 = (bf16[4,640,64]{1,2,0:T(8,128)(2,1)S(1)}, bf16[4,640,64]{1,2,0:T(8,128)(2,1)}, u32[]{:S(2)}) copy-start(bf16[4,640,64]{1,2,0:T(8,128)(2,1)} %param.16) | copy-start | bytes 983044
  3.9 19.0 %all-to-all-start = ((bf16[32,4,1408]{2,1,0:T(4,128)(2,1)}), bf16[32,4,1408]{2,1,0:T(4,128)(2,1)S(1)}, u32[]{:S(2)}, u32[]{:S(2)}) async-start(bf16[32,4,1408]{2,1,0:T(4,128)(2,1)} %get-tuple-element.23), calls=%async_computation | async-start | bytes 720896 | tf_op jit(solution)/shard_map/all_to_all | solution.py:549
  11.1 0.8 %copy-start.11 = (f32[64,256]{1,0:T(8,128)S(1)}, f32[64,256]{1,0:T(8,128)}, u32[]{:S(2)}) copy-start(f32[64,256]{1,0:T(8,128)} %get-tuple-element.24.combine) | copy-start | bytes 196612
  12.3 30.4 %copy-start.3 = (bf16[32,64,320]{2,1,0:T(8,128)(2,1)S(1)}, bf16[32,64,320]{2,1,0:T(8,128)(2,1)}, u32[]{:S(2)}) copy-start(bf16[32,64,320]{2,1,0:T(8,128)(2,1)} %in_right.1) | copy-start | bytes 3932164
  22.9 19.7 %copy-start.7 = (bf16[1280,320]{0,1:T(8,128)(2,1)S(1)}, bf16[1280,320]{0,1:T(8,128)(2,1)}, u32[]{:S(2)}) copy-start(bf16[1280,320]{0,1:T(8,128)(2,1)} %param.14) | copy-start | bytes 2457604
  42.7 1.4 %copy-start.4 = (bf16[32,320,64]{1,2,0:T(8,128)(2,1)S(1)}, bf16[32,320,64]{1,2,0:T(8,128)(2,1)}, u32[]{:S(2)}) copy-start(bf16[32,320,64]{1,2,0:T(8,128)(2,1)} %param.18) | copy-start | bytes 3932164
  46.5 28.4 %copy-start.1 = (bf16[1,256,1280]{2,1,0:T(8,128)(2,1)S(1)}, bf16[1,256,1280]{2,1,0:T(8,128)(2,1)}, u32[]{:S(2)}) copy-start(bf16[1,256,1280]{2,1,0:T(8,128)(2,1)} %param.10) | copy-start | bytes 1966084
  46.5 28.4 %copy-start.8 = (bf16[1280,64]{0,1:T(8,128)(2,1)S(1)}, bf16[1280,64]{0,1:T(8,128)(2,1)}, u32[]{:S(2)}) copy-start(bf16[1280,64]{0,1:T(8,128)(2,1)} %param.12) | copy-start | bytes 491524
  46.5 28.4 %copy-start.10 = (f32[64,256]{1,0:T(8,128)S(1)}, f32[64,256]{1,0:T(8,128)}, u32[]{:S(2)}) copy-start(f32[64,256]{1,0:T(8,128)} %get-tuple-element.31.logits) | copy-start | bytes 196612
  62.5 12.5 %all-to-all-start.4 = ((bf16[32,4,768]{2,1,0:T(4,128)(2,1)}), bf16[32,4,768]{2,1,0:T(4,128)(2,1)S(1)}, u32[]{:S(2)}, u32[]{:S(2)}) async-start(bf16[32,4,768]{2,1,0:T(4,128)(2,1)} %get-tuple-element.30), calls=%async_computation.4 | async-start | bytes 393216 | tf_op jit(solution)/shard_map/all_to_all | solution.py:593

commit v6 on v5

--- a/solution.py
+++ b/solution.py
@@ -550,7 +550,7 @@
     (mixing,) = call(
         mixing_kernel,
         [array(full, slots, count)],
-        [cot_rows, saved, combine, out_right, base_out],
+        [cot_rows, saved, combine, in_left, out_right, base_in, base_out, in_right, out_left],
         2 * count * slots * width,
     )
     first, mixing = lax.optimization_barrier((first, mixing))

time: 77.2 us -> 79.5 us (1.030)
  local copies, waits for them, and re-layouts: 2.29 us -> 10.5 us
  waiting for transfers between devices: 16.4 us -> 8.93 us
  Pallas kernels: 13.2 us -> 14.3 us
    unnamed x24 -> x44, local copies, waits for them, and re-layouts: 2.29 us -> 10.5 us
    all_to_all x1, waiting for transfers between devices: 10.7 us -> 4.97 us  [local(): first = lax.all_to_all(first, BOTH, 0, 0, tiled=True)]
    all_to_all x1, waiting for transfers between devices: 5.73 us -> 3.96 us  [local(): fourth = lax.all_to_all(fourth, BOTH, 0, 0, tiled=True)]
    pallas_call x10, Pallas kernels: 13.2 us -> 14.3 us  [call(): pl.pallas_call(kernel, out_shape=outs, in_specs=[pl.BlockSpec(memory_spac...]
where the time goes in v6:
time: 79.5 us; the launch traced here: 78.7 us
  blocking collectives  34 us (43%)
  Pallas kernels  14.3 us (18%)
  local copies, waits for them, and re-layouts  10.5 us (13%)
  starting transfers between devices  10.2 us (13%)
  waiting for transfers between devices  8.93 us (11%)
  between operations  0.81 us (1%)
    all_to_all x1, blocking collectives, local(): third = lax.all_to_all(third, BOTH, 0, 0, tiled=True)  15 us
    pallas_call x10, Pallas kernels, call(): pl.pallas_call(kernel, out_shape=outs, in_specs=[pl.BlockSpec(memory_spac...  14.3 us
    all_to_all x1, blocking collectives, to_group(): return lax.all_to_all(blocks, 'place', 0, 0, tiled=True)  11.6 us
    unnamed x44, local copies, waits for them, and re-layouts  10.5 us
    all_to_all x1, blocking collectives, to_group(): lax.all_to_all(blocks.reshape(4, *block.shape), ('dp', 'half'), 0, 0, til...  7.38 us
    all_to_all x1, starting transfers between devices, local(): first = lax.all_to_all(first, BOTH, 0, 0, tiled=True)  7.15 us
    all_to_all x1, waiting for transfers between devices, local(): first = lax.all_to_all(first, BOTH, 0, 0, tiled=True)  4.97 us
    all_to_all x1, waiting for transfers between devices, local(): fourth = lax.all_to_all(fourth, BOTH, 0, 0, tiled=True)  3.96 us
  transfers between devices with their start and end apart: 2, of which 2 were waited for; matrix products, arithmetic and copies ran while one was open for 0% of the time, Pallas kernels for 5%

profile of v6, /device:TPU:1, one launch (start us, length us, event | category | flops | bytes accessed | tf_op | source)
XLA Modules:
  0.0 78.7 jit_solution(18038779525589602721)
XLA Ops:
  0.6 0.0 copy-start
  0.6 0.0 copy-start.7
  0.7 0.0 copy-start.15
  0.7 3.2 %shard_map.137 = (bf16[32,4,1408]{2,1,0:T(4,128)(2,1)}, f32[64,256]{1,0:T(8,128)}, f32[64,256]{1,0:T(8,128)}) custom-call(bf16[256,1280]{1,0:T(8,128)(2,1)} %bitcast.20, bf16[256,1280]{1,0:T(8,128)(2,1)} %bitcast.18, bf16[64,1280]{1,0:T(8,128)(2,1)} %bitcast.22), custom_call_target="tpu_custom_call" | custom-call | flops 125829120 | bytes 1966080 | tf_op jit(solution)/shard_map/pallas_call | solution.py:484
  3.9 7.2 %all-to-all-start = ((bf16[32,4,1408]{2,1,0:T(4,128)(2,1)}), bf16[32,4,1408]{2,1,0:T(4,128)(2,1)}, u32[]{:S(2)}, u32[]{:S(2)}) async-start(bf16[32,4,1408]{2,1,0:T(4,128)(2,1)} %get-tuple-element.23), calls=%async_computation | async-start | bytes 720896 | tf_op jit(solution)/shard_map/all_to_all | solution.py:549
  11.0 0.0 copy-done
  11.1 0.0 copy-done.7
  11.1 0.0 copy-done.15
  11.1 0.0 copy-start.1
  11.1 1.4 %copy-done.1 = bf16[32,320,64]{1,2,0:T(8,128)(2,1)S(1)} copy-done((bf16[32,320,64]{1,2,0:T(8,128)(2,1)S(1)}, bf16[32,320,64]{1,2,0:T(8,128)(2,1)}, u32[]{:S(2)}) %copy-start.1) | copy-done | bytes 1310744
  12.5 0.0 copy-start.3
  12.5 1.1 %copy-done.3 = bf16[1280,320]{0,1:T(8,128)(2,1)S(1)} copy-done((bf16[1280,320]{0,1:T(8,128)(2,1)S(1)}, bf16[1280,320]{0,1:T(8,128)(2,1)}, u32[]{:S(2)}) %copy-start.3) | copy-done | bytes 819224
  13.6 0.0 copy-start.5
  13.6 1.1 %copy-done.5 = bf16[320,1280]{1,0:T(8,128)(2,1)S(1)} copy-done((bf16[320,1280]{1,0:T(8,128)(2,1)S(1)}, bf16[320,1280]{1,0:T(8,128)(2,1)}, u32[]{:S(2)}) %copy-start.5) | copy-done | bytes 819224
  14.8 0.0 copy-start.8
  14.8 1.1 %copy-done.8 = bf16[1,256,1280]{2,1,0:T(8,128)(2,1)S(1)} copy-done((bf16[1,256,1280]{2,1,0:T(8,128)(2,1)S(1)}, bf16[1,256,1280]{2,1,0:T(8,128)(2,1)}, u32[]{:S(2)}) %copy-start.8) | copy-done | bytes 655384
  15.9 0.0 copy-start.10
  15.9 1.0 %copy-done.10 = bf16[4,64,640]{2,1,0:T(8,128)(2,1)S(1)} copy-done((bf16[4,64,640]{2,1,0:T(8,128)(2,1)S(1)}, bf16[4,64,640]{2,1,0:T(8,128)(2,1)}, u32[]{:S(2)}) %copy-start.10) | copy-done | bytes 327704
  16.8 0.0 copy-start.16
  16.8 0.8 %copy-done.16 = f32[64,256]{1,0:T(8,128)S(1)} copy-done((f32[64,256]{1,0:T(8,128)S(1)}, f32[64,256]{1,0:T(8,128)}, u32[]{:S(2)}) %copy-start.16) | copy-done | bytes 65560
  17.7 0.4 shard_map.138.mixing
  18.0 0.0 copy-start.2
  18.1 5.0 %all-to-all-done.first = bf16[32,4,1408]{2,1,0:T(4,128)(2,1)} async-done(((bf16[32,4,1408]{2,1,0:T(4,128)(2,1)}), bf16[32,4,1408]{2,1,0:T(4,128)(2,1)}, u32[]{:S(2)}, u32[]{:S(2)}) %all-to-all-start) | async-done | bytes 360480 | tf_op jit(solution)/shard_map/all_to_all | solution.py:549
  23.0 0.0 copy-start.11
  23.0 1.0 %copy-done.11 = bf16[4,64,640]{2,1,0:T(8,128)(2,1)S(1)} copy-done((bf16[4,64,640]{2,1,0:T(8,128)(2,1)S(1)}, bf16[4,64,640]{2,1,0:T(8,128)(2,1)}, u32[]{:S(2)}) %copy-start.11) | copy-done | bytes 327704
  24.0 0.0 copy-start.4
  24.0 1.7 %shard_map.139 = (bf16[8,1536]{1,0:T(8,128)(2,1)S(1)}, f32[8,640]{1,0:T(8,128)S(1)}, bf16[2,8,640]{2,1,0:T(8,128)(2,1)S(1)}, f32[8,128]{1,0:T(8,128)S(1)}) custom-call(bf16[32,4,1408]{2,1,0:T(4,128)(2,1)} %all-to-all-done.first, bf16[4,64,640]{2,1,0:T(8,128)(2,1)S(1)} %bitcast.16, bf16[4,64,640]{2,1,0:T(8,128)(2,1)S(1)} %copy-done.11), custom_call_target="tpu_custom_call" | custom-call | flops 5242880 | bytes 1085440 | tf_op jit(solution)/shard_map/pallas_call | solution.py:484
  25.7 0.0 copy-start.20
  25.8 7.4 %all_to_all.25.blocks = bf16[4,8,1536]{2,1,0:T(8,128)(2,1)S(1)} all-to-all(bf16[4,8,1536]{2,1,0:T(8,128)(2,1)S(1)} %bitcast.24), channel_id=1, replica_groups=mesh['dp'=2,'half'=2,'place'=8] {'dp','half'}, dimensions={0} | all-to-all | bytes 196608 | tf_op jit(solution)/shard_map/all_to_all | solution.py:473
  33.2 11.6 %all_to_all.26.second = bf16[8,2,8,1536]{3,2,1,0:T(8,128)(2,1)S(1)} all-to-all(bf16[8,2,8,1536]{3,2,1,0:T(8,128)(2,1)S(1)} %shard_map.141), channel_id=1, replica_groups=mesh['dp'=2,'half'=2,'place'=8] {'place'}, dimensions={0} | all-to-all | bytes 786432 | tf_op jit(solution)/shard_map/all_to_all | solution.py:477
  44.8 0.0 copy-done.2
  44.8 0.0 copy-done.4
  44.8 0.0 copy-start.6
  44.8 1.1 %copy-done.6 = bf16[320,1280]{1,0:T(8,128)(2,1)S(1)} copy-done((bf16[320,1280]{1,0:T(8,128)(2,1)S(1)}, bf16[320,1280]{1,0:T(8,128)(2,1)}, u32[]{:S(2)}) %copy-start.6) | copy-done | bytes 819224
  46.0 2.4 %shard_map.142 = (bf16[32,8,768]{2,1,0:T(8,128)(2,1)S(1)}, f32[2,64,320]{2,1,0:T(8,128)S(1)}, f32[2,64,64]{2,1,0:T(8,128)S(1)}) custom-call(bf16[8,2,8,1536]{3,2,1,0:T(8,128)(2,1)S(1)} %all_to_all.26.second, bf16[320,1280]{1,0:T(8,128)(2,1)S(1)} %bitcast.14, bf16[320,1280]{1,0:T(8,128)(2,1)S(1)} %copy-done.6, bf16[32,64,320]{2,1,0:T(8,128)(2,1)S(1)} %copy-done, ...), custom_call_target="tpu_custom_call" | custom-call | flops 188743680 | bytes 5242880 | tf_op jit(solution)/shard_map/pallas_call | solution.py:484
  48.4 0.0 copy-done.20
  48.4 0.0 copy-start.13
  48.4 0.0 copy-start.18
  48.4 0.0 copy-start.9
  48.4 0.0 copy-start.12
  48.4 0.0 copy-start.17
  48.5 0.0 copy-start.21
  48.5 15.0 %all_to_all.27.third = bf16[32,8,768]{2,1,0:T(8,128)(2,1)S(1)} all-to-all(bf16[32,8,768]{2,1,0:T(8,128)(2,1)S(1)} %get-tuple-element.27), channel_id=1, replica_groups=mesh['dp'=2,'half'=2,'place'=8] {'dp','half','place'}, dimensions={0} | all-to-all | bytes 786432 | tf_op jit(solution)/shard_map/all_to_all | solution.py:580
  63.4 1.0 %shard_map.143 = (bf16[32,4,768]{2,1,0:T(4,128)(2,1)}, f32[2,8,64]{2,1,0:T(8,128)S(1)}) custom-call(bf16[32,8,768]{2,1,0:T(8,128)(2,1)S(1)} %all_to_all.27.third, bf16[4,64,640]{2,1,0:T(8,128)(2,1)S(1)} %bitcast.17, f32[8,640]{1,0:T(8,128)S(1)} %get-tuple-element.28.inputs, f32[8,128]{1,0:T(8,128)S(1)} %get-tuple-element.29.stats), custom_call_target="tpu_custom_call" | custom-call | flops 2621440 | bytes 946176 | tf_op jit(solution)/shard_map/pallas_call | solution.py:484
  64.4 0.0 copy-done.13
  64.4 0.0 copy-done.18
  64.4 3.0 %all-to-all-start.4 = ((bf16[32,4,768]{2,1,0:T(4,128)(2,1)}), bf16[32,4,768]{2,1,0:T(4,128)(2,1)S(1)}, u32[]{:S(2)}, u32[]{:S(2)}) async-start(bf16[32,4,768]{2,1,0:T(4,128)(2,1)} %get-tuple-element.30), calls=%async_computation.4 | async-start | bytes 393216 | tf_op jit(solution)/shard_map/all_to_all | solution.py:593
  67.5 0.0 copy-start.14
  67.5 0.9 %copy-done.14 = f32[2,64,320]{2,1,0:T(8,128)S(1)} copy-done((f32[2,64,320]{2,1,0:T(8,128)S(1)}, f32[2,64,320]{2,1,0:T(8,128)}, u32[]{:S(2)}) %copy-start.14) | copy-done | bytes 163864
  68.4 0.0 copy-start.19
  68.4 0.8 %copy-done.19 = f32[2,64,64]{2,1,0:T(8,128)S(1)} copy-done((f32[2,64,64]{2,1,0:T(8,128)S(1)}, f32[2,64,64]{2,1,0:T(8,128)}, u32[]{:S(2)}) %copy-start.19) | copy-done | bytes 32792
  69.2 2.5 %shard_map.146 = (bf16[32,64,320]{2,1,0:T(8,128)(2,1)}, bf16[32,64,320]{2,1,0:T(8,128)(2,1)}) custom-call(f32[2,64,64]{2,1,0:T(8,128)S(1)} %copy-done.19, f32[2,64,320]{2,1,0:T(8,128)S(1)} %copy-done.14), custom_call_target="tpu_custom_call" | custom-call | flops 20971520 | bytes 2818048 | tf_op jit(solution)/shard_map/pallas_call | solution.py:484
  71.8 0.0 copy-done.21
  71.8 1.2 %shard_map.145 = (bf16[4,64,640]{2,1,0:T(8,128)(2,1)}, bf16[4,64,640]{2,1,0:T(8,128)(2,1)}) custom-call(f32[2,8,64]{2,1,0:T(8,128)S(1)} %get-tuple-element.33.left_rows, bf16[2,8,640]{2,1,0:T(8,128)(2,1)S(1)} %copy-done.21), custom_call_target="tpu_custom_call" | custom-call | flops 5242880 | bytes 679936 | tf_op jit(solution)/shard_map/pallas_call | solution.py:484
  72.9 4.0 %all-to-all-done.4.fourth = bf16[32,4,768]{2,1,0:T(4,128)(2,1)S(1)} async-done(((bf16[32,4,768]{2,1,0:T(4,128)(2,1)}), bf16[32,4,768]{2,1,0:T(4,128)(2,1)S(1)}, u32[]{:S(2)}, u32[]{:S(2)}) %all-to-all-start.4) | async-done | bytes 196640 | tf_op jit(solution)/shard_map/all_to_all | solution.py:593
  76.9 0.0 copy-done.9
  76.9 0.0 copy-done.12
  76.9 0.0 copy-done.17
  76.9 1.8 %shard_map.144 = bf16[256,1280]{1,0:T(8,128)(2,1)} custom-call(bf16[32,4,768]{2,1,0:T(4,128)(2,1)S(1)} %all-to-all-done.4.fourth, bf16[256,1280]{1,0:T(8,128)(2,1)S(1)} %bitcast.21, bf16[64,1280]{1,0:T(8,128)(2,1)S(1)} %bitcast.23, f32[64,256]{1,0:T(8,128)S(1)} %copy-done.17, f32[64,256]{1,0:T(8,128)S(1)} %shard_map.138.mixing), custom_call_target="tpu_custom_call" | custom-call | flops 125829120 | bytes 1802240 | tf_op jit(solution)/shard_map/pallas_call | solution.py:484
  (2 shorter events, 0.1 us)
Async XLA Ops:
  0.6 10.4 %copy-start = (bf16[32,64,320]{2,1,0:T(8,128)(2,1)S(1)}, bf16[32,64,320]{2,1,0:T(8,128)(2,1)}, u32[]{:S(2)}) copy-start(bf16[32,64,320]{2,1,0:T(8,128)(2,1)} %in_right.1) | copy-start | bytes 3932164
  0.6 10.4 %copy-start.7 = (bf16[4,640,64]{1,2,0:T(8,128)(2,1)S(1)}, bf16[4,640,64]{1,2,0:T(8,128)(2,1)}, u32[]{:S(2)}) copy-start(bf16[4,640,64]{1,2,0:T(8,128)(2,1)} %param.16) | copy-start | bytes 983044
  0.7 10.4 %copy-start.15 = (bf16[1,64,1280]{2,1,0:T(8,128)(2,1)S(1)}, bf16[1,64,1280]{2,1,0:T(8,128)(2,1)}, u32[]{:S(2)}) copy-start(bf16[1,64,1280]{2,1,0:T(8,128)(2,1)} %param.13) | copy-start | bytes 491524
  3.9 19.1 %all-to-all-start = ((bf16[32,4,1408]{2,1,0:T(4,128)(2,1)}), bf16[32,4,1408]{2,1,0:T(4,128)(2,1)}, u32[]{:S(2)}, u32[]{:S(2)}) async-start(bf16[32,4,1408]{2,1,0:T(4,128)(2,1)} %get-tuple-element.23), calls=%async_computation | async-start | bytes 720896 | tf_op jit(solution)/shard_map/all_to_all | solution.py:549
  11.1 1.4 %copy-start.1 = (bf16[32,320,64]{1,2,0:T(8,128)(2,1)S(1)}, bf16[32,320,64]{1,2,0:T(8,128)(2,1)}, u32[]{:S(2)}) copy-start(bf16[32,320,64]{1,2,0:T(8,128)(2,1)} %param.18) | copy-start | bytes 3932164
  12.5 1.1 %copy-start.3 = (bf16[1280,320]{0,1:T(8,128)(2,1)S(1)}, bf16[1280,320]{0,1:T(8,128)(2,1)}, u32[]{:S(2)}) copy-start(bf16[1280,320]{0,1:T(8,128)(2,1)} %param.14) | copy-start | bytes 2457604
  13.6 1.1 %copy-start.5 = (bf16[320,1280]{1,0:T(8,128)(2,1)S(1)}, bf16[320,1280]{1,0:T(8,128)(2,1)}, u32[]{:S(2)}) copy-start(bf16[320,1280]{1,0:T(8,128)(2,1)} %base_out.1) | copy-start | bytes 2457604
  14.8 1.1 %copy-start.8 = (bf16[1,256,1280]{2,1,0:T(8,128)(2,1)S(1)}, bf16[1,256,1280]{2,1,0:T(8,128)(2,1)}, u32[]{:S(2)}) copy-start(bf16[1,256,1280]{2,1,0:T(8,128)(2,1)} %param.11) | copy-start | bytes 1966084
  15.9 1.0 %copy-start.10 = (bf16[4,64,640]{2,1,0:T(8,128)(2,1)S(1)}, bf16[4,64,640]{2,1,0:T(8,128)(2,1)}, u32[]{:S(2)}) copy-start(bf16[4,64,640]{2,1,0:T(8,128)(2,1)} %out_right.1) | copy-start | bytes 983044
  16.8 0.8 %copy-start.16 = (f32[64,256]{1,0:T(8,128)S(1)}, f32[64,256]{1,0:T(8,128)}, u32[]{:S(2)}) copy-start(f32[64,256]{1,0:T(8,128)} %get-tuple-element.24.combine) | copy-start | bytes 196612
  18.0 26.8 %copy-start.2 = (bf16[32,320,64]{1,2,0:T(8,128)(2,1)S(1)}, bf16[32,320,64]{1,2,0:T(8,128)(2,1)}, u32[]{:S(2)}) copy-start(bf16[32,320,64]{1,2,0:T(8,128)(2,1)} %param.18) | copy-start | bytes 3932164
  23.0 1.0 %copy-start.11 = (bf16[4,64,640]{2,1,0:T(8,128)(2,1)S(1)}, bf16[4,64,640]{2,1,0:T(8,128)(2,1)}, u32[]{:S(2)}) copy-start(bf16[4,64,640]{2,1,0:T(8,128)(2,1)} %out_right.1) | copy-start | bytes 983044
  24.0 20.8 %copy-start.4 = (bf16[1280,320]{0,1:T(8,128)(2,1)S(1)}, bf16[1280,320]{0,1:T(8,128)(2,1)}, u32[]{:S(2)}) copy-start(bf16[1280,320]{0,1:T(8,128)(2,1)} %param.14) | copy-start | bytes 2457604
  25.7 22.7 %copy-start.20 = (bf16[2,8,640]{2,1,0:T(8,128)(2,1)}, bf16[2,8,640]{2,1,0:T(8,128)(2,1)S(1)}, u32[]{:S(2)}) copy-start(bf16[2,8,640]{2,1,0:T(8,128)(2,1)S(1)} %get-tuple-element.34.right_rows) | copy-start | bytes 61444
  44.8 1.1 %copy-start.6 = (bf16[320,1280]{1,0:T(8,128)(2,1)S(1)}, bf16[320,1280]{1,0:T(8,128)(2,1)}, u32[]{:S(2)}) copy-start(bf16[320,1280]{1,0:T(8,128)(2,1)} %base_out.1) | copy-start | bytes 2457604
  48.4 16.0 %copy-start.13 = (f32[2,64,320]{2,1,0:T(8,128)}, f32[2,64,320]{2,1,0:T(8,128)S(1)}, u32[]{:S(2)}) copy-start(f32[2,64,320]{2,1,0:T(8,128)S(1)} %get-tuple-element.37.right_rows) | copy-start | bytes 491524
  48.4 16.0 %copy-start.18 = (f32[2,64,64]{2,1,0:T(8,128)}, f32[2,64,64]{2,1,0:T(8,128)S(1)}, u32[]{:S(2)}) copy-start(f32[2,64,64]{2,1,0:T(8,128)S(1)} %get-tuple-element.36.left_rows) | copy-start | bytes 98308
  48.4 28.5 %copy-start.9 = (bf16[1,256,1280]{2,1,0:T(8,128)(2,1)S(1)}, bf16[1,256,1280]{2,1,0:T(8,128)(2,1)}, u32[]{:S(2)}) copy-start(bf16[1,256,1280]{2,1,0:T(8,128)(2,1)} %param.10) | copy-start | bytes 1966084
  48.4 28.5 %copy-start.12 = (bf16[1280,64]{0,1:T(8,128)(2,1)S(1)}, bf16[1280,64]{0,1:T(8,128)(2,1)}, u32[]{:S(2)}) copy-start(bf16[1280,64]{0,1:T(8,128)(2,1)} %param.12) | copy-start | bytes 491524
  48.4 28.5 %copy-start.17 = (f32[64,256]{1,0:T(8,128)S(1)}, f32[64,256]{1,0:T(8,128)}, u32[]{:S(2)}) copy-start(f32[64,256]{1,0:T(8,128)} %get-tuple-element.31.logits) | copy-start | bytes 196612
  48.5 23.3 %copy-start.21 = (bf16[2,8,640]{2,1,0:T(8,128)(2,1)S(1)}, bf16[2,8,640]{2,1,0:T(8,128)(2,1)}, u32[]{:S(2)}) copy-start(bf16[2,8,640]{2,1,0:T(8,128)(2,1)} %copy-done.20) | copy-start | bytes 61444
  64.4 12.5 %all-to-all-start.4 = ((bf16[32,4,768]{2,1,0:T(4,128)(2,1)}), bf16[32,4,768]{2,1,0:T(4,128)(2,1)S(1)}, u32[]{:S(2)}, u32[]{:S(2)}) async-start(bf16[32,4,768]{2,1,0:T(4,128)(2,1)} %get-tuple-element.30), calls=%async_computation.4 | async-start | bytes 393216 | tf_op jit(solution)/shard_map/all_to_all | solution.py:593
  67.5 0.9 %copy-start.14 = (f32[2,64,320]{2,1,0:T(8,128)S(1)}, f32[2,64,320]{2,1,0:T(8,128)}, u32[]{:S(2)}) copy-start(f32[2,64,320]{2,1,0:T(8,128)} %copy-done.13) | copy-start | bytes 491524
  68.4 0.8 %copy-start.19 = (f32[2,64,64]{2,1,0:T(8,128)S(1)}, f32[2,64,64]{2,1,0:T(8,128)}, u32[]{:S(2)}) copy-start(f32[2,64,64]{2,1,0:T(8,128)} %copy-done.18) | copy-start | bytes 98308

commit v7 on v6

--- a/solution.py
+++ b/solution.py
@@ -278,7 +278,8 @@
 
 
 def mixing_kernel(cotangent, saved, combine, *rest):
-    *_, out = rest
+    *_, table, out, table_out = rest
+    table_out[...] = table[...]
     mixing = dot_last(saved[...], cotangent[...])
     weights = combine[...]
     out[...] = weights * (mixing - jnp.sum(weights * mixing, axis=0, keepdims=True))
@@ -547,13 +548,13 @@
         60,
     )
     first = lax.all_to_all(first, BOTH, 0, 0, tiled=True)
-    (mixing,) = call(
+    mixing, out_left = call(
         mixing_kernel,
-        [array(full, slots, count)],
-        [cot_rows, saved, combine, in_left, out_right, base_in, base_out, in_right, out_left],
+        [array(full, slots, count), array(low, *out_left.shape)],
+        [cot_rows, saved, combine, out_right, base_out, out_left],
         2 * count * slots * width,
     )
-    first, mixing = lax.optimization_barrier((first, mixing))
+    first, mixing, out_left = lax.optimization_barrier((first, mixing, out_left))
     second, inputs, lows, stats = call(
         functools.partial(owner_kernel, groups),
         [

time: 79.5 us -> 77.2 us (0.971)
  local copies, waits for them, and re-layouts: 10.5 us -> 4.83 us
  waiting for transfers between devices: 8.93 us -> 13.7 us
  Pallas kernels: 14.3 us -> 13.4 us
    unnamed x44 -> x28, local copies, waits for them, and re-layouts: 10.5 us -> 4.83 us
    all_to_all x1, waiting for transfers between devices: 4.97 us -> 7.98 us  [local(): first = lax.all_to_all(first, BOTH, 0, 0, tiled=True)]
    all_to_all x1, waiting for transfers between devices: 3.96 us -> 5.74 us  [local(): fourth = lax.all_to_all(fourth, BOTH, 0, 0, tiled=True)]
    pallas_call x10, Pallas kernels: 14.3 us -> 13.4 us  [call(): pl.pallas_call(kernel, out_shape=outs, in_specs=[pl.BlockSpec(memory_spac...]
where the time goes in v7:
time: 77.2 us; the launch traced here: 76.8 us
  blocking collectives  34 us (44%)
  waiting for transfers between devices  13.7 us (18%)
  Pallas kernels  13.4 us (17%)
  starting transfers between devices  10.1 us (13%)
  local copies, waits for them, and re-layouts  4.83 us (6%)
  between operations  0.78 us (1%)
    all_to_all x1, blocking collectives, local(): third = lax.all_to_all(third, BOTH, 0, 0, tiled=True)  15 us
    pallas_call x10, Pallas kernels, call(): pl.pallas_call(kernel, out_shape=outs, in_specs=[pl.BlockSpec(memory_spac...  13.4 us
    all_to_all x1, blocking collectives, to_group(): return lax.all_to_all(blocks, 'place', 0, 0, tiled=True)  11.6 us
    all_to_all x1, waiting for transfers between devices, local(): first = lax.all_to_all(first, BOTH, 0, 0, tiled=True)  7.98 us
    all_to_all x1, blocking collectives, to_group(): lax.all_to_all(blocks.reshape(4, *block.shape), ('dp', 'half'), 0, 0, til...  7.38 us
    all_to_all x1, starting transfers between devices, local(): first = lax.all_to_all(first, BOTH, 0, 0, tiled=True)  7.1 us
    all_to_all x1, waiting for transfers between devices, local(): fourth = lax.all_to_all(fourth, BOTH, 0, 0, tiled=True)  5.74 us
    unnamed x28, local copies, waits for them, and re-layouts  4.83 us
  transfers between devices with their start and end apart: 2, of which 2 were waited for; matrix products, arithmetic and copies ran while one was open for 0% of the time, Pallas kernels for 5%

profile of v7, /device:TPU:1, one launch (start us, length us, event | category | flops | bytes accessed | tf_op | source)
XLA Modules:
  0.0 76.8 jit_solution(12392545740352008366)
XLA Ops:
  0.6 0.0 copy-start.1
  0.6 0.0 copy-start.7
  0.7 0.0 copy-start
  0.7 0.0 copy-start.11
  0.7 3.2 %shard_map.137 = (bf16[32,4,1408]{2,1,0:T(4,128)(2,1)}, f32[64,256]{1,0:T(8,128)}, f32[64,256]{1,0:T(8,128)}) custom-call(bf16[256,1280]{1,0:T(8,128)(2,1)} %bitcast.13, bf16[256,1280]{1,0:T(8,128)(2,1)} %bitcast.11, bf16[64,1280]{1,0:T(8,128)(2,1)} %bitcast.19), custom_call_target="tpu_custom_call" | custom-call | flops 125829120 | bytes 1966080 | tf_op jit(solution)/shard_map/pallas_call | solution.py:485
  3.9 7.1 %all-to-all-start = ((bf16[32,4,1408]{2,1,0:T(4,128)(2,1)}), bf16[32,4,1408]{2,1,0:T(4,128)(2,1)S(1)}, u32[]{:S(2)}, u32[]{:S(2)}) async-start(bf16[32,4,1408]{2,1,0:T(4,128)(2,1)} %get-tuple-element.26), calls=%async_computation | async-start | bytes 720896 | tf_op jit(solution)/shard_map/all_to_all | solution.py:550
  11.0 0.0 copy-done.1
  11.0 0.0 copy-done.7
  11.0 0.0 copy-done
  11.0 0.0 copy-done.11
  11.0 0.0 copy-start.3
  11.1 1.4 %copy-done.3 = bf16[32,320,64]{1,2,0:T(8,128)(2,1)S(1)} copy-done((bf16[32,320,64]{1,2,0:T(8,128)(2,1)S(1)}, bf16[32,320,64]{1,2,0:T(8,128)(2,1)}, u32[]{:S(2)}) %copy-start.3) | copy-done | bytes 1310744
  12.5 0.0 copy-start.12
  12.5 0.8 %copy-done.12 = f32[64,256]{1,0:T(8,128)S(1)} copy-done((f32[64,256]{1,0:T(8,128)S(1)}, f32[64,256]{1,0:T(8,128)}, u32[]{:S(2)}) %copy-start.12) | copy-done | bytes 65560
  13.3 0.0 copy-start.8
  13.3 0.5 shard_map.138
  13.8 0.0 copy-start.5
  13.8 1.1 %copy-done.5 = bf16[32,64,320]{2,1,0:T(8,128)(2,1)} copy-done((bf16[32,64,320]{2,1,0:T(8,128)(2,1)}, bf16[32,64,320]{2,1,0:T(8,128)(2,1)S(1)}, u32[]{:S(2)}) %copy-start.5) | copy-done | bytes 1310744
  14.9 0.0 copy-start.4
  14.9 8.0 %all-to-all-done.first = bf16[32,4,1408]{2,1,0:T(4,128)(2,1)S(1)} async-done(((bf16[32,4,1408]{2,1,0:T(4,128)(2,1)}), bf16[32,4,1408]{2,1,0:T(4,128)(2,1)S(1)}, u32[]{:S(2)}, u32[]{:S(2)}) %all-to-all-start) | async-done | bytes 360480 | tf_op jit(solution)/shard_map/all_to_all | solution.py:550
  22.9 0.0 copy-start.9
  22.9 0.0 copy-done.8
  22.9 0.7 shard_map.139
  23.6 7.4 %all_to_all.25.blocks = bf16[4,8,1536]{2,1,0:T(8,128)(2,1)S(1)} all-to-all(bf16[4,8,1536]{2,1,0:T(8,128)(2,1)S(1)} %bitcast.21), channel_id=1, replica_groups=mesh['dp'=2,'half'=2,'place'=8] {'dp','half'}, dimensions={0} | all-to-all | bytes 196608 | tf_op jit(solution)/shard_map/all_to_all | solution.py:474
  31.0 11.6 %all_to_all.26.second = bf16[8,2,8,1536]{3,2,1,0:T(8,128)(2,1)S(1)} all-to-all(bf16[8,2,8,1536]{3,2,1,0:T(8,128)(2,1)S(1)} %shard_map.141), channel_id=1, replica_groups=mesh['dp'=2,'half'=2,'place'=8] {'place'}, dimensions={0} | all-to-all | bytes 786432 | tf_op jit(solution)/shard_map/all_to_all | solution.py:478
  42.7 0.0 copy-done.4
  42.7 0.0 copy-done.9
  42.7 0.0 copy-start.6
  42.7 1.4 %copy-done.6 = bf16[32,64,320]{2,1,0:T(8,128)(2,1)S(1)} copy-done((bf16[32,64,320]{2,1,0:T(8,128)(2,1)S(1)}, bf16[32,64,320]{2,1,0:T(8,128)(2,1)}, u32[]{:S(2)}) %copy-start.6) | copy-done | bytes 1310744
  44.1 2.4 %shard_map.142 = (bf16[32,8,768]{2,1,0:T(8,128)(2,1)S(1)}, f32[2,64,320]{2,1,0:T(8,128)S(1)}, f32[2,64,64]{2,1,0:T(8,128)S(1)}) custom-call(bf16[8,2,8,1536]{3,2,1,0:T(8,128)(2,1)S(1)} %all_to_all.26.second, bf16[320,1280]{1,0:T(8,128)(2,1)S(1)} %bitcast.18, bf16[320,1280]{1,0:T(8,128)(2,1)S(1)} %copy-done, bf16[32,64,320]{2,1,0:T(8,128)(2,1)S(1)} %copy-done.4, ...), custom_call_target="tpu_custom_call" | custom-call | flops 188743680 | bytes 5242880 | tf_op jit(solution)/shard_map/pallas_call | solution.py:485
  46.5 0.0 copy-start.2
  46.5 0.0 copy-start.10
  46.5 0.0 copy-start.13
  46.5 15.0 %all_to_all.27.third = bf16[32,8,768]{2,1,0:T(8,128)(2,1)S(1)} all-to-all(bf16[32,8,768]{2,1,0:T(8,128)(2,1)S(1)} %get-tuple-element.33), channel_id=1, replica_groups=mesh['dp'=2,'half'=2,'place'=8] {'dp','half','place'}, dimensions={0} | all-to-all | bytes 786432 | tf_op jit(solution)/shard_map/all_to_all | solution.py:581
  61.5 1.0 %shard_map.143 = (bf16[32,4,768]{2,1,0:T(4,128)(2,1)}, f32[2,8,64]{2,1,0:T(8,128)S(1)}) custom-call(bf16[32,8,768]{2,1,0:T(8,128)(2,1)S(1)} %all_to_all.27.third, bf16[4,64,640]{2,1,0:T(8,128)(2,1)S(1)} %bitcast.17, f32[8,640]{1,0:T(8,128)S(1)} %get-tuple-element.34.inputs, f32[8,128]{1,0:T(8,128)S(1)} %get-tuple-element.35.stats), custom_call_target="tpu_custom_call" | custom-call | flops 2621440 | bytes 946176 | tf_op jit(solution)/shard_map/pallas_call | solution.py:485
  62.5 3.0 %all-to-all-start.4 = ((bf16[32,4,768]{2,1,0:T(4,128)(2,1)}), bf16[32,4,768]{2,1,0:T(4,128)(2,1)S(1)}, u32[]{:S(2)}, u32[]{:S(2)}) async-start(bf16[32,4,768]{2,1,0:T(4,128)(2,1)} %get-tuple-element.36), calls=%async_computation.4 | async-start | bytes 393216 | tf_op jit(solution)/shard_map/all_to_all | solution.py:594
  65.5 2.5 %shard_map.146 = (bf16[32,64,320]{2,1,0:T(8,128)(2,1)}, bf16[32,64,320]{2,1,0:T(8,128)(2,1)}) custom-call(f32[2,64,64]{2,1,0:T(8,128)S(1)} %get-tuple-element.42.left_rows, f32[2,64,320]{2,1,0:T(8,128)S(1)} %get-tuple-element.43.right_rows), custom_call_target="tpu_custom_call" | custom-call | flops 20971520 | bytes 2818048 | tf_op jit(solution)/shard_map/pallas_call | solution.py:485
  68.0 1.2 %shard_map.145 = (bf16[4,64,640]{2,1,0:T(8,128)(2,1)}, bf16[4,64,640]{2,1,0:T(8,128)(2,1)}) custom-call(f32[2,8,64]{2,1,0:T(8,128)S(1)} %get-tuple-element.39.left_rows, bf16[2,8,640]{2,1,0:T(8,128)(2,1)S(1)} %get-tuple-element.40.right_rows), custom_call_target="tpu_custom_call" | custom-call | flops 5242880 | bytes 679936 | tf_op jit(solution)/shard_map/pallas_call | solution.py:485
  69.2 5.7 %all-to-all-done.4.fourth = bf16[32,4,768]{2,1,0:T(4,128)(2,1)S(1)} async-done(((bf16[32,4,768]{2,1,0:T(4,128)(2,1)}), bf16[32,4,768]{2,1,0:T(4,128)(2,1)S(1)}, u32[]{:S(2)}, u32[]{:S(2)}) %all-to-all-start.4) | async-done | bytes 196640 | tf_op jit(solution)/shard_map/all_to_all | solution.py:594
  75.0 0.0 copy-done.2
  75.0 0.0 copy-done.10
  75.0 0.0 copy-done.13
  75.0 1.8 %shard_map.144 = bf16[256,1280]{1,0:T(8,128)(2,1)} custom-call(bf16[32,4,768]{2,1,0:T(4,128)(2,1)S(1)} %all-to-all-done.4.fourth, bf16[256,1280]{1,0:T(8,128)(2,1)S(1)} %bitcast.14, bf16[64,1280]{1,0:T(8,128)(2,1)S(1)} %bitcast.20, f32[64,256]{1,0:T(8,128)S(1)} %copy-done.13, f32[64,256]{1,0:T(8,128)S(1)} %get-tuple-element.38.mixing), custom_call_target="tpu_custom_call" | custom-call | flops 125829120 | bytes 1802240 | tf_op jit(solution)/shard_map/pallas_call | solution.py:485
  (2 shorter events, 0.1 us)
Async XLA Ops:
  0.6 10.4 %copy-start.1 = (bf16[1,256,1280]{2,1,0:T(8,128)(2,1)S(1)}, bf16[1,256,1280]{2,1,0:T(8,128)(2,1)}, u32[]{:S(2)}) copy-start(bf16[1,256,1280]{2,1,0:T(8,128)(2,1)} %param.11) | copy-start | bytes 1966084
  0.6 10.4 %copy-start.7 = (bf16[4,64,640]{2,1,0:T(8,128)(2,1)S(1)}, bf16[4,64,640]{2,1,0:T(8,128)(2,1)}, u32[]{:S(2)}) copy-start(bf16[4,64,640]{2,1,0:T(8,128)(2,1)} %out_right.1) | copy-start | bytes 983044
  0.7 10.4 %copy-start = (bf16[320,1280]{1,0:T(8,128)(2,1)S(1)}, bf16[320,1280]{1,0:T(8,128)(2,1)}, u32[]{:S(2)}) copy-start(bf16[320,1280]{1,0:T(8,128)(2,1)} %base_out.1) | copy-start | bytes 2457604
  0.7 10.4 %copy-start.11 = (bf16[1,64,1280]{2,1,0:T(8,128)(2,1)S(1)}, bf16[1,64,1280]{2,1,0:T(8,128)(2,1)}, u32[]{:S(2)}) copy-start(bf16[1,64,1280]{2,1,0:T(8,128)(2,1)} %param.13) | copy-start | bytes 491524
  3.9 19.0 %all-to-all-start = ((bf16[32,4,1408]{2,1,0:T(4,128)(2,1)}), bf16[32,4,1408]{2,1,0:T(4,128)(2,1)S(1)}, u32[]{:S(2)}, u32[]{:S(2)}) async-start(bf16[32,4,1408]{2,1,0:T(4,128)(2,1)} %get-tuple-element.26), calls=%async_computation | async-start | bytes 720896 | tf_op jit(solution)/shard_map/all_to_all | solution.py:550
  11.0 1.4 %copy-start.3 = (bf16[32,320,64]{1,2,0:T(8,128)(2,1)S(1)}, bf16[32,320,64]{1,2,0:T(8,128)(2,1)}, u32[]{:S(2)}) copy-start(bf16[32,320,64]{1,2,0:T(8,128)(2,1)} %param.18) | copy-start | bytes 3932164
  12.5 0.8 %copy-start.12 = (f32[64,256]{1,0:T(8,128)S(1)}, f32[64,256]{1,0:T(8,128)}, u32[]{:S(2)}) copy-start(f32[64,256]{1,0:T(8,128)} %get-tuple-element.27.combine) | copy-start | bytes 196612
  13.3 9.6 %copy-start.8 = (bf16[4,640,64]{1,2,0:T(8,128)(2,1)S(1)}, bf16[4,640,64]{1,2,0:T(8,128)(2,1)}, u32[]{:S(2)}) copy-start(bf16[4,640,64]{1,2,0:T(8,128)(2,1)} %param.16) | copy-start | bytes 983044
  13.8 1.1 %copy-start.5 = (bf16[32,64,320]{2,1,0:T(8,128)(2,1)}, bf16[32,64,320]{2,1,0:T(8,128)(2,1)S(1)}, u32[]{:S(2)}) copy-start(bf16[32,64,320]{2,1,0:T(8,128)(2,1)S(1)} %get-tuple-element.32.out_left) | copy-start | bytes 3932164
  14.9 27.7 %copy-start.4 = (bf16[32,64,320]{2,1,0:T(8,128)(2,1)S(1)}, bf16[32,64,320]{2,1,0:T(8,128)(2,1)}, u32[]{:S(2)}) copy-start(bf16[32,64,320]{2,1,0:T(8,128)(2,1)} %in_right.1) | copy-start | bytes 3932164
  22.9 19.7 %copy-start.9 = (bf16[1280,320]{0,1:T(8,128)(2,1)S(1)}, bf16[1280,320]{0,1:T(8,128)(2,1)}, u32[]{:S(2)}) copy-start(bf16[1280,320]{0,1:T(8,128)(2,1)} %param.14) | copy-start | bytes 2457604
  42.7 1.4 %copy-start.6 = (bf16[32,64,320]{2,1,0:T(8,128)(2,1)S(1)}, bf16[32,64,320]{2,1,0:T(8,128)(2,1)}, u32[]{:S(2)}) copy-start(bf16[32,64,320]{2,1,0:T(8,128)(2,1)} %copy-done.5) | copy-start | bytes 3932164
  46.5 28.5 %copy-start.2 = (bf16[1,256,1280]{2,1,0:T(8,128)(2,1)S(1)}, bf16[1,256,1280]{2,1,0:T(8,128)(2,1)}, u32[]{:S(2)}) copy-start(bf16[1,256,1280]{2,1,0:T(8,128)(2,1)} %param.10) | copy-start | bytes 1966084
  46.5 28.5 %copy-start.10 = (bf16[1280,64]{0,1:T(8,128)(2,1)S(1)}, bf16[1280,64]{0,1:T(8,128)(2,1)}, u32[]{:S(2)}) copy-start(bf16[1280,64]{0,1:T(8,128)(2,1)} %param.12) | copy-start | bytes 491524
  46.5 28.5 %copy-start.13 = (f32[64,256]{1,0:T(8,128)S(1)}, f32[64,256]{1,0:T(8,128)}, u32[]{:S(2)}) copy-start(f32[64,256]{1,0:T(8,128)} %get-tuple-element.37.logits) | copy-start | bytes 196612
  62.5 12.5 %all-to-all-start.4 = ((bf16[32,4,768]{2,1,0:T(4,128)(2,1)}), bf16[32,4,768]{2,1,0:T(4,128)(2,1)S(1)}, u32[]{:S(2)}, u32[]{:S(2)}) async-start(bf16[32,4,768]{2,1,0:T(4,128)(2,1)} %get-tuple-element.36), calls=%async_computation.4 | async-start | bytes 393216 | tf_op jit(solution)/shard_map/all_to_all | solution.py:594

commit v8 on v6

--- a/solution.py
+++ b/solution.py
@@ -267,26 +267,31 @@
     copies[2].wait()
     grads = dot_plain(combine.astype(jnp.bfloat16), cotangent[...]).astype(jnp.bfloat16)
     width = inputs.shape[1] // groups
+    places = ring // groups
     for group in range(groups):
-        columns = slice(group * width, (group + 1) * width)
-        for place in range(ring):
-            rows = slice(place * owned, (place + 1) * owned)
-            block = group * ring + place
-            first[block, :, :width] = inputs[rows, columns]
-            first[block, :, width : 2 * width] = grads[rows, columns]
-            first[block, :, 2 * width :] = stats[rows, :]
+        for half in range(groups):
+            columns = slice(half * width, (half + 1) * width)
+            for place in range(places):
+                start = (group * places + place) * owned
+                rows = slice(start, start + owned)
+                block = group * ring + half * places + place
+                first[block, :, :width] = inputs[rows, columns]
+                first[block, :, width : 2 * width] = grads[rows, columns]
+                first[block, :, 2 * width :] = stats[rows, :]
 
 
 def mixing_kernel(cotangent, saved, combine, *rest):
-    *_, out = rest
+    *_, out_left, in_right, out, out_left_near, in_right_near = rest
+    out_left_near[...] = out_left[...]
+    in_right_near[...] = in_right[...]
     mixing = dot_last(saved[...], cotangent[...])
     weights = combine[...]
     out[...] = weights * (mixing - jnp.sum(weights * mixing, axis=0, keepdims=True))
 
 
-def owner_kernel(groups, first, in_left, out_right, second, inputs_out, lows_out, stats_out):
+def owner_kernel(groups, width, first, second, across):
     ring = first.shape[0] // groups
-    owned, rank, width = in_left.shape
+    owned = first.shape[1]
     inputs, grads, stats_rows = [], [], []
     for group in range(groups):
         rows = slice(group * ring, (group + 1) * ring)
@@ -301,36 +306,35 @@
         grads.append(jnp.sum(first[rows, :, width : 2 * width].astype(jnp.float32), axis=0))
         stats_rows.append(in_lanes([*halves(peak), *halves(total)], (owned, STATS)))
     inputs, grads = jnp.concatenate(inputs, axis=0), jnp.concatenate(grads, axis=0)
-    inputs_out[...] = inputs
-    stats_out[...] = jnp.concatenate(stats_rows, axis=0)
-    inputs_low, grads_low = inputs.astype(jnp.bfloat16), grads.astype(jnp.bfloat16)
+    stats = jnp.concatenate(stats_rows, axis=0)
+    high, low = halves(inputs)
+    block = jnp.concatenate([high, grads], axis=1).astype(jnp.bfloat16)
+    for place in range(second.shape[0]):
+        second[place] = block
+    across[...] = jnp.concatenate([high, grads, low, stats], axis=1).astype(jnp.bfloat16)
+
+
+def rank_kernel(across, in_left, out_right, ranks, inputs_out, lows_out, stats_out):
+    owned, rank, width = in_left.shape
+    inputs_low, grads_low = across[:, :width], across[:, width : 2 * width]
+    inputs_out[...] = inputs_low.astype(jnp.float32) + across[
+        :, 2 * width : 3 * width
+    ].astype(jnp.float32)
+    stats_out[...] = across[:, 3 * width :].astype(jnp.float32)
     lows_out[0] = inputs_low
     lows_out[1] = grads_low
     up = dot_last(inputs_low, in_left[...].reshape(owned * rank, width))
     back = dot_last(grads_low, out_right[...].reshape(owned * rank, width))
-    ranks = [*halves(from_own_block(up, owned)), *halves(from_own_block(back, owned))]
-    ranks = jnp.concatenate(ranks, axis=1).astype(jnp.bfloat16)
-    block = jnp.concatenate([inputs_low, grads_low, ranks], axis=1)
-    second[...] = block
-
-
-def spread_kernel(block, out):
-    for group in range(2):
-        for half in range(2):
-            out[group, half] = block[...]
-
-
-def pack_kernel(blocks, out):
-    group = lax.axis_index("dp")
-    for number in range(2):
-        block = blocks[2 * number + group]
-        for place in range(out.shape[0]):
-            out[place, number] = block
+    block = [*halves(from_own_block(up, owned)), *halves(from_own_block(back, owned))]
+    block = jnp.concatenate(block, axis=1).astype(jnp.bfloat16)
+    for place in range(ranks.shape[0]):
+        ranks[place] = block
 
 
 def hidden_kernel(
     groups,
     second,
+    factors,
     base_in,
     base_out,
     in_right,
@@ -340,7 +344,7 @@
     ranks_out,
 ):
     members, rank, hidden = in_right.shape
-    rows = second.shape[2]
+    rows = second.shape[1]
     owned = rows // groups
     places = members // owned
     width = base_in.shape[1] // groups
@@ -349,7 +353,7 @@
 
     def gathered(columns):
         taken = [
-            second[:, half, :, columns].astype(jnp.float32)
+            second[half * places : (half + 1) * places, :, columns].astype(jnp.float32)
             for half in range(groups)
         ]
         return [part.reshape(places * rows, part.shape[2]) for part in taken]
@@ -371,7 +375,10 @@
             taken.append(from_own_block(wide, owned))
         return jnp.concatenate(taken, axis=0)
 
-    ranks = functools.reduce(jnp.add, gathered(slice(2 * width, 2 * width + 4 * rank)))
+    ranks = jnp.zeros((places * rows, 4 * rank), jnp.float32)
+    for half in range(groups):
+        part = factors[pl.ds(half * ring + group * places, places)].astype(jnp.float32)
+        ranks = ranks + part.reshape(ranks.shape)
     up = (ranks[:, :rank] + ranks[:, rank : 2 * rank]).astype(jnp.bfloat16)
     back = (ranks[:, 2 * rank : 3 * rank] + ranks[:, 3 * rank :]).astype(jnp.bfloat16)
     preact = low_rank(up, in_right)
@@ -465,16 +472,16 @@
     out[...] = dot_first(left, right).astype(jnp.bfloat16)
 
 
-def to_group(block):
+def to_home(block):
     places = lax.axis_size("place")
-    (blocks,) = call(
-        spread_kernel, [array(block.dtype, 2, 2, *block.shape)], [block], 0
-    )
-    blocks = lax.all_to_all(blocks.reshape(4, *block.shape), ("dp", "half"), 0, 0, tiled=True)
-    (blocks,) = call(
-        pack_kernel, [array(block.dtype, places, 2, *block.shape)], [blocks], 0
-    )
-    return lax.all_to_all(blocks, "place", 0, 0, tiled=True)
+    ring = 2 * places
+    pairs = [
+        (group * ring + half * places + place, half * ring + group * places + place)
+        for group in range(2)
+        for half in range(2)
+        for place in range(places)
+    ]
+    return lax.ppermute(block, BOTH, pairs)
 
 
 def call(kernel, outs, args, flops, far=(), scratch=(), grant=24):
@@ -547,25 +554,38 @@
         60,
     )
     first = lax.all_to_all(first, BOTH, 0, 0, tiled=True)
-    (mixing,) = call(
+    mixing, out_left, in_right = call(
         mixing_kernel,
-        [array(full, slots, count)],
-        [cot_rows, saved, combine, in_left, out_right, base_in, base_out, in_right, out_left],
+        [array(full, slots, count), array(low, *out_left.shape), array(low, *in_right.shape)],
+        [cot_rows, saved, combine, out_right, base_out, out_left, in_right],
         2 * count * slots * width,
     )
-    first, mixing = lax.optimization_barrier((first, mixing))
-    second, inputs, lows, stats = call(
-        functools.partial(owner_kernel, groups),
+    first, mixing, out_left, in_right = lax.optimization_barrier(
+        (first, mixing, out_left, in_right)
+    )
+    second, across = call(
+        functools.partial(owner_kernel, groups, slice_width),
         [
-            array(low, rows, 2 * slice_width + 4 * rank),
+            array(low, ring, rows, 2 * slice_width),
+            array(low, rows, 3 * slice_width + STATS),
+        ],
+        [first],
+        0,
+    )
+    across = to_home(across)
+    second = lax.all_to_all(second, SEQ, 0, 0, tiled=True)
+    factors, inputs, lows, stats = call(
+        rank_kernel,
+        [
+            array(low, devices, rows, 4 * rank),
             array(full, rows, slice_width),
             array(low, 2, rows, slice_width),
             array(full, rows, STATS),
         ],
-        [first, in_left, out_right],
+        [across, in_left, out_right],
         4 * rows * owned * rank * slice_width,
     )
-    second = to_group(second)
+    factors = lax.all_to_all(factors, BOTH, 0, 0, tiled=True)
     total_rows = groups * members
     third, pair, ranks = call(
         functools.partial(hidden_kernel, groups),
@@ -574,7 +594,7 @@
             array(full, 2, total_rows, hidden),
             array(full, 2, total_rows, rank),
         ],
-        [second, base_in, base_out, in_right, out_left],
+        [second, factors, base_in, base_out, in_right, out_left],
         6 * total_rows * hidden * (width + owned * rank),
     )
     third = lax.all_to_all(third, BOTH, 0, 0, tiled=True)

time: 79.5 us -> 92.5 us (1.16)
  blocking collectives: 34 us -> 46.5 us
  waiting for transfers between devices: 8.93 us -> 10.3 us
    all_to_all x2, blocking collectives: 19 us -> 31.7 us  [the longest x1 18.1 us: local(): factors = lax.all_to_all(factors, BOTH, 0, 0, tiled=True)]
    all_to_all x1, waiting for transfers between devices: 3.96 us -> 5.73 us  [local(): fourth = lax.all_to_all(fourth, BOTH, 0, 0, tiled=True)]
    unnamed x44 -> x32, local copies, waits for them, and re-layouts: 10.5 us -> 9.79 us
    pallas_call x10 -> x9, Pallas kernels: 14.3 us -> 13.6 us  [call(): pl.pallas_call(kernel, out_shape=outs, in_specs=[pl.BlockSpec(memory_spac...]
  transfers between devices with their start and end apart: 2 -> 3, of which waited for: 2 -> 2; matrix products, arithmetic and copies ran while one was open for 0% -> 0% of each run, Pallas kernels for 5% -> 5%
where the time goes in v8:
time: 92.5 us; the launch traced here: 91.9 us
  blocking collectives  46.5 us (50%)
  Pallas kernels  13.6 us (15%)
  starting transfers between devices  10.9 us (12%)
  waiting for transfers between devices  10.3 us (11%)
  local copies, waits for them, and re-layouts  9.79 us (11%)
    all_to_all x1, blocking collectives, local(): factors = lax.all_to_all(factors, BOTH, 0, 0, tiled=True)  18.1 us
    all_to_all x1, blocking collectives, local(): third = lax.all_to_all(third, BOTH, 0, 0, tiled=True)  14.8 us
    all_to_all x1, blocking collectives, local(): second = lax.all_to_all(second, SEQ, 0, 0, tiled=True)  13.6 us
    pallas_call x9, Pallas kernels, call(): pl.pallas_call(kernel, out_shape=outs, in_specs=[pl.BlockSpec(memory_spac...  13.6 us
    unnamed x32, local copies, waits for them, and re-layouts  9.79 us
    all_to_all x1, starting transfers between devices, local(): first = lax.all_to_all(first, BOTH, 0, 0, tiled=True)  7.1 us
    all_to_all x1, waiting for transfers between devices, local(): fourth = lax.all_to_all(fourth, BOTH, 0, 0, tiled=True)  5.73 us
    all_to_all x1, waiting for transfers between devices, local(): first = lax.all_to_all(first, BOTH, 0, 0, tiled=True)  4.57 us
  transfers between devices with their start and end apart: 3, of which 2 were waited for; matrix products, arithmetic and copies ran while one was open for 0% of the time, Pallas kernels for 5%

profile of v8, /device:TPU:1, one launch (start us, length us, event | category | flops | bytes accessed | tf_op | source)
XLA Modules:
  0.0 91.9 jit_solution(11791361927883792376)
XLA Ops:
  0.6 0.0 copy-start.1
  0.6 0.0 copy-start
  0.7 3.2 %shard_map.137 = (bf16[32,4,1408]{2,1,0:T(4,128)(2,1)}, f32[64,256]{1,0:T(8,128)}, f32[64,256]{1,0:T(8,128)}) custom-call(bf16[256,1280]{1,0:T(8,128)(2,1)} %bitcast.12, bf16[256,1280]{1,0:T(8,128)(2,1)} %bitcast.10, bf16[64,1280]{1,0:T(8,128)(2,1)} %bitcast.18), custom_call_target="tpu_custom_call" | custom-call | flops 125829120 | bytes 1966080 | tf_op jit(solution)/shard_map/pallas_call | solution.py:491
  3.8 7.1 %all-to-all-start = ((bf16[32,4,1408]{2,1,0:T(4,128)(2,1)}), bf16[32,4,1408]{2,1,0:T(4,128)(2,1)S(1)}, u32[]{:S(2)}, u32[]{:S(2)}) async-start(bf16[32,4,1408]{2,1,0:T(4,128)(2,1)} %get-tuple-element.30), calls=%async_computation | async-start | bytes 720896 | tf_op jit(solution)/shard_map/all_to_all | solution.py:556
  11.0 0.0 copy-done.1
  11.0 0.0 copy-done
  11.0 0.0 copy-start.3
  11.0 1.4 %copy-done.3 = bf16[32,320,64]{1,2,0:T(8,128)(2,1)S(1)} copy-done((bf16[32,320,64]{1,2,0:T(8,128)(2,1)S(1)}, bf16[32,320,64]{1,2,0:T(8,128)(2,1)}, u32[]{:S(2)}) %copy-start.3) | copy-done | bytes 1310744
  12.4 0.0 copy-start.4
  12.4 1.4 %copy-done.4 = bf16[32,64,320]{2,1,0:T(8,128)(2,1)S(1)} copy-done((bf16[32,64,320]{2,1,0:T(8,128)(2,1)S(1)}, bf16[32,64,320]{2,1,0:T(8,128)(2,1)}, u32[]{:S(2)}) %copy-start.4) | copy-done | bytes 1310744
  13.8 0.0 copy-start.7
  13.8 1.0 %copy-done.7 = bf16[4,64,640]{2,1,0:T(8,128)(2,1)S(1)} copy-done((bf16[4,64,640]{2,1,0:T(8,128)(2,1)S(1)}, bf16[4,64,640]{2,1,0:T(8,128)(2,1)}, u32[]{:S(2)}) %copy-start.7) | copy-done | bytes 327704
  14.8 0.0 copy-start.13
  14.8 0.9 copy-done.13
  15.7 0.0 copy-start.14
  15.7 0.8 copy-done.14
  16.5 0.6 shard_map.138
  17.2 0.0 copy-start.5
  17.2 1.1 %copy-done.5 = bf16[32,64,320]{2,1,0:T(8,128)(2,1)} copy-done((bf16[32,64,320]{2,1,0:T(8,128)(2,1)}, bf16[32,64,320]{2,1,0:T(8,128)(2,1)S(1)}, u32[]{:S(2)}) %copy-start.5) | copy-done | bytes 1310744
  18.3 4.6 %all-to-all-done.first = bf16[32,4,1408]{2,1,0:T(4,128)(2,1)S(1)} async-done(((bf16[32,4,1408]{2,1,0:T(4,128)(2,1)}), bf16[32,4,1408]{2,1,0:T(4,128)(2,1)S(1)}, u32[]{:S(2)}, u32[]{:S(2)}) %all-to-all-start) | async-done | bytes 360480 | tf_op jit(solution)/shard_map/all_to_all | solution.py:556
  22.9 0.0 copy-start.6
  22.9 0.4 shard_map.139
  23.3 0.8 collective-permute-start
  24.1 0.0 collective-permute-done.across
  24.1 0.0 copy-start.8
  24.1 1.0 %copy-done.8 = bf16[4,64,640]{2,1,0:T(8,128)(2,1)S(1)} copy-done((bf16[4,64,640]{2,1,0:T(8,128)(2,1)S(1)}, bf16[4,64,640]{2,1,0:T(8,128)(2,1)}, u32[]{:S(2)}) %copy-start.8) | copy-done | bytes 327704
  25.1 0.0 copy-start.9
  25.1 1.0 %copy-done.9 = bf16[4,640,64]{1,2,0:T(8,128)(2,1)S(1)} copy-done((bf16[4,640,64]{1,2,0:T(8,128)(2,1)S(1)}, bf16[4,640,64]{1,2,0:T(8,128)(2,1)}, u32[]{:S(2)}) %copy-start.9) | copy-done | bytes 327704
  26.1 0.4 shard_map.140
  26.5 18.1 %all_to_all.25.factors = bf16[32,8,256]{2,1,0:T(8,128)(2,1)S(1)} all-to-all(bf16[32,8,256]{2,1,0:T(8,128)(2,1)S(1)} %get-tuple-element.38), channel_id=1, replica_groups=mesh['dp'=2,'half'=2,'place'=8] {'dp','half','place'}, dimensions={0} | all-to-all | bytes 262144 | tf_op jit(solution)/shard_map/all_to_all | solution.py:588
  44.6 13.6 %all_to_all.26.second = bf16[16,8,1280]{2,1,0:T(8,128)(2,1)S(1)} all-to-all(bf16[16,8,1280]{2,1,0:T(8,128)(2,1)S(1)} %get-tuple-element.36), channel_id=1, replica_groups=mesh['dp'=2,'half'=2,'place'=8] {'half','place'}, dimensions={0} | all-to-all | bytes 655360 | tf_op jit(solution)/shard_map/all_to_all | solution.py:576
  58.2 0.0 copy-done.6
  58.2 0.0 copy-start.11
  58.2 1.1 %copy-done.11 = bf16[1280,320]{0,1:T(8,128)(2,1)S(1)} copy-done((bf16[1280,320]{0,1:T(8,128)(2,1)S(1)}, bf16[1280,320]{0,1:T(8,128)(2,1)}, u32[]{:S(2)}) %copy-start.11) | copy-done | bytes 819224
  59.4 0.0 copy-start.10
  59.4 2.4 %shard_map.141 = (bf16[32,8,768]{2,1,0:T(8,128)(2,1)S(1)}, f32[2,64,320]{2,1,0:T(8,128)S(1)}, f32[2,64,64]{2,1,0:T(8,128)S(1)}) custom-call(bf16[16,8,1280]{2,1,0:T(8,128)(2,1)S(1)} %all_to_all.26.second, bf16[32,8,256]{2,1,0:T(8,128)(2,1)S(1)} %all_to_all.25.factors, bf16[320,1280]{1,0:T(8,128)(2,1)S(1)} %bitcast.17, bf16[320,1280]{1,0:T(8,128)(2,1)S(1)} %copy-done, ...), custom_call_target="tpu_custom_call" | custom-call | flops 188743680 | bytes 5308416 | tf_op jit(solution)/shard_map/pallas_call | solution.py:491
  61.8 0.0 copy-start.2
  61.8 0.0 copy-start.12
  61.8 0.0 copy-start.15
  61.8 14.8 %all_to_all.27.third = bf16[32,8,768]{2,1,0:T(8,128)(2,1)S(1)} all-to-all(bf16[32,8,768]{2,1,0:T(8,128)(2,1)S(1)} %get-tuple-element.41), channel_id=1, replica_groups=mesh['dp'=2,'half'=2,'place'=8] {'dp','half','place'}, dimensions={0} | all-to-all | bytes 786432 | tf_op jit(solution)/shard_map/all_to_all | solution.py:600
  76.6 0.0 copy-done.10
  76.6 1.0 %shard_map.142 = (bf16[32,4,768]{2,1,0:T(4,128)(2,1)}, f32[2,8,64]{2,1,0:T(8,128)S(1)}) custom-call(bf16[32,8,768]{2,1,0:T(8,128)(2,1)S(1)} %all_to_all.27.third, bf16[4,64,640]{2,1,0:T(8,128)(2,1)S(1)} %bitcast.16, f32[8,640]{1,0:T(8,128)S(1)} %get-tuple-element.42.inputs, f32[8,128]{1,0:T(8,128)S(1)} %get-tuple-element.43.stats), custom_call_target="tpu_custom_call" | custom-call | flops 2621440 | bytes 946176 | tf_op jit(solution)/shard_map/pallas_call | solution.py:491
  77.6 3.0 %all-to-all-start.4 = ((bf16[32,4,768]{2,1,0:T(4,128)(2,1)}), bf16[32,4,768]{2,1,0:T(4,128)(2,1)S(1)}, u32[]{:S(2)}, u32[]{:S(2)}) async-start(bf16[32,4,768]{2,1,0:T(4,128)(2,1)} %get-tuple-element.44), calls=%async_computation.4 | async-start | bytes 393216 | tf_op jit(solution)/shard_map/all_to_all | solution.py:613
  80.7 2.5 %shard_map.145 = (bf16[32,64,320]{2,1,0:T(8,128)(2,1)}, bf16[32,64,320]{2,1,0:T(8,128)(2,1)}) custom-call(f32[2,64,64]{2,1,0:T(8,128)S(1)} %get-tuple-element.50.left_rows, f32[2,64,320]{2,1,0:T(8,128)S(1)} %get-tuple-element.51.right_rows), custom_call_target="tpu_custom_call" | custom-call | flops 20971520 | bytes 2818048 | tf_op jit(solution)/shard_map/pallas_call | solution.py:491
  83.2 1.2 %shard_map.144 = (bf16[4,64,640]{2,1,0:T(8,128)(2,1)}, bf16[4,64,640]{2,1,0:T(8,128)(2,1)}) custom-call(f32[2,8,64]{2,1,0:T(8,128)S(1)} %get-tuple-element.47.left_rows, bf16[2,8,640]{2,1,0:T(8,128)(2,1)S(1)} %get-tuple-element.48.right_rows), custom_call_target="tpu_custom_call" | custom-call | flops 5242880 | bytes 679936 | tf_op jit(solution)/shard_map/pallas_call | solution.py:491
  84.4 5.7 %all-to-all-done.4.fourth = bf16[32,4,768]{2,1,0:T(4,128)(2,1)S(1)} async-done(((bf16[32,4,768]{2,1,0:T(4,128)(2,1)}), bf16[32,4,768]{2,1,0:T(4,128)(2,1)S(1)}, u32[]{:S(2)}, u32[]{:S(2)}) %all-to-all-start.4) | async-done | bytes 196640 | tf_op jit(solution)/shard_map/all_to_all | solution.py:613
  90.1 0.0 copy-done.2
  90.1 0.0 copy-done.12
  90.1 0.0 copy-done.15
  90.1 1.8 %shard_map.143 = bf16[256,1280]{1,0:T(8,128)(2,1)} custom-call(bf16[32,4,768]{2,1,0:T(4,128)(2,1)S(1)} %all-to-all-done.4.fourth, bf16[256,1280]{1,0:T(8,128)(2,1)S(1)} %bitcast.13, bf16[64,1280]{1,0:T(8,128)(2,1)S(1)} %bitcast.19, f32[64,256]{1,0:T(8,128)S(1)} %copy-done.15, f32[64,256]{1,0:T(8,128)S(1)} %get-tuple-element.46.mixing), custom_call_target="tpu_custom_call" | custom-call | flops 125829120 | bytes 1802240 | tf_op jit(solution)/shard_map/pallas_call | solution.py:491
Async XLA Ops:
  0.6 10.3 %copy-start.1 = (bf16[1,256,1280]{2,1,0:T(8,128)(2,1)S(1)}, bf16[1,256,1280]{2,1,0:T(8,128)(2,1)}, u32[]{:S(2)}) copy-start(bf16[1,256,1280]{2,1,0:T(8,128)(2,1)} %param.11) | copy-start | bytes 1966084
  0.6 10.3 %copy-start = (bf16[320,1280]{1,0:T(8,128)(2,1)S(1)}, bf16[320,1280]{1,0:T(8,128)(2,1)}, u32[]{:S(2)}) copy-start(bf16[320,1280]{1,0:T(8,128)(2,1)} %base_out.1) | copy-start | bytes 2457604
  3.8 19.0 %all-to-all-start = ((bf16[32,4,1408]{2,1,0:T(4,128)(2,1)}), bf16[32,4,1408]{2,1,0:T(4,128)(2,1)S(1)}, u32[]{:S(2)}, u32[]{:S(2)}) async-start(bf16[32,4,1408]{2,1,0:T(4,128)(2,1)} %get-tuple-element.30), calls=%async_computation | async-start | bytes 720896 | tf_op jit(solution)/shard_map/all_to_all | solution.py:556
  11.0 1.4 %copy-start.3 = (bf16[32,320,64]{1,2,0:T(8,128)(2,1)S(1)}, bf16[32,320,64]{1,2,0:T(8,128)(2,1)}, u32[]{:S(2)}) copy-start(bf16[32,320,64]{1,2,0:T(8,128)(2,1)} %param.18) | copy-start | bytes 3932164
  12.4 1.4 %copy-start.4 = (bf16[32,64,320]{2,1,0:T(8,128)(2,1)S(1)}, bf16[32,64,320]{2,1,0:T(8,128)(2,1)}, u32[]{:S(2)}) copy-start(bf16[32,64,320]{2,1,0:T(8,128)(2,1)} %rest_3_.1) | copy-start | bytes 3932164
  13.8 1.0 %copy-start.7 = (bf16[4,64,640]{2,1,0:T(8,128)(2,1)S(1)}, bf16[4,64,640]{2,1,0:T(8,128)(2,1)}, u32[]{:S(2)}) copy-start(bf16[4,64,640]{2,1,0:T(8,128)(2,1)} %out_right.1) | copy-start | bytes 983044
  14.8 0.9 copy-start.13
  15.7 0.8 copy-start.14
  17.2 1.1 %copy-start.5 = (bf16[32,64,320]{2,1,0:T(8,128)(2,1)}, bf16[32,64,320]{2,1,0:T(8,128)(2,1)S(1)}, u32[]{:S(2)}) copy-start(bf16[32,64,320]{2,1,0:T(8,128)(2,1)S(1)} %get-tuple-element.39.in_right) | copy-start | bytes 3932164
  22.9 35.3 %copy-start.6 = (bf16[32,64,320]{2,1,0:T(8,128)(2,1)S(1)}, bf16[32,64,320]{2,1,0:T(8,128)(2,1)}, u32[]{:S(2)}) copy-start(bf16[32,64,320]{2,1,0:T(8,128)(2,1)} %copy-done.5) | copy-start | bytes 3932164
  23.3 0.8 collective-permute-start
  24.1 1.0 %copy-start.8 = (bf16[4,64,640]{2,1,0:T(8,128)(2,1)S(1)}, bf16[4,64,640]{2,1,0:T(8,128)(2,1)}, u32[]{:S(2)}) copy-start(bf16[4,64,640]{2,1,0:T(8,128)(2,1)} %out_right.1) | copy-start | bytes 983044
  25.1 1.0 %copy-start.9 = (bf16[4,640,64]{1,2,0:T(8,128)(2,1)S(1)}, bf16[4,640,64]{1,2,0:T(8,128)(2,1)}, u32[]{:S(2)}) copy-start(bf16[4,640,64]{1,2,0:T(8,128)(2,1)} %param.16) | copy-start | bytes 983044
  58.2 1.1 %copy-start.11 = (bf16[1280,320]{0,1:T(8,128)(2,1)S(1)}, bf16[1280,320]{0,1:T(8,128)(2,1)}, u32[]{:S(2)}) copy-start(bf16[1280,320]{0,1:T(8,128)(2,1)} %param.14) | copy-start | bytes 2457604
  59.4 17.2 %copy-start.10 = (bf16[4,640,64]{1,2,0:T(8,128)(2,1)S(1)}, bf16[4,640,64]{1,2,0:T(8,128)(2,1)}, u32[]{:S(2)}) copy-start(bf16[4,640,64]{1,2,0:T(8,128)(2,1)} %param.16) | copy-start | bytes 983044
  61.8 28.3 %copy-start.2 = (bf16[1,256,1280]{2,1,0:T(8,128)(2,1)S(1)}, bf16[1,256,1280]{2,1,0:T(8,128)(2,1)}, u32[]{:S(2)}) copy-start(bf16[1,256,1280]{2,1,0:T(8,128)(2,1)} %param.10) | copy-start | bytes 1966084
  61.8 28.3 %copy-start.12 = (bf16[1280,64]{0,1:T(8,128)(2,1)S(1)}, bf16[1280,64]{0,1:T(8,128)(2,1)}, u32[]{:S(2)}) copy-start(bf16[1280,64]{0,1:T(8,128)(2,1)} %param.12) | copy-start | bytes 491524
  61.8 28.3 %copy-start.15 = (f32[64,256]{1,0:T(8,128)S(1)}, f32[64,256]{1,0:T(8,128)}, u32[]{:S(2)}) copy-start(f32[64,256]{1,0:T(8,128)} %get-tuple-element.45.logits) | copy-start | bytes 196612
  77.6 12.5 %all-to-all-start.4 = ((bf16[32,4,768]{2,1,0:T(4,128)(2,1)}), bf16[32,4,768]{2,1,0:T(4,128)(2,1)S(1)}, u32[]{:S(2)}, u32[]{:S(2)}) async-start(bf16[32,4,768]{2,1,0:T(4,128)(2,1)} %get-tuple-element.44), calls=%async_computation.4 | async-start | bytes 393216 | tf_op jit(solution)/shard_map/all_to_all | solution.py:613

commit v9 on v6

--- a/solution.py
+++ b/solution.py
@@ -9,6 +9,7 @@
 
 SEQ = ("half", "place")
 BOTH = ("dp", *SEQ)
+HALF = ("dp", "place")
 STATS = 128
 
 
@@ -278,7 +279,9 @@
 
 
 def mixing_kernel(cotangent, saved, combine, *rest):
-    *_, out = rest
+    *_, out_left, in_right, out, out_left_near, in_right_near = rest
+    out_left_near[...] = out_left[...]
+    in_right_near[...] = in_right[...]
     mixing = dot_last(saved[...], cotangent[...])
     weights = combine[...]
     out[...] = weights * (mixing - jnp.sum(weights * mixing, axis=0, keepdims=True))
@@ -314,18 +317,10 @@
     second[...] = block
 
 
-def spread_kernel(block, out):
-    for group in range(2):
-        for half in range(2):
-            out[group, half] = block[...]
-
-
 def pack_kernel(blocks, out):
-    group = lax.axis_index("dp")
-    for number in range(2):
-        block = blocks[2 * number + group]
-        for place in range(out.shape[0]):
-            out[place, number] = block
+    for group in range(out.shape[0]):
+        for place in range(out.shape[1]):
+            out[group, place] = blocks[group]
 
 
 def hidden_kernel(
@@ -340,16 +335,14 @@
     ranks_out,
 ):
     members, rank, hidden = in_right.shape
-    rows = second.shape[2]
+    rows = second.shape[1]
     owned = rows // groups
     places = members // owned
     width = base_in.shape[1] // groups
-    ring = third.shape[0] // groups
-    group = lax.axis_index("dp")
 
     def gathered(columns):
         taken = [
-            second[:, half, :, columns].astype(jnp.float32)
+            second[half * places : (half + 1) * places, :, columns].astype(jnp.float32)
             for half in range(groups)
         ]
         return [part.reshape(places * rows, part.shape[2]) for part in taken]
@@ -398,12 +391,11 @@
     down = to_rank(preact_grad, in_right)
     value = to_rank(hidden_low, out_left)
     ranks = jnp.concatenate([down, value], axis=1).astype(jnp.bfloat16)
-    third[...] = jnp.zeros(third.shape, jnp.bfloat16)
     for half in range(groups):
         columns = slice(half * width, (half + 1) * width)
         for place in range(places):
             taken = slice(place * rows, (place + 1) * rows)
-            block = half * ring + group * places + place
+            block = half * places + place
             third[block, :, :width] = slot_term[taken, columns]
             third[block, :, width:] = ranks[taken]
 
@@ -420,10 +412,17 @@
             )
 
 
-def finish_kernel(groups, ring, third, in_left, inputs, stats, fourth, ranks_out):
+def halves_kernel(third, own, other):
+    places = third.shape[0] // 2
+    here = lax.axis_index("half")
+    for out, group in ((own, here), (other, 1 - here)):
+        taken = third[pl.ds(group * places, places)].astype(jnp.float32)
+        out[...] = jnp.sum(taken, axis=0)
+
+
+def finish_kernel(groups, ring, own, others, in_left, inputs, stats, fourth, ranks_out):
     owned, rank, width = in_left.shape
-    sender = lax.axis_index("half")
-    summed = jnp.sum(third[pl.ds(sender * ring, ring)].astype(jnp.float32), axis=0)
+    summed = own[...] + others[1 - lax.axis_index("half")]
     ranks = summed[:, width:].astype(jnp.bfloat16).astype(jnp.float32)
     ranks_out[0] = ranks[:, :rank]
     ranks_out[1] = ranks[:, rank:]
@@ -465,16 +464,14 @@
     out[...] = dot_first(left, right).astype(jnp.bfloat16)
 
 
-def to_group(block):
+def to_group(block, groups):
     places = lax.axis_size("place")
+    blocks = lax.all_gather(block, "half", axis=0)
     (blocks,) = call(
-        spread_kernel, [array(block.dtype, 2, 2, *block.shape)], [block], 0
-    )
-    blocks = lax.all_to_all(blocks.reshape(4, *block.shape), ("dp", "half"), 0, 0, tiled=True)
-    (blocks,) = call(
-        pack_kernel, [array(block.dtype, places, 2, *block.shape)], [blocks], 0
-    )
-    return lax.all_to_all(blocks, "place", 0, 0, tiled=True)
+        pack_kernel, [array(block.dtype, groups, places, *block.shape)], [blocks], 0
+    )
+    blocks = blocks.reshape(groups * places, *block.shape)
+    return lax.all_to_all(blocks, HALF, 0, 0, tiled=True)
 
 
 def call(kernel, outs, args, flops, far=(), scratch=(), grant=24):
@@ -547,13 +544,15 @@
         60,
     )
     first = lax.all_to_all(first, BOTH, 0, 0, tiled=True)
-    (mixing,) = call(
+    mixing, out_left, in_right = call(
         mixing_kernel,
-        [array(full, slots, count)],
-        [cot_rows, saved, combine, in_left, out_right, base_in, base_out, in_right, out_left],
+        [array(full, slots, count), array(low, *out_left.shape), array(low, *in_right.shape)],
+        [cot_rows, saved, combine, out_right, base_out, out_left, in_right],
         2 * count * slots * width,
     )
-    first, mixing = lax.optimization_barrier((first, mixing))
+    first, mixing, out_left, in_right = lax.optimization_barrier(
+        (first, mixing, out_left, in_right)
+    )
     second, inputs, lows, stats = call(
         functools.partial(owner_kernel, groups),
         [
@@ -565,29 +564,31 @@
         [first, in_left, out_right],
         4 * rows * owned * rank * slice_width,
     )
-    second = to_group(second)
+    second = to_group(second, groups)
     total_rows = groups * members
     third, pair, ranks = call(
         functools.partial(hidden_kernel, groups),
         [
-            array(low, devices, rows, slice_width + 2 * rank),
+            array(low, ring, rows, slice_width + 2 * rank),
             array(full, 2, total_rows, hidden),
             array(full, 2, total_rows, rank),
         ],
         [second, base_in, base_out, in_right, out_left],
         6 * total_rows * hidden * (width + owned * rank),
     )
-    third = lax.all_to_all(third, BOTH, 0, 0, tiled=True)
+    third = lax.all_to_all(third, HALF, 0, 0, tiled=True)
     grad_in_right, grad_out_left = call(
         functools.partial(outer_kernel, owned),
         [array(low, members, rank, hidden)] * 2,
         [ranks, pair],
         4 * members * rank * hidden * rows,
     )
+    own, other = call(halves_kernel, [array(full, rows, slice_width + 2 * rank)] * 2, [third], 0)
+    others = lax.all_gather(other, "half", axis=0)
     fourth, ranks = call(
         functools.partial(finish_kernel, groups, ring),
         [array(low, devices, owned, slice_width + STATS), array(full, 2, rows, rank)],
-        [third, in_left, inputs, stats],
+        [own, others, in_left, inputs, stats],
         2 * rows * owned * rank * slice_width,
     )
     fourth = lax.all_to_all(fourth, BOTH, 0, 0, tiled=True)

time: 79.5 us -> 77.4 us (0.974)
  blocking collectives: 34 us -> 30.8 us
  starting transfers between devices: 10.2 us -> 11.6 us
  waiting for transfers between devices: 8.93 us -> 10.3 us
  Pallas kernels: 14.3 us -> 13.5 us
    all_to_all x3 -> x2, blocking collectives: 34 us -> 22.2 us  [the longest x1 12.5 us: to_group(): return lax.all_to_all(blocks, HALF, 0, 0, tiled=True)]
    all_gather x0 -> x2, blocking collectives: none -> 8.58 us  [the longest x1 4.33 us: to_group(): blocks = lax.all_gather(block, 'half', axis=0)]
    all_to_all x1, waiting for transfers between devices: 3.96 us -> 5.73 us  [local(): fourth = lax.all_to_all(fourth, BOTH, 0, 0, tiled=True)]
    all_to_all x1, starting transfers between devices: 3.04 us -> 4.5 us  [local(): fourth = lax.all_to_all(fourth, BOTH, 0, 0, tiled=True)]
    pallas_call x10, Pallas kernels: 14.3 us -> 13.5 us  [call(): pl.pallas_call(kernel, out_shape=outs, in_specs=[pl.BlockSpec(memory_spac...]
    unnamed x44 -> x30, local copies, waits for them, and re-layouts: 10.5 us -> 9.91 us
  transfers between devices with their start and end apart: 2 -> 2, of which waited for: 2 -> 2; matrix products, arithmetic and copies ran while one was open for 0% -> 0% of each run, Pallas kernels for 5% -> 6%
where the time goes in v9:
time: 77.4 us; the launch traced here: 76.8 us
  blocking collectives  30.8 us (40%)
  Pallas kernels  13.5 us (17%)
  starting transfers between devices  11.6 us (15%)
  waiting for transfers between devices  10.3 us (13%)
  local copies, waits for them, and re-layouts  9.91 us (13%)
    pallas_call x10, Pallas kernels, call(): pl.pallas_call(kernel, out_shape=outs, in_specs=[pl.BlockSpec(memory_spac...  13.5 us
    all_to_all x1, blocking collectives, to_group(): return lax.all_to_all(blocks, HALF, 0, 0, tiled=True)  12.5 us
    unnamed x30, local copies, waits for them, and re-layouts  9.91 us
    all_to_all x1, blocking collectives, local(): third = lax.all_to_all(third, HALF, 0, 0, tiled=True)  9.76 us
    all_to_all x1, starting transfers between devices, local(): first = lax.all_to_all(first, BOTH, 0, 0, tiled=True)  7.1 us
    all_to_all x1, waiting for transfers between devices, local(): fourth = lax.all_to_all(fourth, BOTH, 0, 0, tiled=True)  5.73 us
    all_to_all x1, waiting for transfers between devices, local(): first = lax.all_to_all(first, BOTH, 0, 0, tiled=True)  4.57 us
    all_to_all x1, starting transfers between devices, local(): fourth = lax.all_to_all(fourth, BOTH, 0, 0, tiled=True)  4.5 us
  transfers between devices with their start and end apart: 2, of which 2 were waited for; matrix products, arithmetic and copies ran while one was open for 0% of the time, Pallas kernels for 6%

profile of v9, /device:TPU:1, one launch (start us, length us, event | category | flops | bytes accessed | tf_op | source)
XLA Modules:
  0.0 76.8 jit_solution(3678574344152674513)
XLA Ops:
  0.6 0.0 copy-start.1
  0.6 0.0 copy-start
  0.7 3.2 %shard_map.137 = (bf16[32,4,1408]{2,1,0:T(4,128)(2,1)}, f32[64,256]{1,0:T(8,128)}, f32[64,256]{1,0:T(8,128)}) custom-call(bf16[256,1280]{1,0:T(8,128)(2,1)} %bitcast.15, bf16[256,1280]{1,0:T(8,128)(2,1)} %bitcast.13, bf16[64,1280]{1,0:T(8,128)(2,1)} %bitcast.22), custom_call_target="tpu_custom_call" | custom-call | flops 125829120 | bytes 1966080 | tf_op jit(solution)/shard_map/pallas_call | solution.py:481
  3.8 7.1 %all-to-all-start = ((bf16[32,4,1408]{2,1,0:T(4,128)(2,1)}), bf16[32,4,1408]{2,1,0:T(4,128)(2,1)S(1)}, u32[]{:S(2)}, u32[]{:S(2)}) async-start(bf16[32,4,1408]{2,1,0:T(4,128)(2,1)} %get-tuple-element.30), calls=%async_computation | async-start | bytes 720896 | tf_op jit(solution)/shard_map/all_to_all | solution.py:546
  11.0 0.0 copy-done.1
  11.0 0.0 copy-done
  11.0 0.0 copy-start.3
  11.0 1.4 %copy-done.3 = bf16[32,320,64]{1,2,0:T(8,128)(2,1)S(1)} copy-done((bf16[32,320,64]{1,2,0:T(8,128)(2,1)S(1)}, bf16[32,320,64]{1,2,0:T(8,128)(2,1)}, u32[]{:S(2)}) %copy-start.3) | copy-done | bytes 1310744
  12.4 0.0 copy-start.4
  12.4 1.4 %copy-done.4 = bf16[32,64,320]{2,1,0:T(8,128)(2,1)S(1)} copy-done((bf16[32,64,320]{2,1,0:T(8,128)(2,1)S(1)}, bf16[32,64,320]{2,1,0:T(8,128)(2,1)}, u32[]{:S(2)}) %copy-start.4) | copy-done | bytes 1310744
  13.8 0.0 copy-start.7
  13.8 1.0 %copy-done.7 = bf16[4,64,640]{2,1,0:T(8,128)(2,1)S(1)} copy-done((bf16[4,64,640]{2,1,0:T(8,128)(2,1)S(1)}, bf16[4,64,640]{2,1,0:T(8,128)(2,1)}, u32[]{:S(2)}) %copy-start.7) | copy-done | bytes 327704
  14.8 0.0 copy-start.12
  14.8 0.9 %copy-done.12 = bf16[1,64,1280]{2,1,0:T(8,128)(2,1)S(1)} copy-done((bf16[1,64,1280]{2,1,0:T(8,128)(2,1)S(1)}, bf16[1,64,1280]{2,1,0:T(8,128)(2,1)}, u32[]{:S(2)}) %copy-start.12) | copy-done | bytes 163864
  15.7 0.0 copy-start.13
  15.7 0.8 %copy-done.13 = f32[64,256]{1,0:T(8,128)S(1)} copy-done((f32[64,256]{1,0:T(8,128)S(1)}, f32[64,256]{1,0:T(8,128)}, u32[]{:S(2)}) %copy-start.13) | copy-done | bytes 65560
  16.5 0.6 shard_map.138
  17.2 0.0 copy-start.5
  17.2 1.1 %copy-done.5 = bf16[32,64,320]{2,1,0:T(8,128)(2,1)} copy-done((bf16[32,64,320]{2,1,0:T(8,128)(2,1)}, bf16[32,64,320]{2,1,0:T(8,128)(2,1)S(1)}, u32[]{:S(2)}) %copy-start.5) | copy-done | bytes 1310744
  18.3 4.6 %all-to-all-done.first = bf16[32,4,1408]{2,1,0:T(4,128)(2,1)S(1)} async-done(((bf16[32,4,1408]{2,1,0:T(4,128)(2,1)}), bf16[32,4,1408]{2,1,0:T(4,128)(2,1)S(1)}, u32[]{:S(2)}, u32[]{:S(2)}) %all-to-all-start) | async-done | bytes 360480 | tf_op jit(solution)/shard_map/all_to_all | solution.py:546
  22.9 0.0 copy-start.6
  22.9 0.0 copy-start.8
  22.9 1.1 %copy-done.8 = bf16[4,64,640]{2,1,0:T(8,128)(2,1)S(1)} copy-done((bf16[4,64,640]{2,1,0:T(8,128)(2,1)S(1)}, bf16[4,64,640]{2,1,0:T(8,128)(2,1)}, u32[]{:S(2)}) %copy-start.8) | copy-done | bytes 327704
  24.0 0.0 copy-start.9
  24.0 1.0 %copy-done.9 = bf16[4,640,64]{1,2,0:T(8,128)(2,1)S(1)} copy-done((bf16[4,640,64]{1,2,0:T(8,128)(2,1)S(1)}, bf16[4,640,64]{1,2,0:T(8,128)(2,1)}, u32[]{:S(2)}) %copy-start.9) | copy-done | bytes 327704
  25.0 0.7 shard_map.139
  25.6 4.3 %all-gather = bf16[16,1536]{1,0:T(8,128)(2,1)S(1)} all-gather(bf16[8,1536]{1,0:T(8,128)(2,1)S(1)} %get-tuple-element.36), channel_id=2, replica_groups=mesh['dp'=2,'half'=2,'place'=8] {'half'}, dimensions={0}, use_global_device_ids=true | all-gather | bytes 73728 | tf_op jit(solution)/shard_map/all_gather | solution.py:469
  30.0 12.5 %all_to_all.20.second = bf16[16,8,1536]{2,1,0:T(8,128)(2,1)S(1)} all-to-all(bf16[16,8,1536]{2,1,0:T(8,128)(2,1)S(1)} %bitcast.17), channel_id=1, replica_groups=mesh['dp'=2,'half'=2,'place'=8] {'dp','place'}, dimensions={0} | all-to-all | bytes 786432 | tf_op jit(solution)/shard_map/all_to_all | solution.py:474
  42.4 0.0 copy-done.6
  42.4 0.0 copy-start.10
  42.4 1.1 %copy-done.10 = bf16[1280,320]{0,1:T(8,128)(2,1)S(1)} copy-done((bf16[1280,320]{0,1:T(8,128)(2,1)S(1)}, bf16[1280,320]{0,1:T(8,128)(2,1)}, u32[]{:S(2)}) %copy-start.10) | copy-done | bytes 819224
  43.6 2.4 %shard_map.141 = (bf16[16,8,768]{2,1,0:T(8,128)(2,1)S(1)}, f32[2,64,320]{2,1,0:T(8,128)S(1)}, f32[2,64,64]{2,1,0:T(8,128)S(1)}) custom-call(bf16[16,8,1536]{2,1,0:T(8,128)(2,1)S(1)} %all_to_all.20.second, bf16[320,1280]{1,0:T(8,128)(2,1)S(1)} %bitcast.21, bf16[320,1280]{1,0:T(8,128)(2,1)S(1)} %copy-done, bf16[32,64,320]{2,1,0:T(8,128)(2,1)S(1)} %copy-done.6, ...), custom_call_target="tpu_custom_call" | custom-call | flops 188743680 | bytes 5046272 | tf_op jit(solution)/shard_map/pallas_call | solution.py:481
  46.0 0.0 copy-start.2
  46.0 0.0 copy-start.11
  46.0 0.0 copy-start.14
  46.0 9.8 %all_to_all.21.third = bf16[16,8,768]{2,1,0:T(8,128)(2,1)S(1)} all-to-all(bf16[16,8,768]{2,1,0:T(8,128)(2,1)S(1)} %get-tuple-element.39), channel_id=1, replica_groups=mesh['dp'=2,'half'=2,'place'=8] {'dp','place'}, dimensions={0} | all-to-all | bytes 393216 | tf_op jit(solution)/shard_map/all_to_all | solution.py:579
  55.8 4.3 %all-gather.1 = f32[16,768]{1,0:T(8,128)S(1)} all-gather(f32[8,768]{1,0:T(8,128)S(1)} %get-tuple-element.41), channel_id=3, replica_groups=mesh['dp'=2,'half'=2,'place'=8] {'half'}, dimensions={0}, use_global_device_ids=true | all-gather | bytes 73728 | tf_op jit(solution)/shard_map/all_gather | solution.py:587
  60.1 1.0 %shard_map.143 = (bf16[32,4,768]{2,1,0:T(4,128)(2,1)}, f32[2,8,64]{2,1,0:T(8,128)S(1)}) custom-call(f32[8,768]{1,0:T(8,128)S(1)} %get-tuple-element.40.own, f32[2,8,768]{2,1,0:T(8,128)S(1)} %bitcast.25, bf16[4,64,640]{2,1,0:T(8,128)(2,1)S(1)} %bitcast.20, f32[8,640]{1,0:T(8,128)S(1)} %get-tuple-element.42.inputs, f32[8,128]{1,0:T(8,128)S(1)} %get-tuple-element.43.stats), custom_call_target="tpu_custom_call" | custom-call | flops 2621440 | bytes 626688 | tf_op jit(solution)/shard_map/pallas_call | solution.py:481
  61.1 4.5 %all-to-all-start.3 = ((bf16[32,4,768]{2,1,0:T(4,128)(2,1)}), bf16[32,4,768]{2,1,0:T(4,128)(2,1)S(1)}, u32[]{:S(2)}, u32[]{:S(2)}) async-start(bf16[32,4,768]{2,1,0:T(4,128)(2,1)} %get-tuple-element.44), calls=%async_computation.3 | async-start | bytes 393216 | tf_op jit(solution)/shard_map/all_to_all | solution.py:594
  65.6 2.5 %shard_map.146 = (bf16[32,64,320]{2,1,0:T(8,128)(2,1)}, bf16[32,64,320]{2,1,0:T(8,128)(2,1)}) custom-call(f32[2,64,64]{2,1,0:T(8,128)S(1)} %get-tuple-element.50.left_rows, f32[2,64,320]{2,1,0:T(8,128)S(1)} %get-tuple-element.51.right_rows), custom_call_target="tpu_custom_call" | custom-call | flops 20971520 | bytes 2818048 | tf_op jit(solution)/shard_map/pallas_call | solution.py:481
  68.1 1.2 %shard_map.145 = (bf16[4,64,640]{2,1,0:T(8,128)(2,1)}, bf16[4,64,640]{2,1,0:T(8,128)(2,1)}) custom-call(f32[2,8,64]{2,1,0:T(8,128)S(1)} %get-tuple-element.47.left_rows, bf16[2,8,640]{2,1,0:T(8,128)(2,1)S(1)} %get-tuple-element.48.right_rows), custom_call_target="tpu_custom_call" | custom-call | flops 5242880 | bytes 679936 | tf_op jit(solution)/shard_map/pallas_call | solution.py:481
  69.3 5.7 %all-to-all-done.3.fourth = bf16[32,4,768]{2,1,0:T(4,128)(2,1)S(1)} async-done(((bf16[32,4,768]{2,1,0:T(4,128)(2,1)}), bf16[32,4,768]{2,1,0:T(4,128)(2,1)S(1)}, u32[]{:S(2)}, u32[]{:S(2)}) %all-to-all-start.3) | async-done | bytes 196640 | tf_op jit(solution)/shard_map/all_to_all | solution.py:594
  75.0 0.0 copy-done.2
  75.0 0.0 copy-done.11
  75.0 0.0 copy-done.14
  75.0 1.8 %shard_map.144 = bf16[256,1280]{1,0:T(8,128)(2,1)} custom-call(bf16[32,4,768]{2,1,0:T(4,128)(2,1)S(1)} %all-to-all-done.3.fourth, bf16[256,1280]{1,0:T(8,128)(2,1)S(1)} %bitcast.16, bf16[64,1280]{1,0:T(8,128)(2,1)S(1)} %bitcast.23, f32[64,256]{1,0:T(8,128)S(1)} %copy-done.14, f32[64,256]{1,0:T(8,128)S(1)} %get-tuple-element.46.mixing), custom_call_target="tpu_custom_call" | custom-call | flops 125829120 | bytes 1802240 | tf_op jit(solution)/shard_map/pallas_call | solution.py:481
  (2 shorter events, 0.1 us)
Async XLA Ops:
  0.6 10.3 %copy-start.1 = (bf16[1,256,1280]{2,1,0:T(8,128)(2,1)S(1)}, bf16[1,256,1280]{2,1,0:T(8,128)(2,1)}, u32[]{:S(2)}) copy-start(bf16[1,256,1280]{2,1,0:T(8,128)(2,1)} %param.11) | copy-start | bytes 1966084
  0.6 10.3 %copy-start = (bf16[320,1280]{1,0:T(8,128)(2,1)S(1)}, bf16[320,1280]{1,0:T(8,128)(2,1)}, u32[]{:S(2)}) copy-start(bf16[320,1280]{1,0:T(8,128)(2,1)} %base_out.1) | copy-start | bytes 2457604
  3.8 19.0 %all-to-all-start = ((bf16[32,4,1408]{2,1,0:T(4,128)(2,1)}), bf16[32,4,1408]{2,1,0:T(4,128)(2,1)S(1)}, u32[]{:S(2)}, u32[]{:S(2)}) async-start(bf16[32,4,1408]{2,1,0:T(4,128)(2,1)} %get-tuple-element.30), calls=%async_computation | async-start | bytes 720896 | tf_op jit(solution)/shard_map/all_to_all | solution.py:546
  11.0 1.4 %copy-start.3 = (bf16[32,320,64]{1,2,0:T(8,128)(2,1)S(1)}, bf16[32,320,64]{1,2,0:T(8,128)(2,1)}, u32[]{:S(2)}) copy-start(bf16[32,320,64]{1,2,0:T(8,128)(2,1)} %param.18) | copy-start | bytes 3932164
  12.4 1.4 %copy-start.4 = (bf16[32,64,320]{2,1,0:T(8,128)(2,1)S(1)}, bf16[32,64,320]{2,1,0:T(8,128)(2,1)}, u32[]{:S(2)}) copy-start(bf16[32,64,320]{2,1,0:T(8,128)(2,1)} %rest_3_.1) | copy-start | bytes 3932164
  13.8 1.0 %copy-start.7 = (bf16[4,64,640]{2,1,0:T(8,128)(2,1)S(1)}, bf16[4,64,640]{2,1,0:T(8,128)(2,1)}, u32[]{:S(2)}) copy-start(bf16[4,64,640]{2,1,0:T(8,128)(2,1)} %out_right.1) | copy-start | bytes 983044
  14.8 0.9 %copy-start.12 = (bf16[1,64,1280]{2,1,0:T(8,128)(2,1)S(1)}, bf16[1,64,1280]{2,1,0:T(8,128)(2,1)}, u32[]{:S(2)}) copy-start(bf16[1,64,1280]{2,1,0:T(8,128)(2,1)} %param.13) | copy-start | bytes 491524
  15.7 0.8 %copy-start.13 = (f32[64,256]{1,0:T(8,128)S(1)}, f32[64,256]{1,0:T(8,128)}, u32[]{:S(2)}) copy-start(f32[64,256]{1,0:T(8,128)} %get-tuple-element.31.combine) | copy-start | bytes 196612
  17.2 1.1 %copy-start.5 = (bf16[32,64,320]{2,1,0:T(8,128)(2,1)}, bf16[32,64,320]{2,1,0:T(8,128)(2,1)S(1)}, u32[]{:S(2)}) copy-start(bf16[32,64,320]{2,1,0:T(8,128)(2,1)S(1)} %get-tuple-element.37.in_right) | copy-start | bytes 3932164
  22.9 19.6 %copy-start.6 = (bf16[32,64,320]{2,1,0:T(8,128)(2,1)S(1)}, bf16[32,64,320]{2,1,0:T(8,128)(2,1)}, u32[]{:S(2)}) copy-start(bf16[32,64,320]{2,1,0:T(8,128)(2,1)} %copy-done.5) | copy-start | bytes 3932164
  22.9 1.1 %copy-start.8 = (bf16[4,64,640]{2,1,0:T(8,128)(2,1)S(1)}, bf16[4,64,640]{2,1,0:T(8,128)(2,1)}, u32[]{:S(2)}) copy-start(bf16[4,64,640]{2,1,0:T(8,128)(2,1)} %out_right.1) | copy-start | bytes 983044
  24.0 1.0 %copy-start.9 = (bf16[4,640,64]{1,2,0:T(8,128)(2,1)S(1)}, bf16[4,640,64]{1,2,0:T(8,128)(2,1)}, u32[]{:S(2)}) copy-start(bf16[4,640,64]{1,2,0:T(8,128)(2,1)} %param.16) | copy-start | bytes 983044
  42.4 1.1 %copy-start.10 = (bf16[1280,320]{0,1:T(8,128)(2,1)S(1)}, bf16[1280,320]{0,1:T(8,128)(2,1)}, u32[]{:S(2)}) copy-start(bf16[1280,320]{0,1:T(8,128)(2,1)} %param.14) | copy-start | bytes 2457604
  46.0 29.0 %copy-start.2 = (bf16[1,256,1280]{2,1,0:T(8,128)(2,1)S(1)}, bf16[1,256,1280]{2,1,0:T(8,128)(2,1)}, u32[]{:S(2)}) copy-start(bf16[1,256,1280]{2,1,0:T(8,128)(2,1)} %param.10) | copy-start | bytes 1966084
  46.0 29.0 %copy-start.11 = (bf16[1280,64]{0,1:T(8,128)(2,1)S(1)}, bf16[1280,64]{0,1:T(8,128)(2,1)}, u32[]{:S(2)}) copy-start(bf16[1280,64]{0,1:T(8,128)(2,1)} %param.12) | copy-start | bytes 491524
  46.0 29.0 %copy-start.14 = (f32[64,256]{1,0:T(8,128)S(1)}, f32[64,256]{1,0:T(8,128)}, u32[]{:S(2)}) copy-start(f32[64,256]{1,0:T(8,128)} %get-tuple-element.45.logits) | copy-start | bytes 196612
  61.1 13.9 %all-to-all-start.3 = ((bf16[32,4,768]{2,1,0:T(4,128)(2,1)}), bf16[32,4,768]{2,1,0:T(4,128)(2,1)S(1)}, u32[]{:S(2)}, u32[]{:S(2)}) async-start(bf16[32,4,768]{2,1,0:T(4,128)(2,1)} %get-tuple-element.44), calls=%async_computation.3 | async-start | bytes 393216 | tf_op jit(solution)/shard_map/all_to_all | solution.py:594

commit v10 on v9

--- a/solution.py
+++ b/solution.py
@@ -278,13 +278,23 @@
             first[block, :, 2 * width :] = stats[rows, :]
 
 
-def mixing_kernel(cotangent, saved, combine, *rest):
-    *_, out_left, in_right, out, out_left_near, in_right_near = rest
-    out_left_near[...] = out_left[...]
-    in_right_near[...] = in_right[...]
+def mixing_kernel(cotangent, saved, combine, out):
     mixing = dot_last(saved[...], cotangent[...])
     weights = combine[...]
     out[...] = weights * (mixing - jnp.sum(weights * mixing, axis=0, keepdims=True))
+
+
+def load_kernel(after, *refs):
+    count = len(refs) // 2
+    arrived = refs[-1]
+    copies = [
+        pltpu.make_async_copy(refs[number], refs[count + number], arrived.at[number])
+        for number in range(count)
+    ]
+    for copy in copies:
+        copy.start()
+    for copy in copies:
+        copy.wait()
 
 
 def owner_kernel(groups, first, in_left, out_right, second, inputs_out, lows_out, stats_out):
@@ -544,15 +554,18 @@
         60,
     )
     first = lax.all_to_all(first, BOTH, 0, 0, tiled=True)
-    mixing, out_left, in_right = call(
-        mixing_kernel,
-        [array(full, slots, count), array(low, *out_left.shape), array(low, *in_right.shape)],
-        [cot_rows, saved, combine, out_right, base_out, out_left, in_right],
-        2 * count * slots * width,
-    )
-    first, mixing, out_left, in_right = lax.optimization_barrier(
-        (first, mixing, out_left, in_right)
-    )
+    weights = [in_left, out_right, base_in, base_out, in_right, out_left]
+    weights = call(
+        load_kernel,
+        [array(low, *weight.shape) for weight in weights],
+        [combine, *weights],
+        0,
+        range(len(weights) + 1),
+        [pltpu.SemaphoreType.DMA((len(weights),))],
+        46,
+    )
+    first, *weights = lax.optimization_barrier((first, *weights))
+    in_left, out_right, base_in, base_out, in_right, out_left = weights
     second, inputs, lows, stats = call(
         functools.partial(owner_kernel, groups),
         [
@@ -590,6 +603,12 @@
         [array(low, devices, owned, slice_width + STATS), array(full, 2, rows, rank)],
         [own, others, in_left, inputs, stats],
         2 * rows * owned * rank * slice_width,
+    )
+    (mixing,) = call(
+        mixing_kernel,
+        [array(full, slots, count)],
+        [cot_rows, saved, combine],
+        2 * count * slots * width,
     )
     fourth = lax.all_to_all(fourth, BOTH, 0, 0, tiled=True)
     grad_in_left, grad_out_right = call(

time: 77.4 us -> 77 us (level)
  waiting for transfers between devices: 10.3 us -> 5.56 us
  Pallas kernels: 13.5 us -> 15.4 us
  local copies, waits for them, and re-layouts: 9.91 us -> 11.2 us
    all_to_all x1, waiting for transfers between devices: 4.57 us -> 1.28 us  [local(): first = lax.all_to_all(first, BOTH, 0, 0, tiled=True)]
    pallas_call x10 -> x11, Pallas kernels: 13.5 us -> 15.4 us  [call(): pl.pallas_call(kernel, out_shape=outs, in_specs=[pl.BlockSpec(memory_spac...]
    all_to_all x1, waiting for transfers between devices: 5.73 us -> 4.28 us  [local(): fourth = lax.all_to_all(fourth, BOTH, 0, 0, tiled=True)]
    unnamed x30 -> x44, local copies, waits for them, and re-layouts: 9.91 us -> 11.2 us
  transfers between devices with their start and end apart: 2 -> 2, of which waited for: 2 -> 2; matrix products, arithmetic and copies ran while one was open for 0% -> 0% of each run, Pallas kernels for 6% -> 8%
where the time goes in v10:
time: 77 us; the launch traced here: 76.3 us
  blocking collectives  31.2 us (41%)
  Pallas kernels  15.4 us (20%)
  starting transfers between devices  12.2 us (16%)
  local copies, waits for them, and re-layouts  11.2 us (15%)
  waiting for transfers between devices  5.56 us (7%)
  between operations  0.78 us (1%)
    pallas_call x11, Pallas kernels, call(): pl.pallas_call(kernel, out_shape=outs, in_specs=[pl.BlockSpec(memory_spac...  15.4 us
    all_to_all x1, blocking collectives, to_group(): return lax.all_to_all(blocks, HALF, 0, 0, tiled=True)  12.8 us
    unnamed x44, local copies, waits for them, and re-layouts  11.2 us
    all_to_all x1, blocking collectives, local(): third = lax.all_to_all(third, HALF, 0, 0, tiled=True)  9.76 us
    all_to_all x1, starting transfers between devices, local(): first = lax.all_to_all(first, BOTH, 0, 0, tiled=True)  7.1 us
    all_to_all x1, starting transfers between devices, local(): fourth = lax.all_to_all(fourth, BOTH, 0, 0, tiled=True)  5.12 us
    all_gather x1, blocking collectives, to_group(): blocks = lax.all_gather(block, 'half', axis=0)  4.36 us
    all_to_all x1, waiting for transfers between devices, local(): fourth = lax.all_to_all(fourth, BOTH, 0, 0, tiled=True)  4.28 us
  transfers between devices with their start and end apart: 2, of which 2 were waited for; matrix products, arithmetic and copies ran while one was open for 0% of the time, Pallas kernels for 8%

profile of v10, /device:TPU:1, one launch (start us, length us, event | category | flops | bytes accessed | tf_op | source)
XLA Modules:
  0.0 76.3 jit_solution(15963405221066169759)
XLA Ops:
  0.6 3.1 %shard_map.137 = (bf16[32,4,1408]{2,1,0:T(4,128)(2,1)}, f32[64,256]{1,0:T(8,128)}, f32[64,256]{1,0:T(8,128)}) custom-call(bf16[256,1280]{1,0:T(8,128)(2,1)} %bitcast.13, bf16[256,1280]{1,0:T(8,128)(2,1)} %bitcast.15, bf16[64,1280]{1,0:T(8,128)(2,1)} %bitcast.19), custom_call_target="tpu_custom_call" | custom-call | flops 125829120 | bytes 1966080 | tf_op jit(solution)/shard_map/pallas_call | solution.py:491
  3.7 7.1 %all-to-all-start = ((bf16[32,4,1408]{2,1,0:T(4,128)(2,1)}), bf16[32,4,1408]{2,1,0:T(4,128)(2,1)S(1)}, u32[]{:S(2)}, u32[]{:S(2)}) async-start(bf16[32,4,1408]{2,1,0:T(4,128)(2,1)} %get-tuple-element.36), calls=%async_computation | async-start | bytes 720896 | tf_op jit(solution)/shard_map/all_to_all | solution.py:556
  10.8 0.0 copy-start.9
  10.9 1.1 %copy-done.9 = bf16[1280,320]{0,1:T(8,128)(2,1)S(1)} copy-done((bf16[1280,320]{0,1:T(8,128)(2,1)S(1)}, bf16[1280,320]{0,1:T(8,128)(2,1)}, u32[]{:S(2)}) %copy-start.9) | copy-done | bytes 819224
  12.0 0.0 copy-start.10
  12.0 1.1 %copy-done.10 = bf16[320,1280]{1,0:T(8,128)(2,1)S(1)} copy-done((bf16[320,1280]{1,0:T(8,128)(2,1)S(1)}, bf16[320,1280]{1,0:T(8,128)(2,1)}, u32[]{:S(2)}) %copy-start.10) | copy-done | bytes 819224
  13.1 0.0 copy-start.14
  13.1 1.0 %copy-done.14 = bf16[4,640,64]{1,2,0:T(8,128)(2,1)S(1)} copy-done((bf16[4,640,64]{1,2,0:T(8,128)(2,1)S(1)}, bf16[4,640,64]{1,2,0:T(8,128)(2,1)}, u32[]{:S(2)}) %copy-start.14) | copy-done | bytes 327704
  14.1 0.0 copy-start.15
  14.1 1.0 %copy-done.15 = bf16[4,64,640]{2,1,0:T(8,128)(2,1)S(1)} copy-done((bf16[4,64,640]{2,1,0:T(8,128)(2,1)S(1)}, bf16[4,64,640]{2,1,0:T(8,128)(2,1)}, u32[]{:S(2)}) %copy-start.15) | copy-done | bytes 327704
  15.1 0.0 copy-start.16
  15.1 0.8 %copy-done.16 = f32[64,256]{1,0:T(8,128)S(1)} copy-done((f32[64,256]{1,0:T(8,128)S(1)}, f32[64,256]{1,0:T(8,128)}, u32[]{:S(2)}) %copy-start.16) | copy-done | bytes 65560
  15.9 2.3 %shard_map.138 = (bf16[4,64,640]{2,1,0:T(8,128)(2,1)S(1)}, bf16[4,64,640]{2,1,0:T(8,128)(2,1)S(1)}, bf16[320,1280]{1,0:T(8,128)(2,1)S(1)}, bf16[320,1280]{1,0:T(...) custom-call(f32[64,256]{1,0:T(8,128)S(1)} %copy-done.16, ...), custom_call_target="tpu_custom_call" | custom-call | bytes 9895936 | tf_op jit(solution)/shard_map/pallas_call | solution.py:491
  18.3 0.0 copy-start.2
  18.3 0.7 copy-done.2
  19.0 0.0 copy-start.5
  19.0 0.9 %copy-done.5 = bf16[320,1280]{1,0:T(8,128)(2,1)} copy-done((bf16[320,1280]{1,0:T(8,128)(2,1)}, bf16[320,1280]{1,0:T(8,128)(2,1)S(1)}, u32[]{:S(2)}) %copy-start.5) | copy-done | bytes 819224
  19.9 0.0 copy-start.7
  19.9 0.9 %copy-done.7 = bf16[320,1280]{1,0:T(8,128)(2,1)} copy-done((bf16[320,1280]{1,0:T(8,128)(2,1)}, bf16[320,1280]{1,0:T(8,128)(2,1)S(1)}, u32[]{:S(2)}) %copy-start.7) | copy-done | bytes 819224
  20.8 0.0 copy-start.12
  20.8 0.7 copy-done.12
  21.5 1.3 %all-to-all-done.first = bf16[32,4,1408]{2,1,0:T(4,128)(2,1)S(1)} async-done(((bf16[32,4,1408]{2,1,0:T(4,128)(2,1)}), bf16[32,4,1408]{2,1,0:T(4,128)(2,1)S(1)}, u32[]{:S(2)}, u32[]{:S(2)}) %all-to-all-start) | async-done | bytes 360480 | tf_op jit(solution)/shard_map/all_to_all | solution.py:556
  22.8 0.0 copy-start.3
  22.8 1.0 %copy-done.3 = bf16[4,64,640]{2,1,0:T(8,128)(2,1)S(1)} copy-done((bf16[4,64,640]{2,1,0:T(8,128)(2,1)S(1)}, bf16[4,64,640]{2,1,0:T(8,128)(2,1)}, u32[]{:S(2)}) %copy-start.3) | copy-done | bytes 327704
  23.7 0.0 copy-start.13
  23.7 1.0 %copy-done.13 = bf16[4,64,640]{2,1,0:T(8,128)(2,1)S(1)} copy-done((bf16[4,64,640]{2,1,0:T(8,128)(2,1)S(1)}, bf16[4,64,640]{2,1,0:T(8,128)(2,1)}, u32[]{:S(2)}) %copy-start.13) | copy-done | bytes 327704
  24.7 0.0 copy-start.6
  24.7 0.0 copy-start.8
  24.7 0.7 shard_map.139
  25.4 0.0 copy-start.20
  25.4 4.4 %all-gather = bf16[16,1536]{1,0:T(8,128)(2,1)S(1)} all-gather(bf16[8,1536]{1,0:T(8,128)(2,1)S(1)} %get-tuple-element.47), channel_id=2, replica_groups=mesh['dp'=2,'half'=2,'place'=8] {'half'}, dimensions={0}, use_global_device_ids=true | all-gather | bytes 73728 | tf_op jit(solution)/shard_map/all_gather | solution.py:479
  29.8 12.8 %all_to_all.20.second = bf16[16,8,1536]{2,1,0:T(8,128)(2,1)S(1)} all-to-all(bf16[16,8,1536]{2,1,0:T(8,128)(2,1)S(1)} %bitcast.17), channel_id=1, replica_groups=mesh['dp'=2,'half'=2,'place'=8] {'dp','place'}, dimensions={0} | all-to-all | bytes 786432 | tf_op jit(solution)/shard_map/all_to_all | solution.py:484
  42.5 0.0 copy-done.6
  42.5 0.0 copy-done.8
  42.5 0.0 copy-start.4
  42.5 0.0 copy-start.17
  42.6 0.0 copy-start.19
  42.6 2.4 %shard_map.141 = (bf16[16,8,768]{2,1,0:T(8,128)(2,1)S(1)}, f32[2,64,320]{2,1,0:T(8,128)S(1)}, f32[2,64,64]{2,1,0:T(8,128)S(1)}) custom-call(bf16[16,8,1536]{2,1,0:T(8,128)(2,1)S(1)} %all_to_all.20.second, bf16[320,1280]{1,0:T(8,128)(2,1)S(1)} %copy-done.6, bf16[320,1280]{1,0:T(8,128)(2,1)S(1)} %copy-done.8, ...), custom_call_target="tpu_custom_call" | custom-call | flops 188743680 | bytes 5046272 | tf_op jit(solution)/shard_map/pallas_call | solution.py:491
  45.0 0.0 copy-done.20
  45.0 0.0 copy-start.1
  45.0 0.0 copy-start
  45.0 0.0 copy-start.11
  45.0 0.0 copy-start.21
  45.0 9.8 %all_to_all.21.third = bf16[16,8,768]{2,1,0:T(8,128)(2,1)S(1)} all-to-all(bf16[16,8,768]{2,1,0:T(8,128)(2,1)S(1)} %get-tuple-element.52), channel_id=1, replica_groups=mesh['dp'=2,'half'=2,'place'=8] {'dp','place'}, dimensions={0} | all-to-all | bytes 393216 | tf_op jit(solution)/shard_map/all_to_all | solution.py:592
  54.8 4.3 %all-gather.1 = f32[16,768]{1,0:T(8,128)S(1)} all-gather(f32[8,768]{1,0:T(8,128)S(1)} %get-tuple-element.54), channel_id=3, replica_groups=mesh['dp'=2,'half'=2,'place'=8] {'half'}, dimensions={0}, use_global_device_ids=true | all-gather | bytes 73728 | tf_op jit(solution)/shard_map/all_gather | solution.py:600
  59.1 0.0 copy-done.4
  59.1 1.0 %shard_map.143 = (bf16[32,4,768]{2,1,0:T(4,128)(2,1)}, f32[2,8,64]{2,1,0:T(8,128)S(1)}) custom-call(f32[8,768]{1,0:T(8,128)S(1)} %get-tuple-element.53.own, f32[2,8,768]{2,1,0:T(8,128)S(1)} %bitcast.23, bf16[4,64,640]{2,1,0:T(8,128)(2,1)S(1)} %copy-done.4, f32[8,640]{1,0:T(8,128)S(1)} %get-tuple-element.55.inputs, f32[8,128]{1,0:T(8,128)S(1)} %get-tuple-element.56.stats), custom_call_target="tpu_custom_call" | custom-call | flops 2621440 | bytes 626688 | tf_op jit(solution)/shard_map/pallas_call | solution.py:491
  60.1 5.1 %all-to-all-start.3 = ((bf16[32,4,768]{2,1,0:T(4,128)(2,1)}), bf16[32,4,768]{2,1,0:T(4,128)(2,1)S(1)}, u32[]{:S(2)}, u32[]{:S(2)}) async-start(bf16[32,4,768]{2,1,0:T(4,128)(2,1)} %get-tuple-element.57), calls=%async_computation.3 | async-start | bytes 393216 | tf_op jit(solution)/shard_map/all_to_all | solution.py:613
  65.2 0.0 copy-done.17
  65.2 0.0 copy-done.1
  65.2 0.0 copy-start.18
  65.2 0.9 %copy-done.18 = bf16[1,64,1280]{2,1,0:T(8,128)(2,1)S(1)} copy-done((bf16[1,64,1280]{2,1,0:T(8,128)(2,1)S(1)}, bf16[1,64,1280]{2,1,0:T(8,128)(2,1)}, u32[]{:S(2)}) %copy-start.18) | copy-done | bytes 163864
  66.1 0.4 shard_map.144.mixing
  66.5 2.5 %shard_map.147 = (bf16[32,64,320]{2,1,0:T(8,128)(2,1)}, bf16[32,64,320]{2,1,0:T(8,128)(2,1)}) custom-call(f32[2,64,64]{2,1,0:T(8,128)S(1)} %get-tuple-element.62.left_rows, f32[2,64,320]{2,1,0:T(8,128)S(1)} %get-tuple-element.63.right_rows), custom_call_target="tpu_custom_call" | custom-call | flops 20971520 | bytes 2818048 | tf_op jit(solution)/shard_map/pallas_call | solution.py:491
  69.0 0.0 copy-done.21
  69.0 1.2 %shard_map.146 = (bf16[4,64,640]{2,1,0:T(8,128)(2,1)}, bf16[4,64,640]{2,1,0:T(8,128)(2,1)}) custom-call(f32[2,8,64]{2,1,0:T(8,128)S(1)} %get-tuple-element.59.left_rows, bf16[2,8,640]{2,1,0:T(8,128)(2,1)S(1)} %copy-done.21), custom_call_target="tpu_custom_call" | custom-call | flops 5242880 | bytes 679936 | tf_op jit(solution)/shard_map/pallas_call | solution.py:491
  70.2 4.3 %all-to-all-done.3.fourth = bf16[32,4,768]{2,1,0:T(4,128)(2,1)S(1)} async-done(((bf16[32,4,768]{2,1,0:T(4,128)(2,1)}), bf16[32,4,768]{2,1,0:T(4,128)(2,1)S(1)}, u32[]{:S(2)}, u32[]{:S(2)}) %all-to-all-start.3) | async-done | bytes 196640 | tf_op jit(solution)/shard_map/all_to_all | solution.py:613
  74.5 0.0 copy-done.19
  74.5 0.0 copy-done
  74.5 0.0 copy-done.11
  74.5 1.8 %shard_map.145 = bf16[256,1280]{1,0:T(8,128)(2,1)} custom-call(bf16[32,4,768]{2,1,0:T(4,128)(2,1)S(1)} %all-to-all-done.3.fourth, bf16[256,1280]{1,0:T(8,128)(2,1)S(1)} %bitcast.14, bf16[64,1280]{1,0:T(8,128)(2,1)S(1)} %bitcast.20, f32[64,256]{1,0:T(8,128)S(1)} %copy-done.19, f32[64,256]{1,0:T(8,128)S(1)} %shard_map.144.mixing), custom_call_target="tpu_custom_call" | custom-call | flops 125829120 | bytes 1802240 | tf_op jit(solution)/shard_map/pallas_call | solution.py:491
  (2 shorter events, 0.1 us)
Async XLA Ops:
  3.7 19.0 %all-to-all-start = ((bf16[32,4,1408]{2,1,0:T(4,128)(2,1)}), bf16[32,4,1408]{2,1,0:T(4,128)(2,1)S(1)}, u32[]{:S(2)}, u32[]{:S(2)}) async-start(bf16[32,4,1408]{2,1,0:T(4,128)(2,1)} %get-tuple-element.36), calls=%async_computation | async-start | bytes 720896 | tf_op jit(solution)/shard_map/all_to_all | solution.py:556
  10.8 1.1 %copy-start.9 = (bf16[1280,320]{0,1:T(8,128)(2,1)S(1)}, bf16[1280,320]{0,1:T(8,128)(2,1)}, u32[]{:S(2)}) copy-start(bf16[1280,320]{0,1:T(8,128)(2,1)} %param.14) | copy-start | bytes 2457604
  12.0 1.1 %copy-start.10 = (bf16[320,1280]{1,0:T(8,128)(2,1)S(1)}, bf16[320,1280]{1,0:T(8,128)(2,1)}, u32[]{:S(2)}) copy-start(bf16[320,1280]{1,0:T(8,128)(2,1)} %refs_3_.1) | copy-start | bytes 2457604
  13.1 1.0 %copy-start.14 = (bf16[4,640,64]{1,2,0:T(8,128)(2,1)S(1)}, bf16[4,640,64]{1,2,0:T(8,128)(2,1)}, u32[]{:S(2)}) copy-start(bf16[4,640,64]{1,2,0:T(8,128)(2,1)} %param.16) | copy-start | bytes 983044
  14.1 1.0 %copy-start.15 = (bf16[4,64,640]{2,1,0:T(8,128)(2,1)S(1)}, bf16[4,64,640]{2,1,0:T(8,128)(2,1)}, u32[]{:S(2)}) copy-start(bf16[4,64,640]{2,1,0:T(8,128)(2,1)} %refs_1_.1) | copy-start | bytes 983044
  15.1 0.8 %copy-start.16 = (f32[64,256]{1,0:T(8,128)S(1)}, f32[64,256]{1,0:T(8,128)}, u32[]{:S(2)}) copy-start(f32[64,256]{1,0:T(8,128)} %get-tuple-element.37.after.combine) | copy-start | bytes 196612
  18.3 0.7 copy-start.2
  19.0 0.9 %copy-start.5 = (bf16[320,1280]{1,0:T(8,128)(2,1)}, bf16[320,1280]{1,0:T(8,128)(2,1)S(1)}, u32[]{:S(2)}) copy-start(bf16[320,1280]{1,0:T(8,128)(2,1)S(1)} %get-tuple-element.48.base_in) | copy-start | bytes 2457604
  19.9 0.9 %copy-start.7 = (bf16[320,1280]{1,0:T(8,128)(2,1)}, bf16[320,1280]{1,0:T(8,128)(2,1)S(1)}, u32[]{:S(2)}) copy-start(bf16[320,1280]{1,0:T(8,128)(2,1)S(1)} %get-tuple-element.49.base_out) | copy-start | bytes 2457604
  20.8 0.7 copy-start.12
  22.8 1.0 %copy-start.3 = (bf16[4,64,640]{2,1,0:T(8,128)(2,1)S(1)}, bf16[4,64,640]{2,1,0:T(8,128)(2,1)}, u32[]{:S(2)}) copy-start(bf16[4,64,640]{2,1,0:T(8,128)(2,1)} %copy-done.2) | copy-start | bytes 983044
  23.7 1.0 %copy-start.13 = (bf16[4,64,640]{2,1,0:T(8,128)(2,1)S(1)}, bf16[4,64,640]{2,1,0:T(8,128)(2,1)}, u32[]{:S(2)}) copy-start(bf16[4,64,640]{2,1,0:T(8,128)(2,1)} %copy-done.12) | copy-start | bytes 983044
  24.7 17.8 %copy-start.6 = (bf16[320,1280]{1,0:T(8,128)(2,1)S(1)}, bf16[320,1280]{1,0:T(8,128)(2,1)}, u32[]{:S(2)}) copy-start(bf16[320,1280]{1,0:T(8,128)(2,1)} %copy-done.5) | copy-start | bytes 2457604
  24.7 17.8 %copy-start.8 = (bf16[320,1280]{1,0:T(8,128)(2,1)S(1)}, bf16[320,1280]{1,0:T(8,128)(2,1)}, u32[]{:S(2)}) copy-start(bf16[320,1280]{1,0:T(8,128)(2,1)} %copy-done.7) | copy-start | bytes 2457604
  25.4 19.6 %copy-start.20 = (bf16[2,8,640]{2,1,0:T(8,128)(2,1)}, bf16[2,8,640]{2,1,0:T(8,128)(2,1)S(1)}, u32[]{:S(2)}) copy-start(bf16[2,8,640]{2,1,0:T(8,128)(2,1)S(1)} %get-tuple-element.60.right_rows) | copy-start | bytes 61444
  42.5 16.5 %copy-start.4 = (bf16[4,64,640]{2,1,0:T(8,128)(2,1)S(1)}, bf16[4,64,640]{2,1,0:T(8,128)(2,1)}, u32[]{:S(2)}) copy-start(bf16[4,64,640]{2,1,0:T(8,128)(2,1)} %copy-done.2) | copy-start | bytes 983044
  42.5 22.7 %copy-start.17 = (f32[64,256]{1,0:T(8,128)S(1)}, f32[64,256]{1,0:T(8,128)}, u32[]{:S(2)}) copy-start(f32[64,256]{1,0:T(8,128)} %get-tuple-element.37.after.combine) | copy-start | bytes 196612
  42.6 32.0 %copy-start.19 = (f32[64,256]{1,0:T(8,128)S(1)}, f32[64,256]{1,0:T(8,128)}, u32[]{:S(2)}) copy-start(f32[64,256]{1,0:T(8,128)} %get-tuple-element.58.logits) | copy-start | bytes 196612
  45.0 20.2 %copy-start.1 = (bf16[1,256,1280]{2,1,0:T(8,128)(2,1)S(1)}, bf16[1,256,1280]{2,1,0:T(8,128)(2,1)}, u32[]{:S(2)}) copy-start(bf16[1,256,1280]{2,1,0:T(8,128)(2,1)} %param.11) | copy-start | bytes 1966084
  45.0 29.5 %copy-start = (bf16[1,256,1280]{2,1,0:T(8,128)(2,1)S(1)}, bf16[1,256,1280]{2,1,0:T(8,128)(2,1)}, u32[]{:S(2)}) copy-start(bf16[1,256,1280]{2,1,0:T(8,128)(2,1)} %param.10) | copy-start | bytes 1966084
  45.0 29.5 %copy-start.11 = (bf16[1280,64]{0,1:T(8,128)(2,1)S(1)}, bf16[1280,64]{0,1:T(8,128)(2,1)}, u32[]{:S(2)}) copy-start(bf16[1280,64]{0,1:T(8,128)(2,1)} %param.12) | copy-start | bytes 491524
  45.0 24.0 %copy-start.21 = (bf16[2,8,640]{2,1,0:T(8,128)(2,1)S(1)}, bf16[2,8,640]{2,1,0:T(8,128)(2,1)}, u32[]{:S(2)}) copy-start(bf16[2,8,640]{2,1,0:T(8,128)(2,1)} %copy-done.20) | copy-start | bytes 61444
  60.1 14.4 %all-to-all-start.3 = ((bf16[32,4,768]{2,1,0:T(4,128)(2,1)}), bf16[32,4,768]{2,1,0:T(4,128)(2,1)S(1)}, u32[]{:S(2)}, u32[]{:S(2)}) async-start(bf16[32,4,768]{2,1,0:T(4,128)(2,1)} %get-tuple-element.57), calls=%async_computation.3 | async-start | bytes 393216 | tf_op jit(solution)/shard_map/all_to_all | solution.py:613
  65.2 0.9 %copy-start.18 = (bf16[1,64,1280]{2,1,0:T(8,128)(2,1)S(1)}, bf16[1,64,1280]{2,1,0:T(8,128)(2,1)}, u32[]{:S(2)}) copy-start(bf16[1,64,1280]{2,1,0:T(8,128)(2,1)} %param.13) | copy-start | bytes 491524

commit v11 on v9

--- a/solution.py
+++ b/solution.py
@@ -278,10 +278,7 @@
             first[block, :, 2 * width :] = stats[rows, :]
 
 
-def mixing_kernel(cotangent, saved, combine, *rest):
-    *_, out_left, in_right, out, out_left_near, in_right_near = rest
-    out_left_near[...] = out_left[...]
-    in_right_near[...] = in_right[...]
+def mixing_kernel(cotangent, saved, combine, out):
     mixing = dot_last(saved[...], cotangent[...])
     weights = combine[...]
     out[...] = weights * (mixing - jnp.sum(weights * mixing, axis=0, keepdims=True))
@@ -544,15 +541,6 @@
         60,
     )
     first = lax.all_to_all(first, BOTH, 0, 0, tiled=True)
-    mixing, out_left, in_right = call(
-        mixing_kernel,
-        [array(full, slots, count), array(low, *out_left.shape), array(low, *in_right.shape)],
-        [cot_rows, saved, combine, out_right, base_out, out_left, in_right],
-        2 * count * slots * width,
-    )
-    first, mixing, out_left, in_right = lax.optimization_barrier(
-        (first, mixing, out_left, in_right)
-    )
     second, inputs, lows, stats = call(
         functools.partial(owner_kernel, groups),
         [
@@ -590,6 +578,12 @@
         [array(low, devices, owned, slice_width + STATS), array(full, 2, rows, rank)],
         [own, others, in_left, inputs, stats],
         2 * rows * owned * rank * slice_width,
+    )
+    (mixing,) = call(
+        mixing_kernel,
+        [array(full, slots, count)],
+        [cot_rows, saved, combine],
+        2 * count * slots * width,
     )
     fourth = lax.all_to_all(fourth, BOTH, 0, 0, tiled=True)
     grad_in_left, grad_out_right = call(

time: 77.4 us -> 76.2 us (0.984)
  blocking collectives: 30.8 us -> 49.9 us
  local copies, waits for them, and re-layouts: 9.91 us -> 2.16 us
  starting transfers between devices: 11.6 us -> 4.5 us
  waiting for transfers between devices: 10.3 us -> 5.33 us
    all_to_all x0 -> x1, blocking collectives: none -> 19 us  [local(): first = lax.all_to_all(first, BOTH, 0, 0, tiled=True)]
    unnamed x30 -> x24, local copies, waits for them, and re-layouts: 9.91 us -> 2.16 us
    all_to_all x1 -> x0, starting transfers between devices: 7.1 us -> none  [local(): first = lax.all_to_all(first, BOTH, 0, 0, tiled=True)]
    all_to_all x1 -> x0, waiting for transfers between devices: 4.57 us -> none  [local(): first = lax.all_to_all(first, BOTH, 0, 0, tiled=True)]
  transfers between devices with their start and end apart: 2 -> 1, of which waited for: 2 -> 1; matrix products, arithmetic and copies ran while one was open for 0% -> 0% of each run, Pallas kernels for 6% -> 5%
where the time goes in v11:
time: 76.2 us; the launch traced here: 75.8 us
  blocking collectives  49.9 us (65%)
  Pallas kernels  13.2 us (17%)
  waiting for transfers between devices  5.33 us (7%)
  starting transfers between devices  4.5 us (6%)
  local copies, waits for them, and re-layouts  2.16 us (3%)
    all_to_all x1, blocking collectives, local(): first = lax.all_to_all(first, BOTH, 0, 0, tiled=True)  19 us
    pallas_call x10, Pallas kernels, call(): pl.pallas_call(kernel, out_shape=outs, in_specs=[pl.BlockSpec(memory_spac...  13.2 us
    all_to_all x1, blocking collectives, to_group(): return lax.all_to_all(blocks, HALF, 0, 0, tiled=True)  12.5 us
    all_to_all x1, blocking collectives, local(): third = lax.all_to_all(third, HALF, 0, 0, tiled=True)  9.76 us
    all_to_all x1, waiting for transfers between devices, local(): fourth = lax.all_to_all(fourth, BOTH, 0, 0, tiled=True)  5.33 us
    all_to_all x1, starting transfers between devices, local(): fourth = lax.all_to_all(fourth, BOTH, 0, 0, tiled=True)  4.5 us
    all_gather x1, blocking collectives, to_group(): blocks = lax.all_gather(block, 'half', axis=0)  4.33 us
    all_gather x1, blocking collectives, local(): others = lax.all_gather(other, 'half', axis=0)  4.25 us
  transfers between devices with their start and end apart: 1, of which 1 were waited for; matrix products, arithmetic and copies ran while one was open for 0% of the time, Pallas kernels for 5%

profile of v11, /device:TPU:1, one launch (start us, length us, event | category | flops | bytes accessed | tf_op | source)
XLA Modules:
  0.0 75.8 jit_solution(4652105529131761553)
XLA Ops:
  0.6 0.0 copy-start.4
  0.6 0.0 copy-start.3
  0.7 3.2 %shard_map.137 = (bf16[32,4,1408]{2,1,0:T(4,128)(2,1)}, f32[64,256]{1,0:T(8,128)}, f32[64,256]{1,0:T(8,128)}) custom-call(bf16[256,1280]{1,0:T(8,128)(2,1)} %bitcast.13, bf16[256,1280]{1,0:T(8,128)(2,1)} %bitcast.15, bf16[64,1280]{1,0:T(8,128)(2,1)} %bitcast.22), custom_call_target="tpu_custom_call" | custom-call | flops 125829120 | bytes 1966080 | tf_op jit(solution)/shard_map/pallas_call | solution.py:478
  3.9 0.0 copy-start.2
  3.9 0.0 copy-start.5
  3.9 19.0 %all_to_all.20.first = bf16[32,4,1408]{2,1,0:T(4,128)(2,1)S(1)} all-to-all(bf16[32,4,1408]{2,1,0:T(4,128)(2,1)} %get-tuple-element.23), channel_id=1, replica_groups=mesh['dp'=2,'half'=2,'place'=8] {'dp','half','place'}, dimensions={0} | all-to-all | bytes 720896 | tf_op jit(solution)/shard_map/all_to_all | solution.py:543
  22.9 0.0 copy-done.4
  22.9 0.0 copy-start.8
  22.9 1.0 %copy-done.8 = bf16[4,64,640]{2,1,0:T(8,128)(2,1)S(1)} copy-done((bf16[4,64,640]{2,1,0:T(8,128)(2,1)S(1)}, bf16[4,64,640]{2,1,0:T(8,128)(2,1)}, u32[]{:S(2)}) %copy-start.8) | copy-done | bytes 327704
  23.9 0.7 shard_map.138
  24.6 4.3 %all-gather = bf16[16,1536]{1,0:T(8,128)(2,1)S(1)} all-gather(bf16[8,1536]{1,0:T(8,128)(2,1)S(1)} %get-tuple-element.24), channel_id=2, replica_groups=mesh['dp'=2,'half'=2,'place'=8] {'half'}, dimensions={0}, use_global_device_ids=true | all-gather | bytes 73728 | tf_op jit(solution)/shard_map/all_gather | solution.py:466
  28.9 12.5 %all_to_all.21.second = bf16[16,8,1536]{2,1,0:T(8,128)(2,1)S(1)} all-to-all(bf16[16,8,1536]{2,1,0:T(8,128)(2,1)S(1)} %bitcast.17), channel_id=1, replica_groups=mesh['dp'=2,'half'=2,'place'=8] {'dp','place'}, dimensions={0} | all-to-all | bytes 786432 | tf_op jit(solution)/shard_map/all_to_all | solution.py:471
  41.4 0.0 copy-done.3
  41.4 0.0 copy-done.2
  41.4 0.0 copy-done.5
  41.4 0.0 copy-start.6
  41.4 1.1 %copy-done.6 = bf16[320,1280]{1,0:T(8,128)(2,1)S(1)} copy-done((bf16[320,1280]{1,0:T(8,128)(2,1)S(1)}, bf16[320,1280]{1,0:T(8,128)(2,1)}, u32[]{:S(2)}) %copy-start.6) | copy-done | bytes 819224
  42.6 0.0 copy-start.9
  42.6 0.0 copy-start.11
  42.6 2.4 %shard_map.140 = (bf16[16,8,768]{2,1,0:T(8,128)(2,1)S(1)}, f32[2,64,320]{2,1,0:T(8,128)S(1)}, f32[2,64,64]{2,1,0:T(8,128)S(1)}) custom-call(bf16[16,8,1536]{2,1,0:T(8,128)(2,1)S(1)} %all_to_all.21.second, bf16[320,1280]{1,0:T(8,128)(2,1)S(1)} %bitcast.21, bf16[320,1280]{1,0:T(8,128)(2,1)S(1)} %copy-done.6, bf16[32,64,320]{2,1,0:T(8,128)(2,1)S(1)} %copy-done.2, ...), custom_call_target="tpu_custom_call" | custom-call | flops 188743680 | bytes 5046272 | tf_op jit(solution)/shard_map/pallas_call | solution.py:478
  45.0 0.0 copy-start.1
  45.0 0.0 copy-start
  45.0 0.0 copy-start.7
  45.0 0.0 copy-start.10
  45.0 9.8 %all_to_all.22.third = bf16[16,8,768]{2,1,0:T(8,128)(2,1)S(1)} all-to-all(bf16[16,8,768]{2,1,0:T(8,128)(2,1)S(1)} %get-tuple-element.25), channel_id=1, replica_groups=mesh['dp'=2,'half'=2,'place'=8] {'dp','place'}, dimensions={0} | all-to-all | bytes 393216 | tf_op jit(solution)/shard_map/all_to_all | solution.py:567
  54.8 4.3 %all-gather.1 = f32[16,768]{1,0:T(8,128)S(1)} all-gather(f32[8,768]{1,0:T(8,128)S(1)} %get-tuple-element.27), channel_id=3, replica_groups=mesh['dp'=2,'half'=2,'place'=8] {'half'}, dimensions={0}, use_global_device_ids=true | all-gather | bytes 73728 | tf_op jit(solution)/shard_map/all_gather | solution.py:575
  59.1 1.0 %shard_map.142 = (bf16[32,4,768]{2,1,0:T(4,128)(2,1)}, f32[2,8,64]{2,1,0:T(8,128)S(1)}) custom-call(f32[8,768]{1,0:T(8,128)S(1)} %get-tuple-element.26.own, f32[2,8,768]{2,1,0:T(8,128)S(1)} %bitcast.25, bf16[4,64,640]{2,1,0:T(8,128)(2,1)S(1)} %bitcast.20, f32[8,640]{1,0:T(8,128)S(1)} %get-tuple-element.28.inputs, f32[8,128]{1,0:T(8,128)S(1)} %get-tuple-element.29.stats), custom_call_target="tpu_custom_call" | custom-call | flops 2621440 | bytes 626688 | tf_op jit(solution)/shard_map/pallas_call | solution.py:478
  60.0 4.5 %all-to-all-start.3 = ((bf16[32,4,768]{2,1,0:T(4,128)(2,1)}), bf16[32,4,768]{2,1,0:T(4,128)(2,1)S(1)}, u32[]{:S(2)}, u32[]{:S(2)}) async-start(bf16[32,4,768]{2,1,0:T(4,128)(2,1)} %get-tuple-element.30), calls=%async_computation.3 | async-start | bytes 393216 | tf_op jit(solution)/shard_map/all_to_all | solution.py:588
  64.6 0.0 copy-done.9
  64.6 0.0 copy-done.11
  64.6 0.0 copy-done.1
  64.6 0.4 shard_map.143.mixing
  65.0 2.5 %shard_map.146 = (bf16[32,64,320]{2,1,0:T(8,128)(2,1)}, bf16[32,64,320]{2,1,0:T(8,128)(2,1)}) custom-call(f32[2,64,64]{2,1,0:T(8,128)S(1)} %get-tuple-element.36.left_rows, f32[2,64,320]{2,1,0:T(8,128)S(1)} %get-tuple-element.37.right_rows), custom_call_target="tpu_custom_call" | custom-call | flops 20971520 | bytes 2818048 | tf_op jit(solution)/shard_map/pallas_call | solution.py:478
  67.5 1.2 %shard_map.145 = (bf16[4,64,640]{2,1,0:T(8,128)(2,1)}, bf16[4,64,640]{2,1,0:T(8,128)(2,1)}) custom-call(f32[2,8,64]{2,1,0:T(8,128)S(1)} %get-tuple-element.33.left_rows, bf16[2,8,640]{2,1,0:T(8,128)(2,1)S(1)} %get-tuple-element.34.right_rows), custom_call_target="tpu_custom_call" | custom-call | flops 5242880 | bytes 679936 | tf_op jit(solution)/shard_map/pallas_call | solution.py:478
  68.7 5.3 %all-to-all-done.3.fourth = bf16[32,4,768]{2,1,0:T(4,128)(2,1)S(1)} async-done(((bf16[32,4,768]{2,1,0:T(4,128)(2,1)}), bf16[32,4,768]{2,1,0:T(4,128)(2,1)S(1)}, u32[]{:S(2)}, u32[]{:S(2)}) %all-to-all-start.3) | async-done | bytes 196640 | tf_op jit(solution)/shard_map/all_to_all | solution.py:588
  74.0 0.0 copy-done
  74.0 0.0 copy-done.7
  74.0 0.0 copy-done.10
  74.0 1.8 %shard_map.144 = bf16[256,1280]{1,0:T(8,128)(2,1)} custom-call(bf16[32,4,768]{2,1,0:T(4,128)(2,1)S(1)} %all-to-all-done.3.fourth, bf16[256,1280]{1,0:T(8,128)(2,1)S(1)} %bitcast.14, bf16[64,1280]{1,0:T(8,128)(2,1)S(1)} %bitcast.23, f32[64,256]{1,0:T(8,128)S(1)} %copy-done.10, f32[64,256]{1,0:T(8,128)S(1)} %shard_map.143.mixing), custom_call_target="tpu_custom_call" | custom-call | flops 125829120 | bytes 1802240 | tf_op jit(solution)/shard_map/pallas_call | solution.py:478
  (2 shorter events, 0.1 us)
Async XLA Ops:
  0.6 22.3 %copy-start.4 = (bf16[4,640,64]{1,2,0:T(8,128)(2,1)S(1)}, bf16[4,640,64]{1,2,0:T(8,128)(2,1)}, u32[]{:S(2)}) copy-start(bf16[4,640,64]{1,2,0:T(8,128)(2,1)} %param.16) | copy-start | bytes 983044
  0.6 40.8 %copy-start.3 = (bf16[32,320,64]{1,2,0:T(8,128)(2,1)S(1)}, bf16[32,320,64]{1,2,0:T(8,128)(2,1)}, u32[]{:S(2)}) copy-start(bf16[32,320,64]{1,2,0:T(8,128)(2,1)} %param.18) | copy-start | bytes 3932164
  3.9 37.5 %copy-start.2 = (bf16[32,64,320]{2,1,0:T(8,128)(2,1)S(1)}, bf16[32,64,320]{2,1,0:T(8,128)(2,1)}, u32[]{:S(2)}) copy-start(bf16[32,64,320]{2,1,0:T(8,128)(2,1)} %in_right.1) | copy-start | bytes 3932164
  3.9 37.5 %copy-start.5 = (bf16[1280,320]{0,1:T(8,128)(2,1)S(1)}, bf16[1280,320]{0,1:T(8,128)(2,1)}, u32[]{:S(2)}) copy-start(bf16[1280,320]{0,1:T(8,128)(2,1)} %param.14) | copy-start | bytes 2457604
  22.9 1.0 %copy-start.8 = (bf16[4,64,640]{2,1,0:T(8,128)(2,1)S(1)}, bf16[4,64,640]{2,1,0:T(8,128)(2,1)}, u32[]{:S(2)}) copy-start(bf16[4,64,640]{2,1,0:T(8,128)(2,1)} %out_right.1) | copy-start | bytes 983044
  41.4 1.1 %copy-start.6 = (bf16[320,1280]{1,0:T(8,128)(2,1)S(1)}, bf16[320,1280]{1,0:T(8,128)(2,1)}, u32[]{:S(2)}) copy-start(bf16[320,1280]{1,0:T(8,128)(2,1)} %base_out.1) | copy-start | bytes 2457604
  42.6 22.0 %copy-start.9 = (bf16[1,64,1280]{2,1,0:T(8,128)(2,1)S(1)}, bf16[1,64,1280]{2,1,0:T(8,128)(2,1)}, u32[]{:S(2)}) copy-start(bf16[1,64,1280]{2,1,0:T(8,128)(2,1)} %param.13) | copy-start | bytes 491524
  42.6 22.0 %copy-start.11 = (f32[64,256]{1,0:T(8,128)S(1)}, f32[64,256]{1,0:T(8,128)}, u32[]{:S(2)}) copy-start(f32[64,256]{1,0:T(8,128)} %get-tuple-element.32.combine) | copy-start | bytes 196612
  45.0 19.6 %copy-start.1 = (bf16[1,256,1280]{2,1,0:T(8,128)(2,1)S(1)}, bf16[1,256,1280]{2,1,0:T(8,128)(2,1)}, u32[]{:S(2)}) copy-start(bf16[1,256,1280]{2,1,0:T(8,128)(2,1)} %param.11) | copy-start | bytes 1966084
  45.0 29.0 %copy-start = (bf16[1,256,1280]{2,1,0:T(8,128)(2,1)S(1)}, bf16[1,256,1280]{2,1,0:T(8,128)(2,1)}, u32[]{:S(2)}) copy-start(bf16[1,256,1280]{2,1,0:T(8,128)(2,1)} %param.10) | copy-start | bytes 1966084
  45.0 29.0 %copy-start.7 = (bf16[1280,64]{0,1:T(8,128)(2,1)S(1)}, bf16[1280,64]{0,1:T(8,128)(2,1)}, u32[]{:S(2)}) copy-start(bf16[1280,64]{0,1:T(8,128)(2,1)} %param.12) | copy-start | bytes 491524
  45.0 29.0 %copy-start.10 = (f32[64,256]{1,0:T(8,128)S(1)}, f32[64,256]{1,0:T(8,128)}, u32[]{:S(2)}) copy-start(f32[64,256]{1,0:T(8,128)} %get-tuple-element.31.logits) | copy-start | bytes 196612
  60.0 13.9 %all-to-all-start.3 = ((bf16[32,4,768]{2,1,0:T(4,128)(2,1)}), bf16[32,4,768]{2,1,0:T(4,128)(2,1)S(1)}, u32[]{:S(2)}, u32[]{:S(2)}) async-start(bf16[32,4,768]{2,1,0:T(4,128)(2,1)} %get-tuple-element.30), calls=%async_computation.3 | async-start | bytes 393216 | tf_op jit(solution)/shard_map/all_to_all | solution.py:588

commit v12 on v11

--- a/solution.py
+++ b/solution.py
@@ -11,6 +11,7 @@
 BOTH = ("dp", *SEQ)
 HALF = ("dp", "place")
 STATS = 128
+FLOPS_BESIDE_EXCHANGE = 10**10
 
 
 def gelu_backward(preact, upstream):
@@ -465,7 +466,7 @@
     places = lax.axis_size("place")
     blocks = lax.all_gather(block, "half", axis=0)
     (blocks,) = call(
-        pack_kernel, [array(block.dtype, groups, places, *block.shape)], [blocks], 0
+        pack_kernel, [array(block.dtype, groups, places, *block.shape)], [blocks], FLOPS_BESIDE_EXCHANGE
     )
     blocks = blocks.reshape(groups * places, *block.shape)
     return lax.all_to_all(blocks, HALF, 0, 0, tiled=True)
@@ -534,7 +535,7 @@
             array(full, slots, count),
         ],
         [image_rows, cot_rows, router],
-        6 * count * slots * width,
+        6 * count * slots * width + FLOPS_BESIDE_EXCHANGE,
         (0, 1, 2),
         [pltpu.VMEM((count, width), low)] * 2
         + [pltpu.VMEM((slots, width), low), pltpu.SemaphoreType.DMA((3,))],

time: 76.2 us -> 74.3 us (0.975)
  local copies, waits for them, and re-layouts: 2.16 us -> 0.05 us
    unnamed x24, local copies, waits for them, and re-layouts: 2.16 us -> 0.05 us
where the time goes in v12:
time: 74.3 us; the launch traced here: 73.9 us
  blocking collectives  50.1 us (67%)
  Pallas kernels  13.1 us (18%)
  waiting for transfers between devices  5.34 us (7%)
  starting transfers between devices  4.5 us (6%)
  between operations  0.76 us (1%)
    all_to_all x1, blocking collectives, local(): first = lax.all_to_all(first, BOTH, 0, 0, tiled=True)  19 us
    pallas_call x10, Pallas kernels, call(): pl.pallas_call(kernel, out_shape=outs, in_specs=[pl.BlockSpec(memory_spac...  13.1 us
    all_to_all x1, blocking collectives, to_group(): return lax.all_to_all(blocks, HALF, 0, 0, tiled=True)  12.7 us
    all_to_all x1, blocking collectives, local(): third = lax.all_to_all(third, HALF, 0, 0, tiled=True)  9.76 us
    all_to_all x1, waiting for transfers between devices, local(): fourth = lax.all_to_all(fourth, BOTH, 0, 0, tiled=True)  5.34 us
    all_to_all x1, starting transfers between devices, local(): fourth = lax.all_to_all(fourth, BOTH, 0, 0, tiled=True)  4.5 us
    all_gather x1, blocking collectives, to_group(): blocks = lax.all_gather(block, 'half', axis=0)  4.33 us
    all_gather x1, blocking collectives, local(): others = lax.all_gather(other, 'half', axis=0)  4.25 us
  transfers between devices with their start and end apart: 1, of which 1 were waited for; matrix products, arithmetic and copies ran while one was open for 0% of the time, Pallas kernels for 5%

profile of v12, /device:TPU:1, one launch (start us, length us, event | category | flops | bytes accessed | tf_op | source)
XLA Modules:
  0.0 73.9 jit_solution(12060916426491580899)
XLA Ops:
  0.6 0.0 copy-start.2
  0.6 0.0 copy-start.7
  0.7 3.1 %shard_map.137 = (bf16[32,4,1408]{2,1,0:T(4,128)(2,1)}, f32[64,256]{1,0:T(8,128)}, f32[64,256]{1,0:T(8,128)}) custom-call(bf16[256,1280]{1,0:T(8,128)(2,1)} %bitcast.17, bf16[256,1280]{1,0:T(8,128)(2,1)} %bitcast.19, bf16[64,1280]{1,0:T(8,128)(2,1)} %bitcast.23), custom_call_target="tpu_custom_call" | custom-call | flops 10125829120 | bytes 1966080 | tf_op jit(solution)/shard_map/pallas_call | solution.py:479
  3.8 19.0 %all_to_all.20.first = bf16[32,4,1408]{2,1,0:T(4,128)(2,1)S(1)} all-to-all(bf16[32,4,1408]{2,1,0:T(4,128)(2,1)} %get-tuple-element.23), channel_id=1, replica_groups=mesh['dp'=2,'half'=2,'place'=8] {'dp','half','place'}, dimensions={0} | all-to-all | bytes 720896 | tf_op jit(solution)/shard_map/all_to_all | solution.py:544
  22.8 0.0 copy-done.2
  22.8 0.0 copy-done.7
  22.8 0.7 shard_map.138
  23.5 4.3 %all-gather = bf16[16,1536]{1,0:T(8,128)(2,1)S(1)} all-gather(bf16[8,1536]{1,0:T(8,128)(2,1)S(1)} %get-tuple-element.24), channel_id=2, replica_groups=mesh['dp'=2,'half'=2,'place'=8] {'half'}, dimensions={0}, use_global_device_ids=true | all-gather | bytes 73728 | tf_op jit(solution)/shard_map/all_gather | solution.py:467
  27.8 0.0 copy-start
  27.8 0.0 copy-start.1
  27.8 0.0 copy-start.3
  27.8 0.0 copy-start.4
  27.9 12.7 %all_to_all.21.second = bf16[16,8,1536]{2,1,0:T(8,128)(2,1)S(1)} all-to-all(bf16[16,8,1536]{2,1,0:T(8,128)(2,1)S(1)} %bitcast.21), channel_id=1, replica_groups=mesh['dp'=2,'half'=2,'place'=8] {'dp','place'}, dimensions={0} | all-to-all | bytes 786432 | tf_op jit(solution)/shard_map/all_to_all | solution.py:472
  40.6 0.0 copy-done
  40.6 0.0 copy-done.1
  40.6 0.0 copy-done.3
  40.6 0.0 copy-done.4
  40.6 0.0 copy-start.9
  40.6 0.0 copy-start.11
  40.7 2.4 %shard_map.140 = (bf16[16,8,768]{2,1,0:T(8,128)(2,1)S(1)}, f32[2,64,320]{2,1,0:T(8,128)S(1)}, f32[2,64,64]{2,1,0:T(8,128)S(1)}) custom-call(bf16[16,8,1536]{2,1,0:T(8,128)(2,1)S(1)} %all_to_all.21.second, bf16[320,1280]{1,0:T(8,128)(2,1)S(1)} %bitcast.16, bf16[320,1280]{1,0:T(8,128)(2,1)S(1)} %copy-done.4, bf16[32,64,320]{2,1,0:T(8,128)(2,1)S(1)} %copy-done, ...), custom_call_target="tpu_custom_call" | custom-call | flops 188743680 | bytes 5046272 | tf_op jit(solution)/shard_map/pallas_call | solution.py:479
  43.1 0.0 copy-start.6
  43.1 0.0 copy-start.5
  43.1 0.0 copy-start.8
  43.1 0.0 copy-start.10
  43.1 9.8 %all_to_all.22.third = bf16[16,8,768]{2,1,0:T(8,128)(2,1)S(1)} all-to-all(bf16[16,8,768]{2,1,0:T(8,128)(2,1)S(1)} %get-tuple-element.25), channel_id=1, replica_groups=mesh['dp'=2,'half'=2,'place'=8] {'dp','place'}, dimensions={0} | all-to-all | bytes 393216 | tf_op jit(solution)/shard_map/all_to_all | solution.py:568
  52.9 4.3 %all-gather.1 = f32[16,768]{1,0:T(8,128)S(1)} all-gather(f32[8,768]{1,0:T(8,128)S(1)} %get-tuple-element.27), channel_id=3, replica_groups=mesh['dp'=2,'half'=2,'place'=8] {'half'}, dimensions={0}, use_global_device_ids=true | all-gather | bytes 73728 | tf_op jit(solution)/shard_map/all_gather | solution.py:576
  57.2 1.0 %shard_map.142 = (bf16[32,4,768]{2,1,0:T(4,128)(2,1)}, f32[2,8,64]{2,1,0:T(8,128)S(1)}) custom-call(f32[8,768]{1,0:T(8,128)S(1)} %get-tuple-element.26.own, f32[2,8,768]{2,1,0:T(8,128)S(1)} %bitcast.22, bf16[4,64,640]{2,1,0:T(8,128)(2,1)S(1)} %bitcast.15, f32[8,640]{1,0:T(8,128)S(1)} %get-tuple-element.28.inputs, f32[8,128]{1,0:T(8,128)S(1)} %get-tuple-element.29.stats), custom_call_target="tpu_custom_call" | custom-call | flops 2621440 | bytes 626688 | tf_op jit(solution)/shard_map/pallas_call | solution.py:479
  58.1 4.5 %all-to-all-start.3 = ((bf16[32,4,768]{2,1,0:T(4,128)(2,1)}), bf16[32,4,768]{2,1,0:T(4,128)(2,1)S(1)}, u32[]{:S(2)}, u32[]{:S(2)}) async-start(bf16[32,4,768]{2,1,0:T(4,128)(2,1)} %get-tuple-element.30), calls=%async_computation.3 | async-start | bytes 393216 | tf_op jit(solution)/shard_map/all_to_all | solution.py:589
  62.6 0.0 copy-done.9
  62.7 0.0 copy-done.11
  62.7 0.0 copy-done.6
  62.7 0.4 shard_map.143.mixing
  63.0 2.5 %shard_map.146 = (bf16[32,64,320]{2,1,0:T(8,128)(2,1)}, bf16[32,64,320]{2,1,0:T(8,128)(2,1)}) custom-call(f32[2,64,64]{2,1,0:T(8,128)S(1)} %get-tuple-element.36.left_rows, f32[2,64,320]{2,1,0:T(8,128)S(1)} %get-tuple-element.37.right_rows), custom_call_target="tpu_custom_call" | custom-call | flops 20971520 | bytes 2818048 | tf_op jit(solution)/shard_map/pallas_call | solution.py:479
  65.6 1.2 %shard_map.145 = (bf16[4,64,640]{2,1,0:T(8,128)(2,1)}, bf16[4,64,640]{2,1,0:T(8,128)(2,1)}) custom-call(f32[2,8,64]{2,1,0:T(8,128)S(1)} %get-tuple-element.33.left_rows, bf16[2,8,640]{2,1,0:T(8,128)(2,1)S(1)} %get-tuple-element.34.right_rows), custom_call_target="tpu_custom_call" | custom-call | flops 5242880 | bytes 679936 | tf_op jit(solution)/shard_map/pallas_call | solution.py:479
  66.7 5.3 %all-to-all-done.3.fourth = bf16[32,4,768]{2,1,0:T(4,128)(2,1)S(1)} async-done(((bf16[32,4,768]{2,1,0:T(4,128)(2,1)}), bf16[32,4,768]{2,1,0:T(4,128)(2,1)S(1)}, u32[]{:S(2)}, u32[]{:S(2)}) %all-to-all-start.3) | async-done | bytes 196640 | tf_op jit(solution)/shard_map/all_to_all | solution.py:589
  72.1 0.0 copy-done.5
  72.1 0.0 copy-done.8
  72.1 0.0 copy-done.10
  72.1 1.8 %shard_map.144 = bf16[256,1280]{1,0:T(8,128)(2,1)} custom-call(bf16[32,4,768]{2,1,0:T(4,128)(2,1)S(1)} %all-to-all-done.3.fourth, bf16[256,1280]{1,0:T(8,128)(2,1)S(1)} %bitcast.18, bf16[64,1280]{1,0:T(8,128)(2,1)S(1)} %bitcast.24, f32[64,256]{1,0:T(8,128)S(1)} %copy-done.10, f32[64,256]{1,0:T(8,128)S(1)} %shard_map.143.mixing), custom_call_target="tpu_custom_call" | custom-call | flops 125829120 | bytes 1802240 | tf_op jit(solution)/shard_map/pallas_call | solution.py:479
  (2 shorter events, 0.1 us)
Async XLA Ops:
  0.6 22.2 %copy-start.2 = (bf16[4,640,64]{1,2,0:T(8,128)(2,1)S(1)}, bf16[4,640,64]{1,2,0:T(8,128)(2,1)}, u32[]{:S(2)}) copy-start(bf16[4,640,64]{1,2,0:T(8,128)(2,1)} %param.16) | copy-start | bytes 983044
  0.6 22.2 %copy-start.7 = (bf16[4,64,640]{2,1,0:T(8,128)(2,1)S(1)}, bf16[4,64,640]{2,1,0:T(8,128)(2,1)}, u32[]{:S(2)}) copy-start(bf16[4,64,640]{2,1,0:T(8,128)(2,1)} %out_right.1) | copy-start | bytes 983044
  27.8 12.8 %copy-start = (bf16[32,64,320]{2,1,0:T(8,128)(2,1)S(1)}, bf16[32,64,320]{2,1,0:T(8,128)(2,1)}, u32[]{:S(2)}) copy-start(bf16[32,64,320]{2,1,0:T(8,128)(2,1)} %in_right.1) | copy-start | bytes 3932164
  27.8 12.8 %copy-start.1 = (bf16[32,320,64]{1,2,0:T(8,128)(2,1)S(1)}, bf16[32,320,64]{1,2,0:T(8,128)(2,1)}, u32[]{:S(2)}) copy-start(bf16[32,320,64]{1,2,0:T(8,128)(2,1)} %param.18) | copy-start | bytes 3932164
  27.8 12.8 %copy-start.3 = (bf16[1280,320]{0,1:T(8,128)(2,1)S(1)}, bf16[1280,320]{0,1:T(8,128)(2,1)}, u32[]{:S(2)}) copy-start(bf16[1280,320]{0,1:T(8,128)(2,1)} %param.14) | copy-start | bytes 2457604
  27.8 12.8 %copy-start.4 = (bf16[320,1280]{1,0:T(8,128)(2,1)S(1)}, bf16[320,1280]{1,0:T(8,128)(2,1)}, u32[]{:S(2)}) copy-start(bf16[320,1280]{1,0:T(8,128)(2,1)} %base_out.1) | copy-start | bytes 2457604
  40.6 22.0 %copy-start.9 = (bf16[1,64,1280]{2,1,0:T(8,128)(2,1)S(1)}, bf16[1,64,1280]{2,1,0:T(8,128)(2,1)}, u32[]{:S(2)}) copy-start(bf16[1,64,1280]{2,1,0:T(8,128)(2,1)} %param.13) | copy-start | bytes 491524
  40.6 22.0 %copy-start.11 = (f32[64,256]{1,0:T(8,128)S(1)}, f32[64,256]{1,0:T(8,128)}, u32[]{:S(2)}) copy-start(f32[64,256]{1,0:T(8,128)} %get-tuple-element.32.combine) | copy-start | bytes 196612
  43.1 19.6 %copy-start.6 = (bf16[1,256,1280]{2,1,0:T(8,128)(2,1)S(1)}, bf16[1,256,1280]{2,1,0:T(8,128)(2,1)}, u32[]{:S(2)}) copy-start(bf16[1,256,1280]{2,1,0:T(8,128)(2,1)} %param.11) | copy-start | bytes 1966084
  43.1 29.0 %copy-start.5 = (bf16[1,256,1280]{2,1,0:T(8,128)(2,1)S(1)}, bf16[1,256,1280]{2,1,0:T(8,128)(2,1)}, u32[]{:S(2)}) copy-start(bf16[1,256,1280]{2,1,0:T(8,128)(2,1)} %param.10) | copy-start | bytes 1966084
  43.1 29.0 %copy-start.8 = (bf16[1280,64]{0,1:T(8,128)(2,1)S(1)}, bf16[1280,64]{0,1:T(8,128)(2,1)}, u32[]{:S(2)}) copy-start(bf16[1280,64]{0,1:T(8,128)(2,1)} %param.12) | copy-start | bytes 491524
  43.1 29.0 %copy-start.10 = (f32[64,256]{1,0:T(8,128)S(1)}, f32[64,256]{1,0:T(8,128)}, u32[]{:S(2)}) copy-start(f32[64,256]{1,0:T(8,128)} %get-tuple-element.31.logits) | copy-start | bytes 196612
  58.1 13.9 %all-to-all-start.3 = ((bf16[32,4,768]{2,1,0:T(4,128)(2,1)}), bf16[32,4,768]{2,1,0:T(4,128)(2,1)S(1)}, u32[]{:S(2)}, u32[]{:S(2)}) async-start(bf16[32,4,768]{2,1,0:T(4,128)(2,1)} %get-tuple-element.30), calls=%async_computation.3 | async-start | bytes 393216 | tf_op jit(solution)/shard_map/all_to_all | solution.py:589

commit v13 on v12

--- a/solution.py
+++ b/solution.py
@@ -229,31 +229,12 @@
     return out
 
 
-def sums_kernel(
-    owned,
-    groups,
-    tokens_far,
-    cotangent_far,
-    router_far,
-    first,
-    logits_out,
-    combine_out,
-    tokens,
-    cotangent,
-    router,
-    arrived,
-):
+def early_kernel(out):
+    out[...] = jnp.zeros(out.shape, out.dtype)
+
+
+def sums_kernel(owned, groups, _, tokens, cotangent, router, first, logits_out, combine_out):
     ring = first.shape[0] // groups
-    copies = [
-        pltpu.make_async_copy(far, near, arrived.at[number])
-        for number, (far, near) in enumerate(
-            [(router_far, router), (tokens_far, tokens), (cotangent_far, cotangent)]
-        )
-    ]
-    for copy in copies:
-        copy.start()
-    copies[0].wait()
-    copies[1].wait()
     image_rows = tokens[...]
     logits = dot_last(router[...], image_rows)
     high, low = halves(jnp.max(logits, axis=1, keepdims=True))
@@ -266,7 +247,6 @@
     stats = in_lanes([high, low, total_high, total_low], (logits.shape[0], STATS))
     stats = stats.astype(jnp.bfloat16)
     inputs = dot_plain(near.astype(jnp.bfloat16), image_rows).astype(jnp.bfloat16)
-    copies[2].wait()
     grads = dot_plain(combine.astype(jnp.bfloat16), cotangent[...]).astype(jnp.bfloat16)
     width = inputs.shape[1] // groups
     for group in range(groups):
@@ -472,18 +452,16 @@
     return lax.all_to_all(blocks, HALF, 0, 0, tiled=True)
 
 
-def call(kernel, outs, args, flops, far=(), scratch=(), grant=24):
+def call(kernel, outs, args, flops):
     size = sum(array.size * array.dtype.itemsize for array in args)
     size += sum(out.size * out.dtype.itemsize for out in outs)
-    spaces = [pltpu.HBM if number in far else pltpu.VMEM for number in range(len(args))]
     return pl.pallas_call(
         kernel,
         out_shape=outs,
-        in_specs=[pl.BlockSpec(memory_space=space) for space in spaces],
+        in_specs=[pl.BlockSpec(memory_space=pltpu.VMEM) for _ in args],
         out_specs=[pl.BlockSpec(memory_space=pltpu.VMEM) for _ in outs],
-        scratch_shapes=scratch,
         cost_estimate=pl.CostEstimate(flops=flops, bytes_accessed=size, transcendentals=0),
-        compiler_params=pltpu.CompilerParams(vmem_limit_bytes=grant * 2**20),
+        compiler_params=pltpu.CompilerParams(vmem_limit_bytes=24 * 2**20),
     )(*args)
 
 
@@ -527,6 +505,7 @@
     image_rows, cot_rows, saved = tokens[0], cotangent[0], slot_outputs[0]
     router, base_in = router.T, base_in.T
     in_left, out_left = in_left.swapaxes(1, 2), out_left.swapaxes(1, 2)
+    (early,) = call(early_kernel, [array(full, 8, 128)], [], FLOPS_BESIDE_EXCHANGE)
     first, logits, combine = call(
         functools.partial(sums_kernel, owned, groups),
         [
@@ -534,12 +513,8 @@
             array(full, slots, count),
             array(full, slots, count),
         ],
-        [image_rows, cot_rows, router],
+        [early, image_rows, cot_rows, router],
         6 * count * slots * width + FLOPS_BESIDE_EXCHANGE,
-        (0, 1, 2),
-        [pltpu.VMEM((count, width), low)] * 2
-        + [pltpu.VMEM((slots, width), low), pltpu.SemaphoreType.DMA((3,))],
-        60,
     )
     first = lax.all_to_all(first, BOTH, 0, 0, tiled=True)
     second, inputs, lows, stats = call(

time: 74.3 us -> 73.2 us (0.985)
  Pallas kernels: 13.1 us -> 11 us
  local copies, waits for them, and re-layouts: 0.05 us -> 1.37 us
    pallas_call x10 -> x11, Pallas kernels: 13.1 us -> 11 us  [call(): pl.pallas_call(kernel, out_shape=outs, in_specs=[pl.BlockSpec(memory_spac...]
    unnamed x24 -> x20, local copies, waits for them, and re-layouts: 0.05 us -> 1.37 us
  transfers between devices with their start and end apart: 1 -> 1, of which waited for: 1 -> 1; matrix products, arithmetic and copies ran while one was open for 0% -> 0% of each run, Pallas kernels for 5% -> 6%
where the time goes in v13:
time: 73.2 us; the launch traced here: 72.9 us
  blocking collectives  49.9 us (68%)
  Pallas kernels  11 us (15%)
  waiting for transfers between devices  5.36 us (7%)
  starting transfers between devices  4.5 us (6%)
  local copies, waits for them, and re-layouts  1.37 us (2%)
    all_to_all x1, blocking collectives, local(): first = lax.all_to_all(first, BOTH, 0, 0, tiled=True)  18.8 us
    all_to_all x1, blocking collectives, to_group(): return lax.all_to_all(blocks, HALF, 0, 0, tiled=True)  12.7 us
    pallas_call x11, Pallas kernels, call(): pl.pallas_call(kernel, out_shape=outs, in_specs=[pl.BlockSpec(memory_spac...  11 us
    all_to_all x1, blocking collectives, local(): third = lax.all_to_all(third, HALF, 0, 0, tiled=True)  9.76 us
    all_to_all x1, waiting for transfers between devices, local(): fourth = lax.all_to_all(fourth, BOTH, 0, 0, tiled=True)  5.36 us
    all_to_all x1, starting transfers between devices, local(): fourth = lax.all_to_all(fourth, BOTH, 0, 0, tiled=True)  4.5 us
    all_gather x1, blocking collectives, to_group(): blocks = lax.all_gather(block, 'half', axis=0)  4.33 us
    all_gather x1, blocking collectives, local(): others = lax.all_gather(other, 'half', axis=0)  4.25 us
  transfers between devices with their start and end apart: 1, of which 1 were waited for; matrix products, arithmetic and copies ran while one was open for 0% of the time, Pallas kernels for 6%

profile of v13, /device:TPU:1, one launch (start us, length us, event | category | flops | bytes accessed | tf_op | source)
XLA Modules:
  0.0 72.9 jit_solution(11672145039474689373)
XLA Ops:
  0.6 0.0 copy-start.8
  0.6 0.0 copy-start.6
  0.7 0.0 copy-start.5
  0.7 0.9 %copy-done.8 = bf16[1280,64]{0,1:T(8,128)(2,1)S(1)} copy-done((bf16[1280,64]{0,1:T(8,128)(2,1)S(1)}, bf16[1280,64]{0,1:T(8,128)(2,1)}, u32[]{:S(2)}) %copy-start.8) | copy-done | bytes 163864
  1.5 0.3 copy-done.6
  1.8 0.2 copy-done.5
  2.0 0.0 copy-start.2
  2.0 0.0 copy-start.7
  2.0 1.0 %shard_map.138 = (bf16[32,4,1408]{2,1,0:T(4,128)(2,1)S(1)}, f32[64,256]{1,0:T(8,128)S(1)}, f32[64,256]{1,0:T(8,128)S(1)}) custom-call(f32[8,128]{1,0:T(8,128)S(1)} %shard_map.137._, bf16[256,1280]{1,0:T(8,128)(2,1)S(1)} %bitcast.17, bf16[256,1280]{1,0:T(8,128)(2,1)S(1)} %bitcast.19, bf16[64,1280]{1,0:T(8,128)(2,1)S(1)} %bitcast.23), custom_call_target="tpu_custom_call" | custom-call | flops 10125829120 | bytes 1970176 | tf_op jit(solution)/shard_map/pallas_call | solution.py:458
  3.0 18.8 %all_to_all.20.first = bf16[32,4,1408]{2,1,0:T(4,128)(2,1)S(1)} all-to-all(bf16[32,4,1408]{2,1,0:T(4,128)(2,1)S(1)} %get-tuple-element.23), channel_id=1, replica_groups=mesh['dp'=2,'half'=2,'place'=8] {'dp','half','place'}, dimensions={0} | all-to-all | bytes 720896 | tf_op jit(solution)/shard_map/all_to_all | solution.py:519
  21.9 0.0 copy-done.2
  21.9 0.0 copy-done.7
  21.9 0.7 shard_map.139
  22.5 4.3 %all-gather = bf16[16,1536]{1,0:T(8,128)(2,1)S(1)} all-gather(bf16[8,1536]{1,0:T(8,128)(2,1)S(1)} %get-tuple-element.24), channel_id=2, replica_groups=mesh['dp'=2,'half'=2,'place'=8] {'half'}, dimensions={0}, use_global_device_ids=true | all-gather | bytes 73728 | tf_op jit(solution)/shard_map/all_gather | solution.py:447
  26.9 0.0 copy-start
  26.9 0.0 copy-start.1
  26.9 0.0 copy-start.3
  26.9 0.0 copy-start.4
  26.9 12.7 %all_to_all.21.second = bf16[16,8,1536]{2,1,0:T(8,128)(2,1)S(1)} all-to-all(bf16[16,8,1536]{2,1,0:T(8,128)(2,1)S(1)} %bitcast.21), channel_id=1, replica_groups=mesh['dp'=2,'half'=2,'place'=8] {'dp','place'}, dimensions={0} | all-to-all | bytes 786432 | tf_op jit(solution)/shard_map/all_to_all | solution.py:452
  39.6 0.0 copy-done
  39.6 0.0 copy-done.1
  39.6 0.0 copy-done.3
  39.7 0.0 copy-done.4
  39.7 2.4 %shard_map.141 = (bf16[16,8,768]{2,1,0:T(8,128)(2,1)S(1)}, f32[2,64,320]{2,1,0:T(8,128)S(1)}, f32[2,64,64]{2,1,0:T(8,128)S(1)}) custom-call(bf16[16,8,1536]{2,1,0:T(8,128)(2,1)S(1)} %all_to_all.21.second, bf16[320,1280]{1,0:T(8,128)(2,1)S(1)} %bitcast.16, bf16[320,1280]{1,0:T(8,128)(2,1)S(1)} %copy-done.4, bf16[32,64,320]{2,1,0:T(8,128)(2,1)S(1)} %copy-done, ...), custom_call_target="tpu_custom_call" | custom-call | flops 188743680 | bytes 5046272 | tf_op jit(solution)/shard_map/pallas_call | solution.py:458
  42.1 0.0 copy-start.9
  42.1 9.8 %all_to_all.22.third = bf16[16,8,768]{2,1,0:T(8,128)(2,1)S(1)} all-to-all(bf16[16,8,768]{2,1,0:T(8,128)(2,1)S(1)} %get-tuple-element.25), channel_id=1, replica_groups=mesh['dp'=2,'half'=2,'place'=8] {'dp','place'}, dimensions={0} | all-to-all | bytes 393216 | tf_op jit(solution)/shard_map/all_to_all | solution.py:543
  51.9 4.3 %all-gather.1 = f32[16,768]{1,0:T(8,128)S(1)} all-gather(f32[8,768]{1,0:T(8,128)S(1)} %get-tuple-element.27), channel_id=3, replica_groups=mesh['dp'=2,'half'=2,'place'=8] {'half'}, dimensions={0}, use_global_device_ids=true | all-gather | bytes 73728 | tf_op jit(solution)/shard_map/all_gather | solution.py:551
  56.1 1.0 %shard_map.143 = (bf16[32,4,768]{2,1,0:T(4,128)(2,1)}, f32[2,8,64]{2,1,0:T(8,128)S(1)}) custom-call(f32[8,768]{1,0:T(8,128)S(1)} %get-tuple-element.26.own, f32[2,8,768]{2,1,0:T(8,128)S(1)} %bitcast.22, bf16[4,64,640]{2,1,0:T(8,128)(2,1)S(1)} %bitcast.15, f32[8,640]{1,0:T(8,128)S(1)} %get-tuple-element.28.inputs, f32[8,128]{1,0:T(8,128)S(1)} %get-tuple-element.29.stats), custom_call_target="tpu_custom_call" | custom-call | flops 2621440 | bytes 626688 | tf_op jit(solution)/shard_map/pallas_call | solution.py:458
  57.1 4.5 %all-to-all-start.3 = ((bf16[32,4,768]{2,1,0:T(4,128)(2,1)}), bf16[32,4,768]{2,1,0:T(4,128)(2,1)S(1)}, u32[]{:S(2)}, u32[]{:S(2)}) async-start(bf16[32,4,768]{2,1,0:T(4,128)(2,1)} %get-tuple-element.30), calls=%async_computation.3 | async-start | bytes 393216 | tf_op jit(solution)/shard_map/all_to_all | solution.py:564
  61.6 0.0 copy-done.9
  61.6 0.4 shard_map.144.mixing
  62.0 2.5 %shard_map.147 = (bf16[32,64,320]{2,1,0:T(8,128)(2,1)}, bf16[32,64,320]{2,1,0:T(8,128)(2,1)}) custom-call(f32[2,64,64]{2,1,0:T(8,128)S(1)} %get-tuple-element.36.left_rows, f32[2,64,320]{2,1,0:T(8,128)S(1)} %get-tuple-element.37.right_rows), custom_call_target="tpu_custom_call" | custom-call | flops 20971520 | bytes 2818048 | tf_op jit(solution)/shard_map/pallas_call | solution.py:458
  64.5 1.2 %shard_map.146 = (bf16[4,64,640]{2,1,0:T(8,128)(2,1)}, bf16[4,64,640]{2,1,0:T(8,128)(2,1)}) custom-call(f32[2,8,64]{2,1,0:T(8,128)S(1)} %get-tuple-element.33.left_rows, bf16[2,8,640]{2,1,0:T(8,128)(2,1)S(1)} %get-tuple-element.34.right_rows), custom_call_target="tpu_custom_call" | custom-call | flops 5242880 | bytes 679936 | tf_op jit(solution)/shard_map/pallas_call | solution.py:458
  65.7 5.4 %all-to-all-done.3.fourth = bf16[32,4,768]{2,1,0:T(4,128)(2,1)S(1)} async-done(((bf16[32,4,768]{2,1,0:T(4,128)(2,1)}), bf16[32,4,768]{2,1,0:T(4,128)(2,1)S(1)}, u32[]{:S(2)}, u32[]{:S(2)}) %all-to-all-start.3) | async-done | bytes 196640 | tf_op jit(solution)/shard_map/all_to_all | solution.py:564
  71.1 1.8 %shard_map.145 = bf16[256,1280]{1,0:T(8,128)(2,1)} custom-call(bf16[32,4,768]{2,1,0:T(4,128)(2,1)S(1)} %all-to-all-done.3.fourth, bf16[256,1280]{1,0:T(8,128)(2,1)S(1)} %bitcast.18, bf16[64,1280]{1,0:T(8,128)(2,1)S(1)} %bitcast.24, f32[64,256]{1,0:T(8,128)S(1)} %get-tuple-element.31.logits, f32[64,256]{1,0:T(8,128)S(1)} %shard_map.144.mixing), custom_call_target="tpu_custom_call" | custom-call | flops 125829120 | bytes 1802240 | tf_op jit(solution)/shard_map/pallas_call | solution.py:458
  (3 shorter events, 0.1 us)
Async XLA Ops:
  0.6 0.9 %copy-start.8 = (bf16[1280,64]{0,1:T(8,128)(2,1)S(1)}, bf16[1280,64]{0,1:T(8,128)(2,1)}, u32[]{:S(2)}) copy-start(bf16[1280,64]{0,1:T(8,128)(2,1)} %param.12) | copy-start | bytes 491524
  0.6 1.2 %copy-start.6 = (bf16[1,256,1280]{2,1,0:T(8,128)(2,1)S(1)}, bf16[1,256,1280]{2,1,0:T(8,128)(2,1)}, u32[]{:S(2)}) copy-start(bf16[1,256,1280]{2,1,0:T(8,128)(2,1)} %param.11) | copy-start | bytes 1966084
  0.7 1.4 %copy-start.5 = (bf16[1,256,1280]{2,1,0:T(8,128)(2,1)S(1)}, bf16[1,256,1280]{2,1,0:T(8,128)(2,1)}, u32[]{:S(2)}) copy-start(bf16[1,256,1280]{2,1,0:T(8,128)(2,1)} %param.10) | copy-start | bytes 1966084
  2.0 19.9 %copy-start.2 = (bf16[4,640,64]{1,2,0:T(8,128)(2,1)S(1)}, bf16[4,640,64]{1,2,0:T(8,128)(2,1)}, u32[]{:S(2)}) copy-start(bf16[4,640,64]{1,2,0:T(8,128)(2,1)} %param.16) | copy-start | bytes 983044
  2.0 19.9 %copy-start.7 = (bf16[4,64,640]{2,1,0:T(8,128)(2,1)S(1)}, bf16[4,64,640]{2,1,0:T(8,128)(2,1)}, u32[]{:S(2)}) copy-start(bf16[4,64,640]{2,1,0:T(8,128)(2,1)} %out_right.1) | copy-start | bytes 983044
  26.9 12.8 %copy-start = (bf16[32,64,320]{2,1,0:T(8,128)(2,1)S(1)}, bf16[32,64,320]{2,1,0:T(8,128)(2,1)}, u32[]{:S(2)}) copy-start(bf16[32,64,320]{2,1,0:T(8,128)(2,1)} %in_right.1) | copy-start | bytes 3932164
  26.9 12.8 %copy-start.1 = (bf16[32,320,64]{1,2,0:T(8,128)(2,1)S(1)}, bf16[32,320,64]{1,2,0:T(8,128)(2,1)}, u32[]{:S(2)}) copy-start(bf16[32,320,64]{1,2,0:T(8,128)(2,1)} %param.18) | copy-start | bytes 3932164
  26.9 12.8 %copy-start.3 = (bf16[1280,320]{0,1:T(8,128)(2,1)S(1)}, bf16[1280,320]{0,1:T(8,128)(2,1)}, u32[]{:S(2)}) copy-start(bf16[1280,320]{0,1:T(8,128)(2,1)} %param.14) | copy-start | bytes 2457604
  26.9 12.8 %copy-start.4 = (bf16[320,1280]{1,0:T(8,128)(2,1)S(1)}, bf16[320,1280]{1,0:T(8,128)(2,1)}, u32[]{:S(2)}) copy-start(bf16[320,1280]{1,0:T(8,128)(2,1)} %base_out.1) | copy-start | bytes 2457604
  42.1 19.5 %copy-start.9 = (bf16[1,64,1280]{2,1,0:T(8,128)(2,1)S(1)}, bf16[1,64,1280]{2,1,0:T(8,128)(2,1)}, u32[]{:S(2)}) copy-start(bf16[1,64,1280]{2,1,0:T(8,128)(2,1)} %param.13) | copy-start | bytes 491524
  57.1 13.9 %all-to-all-start.3 = ((bf16[32,4,768]{2,1,0:T(4,128)(2,1)}), bf16[32,4,768]{2,1,0:T(4,128)(2,1)S(1)}, u32[]{:S(2)}, u32[]{:S(2)}) async-start(bf16[32,4,768]{2,1,0:T(4,128)(2,1)} %get-tuple-element.30), calls=%async_computation.3 | async-start | bytes 393216 | tf_op jit(solution)/shard_map/all_to_all | solution.py:564

commit v14 on v13

--- a/solution.py
+++ b/solution.py
@@ -1,4 +1,5 @@
 import functools
+import math
 
 import jax
 import jax.numpy as jnp
@@ -289,7 +290,7 @@
     lows_out[1] = grads_low
     up = dot_last(inputs_low, in_left[...].reshape(owned * rank, width))
     back = dot_last(grads_low, out_right[...].reshape(owned * rank, width))
-    ranks = [*halves(from_own_block(up, owned)), *halves(from_own_block(back, owned))]
+    ranks = [from_own_block(up, owned), from_own_block(back, owned)]
     ranks = jnp.concatenate(ranks, axis=1).astype(jnp.bfloat16)
     block = jnp.concatenate([inputs_low, grads_low, ranks], axis=1)
     second[...] = block
@@ -342,9 +343,8 @@
             taken.append(from_own_block(wide, owned))
         return jnp.concatenate(taken, axis=0)
 
-    ranks = functools.reduce(jnp.add, gathered(slice(2 * width, 2 * width + 4 * rank)))
-    up = (ranks[:, :rank] + ranks[:, rank : 2 * rank]).astype(jnp.bfloat16)
-    back = (ranks[:, 2 * rank : 3 * rank] + ranks[:, 3 * rank :]).astype(jnp.bfloat16)
+    ranks = functools.reduce(jnp.add, gathered(slice(2 * width, 2 * width + 2 * rank)))
+    up, back = ranks[:, :rank].astype(jnp.bfloat16), ranks[:, rank:].astype(jnp.bfloat16)
     preact = low_rank(up, in_right)
     for half, part in enumerate(gathered(slice(0, width))):
         columns = slice(half * width, (half + 1) * width)
@@ -395,12 +395,12 @@
     here = lax.axis_index("half")
     for out, group in ((own, here), (other, 1 - here)):
         taken = third[pl.ds(group * places, places)].astype(jnp.float32)
-        out[...] = jnp.sum(taken, axis=0)
+        out[...] = jnp.sum(taken, axis=0).astype(out.dtype)
 
 
 def finish_kernel(groups, ring, own, others, in_left, inputs, stats, fourth, ranks_out):
     owned, rank, width = in_left.shape
-    summed = own[...] + others[1 - lax.axis_index("half")]
+    summed = own[...] + others[1 - lax.axis_index("half")].astype(jnp.float32)
     ranks = summed[:, width:].astype(jnp.bfloat16).astype(jnp.float32)
     ranks_out[0] = ranks[:, :rank]
     ranks_out[1] = ranks[:, rank:]
@@ -417,7 +417,7 @@
             fourth[group * ring + place] = rows
 
 
-def tokens_kernel(groups, fourth, tokens, router, logits, mixing, out):
+def tokens_kernel(groups, fourth, tokens, router, logits, mixing, out_far, out, sent):
     blocks, owned, _ = fourth.shape
     ring = blocks // groups
     width = tokens.shape[1] // groups
@@ -439,7 +439,17 @@
     logit_grad = dispatch * (weight_grad - shift) + mixing[...]
     left = jnp.concatenate([dispatch, logit_grad], axis=0).astype(jnp.bfloat16)
     right = jnp.concatenate([grads, router[...]], axis=0)
-    out[...] = dot_first(left, right).astype(jnp.bfloat16)
+    parts = sent.shape[0]
+    size = out.shape[0] // parts
+    copies = []
+    for part in range(parts):
+        rows = slice(part * size, (part + 1) * size)
+        out[rows] = dot_first(left[:, rows], right).astype(jnp.bfloat16)
+        copy = pltpu.make_async_copy(out.at[rows], out_far.at[rows], sent.at[part])
+        copy.start()
+        copies.append(copy)
+    for copy in copies:
+        copy.wait()
 
 
 def to_group(block, groups):
@@ -452,14 +462,15 @@
     return lax.all_to_all(blocks, HALF, 0, 0, tiled=True)
 
 
-def call(kernel, outs, args, flops):
+def call(kernel, outs, args, flops, space=pltpu.VMEM, scratch=()):
     size = sum(array.size * array.dtype.itemsize for array in args)
     size += sum(out.size * out.dtype.itemsize for out in outs)
     return pl.pallas_call(
         kernel,
         out_shape=outs,
         in_specs=[pl.BlockSpec(memory_space=pltpu.VMEM) for _ in args],
-        out_specs=[pl.BlockSpec(memory_space=pltpu.VMEM) for _ in outs],
+        out_specs=[pl.BlockSpec(memory_space=space) for _ in outs],
+        scratch_shapes=scratch,
         cost_estimate=pl.CostEstimate(flops=flops, bytes_accessed=size, transcendentals=0),
         compiler_params=pltpu.CompilerParams(vmem_limit_bytes=24 * 2**20),
     )(*args)
@@ -520,7 +531,7 @@
     second, inputs, lows, stats = call(
         functools.partial(owner_kernel, groups),
         [
-            array(low, rows, 2 * slice_width + 4 * rank),
+            array(low, rows, 2 * slice_width + 2 * rank),
             array(full, rows, slice_width),
             array(low, 2, rows, slice_width),
             array(full, rows, STATS),
@@ -547,7 +558,12 @@
         [ranks, pair],
         4 * members * rank * hidden * rows,
     )
-    own, other = call(halves_kernel, [array(full, rows, slice_width + 2 * rank)] * 2, [third], 0)
+    own, other = call(
+        halves_kernel,
+        [array(kind, rows, slice_width + 2 * rank) for kind in (full, low)],
+        [third],
+        0,
+    )
     others = lax.all_gather(other, "half", axis=0)
     fourth, ranks = call(
         functools.partial(finish_kernel, groups, ring),
@@ -568,11 +584,14 @@
         [ranks, lows],
         4 * owned * rank * slice_width * rows,
     )
+    parts = math.gcd(4, count // 16)
     (token_grad,) = call(
         functools.partial(tokens_kernel, groups),
         [array(low, count, width)],
         [fourth, image_rows, router, logits, mixing],
         6 * count * slots * width,
+        pltpu.HBM,
+        [pltpu.VMEM((count, width), low), pltpu.SemaphoreType.DMA((parts,))],
     )
     return (
         token_grad[None],

time: 73.2 us -> 72.3 us (0.988)
  no operation moved by 1% of the time
where the time goes in v14:
time: 72.3 us; the launch traced here: 72 us
  blocking collectives  49.3 us (68%)
  Pallas kernels  10.7 us (15%)
  waiting for transfers between devices  5.36 us (7%)
  starting transfers between devices  4.5 us (6%)
  local copies, waits for them, and re-layouts  1.37 us (2%)
  between operations  0.74 us (1%)
    all_to_all x1, blocking collectives, local(): first = lax.all_to_all(first, BOTH, 0, 0, tiled=True)  18.8 us
    all_to_all x1, blocking collectives, to_group(): return lax.all_to_all(blocks, HALF, 0, 0, tiled=True)  12.4 us
    pallas_call x11, Pallas kernels, call(): pl.pallas_call(kernel, out_shape=outs, in_specs=[pl.BlockSpec(memory_spac...  10.7 us
    all_to_all x1, blocking collectives, local(): third = lax.all_to_all(third, HALF, 0, 0, tiled=True)  9.62 us
    all_to_all x1, waiting for transfers between devices, local(): fourth = lax.all_to_all(fourth, BOTH, 0, 0, tiled=True)  5.36 us
    all_to_all x1, starting transfers between devices, local(): fourth = lax.all_to_all(fourth, BOTH, 0, 0, tiled=True)  4.5 us
    all_gather x1, blocking collectives, to_group(): blocks = lax.all_gather(block, 'half', axis=0)  4.28 us
    all_gather x1, blocking collectives, local(): others = lax.all_gather(other, 'half', axis=0)  4.15 us
  transfers between devices with their start and end apart: 1, of which 1 were waited for; matrix products, arithmetic and copies ran while one was open for 0% of the time, Pallas kernels for 6%

profile of v14, /device:TPU:1, one launch (start us, length us, event | category | flops | bytes accessed | tf_op | source)
XLA Modules:
  0.0 72.0 jit_solution(3879042156084881662)
XLA Ops:
  0.6 0.0 copy-start.8
  0.6 0.0 copy-start.6
  0.7 0.0 copy-start.5
  0.7 0.9 %copy-done.8 = bf16[1280,64]{0,1:T(8,128)(2,1)S(1)} copy-done((bf16[1280,64]{0,1:T(8,128)(2,1)S(1)}, bf16[1280,64]{0,1:T(8,128)(2,1)}, u32[]{:S(2)}) %copy-start.8) | copy-done | bytes 163864
  1.5 0.3 copy-done.6
  1.8 0.2 copy-done.5
  2.0 0.0 copy-start.2
  2.0 0.0 copy-start.7
  2.0 1.0 %shard_map.138 = (bf16[32,4,1408]{2,1,0:T(4,128)(2,1)S(1)}, f32[64,256]{1,0:T(8,128)S(1)}, f32[64,256]{1,0:T(8,128)S(1)}) custom-call(f32[8,128]{1,0:T(8,128)S(1)} %shard_map.137._, bf16[256,1280]{1,0:T(8,128)(2,1)S(1)} %bitcast.17, bf16[256,1280]{1,0:T(8,128)(2,1)S(1)} %bitcast.19, bf16[64,1280]{1,0:T(8,128)(2,1)S(1)} %bitcast.22), custom_call_target="tpu_custom_call" | custom-call | flops 10125829120 | bytes 1970176 | tf_op jit(solution)/shard_map/pallas_call | solution.py:468
  3.0 18.8 %all_to_all.20.first = bf16[32,4,1408]{2,1,0:T(4,128)(2,1)S(1)} all-to-all(bf16[32,4,1408]{2,1,0:T(4,128)(2,1)S(1)} %get-tuple-element.23), channel_id=1, replica_groups=mesh['dp'=2,'half'=2,'place'=8] {'dp','half','place'}, dimensions={0} | all-to-all | bytes 720896 | tf_op jit(solution)/shard_map/all_to_all | solution.py:530
  21.9 0.0 copy-done.2
  21.9 0.0 copy-done.7
  21.9 0.6 shard_map.139
  22.5 4.3 %all-gather = bf16[16,1408]{1,0:T(8,128)(2,1)S(1)} all-gather(bf16[8,1408]{1,0:T(8,128)(2,1)S(1)} %get-tuple-element.24), channel_id=2, replica_groups=mesh['dp'=2,'half'=2,'place'=8] {'half'}, dimensions={0}, use_global_device_ids=true | all-gather | bytes 67584 | tf_op jit(solution)/shard_map/all_gather | solution.py:457
  26.7 0.0 copy-start
  26.8 0.0 copy-start.1
  26.8 0.0 copy-start.3
  26.8 0.0 copy-start.4
  26.8 12.4 %all_to_all.21.second = bf16[16,8,1408]{2,1,0:T(8,128)(2,1)S(1)} all-to-all(bf16[16,8,1408]{2,1,0:T(8,128)(2,1)S(1)} %bitcast.21), channel_id=1, replica_groups=mesh['dp'=2,'half'=2,'place'=8] {'dp','place'}, dimensions={0} | all-to-all | bytes 720896 | tf_op jit(solution)/shard_map/all_to_all | solution.py:462
  39.2 0.0 copy-done
  39.2 0.0 copy-done.1
  39.2 0.0 copy-done.3
  39.2 0.0 copy-done.4
  39.2 0.0 copy-start.9
  39.2 2.3 %shard_map.141 = (bf16[16,8,768]{2,1,0:T(8,128)(2,1)S(1)}, f32[2,64,320]{2,1,0:T(8,128)S(1)}, f32[2,64,64]{2,1,0:T(8,128)S(1)}) custom-call(bf16[16,8,1408]{2,1,0:T(8,128)(2,1)S(1)} %all_to_all.21.second, bf16[320,1280]{1,0:T(8,128)(2,1)S(1)} %bitcast.16, bf16[320,1280]{1,0:T(8,128)(2,1)S(1)} %copy-done.4, bf16[32,64,320]{2,1,0:T(8,128)(2,1)S(1)} %copy-done, ...), custom_call_target="tpu_custom_call" | custom-call | flops 188743680 | bytes 5013504 | tf_op jit(solution)/shard_map/pallas_call | solution.py:468
  41.6 9.6 %all_to_all.22.third = bf16[16,8,768]{2,1,0:T(8,128)(2,1)S(1)} all-to-all(bf16[16,8,768]{2,1,0:T(8,128)(2,1)S(1)} %get-tuple-element.25), channel_id=1, replica_groups=mesh['dp'=2,'half'=2,'place'=8] {'dp','place'}, dimensions={0} | all-to-all | bytes 393216 | tf_op jit(solution)/shard_map/all_to_all | solution.py:554
  51.2 4.1 %all-gather.1 = bf16[16,768]{1,0:T(8,128)(2,1)S(1)} all-gather(bf16[8,768]{1,0:T(8,128)(2,1)S(1)} %get-tuple-element.27), channel_id=3, replica_groups=mesh['dp'=2,'half'=2,'place'=8] {'half'}, dimensions={0}, use_global_device_ids=true | all-gather | bytes 36864 | tf_op jit(solution)/shard_map/all_gather | solution.py:567
  55.4 1.0 %shard_map.143 = (bf16[32,4,768]{2,1,0:T(4,128)(2,1)}, f32[2,8,64]{2,1,0:T(8,128)S(1)}) custom-call(f32[8,768]{1,0:T(8,128)S(1)} %get-tuple-element.26.own, bf16[2,8,768]{2,1,0:T(8,128)(2,1)S(1)} %bitcast.25, bf16[4,64,640]{2,1,0:T(8,128)(2,1)S(1)} %bitcast.15, f32[8,640]{1,0:T(8,128)S(1)} %get-tuple-element.28.inputs, f32[8,128]{1,0:T(8,128)S(1)} %get-tuple-element.29.stats), custom_call_target="tpu_custom_call" | custom-call | flops 2621440 | bytes 602112 | tf_op jit(solution)/shard_map/pallas_call | solution.py:468
  56.4 4.5 %all-to-all-start.3 = ((bf16[32,4,768]{2,1,0:T(4,128)(2,1)}), bf16[32,4,768]{2,1,0:T(4,128)(2,1)S(1)}, u32[]{:S(2)}, u32[]{:S(2)}) async-start(bf16[32,4,768]{2,1,0:T(4,128)(2,1)} %get-tuple-element.30), calls=%async_computation.3 | async-start | bytes 393216 | tf_op jit(solution)/shard_map/all_to_all | solution.py:580
  60.9 0.0 copy-done.9
  60.9 0.4 shard_map.144.mixing
  61.2 2.5 %shard_map.147 = (bf16[32,64,320]{2,1,0:T(8,128)(2,1)}, bf16[32,64,320]{2,1,0:T(8,128)(2,1)}) custom-call(f32[2,64,64]{2,1,0:T(8,128)S(1)} %get-tuple-element.36.left_rows, f32[2,64,320]{2,1,0:T(8,128)S(1)} %get-tuple-element.37.right_rows), custom_call_target="tpu_custom_call" | custom-call | flops 20971520 | bytes 2818048 | tf_op jit(solution)/shard_map/pallas_call | solution.py:468
  63.8 1.2 %shard_map.146 = (bf16[4,64,640]{2,1,0:T(8,128)(2,1)}, bf16[4,64,640]{2,1,0:T(8,128)(2,1)}) custom-call(f32[2,8,64]{2,1,0:T(8,128)S(1)} %get-tuple-element.33.left_rows, bf16[2,8,640]{2,1,0:T(8,128)(2,1)S(1)} %get-tuple-element.34.right_rows), custom_call_target="tpu_custom_call" | custom-call | flops 5242880 | bytes 679936 | tf_op jit(solution)/shard_map/pallas_call | solution.py:468
  64.9 5.4 %all-to-all-done.3.fourth = bf16[32,4,768]{2,1,0:T(4,128)(2,1)S(1)} async-done(((bf16[32,4,768]{2,1,0:T(4,128)(2,1)}), bf16[32,4,768]{2,1,0:T(4,128)(2,1)S(1)}, u32[]{:S(2)}, u32[]{:S(2)}) %all-to-all-start.3) | async-done | bytes 196640 | tf_op jit(solution)/shard_map/all_to_all | solution.py:580
  70.3 1.7 %shard_map.145 = bf16[256,1280]{1,0:T(8,128)(2,1)} custom-call(bf16[32,4,768]{2,1,0:T(4,128)(2,1)S(1)} %all-to-all-done.3.fourth, bf16[256,1280]{1,0:T(8,128)(2,1)S(1)} %bitcast.18, bf16[64,1280]{1,0:T(8,128)(2,1)S(1)} %bitcast.23, f32[64,256]{1,0:T(8,128)S(1)} %get-tuple-element.31.logits, f32[64,256]{1,0:T(8,128)S(1)} %shard_map.144.mixing), custom_call_target="tpu_custom_call" | custom-call | flops 125829120 | bytes 1802240 | tf_op jit(solution)/shard_map/pallas_call | solution.py:468
  (3 shorter events, 0.1 us)
Async XLA Ops:
  0.6 0.9 %copy-start.8 = (bf16[1280,64]{0,1:T(8,128)(2,1)S(1)}, bf16[1280,64]{0,1:T(8,128)(2,1)}, u32[]{:S(2)}) copy-start(bf16[1280,64]{0,1:T(8,128)(2,1)} %param.12) | copy-start | bytes 491524
  0.6 1.2 %copy-start.6 = (bf16[1,256,1280]{2,1,0:T(8,128)(2,1)S(1)}, bf16[1,256,1280]{2,1,0:T(8,128)(2,1)}, u32[]{:S(2)}) copy-start(bf16[1,256,1280]{2,1,0:T(8,128)(2,1)} %param.11) | copy-start | bytes 1966084
  0.7 1.4 %copy-start.5 = (bf16[1,256,1280]{2,1,0:T(8,128)(2,1)S(1)}, bf16[1,256,1280]{2,1,0:T(8,128)(2,1)}, u32[]{:S(2)}) copy-start(bf16[1,256,1280]{2,1,0:T(8,128)(2,1)} %param.10) | copy-start | bytes 1966084
  2.0 19.9 %copy-start.2 = (bf16[4,640,64]{1,2,0:T(8,128)(2,1)S(1)}, bf16[4,640,64]{1,2,0:T(8,128)(2,1)}, u32[]{:S(2)}) copy-start(bf16[4,640,64]{1,2,0:T(8,128)(2,1)} %param.16) | copy-start | bytes 983044
  2.0 19.9 %copy-start.7 = (bf16[4,64,640]{2,1,0:T(8,128)(2,1)S(1)}, bf16[4,64,640]{2,1,0:T(8,128)(2,1)}, u32[]{:S(2)}) copy-start(bf16[4,64,640]{2,1,0:T(8,128)(2,1)} %out_right.1) | copy-start | bytes 983044
  26.7 12.4 %copy-start = (bf16[32,64,320]{2,1,0:T(8,128)(2,1)S(1)}, bf16[32,64,320]{2,1,0:T(8,128)(2,1)}, u32[]{:S(2)}) copy-start(bf16[32,64,320]{2,1,0:T(8,128)(2,1)} %in_right.1) | copy-start | bytes 3932164
  26.8 12.5 %copy-start.1 = (bf16[32,320,64]{1,2,0:T(8,128)(2,1)S(1)}, bf16[32,320,64]{1,2,0:T(8,128)(2,1)}, u32[]{:S(2)}) copy-start(bf16[32,320,64]{1,2,0:T(8,128)(2,1)} %param.18) | copy-start | bytes 3932164
  26.8 12.5 %copy-start.3 = (bf16[1280,320]{0,1:T(8,128)(2,1)S(1)}, bf16[1280,320]{0,1:T(8,128)(2,1)}, u32[]{:S(2)}) copy-start(bf16[1280,320]{0,1:T(8,128)(2,1)} %param.14) | copy-start | bytes 2457604
  26.8 12.5 %copy-start.4 = (bf16[320,1280]{1,0:T(8,128)(2,1)S(1)}, bf16[320,1280]{1,0:T(8,128)(2,1)}, u32[]{:S(2)}) copy-start(bf16[320,1280]{1,0:T(8,128)(2,1)} %base_out.1) | copy-start | bytes 2457604
  39.2 21.6 %copy-start.9 = (bf16[1,64,1280]{2,1,0:T(8,128)(2,1)S(1)}, bf16[1,64,1280]{2,1,0:T(8,128)(2,1)}, u32[]{:S(2)}) copy-start(bf16[1,64,1280]{2,1,0:T(8,128)(2,1)} %param.13) | copy-start | bytes 491524
  56.4 13.9 %all-to-all-start.3 = ((bf16[32,4,768]{2,1,0:T(4,128)(2,1)}), bf16[32,4,768]{2,1,0:T(4,128)(2,1)S(1)}, u32[]{:S(2)}, u32[]{:S(2)}) async-start(bf16[32,4,768]{2,1,0:T(4,128)(2,1)} %get-tuple-element.30), calls=%async_computation.3 | async-start | bytes 393216 | tf_op jit(solution)/shard_map/all_to_all | solution.py:580

commit v15 on v14

--- a/solution.py
+++ b/solution.py
@@ -8,9 +8,11 @@
 from jax.experimental.pallas import tpu as pltpu
 from jax.sharding import PartitionSpec as P
 
-SEQ = ("half", "place")
+PLACE = ("chip", "core")
+SEQ = ("half", *PLACE)
 BOTH = ("dp", *SEQ)
-HALF = ("dp", "place")
+HALF = ("dp", *PLACE)
+SAME_CORE = ("dp", "half", "chip")
 STATS = 128
 FLOPS_BESIDE_EXCHANGE = 10**10
 
@@ -234,8 +236,11 @@
     out[...] = jnp.zeros(out.shape, out.dtype)
 
 
-def sums_kernel(owned, groups, _, tokens, cotangent, router, first, logits_out, combine_out):
-    ring = first.shape[0] // groups
+def sums_kernel(
+    owned, groups, _, tokens, cotangent, router, own, other, logits_out, combine_out
+):
+    chips = own.shape[0] // groups
+    core = lax.axis_index("core")
     image_rows = tokens[...]
     logits = dot_last(router[...], image_rows)
     high, low = halves(jnp.max(logits, axis=1, keepdims=True))
@@ -250,14 +255,37 @@
     inputs = dot_plain(near.astype(jnp.bfloat16), image_rows).astype(jnp.bfloat16)
     grads = dot_plain(combine.astype(jnp.bfloat16), cotangent[...]).astype(jnp.bfloat16)
     width = inputs.shape[1] // groups
+
+    def block(rows, columns):
+        return jnp.concatenate([inputs[rows, columns], grads[rows, columns], stats[rows]], axis=1)
+
     for group in range(groups):
         columns = slice(group * width, (group + 1) * width)
-        for place in range(ring):
-            rows = slice(place * owned, (place + 1) * owned)
-            block = group * ring + place
-            first[block, :, :width] = inputs[rows, columns]
-            first[block, :, width : 2 * width] = grads[rows, columns]
-            first[block, :, 2 * width :] = stats[rows, :]
+        for chip in range(chips):
+            start = 2 * chip * owned
+            even = block(slice(start, start + owned), columns)
+            odd = block(slice(start + owned, start + 2 * owned), columns)
+            own[group * chips + chip] = jnp.where(core == 0, even, odd)
+            other[group * chips + chip] = jnp.where(core == 0, odd, even)
+
+
+def merge_kernel(width, own, other, out):
+    parts = []
+    for part in (own, other):
+        stats = part[:, :, 2 * width :].astype(jnp.float32)
+        parts.append((stats[:, :, 0:1] + stats[:, :, 1:2], stats[:, :, 2:3] + stats[:, :, 3:4]))
+    peak = jnp.maximum(parts[0][0], parts[1][0])
+    scales = [jnp.exp(part[0] - peak) for part in parts]
+    total = scales[0] * parts[0][1] + scales[1] * parts[1][1]
+    stats = in_lanes([*halves(peak), *halves(total)], own.shape[:2] + (STATS,))
+    inputs = [
+        part[:, :, :width].astype(jnp.float32) * scale
+        for part, scale in zip((own, other), scales, strict=True)
+    ]
+    grads = [part[:, :, width : 2 * width].astype(jnp.float32) for part in (own, other)]
+    out[:, :, :width] = (inputs[0] + inputs[1]).astype(jnp.bfloat16)
+    out[:, :, width : 2 * width] = (grads[0] + grads[1]).astype(jnp.bfloat16)
+    out[:, :, 2 * width :] = stats.astype(jnp.bfloat16)
 
 
 def mixing_kernel(cotangent, saved, combine, out):
@@ -453,7 +481,7 @@
 
 
 def to_group(block, groups):
-    places = lax.axis_size("place")
+    places = lax.axis_size(PLACE)
     blocks = lax.all_gather(block, "half", axis=0)
     (blocks,) = call(
         pack_kernel, [array(block.dtype, groups, places, *block.shape)], [blocks], FLOPS_BESIDE_EXCHANGE
@@ -499,7 +527,7 @@
     owned, slice_width, rank = in_left.shape
     members, _, hidden = in_right.shape
     rows = groups * owned
-    if groups != 2 or ring % 2 or slice_width % 128 or rows % 8 or members % owned:
+    if groups != 2 or ring % 4 or slice_width % 128 or rows % 8 or members % owned:
         return local_plain(
             tokens,
             cotangent,
@@ -517,17 +545,18 @@
     router, base_in = router.T, base_in.T
     in_left, out_left = in_left.swapaxes(1, 2), out_left.swapaxes(1, 2)
     (early,) = call(early_kernel, [array(full, 8, 128)], [], FLOPS_BESIDE_EXCHANGE)
-    first, logits, combine = call(
+    first = array(low, devices // 2, owned, 2 * slice_width + STATS)
+    own, other, logits, combine = call(
         functools.partial(sums_kernel, owned, groups),
-        [
-            array(low, devices, owned, 2 * slice_width + STATS),
-            array(full, slots, count),
-            array(full, slots, count),
-        ],
+        [first, first, array(full, slots, count), array(full, slots, count)],
         [early, image_rows, cot_rows, router],
         6 * count * slots * width + FLOPS_BESIDE_EXCHANGE,
     )
-    first = lax.all_to_all(first, BOTH, 0, 0, tiled=True)
+    other = lax.ppermute(other, "core", [(0, 1), (1, 0)])
+    (first,) = call(
+        functools.partial(merge_kernel, slice_width), [first], [own, other], FLOPS_BESIDE_EXCHANGE
+    )
+    first = lax.all_to_all(first, SAME_CORE, 0, 0, tiled=True)
     second, inputs, lows, stats = call(
         functools.partial(owner_kernel, groups),
         [
@@ -604,7 +633,8 @@
 
 def solution(mesh):
     groups, ring = mesh.shape["dp"], mesh.shape["seq"]
-    split = mesh.devices.reshape(groups, groups, ring // groups)
+    cores = math.gcd(2, ring // groups)
+    split = mesh.devices.reshape(groups, groups, ring // groups // cores, cores)
     mesh = jax.sharding.Mesh(split, BOTH)
     in_specs = (
         P("dp", SEQ, None),

time: 72.3 us -> 71 us (0.982)
  blocking collectives: 49.3 us -> 46.3 us
  waiting for transfers between devices: 5.36 us -> 6.71 us
    all_to_all x1, blocking collectives: 18.8 us -> 14.5 us  [local(): first = lax.all_to_all(first, SAME_CORE, 0, 0, tiled=True)]
    ppermute x0 -> x1, waiting for transfers between devices: none -> 1.36 us  [local(): other = lax.ppermute(other, 'core', [(0, 1), (1, 0)])]
    all_to_all x1, blocking collectives: 12.4 us -> 13.7 us  [to_group(): return lax.all_to_all(blocks, HALF, 0, 0, tiled=True)]
    pallas_call x11 -> x12, Pallas kernels: 10.7 us -> 11 us  [call(): pl.pallas_call(kernel, out_shape=outs, in_specs=[pl.BlockSpec(memory_spac...]
  transfers between devices with their start and end apart: 1 -> 2, of which waited for: 1 -> 2; matrix products, arithmetic and copies ran while one was open for 0% -> 0% of each run, Pallas kernels for 6% -> 6%
where the time goes in v15:
time: 71 us; the launch traced here: 70.7 us
  blocking collectives  46.3 us (65%)
  Pallas kernels  11 us (15%)
  waiting for transfers between devices  6.71 us (9%)
  starting transfers between devices  4.62 us (7%)
  local copies, waits for them, and re-layouts  1.37 us (2%)
  between operations  0.75 us (1%)
    all_to_all x1, blocking collectives, local(): first = lax.all_to_all(first, SAME_CORE, 0, 0, tiled=True)  14.5 us
    all_to_all x1, blocking collectives, to_group(): return lax.all_to_all(blocks, HALF, 0, 0, tiled=True)  13.7 us
    pallas_call x12, Pallas kernels, call(): pl.pallas_call(kernel, out_shape=outs, in_specs=[pl.BlockSpec(memory_spac...  11 us
    all_to_all x1, blocking collectives, local(): third = lax.all_to_all(third, HALF, 0, 0, tiled=True)  9.63 us
    all_to_all x1, waiting for transfers between devices, local(): fourth = lax.all_to_all(fourth, BOTH, 0, 0, tiled=True)  5.35 us
    all_to_all x1, starting transfers between devices, local(): fourth = lax.all_to_all(fourth, BOTH, 0, 0, tiled=True)  4.5 us
    all_gather x1, blocking collectives, to_group(): blocks = lax.all_gather(block, 'half', axis=0)  4.24 us
    all_gather x1, blocking collectives, local(): others = lax.all_gather(other, 'half', axis=0)  4.15 us
  transfers between devices with their start and end apart: 2, of which 2 were waited for; matrix products, arithmetic and copies ran while one was open for 0% of the time, Pallas kernels for 6%

profile of v15, /device:TPU:1, one launch (start us, length us, event | category | flops | bytes accessed | tf_op | source)
XLA Modules:
  0.0 70.7 jit_solution(14319591684787050650)
XLA Ops:
  0.6 0.0 copy-start.8
  0.6 0.0 copy-start.6
  0.7 0.0 copy-start.5
  0.7 0.9 %copy-done.8 = bf16[1280,64]{0,1:T(8,128)(2,1)S(1)} copy-done((bf16[1280,64]{0,1:T(8,128)(2,1)S(1)}, bf16[1280,64]{0,1:T(8,128)(2,1)}, u32[]{:S(2)}) %copy-start.8) | copy-done | bytes 163864
  1.5 0.3 copy-done.6
  1.8 0.2 copy-done.5
  2.0 1.0 %shard_map.138 = (bf16[16,4,1408]{2,1,0:T(4,128)(2,1)S(1)}, bf16[16,4,1408]{2,1,0:T(4,128)(2,1)S(1)}, f32[64,256]{1,0:T(8,128)S(1)}, f32[64,256]{1,0:T(8,128)S(1)}) custom-call(f32[8,128]{1,0:T(8,128)S(1)} %shard_map.137._, bf16[256,1280]{1,0:T(8,128)(2,1)S(1)} %bitcast.17, bf16[256,1280]{1,0:T(8,128)(2,1)S(1)} %bitcast.19, bf16[64,1280]{1,0:T(8,128)(2,1)S(1)} %bitcast.22), custom_call_target="tpu_custom_call" | custom-call | flops 10125829120 | bytes 1970176 | tf_op jit(solution)/shard_map/pallas_call | solution.py:496
  3.0 0.1 collective-permute-start
  3.2 1.4 %collective-permute-done.other = bf16[16,4,1408]{2,1,0:T(4,128)(2,1)S(1)} collective-permute-done((bf16[16,4,1408]{2,1,0:T(4,128)(2,1)S(1)}, bf16[16,4,1408]{2,1,0:T(4,128)(2,1)S(1)}, u32[]{:S(2)}, u32[]{:S(2)}) %collective-permute-start) | collective-permute-done | bytes 180256 | tf_op jit(solution)/shard_map/ppermute | solution.py:555
  4.5 0.0 copy-start.2
  4.5 0.0 copy-start.7
  4.5 0.3 shard_map.139
  4.8 14.5 %all_to_all.20.first = bf16[16,4,1408]{2,1,0:T(4,128)(2,1)S(1)} all-to-all(bf16[16,4,1408]{2,1,0:T(4,128)(2,1)S(1)} %shard_map.139), channel_id=1, replica_groups=mesh['dp'=2,'half'=2,'chip'=4,'core'=2] {'dp','half','chip'}, dimensions={0} | all-to-all | bytes 360448 | tf_op jit(solution)/shard_map/all_to_all | solution.py:559
  19.3 0.0 copy-done.2
  19.3 0.0 copy-done.7
  19.4 0.5 shard_map.140
  19.9 4.2 %all-gather = bf16[16,1408]{1,0:T(8,128)(2,1)S(1)} all-gather(bf16[8,1408]{1,0:T(8,128)(2,1)S(1)} %get-tuple-element.26), channel_id=2, replica_groups=mesh['dp'=2,'half'=2,'chip'=4,'core'=2] {'half'}, dimensions={0}, use_global_device_ids=true | all-gather | bytes 67584 | tf_op jit(solution)/shard_map/all_gather | solution.py:485
  24.1 0.0 copy-start
  24.1 0.0 copy-start.1
  24.1 0.0 copy-start.3
  24.1 0.0 copy-start.4
  24.2 13.7 %all_to_all.21.second = bf16[16,8,1408]{2,1,0:T(8,128)(2,1)S(1)} all-to-all(bf16[16,8,1408]{2,1,0:T(8,128)(2,1)S(1)} %bitcast.21), channel_id=1, replica_groups=mesh['dp'=2,'half'=2,'chip'=4,'core'=2] {'dp','chip','core'}, dimensions={0} | all-to-all | bytes 720896 | tf_op jit(solution)/shard_map/all_to_all | solution.py:490
  37.9 0.0 copy-done
  37.9 0.0 copy-done.1
  37.9 0.0 copy-done.3
  37.9 0.0 copy-done.4
  37.9 0.0 copy-start.9
  38.0 2.3 %shard_map.142 = (bf16[16,8,768]{2,1,0:T(8,128)(2,1)S(1)}, f32[2,64,320]{2,1,0:T(8,128)S(1)}, f32[2,64,64]{2,1,0:T(8,128)S(1)}) custom-call(bf16[16,8,1408]{2,1,0:T(8,128)(2,1)S(1)} %all_to_all.21.second, bf16[320,1280]{1,0:T(8,128)(2,1)S(1)} %bitcast.16, bf16[320,1280]{1,0:T(8,128)(2,1)S(1)} %copy-done.4, bf16[32,64,320]{2,1,0:T(8,128)(2,1)S(1)} %copy-done, ...), custom_call_target="tpu_custom_call" | custom-call | flops 188743680 | bytes 5013504 | tf_op jit(solution)/shard_map/pallas_call | solution.py:496
  40.3 9.6 %all_to_all.22.third = bf16[16,8,768]{2,1,0:T(8,128)(2,1)S(1)} all-to-all(bf16[16,8,768]{2,1,0:T(8,128)(2,1)S(1)} %get-tuple-element.27), channel_id=1, replica_groups=mesh['dp'=2,'half'=2,'chip'=4,'core'=2] {'dp','chip','core'}, dimensions={0} | all-to-all | bytes 393216 | tf_op jit(solution)/shard_map/all_to_all | solution.py:583
  49.9 4.1 %all-gather.1 = bf16[16,768]{1,0:T(8,128)(2,1)S(1)} all-gather(bf16[8,768]{1,0:T(8,128)(2,1)S(1)} %get-tuple-element.29), channel_id=3, replica_groups=mesh['dp'=2,'half'=2,'chip'=4,'core'=2] {'half'}, dimensions={0}, use_global_device_ids=true | all-gather | bytes 36864 | tf_op jit(solution)/shard_map/all_gather | solution.py:596
  54.1 1.0 %shard_map.144 = (bf16[32,4,768]{2,1,0:T(4,128)(2,1)}, f32[2,8,64]{2,1,0:T(8,128)S(1)}) custom-call(f32[8,768]{1,0:T(8,128)S(1)} %get-tuple-element.28.own, bf16[2,8,768]{2,1,0:T(8,128)(2,1)S(1)} %bitcast.25, bf16[4,64,640]{2,1,0:T(8,128)(2,1)S(1)} %bitcast.15, f32[8,640]{1,0:T(8,128)S(1)} %get-tuple-element.30.inputs, f32[8,128]{1,0:T(8,128)S(1)} %get-tuple-element.31.stats), custom_call_target="tpu_custom_call" | custom-call | flops 2621440 | bytes 602112 | tf_op jit(solution)/shard_map/pallas_call | solution.py:496
  55.1 4.5 %all-to-all-start.3 = ((bf16[32,4,768]{2,1,0:T(4,128)(2,1)}), bf16[32,4,768]{2,1,0:T(4,128)(2,1)S(1)}, u32[]{:S(2)}, u32[]{:S(2)}) async-start(bf16[32,4,768]{2,1,0:T(4,128)(2,1)} %get-tuple-element.32), calls=%async_computation.3 | async-start | bytes 393216 | tf_op jit(solution)/shard_map/all_to_all | solution.py:609
  59.6 0.0 copy-done.9
  59.6 0.4 shard_map.145.mixing
  60.0 2.5 %shard_map.148 = (bf16[32,64,320]{2,1,0:T(8,128)(2,1)}, bf16[32,64,320]{2,1,0:T(8,128)(2,1)}) custom-call(f32[2,64,64]{2,1,0:T(8,128)S(1)} %get-tuple-element.38.left_rows, f32[2,64,320]{2,1,0:T(8,128)S(1)} %get-tuple-element.39.right_rows), custom_call_target="tpu_custom_call" | custom-call | flops 20971520 | bytes 2818048 | tf_op jit(solution)/shard_map/pallas_call | solution.py:496
  62.5 1.2 %shard_map.147 = (bf16[4,64,640]{2,1,0:T(8,128)(2,1)}, bf16[4,64,640]{2,1,0:T(8,128)(2,1)}) custom-call(f32[2,8,64]{2,1,0:T(8,128)S(1)} %get-tuple-element.35.left_rows, bf16[2,8,640]{2,1,0:T(8,128)(2,1)S(1)} %get-tuple-element.36.right_rows), custom_call_target="tpu_custom_call" | custom-call | flops 5242880 | bytes 679936 | tf_op jit(solution)/shard_map/pallas_call | solution.py:496
  63.7 5.4 %all-to-all-done.3.fourth = bf16[32,4,768]{2,1,0:T(4,128)(2,1)S(1)} async-done(((bf16[32,4,768]{2,1,0:T(4,128)(2,1)}), bf16[32,4,768]{2,1,0:T(4,128)(2,1)S(1)}, u32[]{:S(2)}, u32[]{:S(2)}) %all-to-all-start.3) | async-done | bytes 196640 | tf_op jit(solution)/shard_map/all_to_all | solution.py:609
  69.0 1.7 %shard_map.146 = bf16[256,1280]{1,0:T(8,128)(2,1)} custom-call(bf16[32,4,768]{2,1,0:T(4,128)(2,1)S(1)} %all-to-all-done.3.fourth, bf16[256,1280]{1,0:T(8,128)(2,1)S(1)} %bitcast.18, bf16[64,1280]{1,0:T(8,128)(2,1)S(1)} %bitcast.23, f32[64,256]{1,0:T(8,128)S(1)} %get-tuple-element.33.logits, f32[64,256]{1,0:T(8,128)S(1)} %shard_map.145.mixing), custom_call_target="tpu_custom_call" | custom-call | flops 125829120 | bytes 1802240 | tf_op jit(solution)/shard_map/pallas_call | solution.py:496
  (3 shorter events, 0.1 us)
Async XLA Ops:
  0.6 0.9 %copy-start.8 = (bf16[1280,64]{0,1:T(8,128)(2,1)S(1)}, bf16[1280,64]{0,1:T(8,128)(2,1)}, u32[]{:S(2)}) copy-start(bf16[1280,64]{0,1:T(8,128)(2,1)} %param.12) | copy-start | bytes 491524
  0.6 1.2 %copy-start.6 = (bf16[1,256,1280]{2,1,0:T(8,128)(2,1)S(1)}, bf16[1,256,1280]{2,1,0:T(8,128)(2,1)}, u32[]{:S(2)}) copy-start(bf16[1,256,1280]{2,1,0:T(8,128)(2,1)} %param.11) | copy-start | bytes 1966084
  0.7 1.4 %copy-start.5 = (bf16[1,256,1280]{2,1,0:T(8,128)(2,1)S(1)}, bf16[1,256,1280]{2,1,0:T(8,128)(2,1)}, u32[]{:S(2)}) copy-start(bf16[1,256,1280]{2,1,0:T(8,128)(2,1)} %param.10) | copy-start | bytes 1966084
  3.0 1.5 %collective-permute-start = (bf16[16,4,1408]{2,1,0:T(4,128)(2,1)S(1)}, bf16[16,4,1408]{2,1,0:T(4,128)(2,1)S(1)}, u32[]{:S(2)}, u32[]{:S(2)}) collective-permute-start(bf16[16,4,1408]{2,1,0:T(4,128)(2,1)S(1)} %get-tuple-element.25), channel_id=1, source_target_pairs={{0,1},{1,0},{2,3},{3,2},{4,5},{5,4},{6,7},{7,6},{8,9},{9,8},{10,11... | collective-permute-start | bytes 540680 | tf_op jit(solution)/shard_map/ppermute | solution.py:555
  4.5 14.8 %copy-start.2 = (bf16[4,640,64]{1,2,0:T(8,128)(2,1)S(1)}, bf16[4,640,64]{1,2,0:T(8,128)(2,1)}, u32[]{:S(2)}) copy-start(bf16[4,640,64]{1,2,0:T(8,128)(2,1)} %param.16) | copy-start | bytes 983044
  4.5 14.8 %copy-start.7 = (bf16[4,64,640]{2,1,0:T(8,128)(2,1)S(1)}, bf16[4,64,640]{2,1,0:T(8,128)(2,1)}, u32[]{:S(2)}) copy-start(bf16[4,64,640]{2,1,0:T(8,128)(2,1)} %out_right.1) | copy-start | bytes 983044
  24.1 13.8 %copy-start = (bf16[32,64,320]{2,1,0:T(8,128)(2,1)S(1)}, bf16[32,64,320]{2,1,0:T(8,128)(2,1)}, u32[]{:S(2)}) copy-start(bf16[32,64,320]{2,1,0:T(8,128)(2,1)} %in_right.1) | copy-start | bytes 3932164
  24.1 13.8 %copy-start.1 = (bf16[32,320,64]{1,2,0:T(8,128)(2,1)S(1)}, bf16[32,320,64]{1,2,0:T(8,128)(2,1)}, u32[]{:S(2)}) copy-start(bf16[32,320,64]{1,2,0:T(8,128)(2,1)} %param.18) | copy-start | bytes 3932164
  24.1 13.8 %copy-start.3 = (bf16[1280,320]{0,1:T(8,128)(2,1)S(1)}, bf16[1280,320]{0,1:T(8,128)(2,1)}, u32[]{:S(2)}) copy-start(bf16[1280,320]{0,1:T(8,128)(2,1)} %param.14) | copy-start | bytes 2457604
  24.1 13.8 %copy-start.4 = (bf16[320,1280]{1,0:T(8,128)(2,1)S(1)}, bf16[320,1280]{1,0:T(8,128)(2,1)}, u32[]{:S(2)}) copy-start(bf16[320,1280]{1,0:T(8,128)(2,1)} %base_out.1) | copy-start | bytes 2457604
  37.9 21.6 %copy-start.9 = (bf16[1,64,1280]{2,1,0:T(8,128)(2,1)S(1)}, bf16[1,64,1280]{2,1,0:T(8,128)(2,1)}, u32[]{:S(2)}) copy-start(bf16[1,64,1280]{2,1,0:T(8,128)(2,1)} %param.13) | copy-start | bytes 491524
  55.1 13.9 %all-to-all-start.3 = ((bf16[32,4,768]{2,1,0:T(4,128)(2,1)}), bf16[32,4,768]{2,1,0:T(4,128)(2,1)S(1)}, u32[]{:S(2)}, u32[]{:S(2)}) async-start(bf16[32,4,768]{2,1,0:T(4,128)(2,1)} %get-tuple-element.32), calls=%async_computation.3 | async-start | bytes 393216 | tf_op jit(solution)/shard_map/all_to_all | solution.py:609

commit v16 on v15

--- a/solution.py
+++ b/solution.py
@@ -11,7 +11,7 @@
 PLACE = ("chip", "core")
 SEQ = ("half", *PLACE)
 BOTH = ("dp", *SEQ)
-HALF = ("dp", *PLACE)
+HALF_CORE = ("dp", "chip")
 SAME_CORE = ("dp", "half", "chip")
 STATS = 128
 FLOPS_BESIDE_EXCHANGE = 10**10
@@ -333,14 +333,17 @@
 def hidden_kernel(
     groups,
     second,
+    second_other,
     base_in,
     base_out,
     in_right,
     out_left,
     third,
+    third_other,
     pair_out,
     ranks_out,
 ):
+    first_core = lax.axis_index("core") == 0
     members, rank, hidden = in_right.shape
     rows = second.shape[1]
     owned = rows // groups
@@ -348,11 +351,17 @@
     width = base_in.shape[1] // groups
 
     def gathered(columns):
-        taken = [
-            second[half * places : (half + 1) * places, :, columns].astype(jnp.float32)
-            for half in range(groups)
-        ]
-        return [part.reshape(places * rows, part.shape[2]) for part in taken]
+        parts = []
+        for half in range(groups):
+            taken = []
+            for chip in range(places // 2):
+                block = half * (places // 2) + chip
+                own = second[block, :, columns].astype(jnp.float32)
+                other = second_other[block, :, columns].astype(jnp.float32)
+                taken.append(jnp.where(first_core, own, other))
+                taken.append(jnp.where(first_core, other, own))
+            parts.append(jnp.concatenate(taken, axis=0))
+        return parts
 
     def low_rank(value, table):
         value = value.astype(jnp.float32)
@@ -393,17 +402,26 @@
     pair_out[1] = hidden_low
     ranks_out[0] = up.astype(jnp.float32)
     ranks_out[1] = back.astype(jnp.float32)
-    slot_term = dot_plain(preact_grad.astype(jnp.bfloat16), base_in[...]).astype(jnp.bfloat16)
+    slot_term = dot_plain(preact_grad.astype(jnp.bfloat16), base_in[...])
     down = to_rank(preact_grad, in_right)
     value = to_rank(hidden_low, out_left)
-    ranks = jnp.concatenate([down, value], axis=1).astype(jnp.bfloat16)
+    ranks = jnp.concatenate([down, value], axis=1)
     for half in range(groups):
         columns = slice(half * width, (half + 1) * width)
-        for place in range(places):
+
+        def block(place):
             taken = slice(place * rows, (place + 1) * rows)
-            block = half * places + place
-            third[block, :, :width] = slot_term[taken, columns]
-            third[block, :, width:] = ranks[taken]
+            return jnp.concatenate([slot_term[taken, columns], ranks[taken]], axis=1)
+
+        for chip in range(places // 2):
+            even, odd = block(2 * chip), block(2 * chip + 1)
+            number = half * (places // 2) + chip
+            third[number] = jnp.where(first_core, even, odd).astype(jnp.bfloat16)
+            third_other[number] = jnp.where(first_core, odd, even).astype(jnp.bfloat16)
+
+
+def add_kernel(own, other, out):
+    out[...] = (own[...].astype(jnp.float32) + other[...].astype(jnp.float32)).astype(out.dtype)
 
 
 def outer_kernel(owned, left_rows, right_rows, *outs):
@@ -426,7 +444,7 @@
         out[...] = jnp.sum(taken, axis=0).astype(out.dtype)
 
 
-def finish_kernel(groups, ring, own, others, in_left, inputs, stats, fourth, ranks_out):
+def finish_kernel(groups, own, others, in_left, inputs, stats, fourth, ranks_out):
     owned, rank, width = in_left.shape
     summed = own[...] + others[1 - lax.axis_index("half")].astype(jnp.float32)
     ranks = summed[:, width:].astype(jnp.bfloat16).astype(jnp.float32)
@@ -441,19 +459,23 @@
     block = jnp.concatenate([grads, tail], axis=1).astype(jnp.bfloat16)
     for group in range(groups):
         rows = block[group * owned : (group + 1) * owned]
-        for place in range(ring):
-            fourth[group * ring + place] = rows
-
-
-def tokens_kernel(groups, fourth, tokens, router, logits, mixing, out_far, out, sent):
+        for place in range(fourth.shape[0] // groups):
+            fourth[group * (fourth.shape[0] // groups) + place] = rows
+
+
+def tokens_kernel(groups, fourth, fourth_other, tokens, router, logits, mixing, out_far, out, sent):
     blocks, owned, _ = fourth.shape
-    ring = blocks // groups
+    chips = blocks // groups
     width = tokens.shape[1] // groups
+    first_core = lax.axis_index("core") == 0
 
     def rows(half, columns):
-        taken = [
-            fourth[half * ring + place, :, columns].astype(jnp.float32) for place in range(ring)
-        ]
+        taken = []
+        for chip in range(chips):
+            own = fourth[half * chips + chip, :, columns].astype(jnp.float32)
+            other = fourth_other[half * chips + chip, :, columns].astype(jnp.float32)
+            taken.append(jnp.where(first_core, own, other))
+            taken.append(jnp.where(first_core, other, own))
         return jnp.concatenate(taken, axis=0)
 
     grads = jnp.concatenate([rows(half, slice(0, width)) for half in range(groups)], axis=1)
@@ -480,14 +502,22 @@
         copy.wait()
 
 
+def swap_cores(blocks):
+    return lax.ppermute(blocks, "core", [(0, 1), (1, 0)])
+
+
 def to_group(block, groups):
-    places = lax.axis_size(PLACE)
+    chips = lax.axis_size("chip")
     blocks = lax.all_gather(block, "half", axis=0)
     (blocks,) = call(
-        pack_kernel, [array(block.dtype, groups, places, *block.shape)], [blocks], FLOPS_BESIDE_EXCHANGE
-    )
-    blocks = blocks.reshape(groups * places, *block.shape)
-    return lax.all_to_all(blocks, HALF, 0, 0, tiled=True)
+        pack_kernel,
+        [array(block.dtype, groups, chips, *block.shape)],
+        [blocks],
+        FLOPS_BESIDE_EXCHANGE,
+    )
+    blocks = blocks.reshape(groups * chips, *block.shape)
+    blocks = lax.all_to_all(blocks, HALF_CORE, 0, 0, tiled=True)
+    return blocks, swap_cores(blocks)
 
 
 def call(kernel, outs, args, flops, space=pltpu.VMEM, scratch=()):
@@ -552,7 +582,7 @@
         [early, image_rows, cot_rows, router],
         6 * count * slots * width + FLOPS_BESIDE_EXCHANGE,
     )
-    other = lax.ppermute(other, "core", [(0, 1), (1, 0)])
+    other = swap_cores(other)
     (first,) = call(
         functools.partial(merge_kernel, slice_width), [first], [own, other], FLOPS_BESIDE_EXCHANGE
     )
@@ -568,25 +598,27 @@
         [first, in_left, out_right],
         4 * rows * owned * rank * slice_width,
     )
-    second = to_group(second, groups)
+    second, second_other = to_group(second, groups)
     total_rows = groups * members
-    third, pair, ranks = call(
+    third = array(low, ring // 2, rows, slice_width + 2 * rank)
+    third, other, pair, hidden_ranks = call(
         functools.partial(hidden_kernel, groups),
         [
-            array(low, ring, rows, slice_width + 2 * rank),
+            third,
+            third,
             array(full, 2, total_rows, hidden),
             array(full, 2, total_rows, rank),
         ],
-        [second, base_in, base_out, in_right, out_left],
+        [second, second_other, base_in, base_out, in_right, out_left],
         6 * total_rows * hidden * (width + owned * rank),
     )
-    third = lax.all_to_all(third, HALF, 0, 0, tiled=True)
-    grad_in_right, grad_out_left = call(
-        functools.partial(outer_kernel, owned),
-        [array(low, members, rank, hidden)] * 2,
-        [ranks, pair],
-        4 * members * rank * hidden * rows,
-    )
+    (third,) = call(
+        add_kernel,
+        [array(third.dtype, *third.shape)],
+        [third, swap_cores(other)],
+        FLOPS_BESIDE_EXCHANGE,
+    )
+    third = lax.all_to_all(third, HALF_CORE, 0, 0, tiled=True)
     own, other = call(
         halves_kernel,
         [array(kind, rows, slice_width + 2 * rank) for kind in (full, low)],
@@ -595,10 +627,20 @@
     )
     others = lax.all_gather(other, "half", axis=0)
     fourth, ranks = call(
-        functools.partial(finish_kernel, groups, ring),
-        [array(low, devices, owned, slice_width + STATS), array(full, 2, rows, rank)],
+        functools.partial(finish_kernel, groups),
+        [array(low, devices // 2, owned, slice_width + STATS), array(full, 2, rows, rank)],
         [own, others, in_left, inputs, stats],
         2 * rows * owned * rank * slice_width,
+    )
+    fourth, combine, pair, hidden_ranks = lax.optimization_barrier(
+        (fourth, combine, pair, hidden_ranks)
+    )
+    fourth = lax.all_to_all(fourth, SAME_CORE, 0, 0, tiled=True)
+    grad_in_right, grad_out_left = call(
+        functools.partial(outer_kernel, owned),
+        [array(low, members, rank, hidden)] * 2,
+        [hidden_ranks, pair],
+        4 * members * rank * hidden * rows,
     )
     (mixing,) = call(
         mixing_kernel,
@@ -606,7 +648,6 @@
         [cot_rows, saved, combine],
         2 * count * slots * width,
     )
-    fourth = lax.all_to_all(fourth, BOTH, 0, 0, tiled=True)
     grad_in_left, grad_out_right = call(
         functools.partial(outer_kernel, owned),
         [array(low, owned, rank, slice_width)] * 2,
@@ -617,7 +658,7 @@
     (token_grad,) = call(
         functools.partial(tokens_kernel, groups),
         [array(low, count, width)],
-        [fourth, image_rows, router, logits, mixing],
+        [fourth, swap_cores(fourth), image_rows, router, logits, mixing],
         6 * count * slots * width,
         pltpu.HBM,
         [pltpu.VMEM((count, width), low), pltpu.SemaphoreType.DMA((parts,))],

time: 71 us -> 72.4 us (1.020)
  starting transfers between devices: 4.62 us -> 8.47 us
  waiting for transfers between devices: 6.71 us -> 3.36 us
  blocking collectives: 46.3 us -> 47.9 us
    ppermute x1 -> x4, starting transfers between devices: 0.12 us -> 8.47 us  [swap_cores(): return lax.ppermute(blocks, 'core', [(0, 1), (1, 0)])]
    all_to_all x1 -> x0, waiting for transfers between devices: 5.35 us -> none  [local(): fourth = lax.all_to_all(fourth, BOTH, 0, 0, tiled=True)]
    all_to_all x1 -> x0, starting transfers between devices: 4.5 us -> none  [local(): fourth = lax.all_to_all(fourth, BOTH, 0, 0, tiled=True)]
    ppermute x1 -> x4, waiting for transfers between devices: 1.36 us -> 3.36 us  [swap_cores(): return lax.ppermute(blocks, 'core', [(0, 1), (1, 0)])]
    all_to_all x2 -> x3, blocking collectives: 23.4 us -> 24.9 us  [the longest x1 9.21 us: local(): fourth = lax.all_to_all(fourth, SAME_CORE, 0, 0, tiled=True)]
    pallas_call x12 -> x13, Pallas kernels: 11 us -> 10.3 us  [call(): pl.pallas_call(kernel, out_shape=outs, in_specs=[pl.BlockSpec(memory_spac...]
  transfers between devices with their start and end apart: 2 -> 4, of which waited for: 2 -> 3; matrix products, arithmetic and copies ran while one was open for 0% -> 0% of each run, Pallas kernels for 6% -> 6%
where the time goes in v16:
time: 72.4 us; the launch traced here: 72.1 us
  blocking collectives  47.9 us (66%)
  Pallas kernels  10.3 us (14%)
  starting transfers between devices  8.47 us (12%)
  waiting for transfers between devices  3.36 us (5%)
  local copies, waits for them, and re-layouts  1.37 us (2%)
  between operations  0.73 us (1%)
    all_to_all x1, blocking collectives, local(): first = lax.all_to_all(first, SAME_CORE, 0, 0, tiled=True)  14.5 us
    pallas_call x13, Pallas kernels, call(): pl.pallas_call(kernel, out_shape=outs, in_specs=[pl.BlockSpec(memory_spac...  10.3 us
    all_to_all x1, blocking collectives, local(): fourth = lax.all_to_all(fourth, SAME_CORE, 0, 0, tiled=True)  9.21 us
    ppermute x4, starting transfers between devices, swap_cores(): return lax.ppermute(blocks, 'core', [(0, 1), (1, 0)])  8.47 us
    all_to_all x1, blocking collectives, to_group(): blocks = lax.all_to_all(blocks, HALF_CORE, 0, 0, tiled=True)  8.2 us
    all_to_all x1, blocking collectives, local(): third = lax.all_to_all(third, HALF_CORE, 0, 0, tiled=True)  7.46 us
    all_gather x1, blocking collectives, local(): others = lax.all_gather(other, 'half', axis=0)  4.25 us
    all_gather x1, blocking collectives, to_group(): blocks = lax.all_gather(block, 'half', axis=0)  4.24 us
  transfers between devices with their start and end apart: 4, of which 3 were waited for; matrix products, arithmetic and copies ran while one was open for 0% of the time, Pallas kernels for 6%

profile of v16, /device:TPU:1, one launch (start us, length us, event | category | flops | bytes accessed | tf_op | source)
XLA Modules:
  0.0 72.1 jit_solution(10994746280989670921)
XLA Ops:
  0.6 0.0 copy-start.8
  0.6 0.0 copy-start.6
  0.7 0.0 copy-start.5
  0.7 0.9 %copy-done.8 = bf16[1280,64]{0,1:T(8,128)(2,1)S(1)} copy-done((bf16[1280,64]{0,1:T(8,128)(2,1)S(1)}, bf16[1280,64]{0,1:T(8,128)(2,1)}, u32[]{:S(2)}) %copy-start.8) | copy-done | bytes 163864
  1.5 0.3 copy-done.6
  1.8 0.2 copy-done.5
  2.0 1.0 %shard_map.138 = (bf16[16,4,1408]{2,1,0:T(4,128)(2,1)S(1)}, bf16[16,4,1408]{2,1,0:T(4,128)(2,1)S(1)}, f32[64,256]{1,0:T(8,128)S(1)}, f32[64,256]{1,0:T(8,128)S(1)}) custom-call(f32[8,128]{1,0:T(8,128)S(1)} %shard_map.137._, bf16[256,1280]{1,0:T(8,128)(2,1)S(1)} %bitcast.17, bf16[256,1280]{1,0:T(8,128)(2,1)S(1)} %bitcast.19, bf16[64,1280]{1,0:T(8,128)(2,1)S(1)} %bitcast.22), custom_call_target="tpu_custom_call" | custom-call | flops 10125829120 | bytes 1970176 | tf_op jit(solution)/shard_map/pallas_call | solution.py:526
  3.0 0.1 collective-permute-start
  3.2 1.4 %collective-permute-done.other = bf16[16,4,1408]{2,1,0:T(4,128)(2,1)S(1)} collective-permute-done((bf16[16,4,1408]{2,1,0:T(4,128)(2,1)S(1)}, bf16[16,4,1408]{2,1,0:T(4,128)(2,1)S(1)}, u32[]{:S(2)}, u32[]{:S(2)}) %collective-permute-start) | collective-permute-done | bytes 180256 | tf_op jit(solution)/shard_map/ppermute | solution.py:506
  4.5 0.0 copy-start.2
  4.5 0.0 copy-start.7
  4.5 0.3 shard_map.139
  4.8 14.5 %all_to_all.20.first = bf16[16,4,1408]{2,1,0:T(4,128)(2,1)S(1)} all-to-all(bf16[16,4,1408]{2,1,0:T(4,128)(2,1)S(1)} %shard_map.139), channel_id=1, replica_groups=mesh['dp'=2,'half'=2,'chip'=4,'core'=2] {'dp','half','chip'}, dimensions={0} | all-to-all | bytes 360448 | tf_op jit(solution)/shard_map/all_to_all | solution.py:589
  19.3 0.0 copy-done.2
  19.4 0.0 copy-done.7
  19.4 0.5 shard_map.140
  19.9 4.2 %all-gather = bf16[16,1408]{1,0:T(8,128)(2,1)S(1)} all-gather(bf16[8,1408]{1,0:T(8,128)(2,1)S(1)} %get-tuple-element.31), channel_id=2, replica_groups=mesh['dp'=2,'half'=2,'chip'=4,'core'=2] {'half'}, dimensions={0}, use_global_device_ids=true | all-gather | bytes 67584 | tf_op jit(solution)/shard_map/all_gather | solution.py:511
  24.1 0.0 copy-start
  24.1 0.0 copy-start.1
  24.1 0.0 copy-start.3
  24.1 0.0 copy-start.4
  24.2 8.2 %all_to_all.21.second = bf16[8,8,1408]{2,1,0:T(8,128)(2,1)S(1)} all-to-all(bf16[8,8,1408]{2,1,0:T(8,128)(2,1)S(1)} %bitcast.21), channel_id=1, replica_groups=mesh['dp'=2,'half'=2,'chip'=4,'core'=2] {'dp','chip'}, dimensions={0} | all-to-all | bytes 360448 | tf_op jit(solution)/shard_map/all_to_all | solution.py:519
  32.4 4.3 %collective-permute-start.1 = (bf16[8,8,1408]{2,1,0:T(8,128)(2,1)S(1)}, bf16[8,8,1408]{2,1,0:T(8,128)(2,1)S(1)}, u32[]{:S(2)}, u32[]{:S(2)}) collective-permute-start(bf16[8,8,1408]{2,1,0:T(8,128)(2,1)S(1)} %all_to_all.21.second), channel_id=1, source_target_pairs={{0,1},{1,0},{2,3},{3,2},{4,5},{5,4},{6,7},{7,6},{8,9},{9,8},{10,11... | collective-permute-start | bytes 540680 | tf_op jit(solution)/shard_map/ppermute | solution.py:506
  36.7 1.0 %collective-permute-done.1.second_other = bf16[8,8,1408]{2,1,0:T(8,128)(2,1)S(1)} collective-permute-done((bf16[8,8,1408]{2,1,0:T(8,128)(2,1)S(1)}, bf16[8,8,1408]{2,1,0:T(8,128)(2,1)S(1)}, u32[]{:S(2)}, u32[]{:S(2)}) %collective-permute-start.1) | collective-permute-done | bytes 180256 | tf_op jit(solution)/shard_map/ppermute | solution.py:506
  37.8 0.0 copy-done
  37.8 0.0 copy-done.1
  37.8 0.0 copy-done.3
  37.8 0.0 copy-done.4
  37.8 2.3 %shard_map.142 = (bf16[8,8,768]{2,1,0:T(8,128)(2,1)S(1)}, bf16[8,8,768]{2,1,0:T(8,128)(2,1)S(1)}, f32[2,64,320]{2,1,0:T(8,128)S(1)}, f32[2,64,64]{2,1,0:T(8,128)S(1)}) custom-call(bf16[8,8,1408]{2,1,0:T(8,128)(2,1)S(1)} %all_to_all.21.second, bf16[8,8,1408]{2,1,0:T(8,128)(2,1)S(1)} %collective-permute-done.1.second_other, bf16[320,1280]{1,0:T(8,128)(2,1)S(1)} %bitcast.16, ...), custom_call_target="tpu_custom_call" | custom-call | flops 188743680 | bytes 5013504 | tf_op jit(solution)/shard_map/pallas_call | solution.py:526
  40.1 0.4 collective-permute-start.2
  40.5 0.9 %collective-permute-done.2.other = bf16[8,8,768]{2,1,0:T(8,128)(2,1)S(1)} collective-permute-done((bf16[8,8,768]{2,1,0:T(8,128)(2,1)S(1)}, bf16[8,8,768]{2,1,0:T(8,128)(2,1)S(1)}, u32[]{:S(2)}, u32[]{:S(2)}) %collective-permute-start.2) | collective-permute-done | bytes 98336 | tf_op jit(solution)/shard_map/ppermute | solution.py:506
  41.5 0.0 copy-start.9
  41.5 7.5 %all_to_all.22.third = bf16[8,8,768]{2,1,0:T(8,128)(2,1)S(1)} all-to-all(bf16[8,8,768]{2,1,0:T(8,128)(2,1)S(1)} %shard_map.143), channel_id=1, replica_groups=mesh['dp'=2,'half'=2,'chip'=4,'core'=2] {'dp','chip'}, dimensions={0} | all-to-all | bytes 196608 | tf_op jit(solution)/shard_map/all_to_all | solution.py:621
  49.0 4.3 %all-gather.1 = bf16[16,768]{1,0:T(8,128)(2,1)S(1)} all-gather(bf16[8,768]{1,0:T(8,128)(2,1)S(1)} %get-tuple-element.35), channel_id=3, replica_groups=mesh['dp'=2,'half'=2,'chip'=4,'core'=2] {'half'}, dimensions={0}, use_global_device_ids=true | all-gather | bytes 36864 | tf_op jit(solution)/shard_map/all_gather | solution.py:628
  53.2 0.3 shard_map.145
  53.5 9.2 %all_to_all.23.fourth = bf16[16,4,768]{2,1,0:T(4,128)(2,1)S(1)} all-to-all(bf16[16,4,768]{2,1,0:T(4,128)(2,1)S(1)} %get-tuple-element.42), channel_id=1, replica_groups=mesh['dp'=2,'half'=2,'chip'=4,'core'=2] {'dp','half','chip'}, dimensions={0} | all-to-all | bytes 196608 | tf_op jit(solution)/shard_map/all_to_all | solution.py:638
  62.7 3.6 %collective-permute-start.3 = (bf16[16,4,768]{2,1,0:T(4,128)(2,1)S(1)}, bf16[16,4,768]{2,1,0:T(4,128)(2,1)S(1)}, u32[]{:S(2)}, u32[]{:S(2)}) collective-permute-start(bf16[16,4,768]{2,1,0:T(4,128)(2,1)S(1)} %all_to_all.23.fourth), channel_id=1, source_target_pairs={{0,1},{1,0},{2,3},{3,2},{4,5},{5,4},{6,7},{7,6},{8,9},{9,8},{10,11... | collective-permute-start | bytes 294920 | tf_op jit(solution)/shard_map/ppermute | solution.py:506
  66.3 1.2 %shard_map.148 = (bf16[4,64,640]{2,1,0:T(8,128)(2,1)}, bf16[4,64,640]{2,1,0:T(8,128)(2,1)}) custom-call(f32[2,8,64]{2,1,0:T(8,128)S(1)} %get-tuple-element.45.left_rows, bf16[2,8,640]{2,1,0:T(8,128)(2,1)S(1)} %get-tuple-element.46.right_rows), custom_call_target="tpu_custom_call" | custom-call | flops 5242880 | bytes 679936 | tf_op jit(solution)/shard_map/pallas_call | solution.py:526
  67.5 2.5 %shard_map.149 = (bf16[32,64,320]{2,1,0:T(8,128)(2,1)}, bf16[32,64,320]{2,1,0:T(8,128)(2,1)}) custom-call(f32[2,64,64]{2,1,0:T(8,128)S(1)} %get-tuple-element.48.left_rows, f32[2,64,320]{2,1,0:T(8,128)S(1)} %get-tuple-element.49.right_rows), custom_call_target="tpu_custom_call" | custom-call | flops 20971520 | bytes 2818048 | tf_op jit(solution)/shard_map/pallas_call | solution.py:526
  70.0 0.0 copy-done.9
  70.0 0.4 shard_map.146.mixing
  70.4 0.0 collective-permute-done.3.fourth_other
  70.4 1.7 %shard_map.147 = bf16[256,1280]{1,0:T(8,128)(2,1)} custom-call(bf16[16,4,768]{2,1,0:T(4,128)(2,1)S(1)} %all_to_all.23.fourth, bf16[16,4,768]{2,1,0:T(4,128)(2,1)S(1)} %collective-permute-done.3.fourth_other, bf16[256,1280]{1,0:T(8,128)(2,1)S(1)} %bitcast.18, bf16[64,1280]{1,0:T(8,128)(2,1)S(1)} %bitcast.23, f32[64,256]{1,0:T(8,128)S(1)} %get-tuple-element.43.logits, ...), custom_call_target="tpu_custom_call" | custom-call | flops 125829120 | bytes 1802240 | tf_op jit(solution)/shard_map/pallas_call | solution.py:526
  (4 shorter events, 0.1 us)
Async XLA Ops:
  0.6 0.9 %copy-start.8 = (bf16[1280,64]{0,1:T(8,128)(2,1)S(1)}, bf16[1280,64]{0,1:T(8,128)(2,1)}, u32[]{:S(2)}) copy-start(bf16[1280,64]{0,1:T(8,128)(2,1)} %param.12) | copy-start | bytes 491524
  0.6 1.2 %copy-start.6 = (bf16[1,256,1280]{2,1,0:T(8,128)(2,1)S(1)}, bf16[1,256,1280]{2,1,0:T(8,128)(2,1)}, u32[]{:S(2)}) copy-start(bf16[1,256,1280]{2,1,0:T(8,128)(2,1)} %param.11) | copy-start | bytes 1966084
  0.7 1.4 %copy-start.5 = (bf16[1,256,1280]{2,1,0:T(8,128)(2,1)S(1)}, bf16[1,256,1280]{2,1,0:T(8,128)(2,1)}, u32[]{:S(2)}) copy-start(bf16[1,256,1280]{2,1,0:T(8,128)(2,1)} %param.10) | copy-start | bytes 1966084
  3.0 1.5 %collective-permute-start = (bf16[16,4,1408]{2,1,0:T(4,128)(2,1)S(1)}, bf16[16,4,1408]{2,1,0:T(4,128)(2,1)S(1)}, u32[]{:S(2)}, u32[]{:S(2)}) collective-permute-start(bf16[16,4,1408]{2,1,0:T(4,128)(2,1)S(1)} %get-tuple-element.30), channel_id=1, source_target_pairs={{0,1},{1,0},{2,3},{3,2},{4,5},{5,4},{6,7},{7,6},{8,9},{9,8},{10,11... | collective-permute-start | bytes 540680 | tf_op jit(solution)/shard_map/ppermute | solution.py:506
  4.5 14.8 %copy-start.2 = (bf16[4,640,64]{1,2,0:T(8,128)(2,1)S(1)}, bf16[4,640,64]{1,2,0:T(8,128)(2,1)}, u32[]{:S(2)}) copy-start(bf16[4,640,64]{1,2,0:T(8,128)(2,1)} %param.16) | copy-start | bytes 983044
  4.5 14.8 %copy-start.7 = (bf16[4,64,640]{2,1,0:T(8,128)(2,1)S(1)}, bf16[4,64,640]{2,1,0:T(8,128)(2,1)}, u32[]{:S(2)}) copy-start(bf16[4,64,640]{2,1,0:T(8,128)(2,1)} %out_right.1) | copy-start | bytes 983044
  24.1 13.6 %copy-start = (bf16[32,64,320]{2,1,0:T(8,128)(2,1)S(1)}, bf16[32,64,320]{2,1,0:T(8,128)(2,1)}, u32[]{:S(2)}) copy-start(bf16[32,64,320]{2,1,0:T(8,128)(2,1)} %in_right.1) | copy-start | bytes 3932164
  24.1 13.6 %copy-start.1 = (bf16[32,320,64]{1,2,0:T(8,128)(2,1)S(1)}, bf16[32,320,64]{1,2,0:T(8,128)(2,1)}, u32[]{:S(2)}) copy-start(bf16[32,320,64]{1,2,0:T(8,128)(2,1)} %param.18) | copy-start | bytes 3932164
  24.1 13.6 %copy-start.3 = (bf16[1280,320]{0,1:T(8,128)(2,1)S(1)}, bf16[1280,320]{0,1:T(8,128)(2,1)}, u32[]{:S(2)}) copy-start(bf16[1280,320]{0,1:T(8,128)(2,1)} %param.14) | copy-start | bytes 2457604
  24.1 13.6 %copy-start.4 = (bf16[320,1280]{1,0:T(8,128)(2,1)S(1)}, bf16[320,1280]{1,0:T(8,128)(2,1)}, u32[]{:S(2)}) copy-start(bf16[320,1280]{1,0:T(8,128)(2,1)} %base_out.1) | copy-start | bytes 2457604
  32.4 5.4 %collective-permute-start.1 = (bf16[8,8,1408]{2,1,0:T(8,128)(2,1)S(1)}, bf16[8,8,1408]{2,1,0:T(8,128)(2,1)S(1)}, u32[]{:S(2)}, u32[]{:S(2)}) collective-permute-start(bf16[8,8,1408]{2,1,0:T(8,128)(2,1)S(1)} %all_to_all.21.second), channel_id=1, source_target_pairs={{0,1},{1,0},{2,3},{3,2},{4,5},{5,4},{6,7},{7,6},{8,9},{9,8},{10,11... | collective-permute-start | bytes 540680 | tf_op jit(solution)/shard_map/ppermute | solution.py:506
  40.1 1.3 %collective-permute-start.2 = (bf16[8,8,768]{2,1,0:T(8,128)(2,1)S(1)}, bf16[8,8,768]{2,1,0:T(8,128)(2,1)S(1)}, u32[]{:S(2)}, u32[]{:S(2)}) collective-permute-start(bf16[8,8,768]{2,1,0:T(8,128)(2,1)S(1)} %get-tuple-element.33), channel_id=1, source_target_pairs={{0,1},{1,0},{2,3},{3,2},{4,5},{5,4},{6,7},{7,6},{8,9},{9,8},{10,11... | collective-permute-start | bytes 294920 | tf_op jit(solution)/shard_map/ppermute | solution.py:506
  41.5 28.6 %copy-start.9 = (bf16[1,64,1280]{2,1,0:T(8,128)(2,1)S(1)}, bf16[1,64,1280]{2,1,0:T(8,128)(2,1)}, u32[]{:S(2)}) copy-start(bf16[1,64,1280]{2,1,0:T(8,128)(2,1)} %param.13) | copy-start | bytes 491524
  62.7 7.7 %collective-permute-start.3 = (bf16[16,4,768]{2,1,0:T(4,128)(2,1)S(1)}, bf16[16,4,768]{2,1,0:T(4,128)(2,1)S(1)}, u32[]{:S(2)}, u32[]{:S(2)}) collective-permute-start(bf16[16,4,768]{2,1,0:T(4,128)(2,1)S(1)} %all_to_all.23.fourth), channel_id=1, source_target_pairs={{0,1},{1,0},{2,3},{3,2},{4,5},{5,4},{6,7},{7,6},{8,9},{9,8},{10,11... | collective-permute-start | bytes 294920 | tf_op jit(solution)/shard_map/ppermute | solution.py:506

commit v17 on v16

--- a/solution.py
+++ b/solution.py
@@ -11,6 +11,7 @@
 PLACE = ("chip", "core")
 SEQ = ("half", *PLACE)
 BOTH = ("dp", *SEQ)
+HALF = ("dp", *PLACE)
 HALF_CORE = ("dp", "chip")
 SAME_CORE = ("dp", "half", "chip")
 STATS = 128
@@ -324,10 +325,12 @@
     second[...] = block
 
 
-def pack_kernel(blocks, out):
+def pack_kernel(own, beside, out):
+    here = lax.axis_index("half")
     for group in range(out.shape[0]):
+        block = jnp.where(here == group, own[...], beside[...])
         for place in range(out.shape[1]):
-            out[group, place] = blocks[group]
+            out[group, place] = block
 
 
 def hidden_kernel(
@@ -339,7 +342,6 @@
     in_right,
     out_left,
     third,
-    third_other,
     pair_out,
     ranks_out,
 ):
@@ -402,26 +404,17 @@
     pair_out[1] = hidden_low
     ranks_out[0] = up.astype(jnp.float32)
     ranks_out[1] = back.astype(jnp.float32)
-    slot_term = dot_plain(preact_grad.astype(jnp.bfloat16), base_in[...])
+    slot_term = dot_plain(preact_grad.astype(jnp.bfloat16), base_in[...]).astype(jnp.bfloat16)
     down = to_rank(preact_grad, in_right)
     value = to_rank(hidden_low, out_left)
-    ranks = jnp.concatenate([down, value], axis=1)
+    ranks = jnp.concatenate([down, value], axis=1).astype(jnp.bfloat16)
     for half in range(groups):
         columns = slice(half * width, (half + 1) * width)
-
-        def block(place):
+        for place in range(places):
             taken = slice(place * rows, (place + 1) * rows)
-            return jnp.concatenate([slot_term[taken, columns], ranks[taken]], axis=1)
-
-        for chip in range(places // 2):
-            even, odd = block(2 * chip), block(2 * chip + 1)
-            number = half * (places // 2) + chip
-            third[number] = jnp.where(first_core, even, odd).astype(jnp.bfloat16)
-            third_other[number] = jnp.where(first_core, odd, even).astype(jnp.bfloat16)
-
-
-def add_kernel(own, other, out):
-    out[...] = (own[...].astype(jnp.float32) + other[...].astype(jnp.float32)).astype(out.dtype)
+            block = half * places + place
+            third[block, :, :width] = slot_term[taken, columns]
+            third[block, :, width:] = ranks[taken]
 
 
 def outer_kernel(owned, left_rows, right_rows, *outs):
@@ -444,9 +437,9 @@
         out[...] = jnp.sum(taken, axis=0).astype(out.dtype)
 
 
-def finish_kernel(groups, own, others, in_left, inputs, stats, fourth, ranks_out):
+def finish_kernel(groups, own, other, in_left, inputs, stats, fourth, ranks_out):
     owned, rank, width = in_left.shape
-    summed = own[...] + others[1 - lax.axis_index("half")].astype(jnp.float32)
+    summed = own[...] + other[...].astype(jnp.float32)
     ranks = summed[:, width:].astype(jnp.bfloat16).astype(jnp.float32)
     ranks_out[0] = ranks[:, :rank]
     ranks_out[1] = ranks[:, rank:]
@@ -502,22 +495,22 @@
         copy.wait()
 
 
-def swap_cores(blocks):
-    return lax.ppermute(blocks, "core", [(0, 1), (1, 0)])
+def swap(blocks, axis):
+    return lax.ppermute(blocks, axis, [(0, 1), (1, 0)])
 
 
 def to_group(block, groups):
     chips = lax.axis_size("chip")
-    blocks = lax.all_gather(block, "half", axis=0)
+    beside = swap(block, "half")
     (blocks,) = call(
         pack_kernel,
         [array(block.dtype, groups, chips, *block.shape)],
-        [blocks],
+        [block, beside],
         FLOPS_BESIDE_EXCHANGE,
     )
     blocks = blocks.reshape(groups * chips, *block.shape)
     blocks = lax.all_to_all(blocks, HALF_CORE, 0, 0, tiled=True)
-    return blocks, swap_cores(blocks)
+    return blocks, swap(blocks, "core")
 
 
 def call(kernel, outs, args, flops, space=pltpu.VMEM, scratch=()):
@@ -582,7 +575,7 @@
         [early, image_rows, cot_rows, router],
         6 * count * slots * width + FLOPS_BESIDE_EXCHANGE,
     )
-    other = swap_cores(other)
+    other = swap(other, "core")
     (first,) = call(
         functools.partial(merge_kernel, slice_width), [first], [own, other], FLOPS_BESIDE_EXCHANGE
     )
@@ -600,36 +593,28 @@
     )
     second, second_other = to_group(second, groups)
     total_rows = groups * members
-    third = array(low, ring // 2, rows, slice_width + 2 * rank)
-    third, other, pair, hidden_ranks = call(
+    third, pair, hidden_ranks = call(
         functools.partial(hidden_kernel, groups),
         [
-            third,
-            third,
+            array(low, ring, rows, slice_width + 2 * rank),
             array(full, 2, total_rows, hidden),
             array(full, 2, total_rows, rank),
         ],
         [second, second_other, base_in, base_out, in_right, out_left],
         6 * total_rows * hidden * (width + owned * rank),
     )
-    (third,) = call(
-        add_kernel,
-        [array(third.dtype, *third.shape)],
-        [third, swap_cores(other)],
-        FLOPS_BESIDE_EXCHANGE,
-    )
-    third = lax.all_to_all(third, HALF_CORE, 0, 0, tiled=True)
+    third = lax.all_to_all(third, HALF, 0, 0, tiled=True)
     own, other = call(
         halves_kernel,
         [array(kind, rows, slice_width + 2 * rank) for kind in (full, low)],
         [third],
         0,
     )
-    others = lax.all_gather(other, "half", axis=0)
+    other = swap(other, "half")
     fourth, ranks = call(
         functools.partial(finish_kernel, groups),
         [array(low, devices // 2, owned, slice_width + STATS), array(full, 2, rows, rank)],
-        [own, others, in_left, inputs, stats],
+        [own, other, in_left, inputs, stats],
         2 * rows * owned * rank * slice_width,
     )
     fourth, combine, pair, hidden_ranks = lax.optimization_barrier(
@@ -654,11 +639,14 @@
         [ranks, lows],
         4 * owned * rank * slice_width * rows,
     )
+    outs = (grad_in_left, grad_in_right, grad_out_left, grad_out_right)
+    fourth, mixing, outs = lax.optimization_barrier((fourth, mixing, outs))
+    grad_in_left, grad_in_right, grad_out_left, grad_out_right = outs
     parts = math.gcd(4, count // 16)
     (token_grad,) = call(
         functools.partial(tokens_kernel, groups),
         [array(low, count, width)],
-        [fourth, swap_cores(fourth), image_rows, router, logits, mixing],
+        [fourth, swap(fourth, "core"), image_rows, router, logits, mixing],
         6 * count * slots * width,
         pltpu.HBM,
         [pltpu.VMEM((count, width), low), pltpu.SemaphoreType.DMA((parts,))],

time: 72.4 us -> 69.4 us (0.959)
  blocking collectives: 47.9 us -> 31.4 us
  waiting for transfers between devices: 3.36 us -> 10.1 us
  starting transfers between devices: 8.47 us -> 14.2 us
    all_gather x2 -> x0, blocking collectives: 8.5 us -> none  [the longest x1 4.25 us: local(): others = lax.all_gather(other, 'half', axis=0)]
    all_to_all x2 -> x1, blocking collectives: 16.7 us -> 8.96 us  [local(): third = lax.all_to_all(third, HALF, 0, 0, tiled=True)]
    ppermute x4 -> x5, waiting for transfers between devices: 3.36 us -> 7.71 us  [swap(): return lax.ppermute(blocks, axis, [(0, 1), (1, 0)])]
    all_to_all x0 -> x1, starting transfers between devices: none -> 3.51 us  [local(): fourth = lax.all_to_all(fourth, SAME_CORE, 0, 0, tiled=True)]
    all_to_all x0 -> x1, waiting for transfers between devices: none -> 2.41 us  [local(): fourth = lax.all_to_all(fourth, SAME_CORE, 0, 0, tiled=True)]
    ppermute x4 -> x5, starting transfers between devices: 8.47 us -> 10.7 us  [swap(): return lax.ppermute(blocks, axis, [(0, 1), (1, 0)])]
    pallas_call x13 -> x12, Pallas kernels: 10.3 us -> 10.9 us  [call(): pl.pallas_call(kernel, out_shape=outs, in_specs=[pl.BlockSpec(memory_spac...]
  transfers between devices with their start and end apart: 4 -> 6, of which waited for: 3 -> 6; matrix products, arithmetic and copies ran while one was open for 0% -> 0% of each run, Pallas kernels for 6% -> 6%
where the time goes in v17:
time: 69.4 us; the launch traced here: 68.8 us
  blocking collectives  31.4 us (45%)
  starting transfers between devices  14.2 us (20%)
  Pallas kernels  10.9 us (16%)
  waiting for transfers between devices  10.1 us (15%)
  local copies, waits for them, and re-layouts  1.4 us (2%)
  between operations  0.74 us (1%)
    all_to_all x1, blocking collectives, local(): first = lax.all_to_all(first, SAME_CORE, 0, 0, tiled=True)  14.5 us
    pallas_call x12, Pallas kernels, call(): pl.pallas_call(kernel, out_shape=outs, in_specs=[pl.BlockSpec(memory_spac...  10.9 us
    ppermute x5, starting transfers between devices, swap(): return lax.ppermute(blocks, axis, [(0, 1), (1, 0)])  10.7 us
    all_to_all x1, blocking collectives, local(): third = lax.all_to_all(third, HALF, 0, 0, tiled=True)  8.96 us
    all_to_all x1, blocking collectives, to_group(): blocks = lax.all_to_all(blocks, HALF_CORE, 0, 0, tiled=True)  7.93 us
    ppermute x5, waiting for transfers between devices, swap(): return lax.ppermute(blocks, axis, [(0, 1), (1, 0)])  7.71 us
    all_to_all x1, starting transfers between devices, local(): fourth = lax.all_to_all(fourth, SAME_CORE, 0, 0, tiled=True)  3.51 us
    all_to_all x1, waiting for transfers between devices, local(): fourth = lax.all_to_all(fourth, SAME_CORE, 0, 0, tiled=True)  2.41 us
  transfers between devices with their start and end apart: 6, of which 6 were waited for; matrix products, arithmetic and copies ran while one was open for 0% of the time, Pallas kernels for 6%

profile of v17, /device:TPU:1, one launch (start us, length us, event | category | flops | bytes accessed | tf_op | source)
XLA Modules:
  0.0 68.8 jit_solution(2572272070489786590)
XLA Ops:
  0.6 0.0 copy-start.8
  0.6 0.0 copy-start.6
  0.7 0.0 copy-start.5
  0.7 0.9 %copy-done.8 = bf16[1280,64]{0,1:T(8,128)(2,1)S(1)} copy-done((bf16[1280,64]{0,1:T(8,128)(2,1)S(1)}, bf16[1280,64]{0,1:T(8,128)(2,1)}, u32[]{:S(2)}) %copy-start.8) | copy-done | bytes 163864
  1.5 0.3 copy-done.6
  1.8 0.2 copy-done.5
  2.0 1.0 %shard_map.138 = (bf16[16,4,1408]{2,1,0:T(4,128)(2,1)S(1)}, bf16[16,4,1408]{2,1,0:T(4,128)(2,1)S(1)}, f32[64,256]{1,0:T(8,128)S(1)}, f32[64,256]{1,0:T(8,128)S(1)}) custom-call(f32[8,128]{1,0:T(8,128)S(1)} %shard_map.137._, bf16[256,1280]{1,0:T(8,128)(2,1)S(1)} %bitcast.15, bf16[256,1280]{1,0:T(8,128)(2,1)S(1)} %bitcast.17, bf16[64,1280]{1,0:T(8,128)(2,1)S(1)} %bitcast.20), custom_call_target="tpu_custom_call" | custom-call | flops 10125829120 | bytes 1970176 | tf_op jit(solution)/shard_map/pallas_call | solution.py:519
  3.0 0.1 collective-permute-start
  3.2 1.4 %collective-permute-done.other = bf16[16,4,1408]{2,1,0:T(4,128)(2,1)S(1)} collective-permute-done((bf16[16,4,1408]{2,1,0:T(4,128)(2,1)S(1)}, bf16[16,4,1408]{2,1,0:T(4,128)(2,1)S(1)}, u32[]{:S(2)}, u32[]{:S(2)}) %collective-permute-start) | collective-permute-done | bytes 180256 | tf_op jit(solution)/shard_map/ppermute | solution.py:499
  4.5 0.0 copy-start.2
  4.5 0.0 copy-start.7
  4.5 0.3 shard_map.139
  4.8 14.5 %all_to_all.20.first = bf16[16,4,1408]{2,1,0:T(4,128)(2,1)S(1)} all-to-all(bf16[16,4,1408]{2,1,0:T(4,128)(2,1)S(1)} %shard_map.139), channel_id=1, replica_groups=mesh['dp'=2,'half'=2,'chip'=4,'core'=2] {'dp','half','chip'}, dimensions={0} | all-to-all | bytes 360448 | tf_op jit(solution)/shard_map/all_to_all | solution.py:582
  19.3 0.0 copy-done.2
  19.3 0.0 copy-done.7
  19.4 0.5 shard_map.140
  19.9 0.0 copy-start
  19.9 0.0 copy-start.1
  19.9 0.0 copy-start.3
  19.9 0.0 copy-start.4
  20.0 1.6 %collective-permute-start.1 = (bf16[8,1408]{1,0:T(8,128)(2,1)S(1)}, bf16[8,1408]{1,0:T(8,128)(2,1)S(1)}, u32[]{:S(2)}, u32[]{:S(2)}) collective-permute-start(bf16[8,1408]{1,0:T(8,128)(2,1)S(1)} %get-tuple-element.36.own), channel_id=1, source_target_pairs={{0,8},{8,0},{1,9},{9,1},{2,10},{10,2},{3,11},{11,3},{4,12},{12,4},... | collective-permute-start | bytes 67592 | tf_op jit(solution)/shard_map/ppermute | solution.py:499
  21.5 2.0 %collective-permute-done.1.beside = bf16[8,1408]{1,0:T(8,128)(2,1)S(1)} collective-permute-done((bf16[8,1408]{1,0:T(8,128)(2,1)S(1)}, bf16[8,1408]{1,0:T(8,128)(2,1)S(1)}, u32[]{:S(2)}, u32[]{:S(2)}) %collective-permute-start.1) | collective-permute-done | bytes 22560 | tf_op jit(solution)/shard_map/ppermute | solution.py:499
  23.6 7.9 %all_to_all.21.second = bf16[8,8,1408]{2,1,0:T(8,128)(2,1)S(1)} all-to-all(bf16[8,8,1408]{2,1,0:T(8,128)(2,1)S(1)} %bitcast.19), channel_id=1, replica_groups=mesh['dp'=2,'half'=2,'chip'=4,'core'=2] {'dp','chip'}, dimensions={0} | all-to-all | bytes 360448 | tf_op jit(solution)/shard_map/all_to_all | solution.py:512
  31.5 4.3 %collective-permute-start.2 = (bf16[8,8,1408]{2,1,0:T(8,128)(2,1)S(1)}, bf16[8,8,1408]{2,1,0:T(8,128)(2,1)S(1)}, u32[]{:S(2)}, u32[]{:S(2)}) collective-permute-start(bf16[8,8,1408]{2,1,0:T(8,128)(2,1)S(1)} %all_to_all.21.second), channel_id=1, source_target_pairs={{0,1},{1,0},{2,3},{3,2},{4,5},{5,4},{6,7},{7,6},{8,9},{9,8},{10,11... | collective-permute-start | bytes 540680 | tf_op jit(solution)/shard_map/ppermute | solution.py:499
  35.9 1.0 %collective-permute-done.2.second_other = bf16[8,8,1408]{2,1,0:T(8,128)(2,1)S(1)} collective-permute-done((bf16[8,8,1408]{2,1,0:T(8,128)(2,1)S(1)}, bf16[8,8,1408]{2,1,0:T(8,128)(2,1)S(1)}, u32[]{:S(2)}, u32[]{:S(2)}) %collective-permute-start.2) | collective-permute-done | bytes 180256 | tf_op jit(solution)/shard_map/ppermute | solution.py:499
  36.9 0.0 copy-done
  36.9 0.0 copy-done.1
  36.9 0.0 copy-done.3
  36.9 0.0 copy-done.4
  36.9 2.3 %shard_map.142 = (bf16[16,8,768]{2,1,0:T(8,128)(2,1)S(1)}, f32[2,64,320]{2,1,0:T(8,128)S(1)}, f32[2,64,64]{2,1,0:T(8,128)S(1)}) custom-call(bf16[8,8,1408]{2,1,0:T(8,128)(2,1)S(1)} %all_to_all.21.second, bf16[8,8,1408]{2,1,0:T(8,128)(2,1)S(1)} %collective-permute-done.2.second_other, bf16[320,1280]{1,0:T(8,128)(2,1)S(1)} %bitcast.14, ...), custom_call_target="tpu_custom_call" | custom-call | flops 188743680 | bytes 5013504 | tf_op jit(solution)/shard_map/pallas_call | solution.py:519
  39.3 0.0 copy-start.9
  39.3 9.0 %all_to_all.22.third = bf16[16,8,768]{2,1,0:T(8,128)(2,1)S(1)} all-to-all(bf16[16,8,768]{2,1,0:T(8,128)(2,1)S(1)} %get-tuple-element.37), channel_id=1, replica_groups=mesh['dp'=2,'half'=2,'chip'=4,'core'=2] {'dp','chip','core'}, dimensions={0} | all-to-all | bytes 393216 | tf_op jit(solution)/shard_map/all_to_all | solution.py:606
  48.3 1.2 %collective-permute-start.3 = (bf16[8,768]{1,0:T(8,128)(2,1)S(1)}, bf16[8,768]{1,0:T(8,128)(2,1)S(1)}, u32[]{:S(2)}, u32[]{:S(2)}) collective-permute-start(bf16[8,768]{1,0:T(8,128)(2,1)S(1)} %get-tuple-element.39), channel_id=1, source_target_pairs={{0,8},{8,0},{1,9},{9,1},{2,10},{10,2},{3,11},{11,3},{4,12},{12,4},... | collective-permute-start | bytes 36872 | tf_op jit(solution)/shard_map/ppermute | solution.py:499
  49.4 2.3 %collective-permute-done.3.other = bf16[8,768]{1,0:T(8,128)(2,1)S(1)} collective-permute-done((bf16[8,768]{1,0:T(8,128)(2,1)S(1)}, bf16[8,768]{1,0:T(8,128)(2,1)S(1)}, u32[]{:S(2)}, u32[]{:S(2)}) %collective-permute-start.3) | collective-permute-done | bytes 12320 | tf_op jit(solution)/shard_map/ppermute | solution.py:499
  51.8 0.9 %shard_map.144 = (bf16[16,4,768]{2,1,0:T(4,128)(2,1)}, f32[2,8,64]{2,1,0:T(8,128)S(1)}) custom-call(f32[8,768]{1,0:T(8,128)S(1)} %get-tuple-element.38.own, bf16[8,768]{1,0:T(8,128)(2,1)S(1)} %collective-permute-done.3.other, bf16[4,64,640]{2,1,0:T(8,128)(2,1)S(1)} %bitcast.13, f32[8,640]{1,0:T(8,128)S(1)} %get-tuple-element.40.inputs, ...), custom_call_target="tpu_custom_call" | custom-call | flops 2621440 | bytes 491520 | tf_op jit(solution)/shard_map/pallas_call | solution.py:519
  52.7 3.5 %all-to-all-start.3 = ((bf16[16,4,768]{2,1,0:T(4,128)(2,1)}), bf16[16,4,768]{2,1,0:T(4,128)(2,1)S(1)}, u32[]{:S(2)}, u32[]{:S(2)}) async-start(bf16[16,4,768]{2,1,0:T(4,128)(2,1)} %get-tuple-element.46), calls=%async_computation.3 | async-start | bytes 196608 | tf_op jit(solution)/shard_map/all_to_all | solution.py:623
  56.2 1.2 %shard_map.146 = (bf16[4,64,640]{2,1,0:T(8,128)(2,1)}, bf16[4,64,640]{2,1,0:T(8,128)(2,1)}) custom-call(f32[2,8,64]{2,1,0:T(8,128)S(1)} %get-tuple-element.48.left_rows, bf16[2,8,640]{2,1,0:T(8,128)(2,1)S(1)} %get-tuple-element.49.right_rows), custom_call_target="tpu_custom_call" | custom-call | flops 5242880 | bytes 679936 | tf_op jit(solution)/shard_map/pallas_call | solution.py:519
  57.4 2.5 %shard_map.147 = (bf16[32,64,320]{2,1,0:T(8,128)(2,1)}, bf16[32,64,320]{2,1,0:T(8,128)(2,1)}) custom-call(f32[2,64,64]{2,1,0:T(8,128)S(1)} %get-tuple-element.51.left_rows, f32[2,64,320]{2,1,0:T(8,128)S(1)} %get-tuple-element.52.right_rows), custom_call_target="tpu_custom_call" | custom-call | flops 20971520 | bytes 2818048 | tf_op jit(solution)/shard_map/pallas_call | solution.py:519
  59.9 0.0 copy-done.9
  59.9 0.4 shard_map.145.mixing
  60.3 2.4 %all-to-all-done.3.fourth = bf16[16,4,768]{2,1,0:T(4,128)(2,1)S(1)} async-done(((bf16[16,4,768]{2,1,0:T(4,128)(2,1)}), bf16[16,4,768]{2,1,0:T(4,128)(2,1)S(1)}, u32[]{:S(2)}, u32[]{:S(2)}) %all-to-all-start.3) | async-done | bytes 98336 | tf_op jit(solution)/shard_map/all_to_all | solution.py:623
  62.7 3.5 %collective-permute-start.4 = (bf16[16,4,768]{2,1,0:T(4,128)(2,1)S(1)}, bf16[16,4,768]{2,1,0:T(4,128)(2,1)S(1)}, u32[]{:S(2)}, u32[]{:S(2)}) collective-permute-start(bf16[16,4,768]{2,1,0:T(4,128)(2,1)S(1)} %all-to-all-done.3.fourth), channel_id=1, source_target_pairs={{0,1},{1,0},{2,3},{3,2},{4,5},{5,4},{6,7},{7,6},{8,9},{9,8},{10,11... | collective-permute-start | bytes 294920 | tf_op jit(solution)/shard_map/ppermute | solution.py:499
  66.2 0.9 %collective-permute-done.4.fourth_other = bf16[16,4,768]{2,1,0:T(4,128)(2,1)S(1)} collective-permute-done((bf16[16,4,768]{2,1,0:T(4,128)(2,1)S(1)}, bf16[16,4,768]{2,1,0:T(4,128)(2,1)S(1)}, u32[]{:S(2)}, u32[]{:S(2)}) %collective-permute-start.4) | collective-permute-done | bytes 98336 | tf_op jit(solution)/shard_map/ppermute | solution.py:499
  67.1 1.7 %shard_map.148 = bf16[256,1280]{1,0:T(8,128)(2,1)} custom-call(bf16[16,4,768]{2,1,0:T(4,128)(2,1)S(1)} %all-to-all-done.3.fourth, bf16[16,4,768]{2,1,0:T(4,128)(2,1)S(1)} %collective-permute-done.4.fourth_other, bf16[256,1280]{1,0:T(8,128)(2,1)S(1)} %bitcast.16, bf16[64,1280]{1,0:T(8,128)(2,1)S(1)} %bitcast.21, f32[64,256]{1,0:T(8,128)S(1)} %get-tuple-element.57.logits, ...), custom_call_target="tpu_custom_call" | custom-call | flops 125829120 | bytes 1802240 | tf_op jit(solution)/shard_map/pallas_call | solution.py:519
  (3 shorter events, 0.0 us)
Async XLA Ops:
  0.6 0.9 %copy-start.8 = (bf16[1280,64]{0,1:T(8,128)(2,1)S(1)}, bf16[1280,64]{0,1:T(8,128)(2,1)}, u32[]{:S(2)}) copy-start(bf16[1280,64]{0,1:T(8,128)(2,1)} %param.12) | copy-start | bytes 491524
  0.6 1.2 %copy-start.6 = (bf16[1,256,1280]{2,1,0:T(8,128)(2,1)S(1)}, bf16[1,256,1280]{2,1,0:T(8,128)(2,1)}, u32[]{:S(2)}) copy-start(bf16[1,256,1280]{2,1,0:T(8,128)(2,1)} %param.11) | copy-start | bytes 1966084
  0.7 1.4 %copy-start.5 = (bf16[1,256,1280]{2,1,0:T(8,128)(2,1)S(1)}, bf16[1,256,1280]{2,1,0:T(8,128)(2,1)}, u32[]{:S(2)}) copy-start(bf16[1,256,1280]{2,1,0:T(8,128)(2,1)} %param.10) | copy-start | bytes 1966084
  3.0 1.5 %collective-permute-start = (bf16[16,4,1408]{2,1,0:T(4,128)(2,1)S(1)}, bf16[16,4,1408]{2,1,0:T(4,128)(2,1)S(1)}, u32[]{:S(2)}, u32[]{:S(2)}) collective-permute-start(bf16[16,4,1408]{2,1,0:T(4,128)(2,1)S(1)} %get-tuple-element.35), channel_id=1, source_target_pairs={{0,1},{1,0},{2,3},{3,2},{4,5},{5,4},{6,7},{7,6},{8,9},{9,8},{10,11... | collective-permute-start | bytes 540680 | tf_op jit(solution)/shard_map/ppermute | solution.py:499
  4.5 14.8 %copy-start.2 = (bf16[4,640,64]{1,2,0:T(8,128)(2,1)S(1)}, bf16[4,640,64]{1,2,0:T(8,128)(2,1)}, u32[]{:S(2)}) copy-start(bf16[4,640,64]{1,2,0:T(8,128)(2,1)} %param.16) | copy-start | bytes 983044
  4.5 14.8 %copy-start.7 = (bf16[4,64,640]{2,1,0:T(8,128)(2,1)S(1)}, bf16[4,64,640]{2,1,0:T(8,128)(2,1)}, u32[]{:S(2)}) copy-start(bf16[4,64,640]{2,1,0:T(8,128)(2,1)} %out_right.1) | copy-start | bytes 983044
  19.9 17.0 %copy-start = (bf16[32,64,320]{2,1,0:T(8,128)(2,1)S(1)}, bf16[32,64,320]{2,1,0:T(8,128)(2,1)}, u32[]{:S(2)}) copy-start(bf16[32,64,320]{2,1,0:T(8,128)(2,1)} %in_right.1) | copy-start | bytes 3932164
  19.9 17.0 %copy-start.1 = (bf16[32,320,64]{1,2,0:T(8,128)(2,1)S(1)}, bf16[32,320,64]{1,2,0:T(8,128)(2,1)}, u32[]{:S(2)}) copy-start(bf16[32,320,64]{1,2,0:T(8,128)(2,1)} %param.18) | copy-start | bytes 3932164
  19.9 17.0 %copy-start.3 = (bf16[1280,320]{0,1:T(8,128)(2,1)S(1)}, bf16[1280,320]{0,1:T(8,128)(2,1)}, u32[]{:S(2)}) copy-start(bf16[1280,320]{0,1:T(8,128)(2,1)} %param.14) | copy-start | bytes 2457604
  19.9 17.0 %copy-start.4 = (bf16[320,1280]{1,0:T(8,128)(2,1)S(1)}, bf16[320,1280]{1,0:T(8,128)(2,1)}, u32[]{:S(2)}) copy-start(bf16[320,1280]{1,0:T(8,128)(2,1)} %base_out.1) | copy-start | bytes 2457604
  20.0 3.6 %collective-permute-start.1 = (bf16[8,1408]{1,0:T(8,128)(2,1)S(1)}, bf16[8,1408]{1,0:T(8,128)(2,1)S(1)}, u32[]{:S(2)}, u32[]{:S(2)}) collective-permute-start(bf16[8,1408]{1,0:T(8,128)(2,1)S(1)} %get-tuple-element.36.own), channel_id=1, source_target_pairs={{0,8},{8,0},{1,9},{9,1},{2,10},{10,2},{3,11},{11,3},{4,12},{12,4},... | collective-permute-start | bytes 67592 | tf_op jit(solution)/shard_map/ppermute | solution.py:499
  31.5 5.4 %collective-permute-start.2 = (bf16[8,8,1408]{2,1,0:T(8,128)(2,1)S(1)}, bf16[8,8,1408]{2,1,0:T(8,128)(2,1)S(1)}, u32[]{:S(2)}, u32[]{:S(2)}) collective-permute-start(bf16[8,8,1408]{2,1,0:T(8,128)(2,1)S(1)} %all_to_all.21.second), channel_id=1, source_target_pairs={{0,1},{1,0},{2,3},{3,2},{4,5},{5,4},{6,7},{7,6},{8,9},{9,8},{10,11... | collective-permute-start | bytes 540680 | tf_op jit(solution)/shard_map/ppermute | solution.py:499
  39.3 20.7 %copy-start.9 = (bf16[1,64,1280]{2,1,0:T(8,128)(2,1)S(1)}, bf16[1,64,1280]{2,1,0:T(8,128)(2,1)}, u32[]{:S(2)}) copy-start(bf16[1,64,1280]{2,1,0:T(8,128)(2,1)} %param.13) | copy-start | bytes 491524
  48.3 3.5 %collective-permute-start.3 = (bf16[8,768]{1,0:T(8,128)(2,1)S(1)}, bf16[8,768]{1,0:T(8,128)(2,1)S(1)}, u32[]{:S(2)}, u32[]{:S(2)}) collective-permute-start(bf16[8,768]{1,0:T(8,128)(2,1)S(1)} %get-tuple-element.39), channel_id=1, source_target_pairs={{0,8},{8,0},{1,9},{9,1},{2,10},{10,2},{3,11},{11,3},{4,12},{12,4},... | collective-permute-start | bytes 36872 | tf_op jit(solution)/shard_map/ppermute | solution.py:499
  52.7 10.0 %all-to-all-start.3 = ((bf16[16,4,768]{2,1,0:T(4,128)(2,1)}), bf16[16,4,768]{2,1,0:T(4,128)(2,1)S(1)}, u32[]{:S(2)}, u32[]{:S(2)}) async-start(bf16[16,4,768]{2,1,0:T(4,128)(2,1)} %get-tuple-element.46), calls=%async_computation.3 | async-start | bytes 196608 | tf_op jit(solution)/shard_map/all_to_all | solution.py:623
  62.7 4.4 %collective-permute-start.4 = (bf16[16,4,768]{2,1,0:T(4,128)(2,1)S(1)}, bf16[16,4,768]{2,1,0:T(4,128)(2,1)S(1)}, u32[]{:S(2)}, u32[]{:S(2)}) collective-permute-start(bf16[16,4,768]{2,1,0:T(4,128)(2,1)S(1)} %all-to-all-done.3.fourth), channel_id=1, source_target_pairs={{0,1},{1,0},{2,3},{3,2},{4,5},{5,4},{6,7},{7,6},{8,9},{9,8},{10,11... | collective-permute-start | bytes 294920 | tf_op jit(solution)/shard_map/ppermute | solution.py:499

commit v18 on v17

--- a/solution.py
+++ b/solution.py
@@ -192,6 +192,10 @@
         "gjr,gjd->jrd", value_own, grads_own, preferred_element_type=jnp.float32
     ).astype(jnp.bfloat16)
     return (token_grad[None], grad_in_left, grad_in_right, grad_out_left, grad_out_right)
+
+
+def dot_turned(left, right):
+    return dot_last(right, left).T
 
 
 def dot_plain(left, right):
@@ -333,10 +337,42 @@
             out[group, place] = block
 
 
+def factor_products(blocks, in_right, out_left, core):
+    members, rank, hidden = in_right.shape
+    rows = blocks.shape[1]
+    chips = blocks.shape[0] // 2
+    owned = members // (2 * chips)
+    start = blocks.shape[2] - 2 * rank
+    ranks = jnp.zeros((chips * rows, 2 * rank), jnp.float32)
+    for half in range(2):
+        part = blocks[half * chips : (half + 1) * chips, :, start:].astype(jnp.float32)
+        ranks = ranks + part.reshape(ranks.shape)
+    out = []
+    for number, table in enumerate((in_right, out_left)):
+        value = ranks[:, number * rank : (number + 1) * rank]
+        value = value.astype(jnp.bfloat16).astype(jnp.float32)
+        taken = []
+        for chip in range(chips):
+            own = own_block(value[chip * rows : (chip + 1) * rows], owned)
+            part = table[pl.ds((2 * chip + core) * owned, owned)].reshape(owned * rank, hidden)
+            taken.append(dot_plain(own, part))
+        out.append((value, jnp.concatenate(taken, axis=0)))
+    return out
+
+
+def near_kernel(second, in_right, out_left, ranks_out, products_out):
+    found = factor_products(second, in_right, out_left, lax.axis_index("core"))
+    for number, (value, product) in enumerate(found):
+        ranks_out[number] = value
+        products_out[number] = product
+
+
 def hidden_kernel(
     groups,
     second,
     second_other,
+    near_ranks,
+    near_products,
     base_in,
     base_out,
     in_right,
@@ -365,13 +401,13 @@
             parts.append(jnp.concatenate(taken, axis=0))
         return parts
 
-    def low_rank(value, table):
-        value = value.astype(jnp.float32)
+    def in_order(near, far):
         taken = []
-        for place in range(places):
-            own = own_block(value[place * rows : (place + 1) * rows], owned)
-            part = table[place * owned : (place + 1) * owned].reshape(owned * rank, hidden)
-            taken.append(dot_plain(own, part))
+        for chip in range(places // 2):
+            own = near[chip * rows : (chip + 1) * rows]
+            other = far[chip * rows : (chip + 1) * rows]
+            taken.append(jnp.where(first_core, own, other))
+            taken.append(jnp.where(first_core, other, own))
         return jnp.concatenate(taken, axis=0)
 
     def to_rank(value, table):
@@ -382,16 +418,15 @@
             taken.append(from_own_block(wide, owned))
         return jnp.concatenate(taken, axis=0)
 
-    ranks = functools.reduce(jnp.add, gathered(slice(2 * width, 2 * width + 2 * rank)))
-    up, back = ranks[:, :rank].astype(jnp.bfloat16), ranks[:, rank:].astype(jnp.bfloat16)
-    preact = low_rank(up, in_right)
+    far = factor_products(second_other, in_right, out_left, 1 - lax.axis_index("core"))
+    up, back = [in_order(near_ranks[number], far[number][0]) for number in range(2)]
+    preact, hidden_grad = [in_order(near_products[number], far[number][1]) for number in range(2)]
     for half, part in enumerate(gathered(slice(0, width))):
         columns = slice(half * width, (half + 1) * width)
-        preact = preact + dot_last(part.astype(jnp.bfloat16), base_in[:, columns])
-    hidden_grad = low_rank(back, out_left)
+        preact = preact + dot_turned(part.astype(jnp.bfloat16), base_in[:, columns])
     for half, part in enumerate(gathered(slice(width, 2 * width))):
         columns = slice(half * width, (half + 1) * width)
-        hidden_grad = hidden_grad + dot_last(part.astype(jnp.bfloat16), base_out[:, columns])
+        hidden_grad = hidden_grad + dot_turned(part.astype(jnp.bfloat16), base_out[:, columns])
     root = 0.7978845608028654
     bent = jnp.tanh(root * (preact + 0.044715 * (preact * preact * preact)))
     hidden_value = 0.5 * preact * (1.0 + bent)
@@ -402,8 +437,8 @@
     preact_grad = (hidden_grad * slope).astype(jnp.bfloat16).astype(jnp.float32)
     pair_out[0] = preact_grad
     pair_out[1] = hidden_low
-    ranks_out[0] = up.astype(jnp.float32)
-    ranks_out[1] = back.astype(jnp.float32)
+    ranks_out[0] = up
+    ranks_out[1] = back
     slot_term = dot_plain(preact_grad.astype(jnp.bfloat16), base_in[...]).astype(jnp.bfloat16)
     down = to_rank(preact_grad, in_right)
     value = to_rank(hidden_low, out_left)
@@ -456,7 +491,29 @@
             fourth[group * (fourth.shape[0] // groups) + place] = rows
 
 
-def tokens_kernel(groups, fourth, fourth_other, tokens, router, logits, mixing, out_far, out, sent):
+def tokens_kernel(
+    groups,
+    fourth,
+    fourth_other,
+    tokens,
+    router,
+    logits,
+    mixing,
+    grad_left,
+    grad_right,
+    out_far,
+    grad_left_far,
+    grad_right_far,
+    out,
+    sent,
+    grads_sent,
+):
+    copies = [
+        pltpu.make_async_copy(grad_left, grad_left_far, grads_sent.at[0]),
+        pltpu.make_async_copy(grad_right, grad_right_far, grads_sent.at[1]),
+    ]
+    for copy in copies:
+        copy.start()
     blocks, owned, _ = fourth.shape
     chips = blocks // groups
     width = tokens.shape[1] // groups
@@ -480,15 +537,16 @@
     dispatch = jnp.exp(logits[...] - peak) / total
     weight_grad = dot_last(grads, tokens[...])
     logit_grad = dispatch * (weight_grad - shift) + mixing[...]
-    left = jnp.concatenate([dispatch, logit_grad], axis=0).astype(jnp.bfloat16)
+    left = jnp.concatenate([dispatch, logit_grad], axis=0).T.astype(jnp.bfloat16)
     right = jnp.concatenate([grads, router[...]], axis=0)
     parts = sent.shape[0]
-    size = out.shape[0] // parts
-    copies = []
+    size = out.shape[1] // parts
     for part in range(parts):
-        rows = slice(part * size, (part + 1) * size)
-        out[rows] = dot_first(left[:, rows], right).astype(jnp.bfloat16)
-        copy = pltpu.make_async_copy(out.at[rows], out_far.at[rows], sent.at[part])
+        columns = slice(part * size, (part + 1) * size)
+        out[:, columns] = dot_plain(left, right[:, columns]).astype(jnp.bfloat16)
+        copy = pltpu.make_async_copy(
+            out.at[:, columns], out_far.at[:, columns], sent.at[part]
+        )
         copy.start()
         copies.append(copy)
     for copy in copies:
@@ -499,9 +557,8 @@
     return lax.ppermute(blocks, axis, [(0, 1), (1, 0)])
 
 
-def to_group(block, groups):
+def to_group(block, beside, groups):
     chips = lax.axis_size("chip")
-    beside = swap(block, "half")
     (blocks,) = call(
         pack_kernel,
         [array(block.dtype, groups, chips, *block.shape)],
@@ -513,9 +570,9 @@
     return blocks, swap(blocks, "core")
 
 
-def call(kernel, outs, args, flops, space=pltpu.VMEM, scratch=()):
-    size = sum(array.size * array.dtype.itemsize for array in args)
-    size += sum(out.size * out.dtype.itemsize for out in outs)
+def call(kernel, outs, args, flops, space=pltpu.VMEM, scratch=(), size=None):
+    if size is None:
+        size = sum(array.size * array.dtype.itemsize for array in (*args, *outs))
     return pl.pallas_call(
         kernel,
         out_shape=outs,
@@ -591,8 +648,24 @@
         [first, in_left, out_right],
         4 * rows * owned * rank * slice_width,
     )
-    second, second_other = to_group(second, groups)
+    second, combine = lax.optimization_barrier((second, combine))
+    beside = swap(second, "half")
+    (mixing,) = call(
+        mixing_kernel,
+        [array(full, slots, count)],
+        [cot_rows, saved, combine],
+        2 * count * slots * width,
+    )
+    beside, mixing = lax.optimization_barrier((beside, mixing))
+    second, second_other = to_group(second, beside, groups)
     total_rows = groups * members
+    near_ranks, near_products = call(
+        near_kernel,
+        [array(full, 2, total_rows // 2, rank), array(full, 2, total_rows // 2, hidden)],
+        [second, in_right, out_left],
+        2 * total_rows * owned * rank * hidden,
+        size=0,
+    )
     third, pair, hidden_ranks = call(
         functools.partial(hidden_kernel, groups),
         [
@@ -600,7 +673,16 @@
             array(full, 2, total_rows, hidden),
             array(full, 2, total_rows, rank),
         ],
-        [second, second_other, base_in, base_out, in_right, out_left],
+        [
+            second,
+            second_other,
+            near_ranks,
+            near_products,
+            base_in,
+            base_out,
+            in_right,
+            out_left,
+        ],
         6 * total_rows * hidden * (width + owned * rank),
     )
     third = lax.all_to_all(third, HALF, 0, 0, tiled=True)
@@ -610,46 +692,56 @@
         [third],
         0,
     )
+    other, pair, hidden_ranks = lax.optimization_barrier((other, pair, hidden_ranks))
     other = swap(other, "half")
+    grad_in_right, grad_out_left = call(
+        functools.partial(outer_kernel, owned),
+        [array(low, members, rank, hidden)] * 2,
+        [hidden_ranks, pair],
+        4 * members * rank * hidden * rows,
+    )
+    other, grad_in_right, grad_out_left = lax.optimization_barrier(
+        (other, grad_in_right, grad_out_left)
+    )
     fourth, ranks = call(
         functools.partial(finish_kernel, groups),
         [array(low, devices // 2, owned, slice_width + STATS), array(full, 2, rows, rank)],
         [own, other, in_left, inputs, stats],
         2 * rows * owned * rank * slice_width,
     )
-    fourth, combine, pair, hidden_ranks = lax.optimization_barrier(
-        (fourth, combine, pair, hidden_ranks)
-    )
     fourth = lax.all_to_all(fourth, SAME_CORE, 0, 0, tiled=True)
-    grad_in_right, grad_out_left = call(
-        functools.partial(outer_kernel, owned),
-        [array(low, members, rank, hidden)] * 2,
-        [hidden_ranks, pair],
-        4 * members * rank * hidden * rows,
-    )
-    (mixing,) = call(
-        mixing_kernel,
-        [array(full, slots, count)],
-        [cot_rows, saved, combine],
-        2 * count * slots * width,
-    )
+    fourth, ranks = lax.optimization_barrier((fourth, ranks))
+    fourth_other = swap(fourth, "core")
     grad_in_left, grad_out_right = call(
         functools.partial(outer_kernel, owned),
         [array(low, owned, rank, slice_width)] * 2,
         [ranks, lows],
         4 * owned * rank * slice_width * rows,
     )
-    outs = (grad_in_left, grad_in_right, grad_out_left, grad_out_right)
-    fourth, mixing, outs = lax.optimization_barrier((fourth, mixing, outs))
-    grad_in_left, grad_in_right, grad_out_left, grad_out_right = outs
-    parts = math.gcd(4, count // 16)
-    (token_grad,) = call(
+    fourth_other, grad_in_left, grad_out_right = lax.optimization_barrier(
+        (fourth_other, grad_in_left, grad_out_right)
+    )
+    parts = width // 256 if width % 256 == 0 else 1
+    token_grad, grad_in_left, grad_out_right = call(
         functools.partial(tokens_kernel, groups),
-        [array(low, count, width)],
-        [fourth, swap(fourth, "core"), image_rows, router, logits, mixing],
+        [array(low, count, width)] + [array(low, owned, rank, slice_width)] * 2,
+        [
+            fourth,
+            fourth_other,
+            image_rows,
+            router,
+            logits,
+            mixing,
+            grad_in_left,
+            grad_out_right,
+        ],
         6 * count * slots * width,
         pltpu.HBM,
-        [pltpu.VMEM((count, width), low), pltpu.SemaphoreType.DMA((parts,))],
+        [
+            pltpu.VMEM((count, width), low),
+            pltpu.SemaphoreType.DMA((parts,)),
+            pltpu.SemaphoreType.DMA((2,)),
+        ],
     )
     return (
         token_grad[None],

time: 69.4 us -> 67.4 us (0.971)
  blocking collectives: 31.4 us -> 40.7 us
  waiting for transfers between devices: 10.1 us -> 4.2 us
  starting transfers between devices: 14.2 us -> 9.81 us
  Pallas kernels: 10.9 us -> 9.65 us
    all_to_all x0 -> x1, blocking collectives: none -> 9.76 us  [local(): fourth = lax.all_to_all(fourth, SAME_CORE, 0, 0, tiled=True)]
    ppermute x5, waiting for transfers between devices: 7.71 us -> 4.2 us  [swap(): return lax.ppermute(blocks, axis, [(0, 1), (1, 0)])]
    all_to_all x1 -> x0, starting transfers between devices: 3.51 us -> none  [local(): fourth = lax.all_to_all(fourth, SAME_CORE, 0, 0, tiled=True)]
    all_to_all x1 -> x0, waiting for transfers between devices: 2.41 us -> none  [local(): fourth = lax.all_to_all(fourth, SAME_CORE, 0, 0, tiled=True)]
    pallas_call x12 -> x13, Pallas kernels: 10.9 us -> 9.65 us  [call(): pl.pallas_call(kernel, out_shape=outs, in_specs=[pl.BlockSpec(memory_spac...]
    ppermute x5, starting transfers between devices: 10.7 us -> 9.81 us  [swap(): return lax.ppermute(blocks, axis, [(0, 1), (1, 0)])]
  transfers between devices with their start and end apart: 6 -> 5, of which waited for: 6 -> 4; matrix products, arithmetic and copies ran while one was open for 0% -> 0% of each run, Pallas kernels for 6% -> 5%
where the time goes in v18:
time: 67.4 us; the launch traced here: 66.8 us
  blocking collectives  40.7 us (60%)
  starting transfers between devices  9.81 us (15%)
  Pallas kernels  9.65 us (14%)
  waiting for transfers between devices  4.2 us (6%)
  local copies, waits for them, and re-layouts  1.72 us (3%)
  between operations  0.74 us (1%)
    all_to_all x1, blocking collectives, local(): first = lax.all_to_all(first, SAME_CORE, 0, 0, tiled=True)  14.5 us
    ppermute x5, starting transfers between devices, swap(): return lax.ppermute(blocks, axis, [(0, 1), (1, 0)])  9.81 us
    all_to_all x1, blocking collectives, local(): fourth = lax.all_to_all(fourth, SAME_CORE, 0, 0, tiled=True)  9.76 us
    pallas_call x13, Pallas kernels, call(): pl.pallas_call(kernel, out_shape=outs, in_specs=[pl.BlockSpec(memory_spac...  9.65 us
    all_to_all x1, blocking collectives, local(): third = lax.all_to_all(third, HALF, 0, 0, tiled=True)  8.48 us
    all_to_all x1, blocking collectives, to_group(): blocks = lax.all_to_all(blocks, HALF_CORE, 0, 0, tiled=True)  7.93 us
    ppermute x5, waiting for transfers between devices, swap(): return lax.ppermute(blocks, axis, [(0, 1), (1, 0)])  4.2 us
    unnamed x20, local copies, waits for them, and re-layouts  1.72 us
  transfers between devices with their start and end apart: 5, of which 4 were waited for; matrix products, arithmetic and copies ran while one was open for 0% of the time, Pallas kernels for 5%

profile of v18, /device:TPU:1, one launch (start us, length us, event | category | flops | bytes accessed | tf_op | source)
XLA Modules:
  0.0 66.8 jit_solution(283385869976199410)
XLA Ops:
  0.6 0.0 copy-start.8
  0.6 0.0 copy-start.6
  0.7 0.0 copy-start.5
  0.7 0.9 %copy-done.8 = bf16[1280,64]{0,1:T(8,128)(2,1)S(1)} copy-done((bf16[1280,64]{0,1:T(8,128)(2,1)S(1)}, bf16[1280,64]{0,1:T(8,128)(2,1)}, u32[]{:S(2)}) %copy-start.8) | copy-done | bytes 163864
  1.5 0.3 copy-done.6
  1.8 0.2 copy-done.5
  2.0 1.0 %shard_map.138 = (bf16[16,4,1408]{2,1,0:T(4,128)(2,1)S(1)}, bf16[16,4,1408]{2,1,0:T(4,128)(2,1)S(1)}, f32[64,256]{1,0:T(8,128)S(1)}, f32[64,256]{1,0:T(8,128)S(1)}) custom-call(f32[8,128]{1,0:T(8,128)S(1)} %shard_map.137._, bf16[256,1280]{1,0:T(8,128)(2,1)S(1)} %bitcast.16, bf16[256,1280]{1,0:T(8,128)(2,1)S(1)} %bitcast.18, bf16[64,1280]{1,0:T(8,128)(2,1)S(1)} %bitcast.21), custom_call_target="tpu_custom_call" | custom-call | flops 10125829120 | bytes 1970176 | tf_op jit(solution)/shard_map/pallas_call | solution.py:576
  3.0 0.1 collective-permute-start
  3.2 1.4 %collective-permute-done.other = bf16[16,4,1408]{2,1,0:T(4,128)(2,1)S(1)} collective-permute-done((bf16[16,4,1408]{2,1,0:T(4,128)(2,1)S(1)}, bf16[16,4,1408]{2,1,0:T(4,128)(2,1)S(1)}, u32[]{:S(2)}, u32[]{:S(2)}) %collective-permute-start) | collective-permute-done | bytes 180256 | tf_op jit(solution)/shard_map/ppermute | solution.py:557
  4.5 0.0 copy-start.2
  4.5 0.0 copy-start.7
  4.5 0.0 copy-start.9
  4.5 0.3 shard_map.139
  4.8 14.5 %all_to_all.20.first = bf16[16,4,1408]{2,1,0:T(4,128)(2,1)S(1)} all-to-all(bf16[16,4,1408]{2,1,0:T(4,128)(2,1)S(1)} %shard_map.139), channel_id=1, replica_groups=mesh['dp'=2,'half'=2,'chip'=4,'core'=2] {'dp','half','chip'}, dimensions={0} | all-to-all | bytes 360448 | tf_op jit(solution)/shard_map/all_to_all | solution.py:639
  19.3 0.0 copy-done.2
  19.4 0.0 copy-done.7
  19.4 0.5 shard_map.140
  19.9 1.5 %collective-permute-start.1 = (bf16[8,1408]{1,0:T(8,128)(2,1)S(1)}, bf16[8,1408]{1,0:T(8,128)(2,1)S(1)}, u32[]{:S(2)}, u32[]{:S(2)}) collective-permute-start(bf16[8,1408]{1,0:T(8,128)(2,1)S(1)} %get-tuple-element.48.own), channel_id=1, source_target_pairs={{0,8},{8,0},{1,9},{9,1},{2,10},{10,2},{3,11},{11,3},{4,12},{12,4},... | collective-permute-start | bytes 67592 | tf_op jit(solution)/shard_map/ppermute | solution.py:557
  21.4 0.0 copy-done.9
  21.4 0.4 shard_map.141.mixing
  21.8 0.0 copy-start
  21.8 0.0 copy-start.1
  21.8 1.6 %collective-permute-done.1.beside = bf16[8,1408]{1,0:T(8,128)(2,1)S(1)} collective-permute-done((bf16[8,1408]{1,0:T(8,128)(2,1)S(1)}, bf16[8,1408]{1,0:T(8,128)(2,1)S(1)}, u32[]{:S(2)}, u32[]{:S(2)}) %collective-permute-start.1) | collective-permute-done | bytes 22560 | tf_op jit(solution)/shard_map/ppermute | solution.py:557
  23.5 7.9 %all_to_all.21.second = bf16[8,8,1408]{2,1,0:T(8,128)(2,1)S(1)} all-to-all(bf16[8,8,1408]{2,1,0:T(8,128)(2,1)S(1)} %bitcast.20), channel_id=1, replica_groups=mesh['dp'=2,'half'=2,'chip'=4,'core'=2] {'dp','chip'}, dimensions={0} | all-to-all | bytes 360448 | tf_op jit(solution)/shard_map/all_to_all | solution.py:569
  31.4 4.3 %collective-permute-start.2 = (bf16[8,8,1408]{2,1,0:T(8,128)(2,1)S(1)}, bf16[8,8,1408]{2,1,0:T(8,128)(2,1)S(1)}, u32[]{:S(2)}, u32[]{:S(2)}) collective-permute-start(bf16[8,8,1408]{2,1,0:T(8,128)(2,1)S(1)} %all_to_all.21.second), channel_id=1, source_target_pairs={{0,1},{1,0},{2,3},{3,2},{4,5},{5,4},{6,7},{7,6},{8,9},{9,8},{10,11... | collective-permute-start | bytes 540680 | tf_op jit(solution)/shard_map/ppermute | solution.py:557
  35.8 0.0 copy-done
  35.8 0.0 copy-done.1
  35.8 0.0 copy-start.3
  35.8 0.0 copy-start.4
  35.8 0.4 shard_map.143
  36.1 0.7 %collective-permute-done.2.second_other = bf16[8,8,1408]{2,1,0:T(8,128)(2,1)S(1)} collective-permute-done((bf16[8,8,1408]{2,1,0:T(8,128)(2,1)S(1)}, bf16[8,8,1408]{2,1,0:T(8,128)(2,1)S(1)}, u32[]{:S(2)}, u32[]{:S(2)}) %collective-permute-start.2) | collective-permute-done | bytes 180256 | tf_op jit(solution)/shard_map/ppermute | solution.py:557
  36.8 0.1 copy-done.3
  36.9 0.2 copy-done.4
  37.2 2.1 %shard_map.144 = (bf16[16,8,768]{2,1,0:T(8,128)(2,1)S(1)}, f32[2,64,320]{2,1,0:T(8,128)S(1)}, f32[2,64,64]{2,1,0:T(8,128)S(1)}) custom-call(bf16[8,8,1408]{2,1,0:T(8,128)(2,1)S(1)} %all_to_all.21.second, bf16[8,8,1408]{2,1,0:T(8,128)(2,1)S(1)} %collective-permute-done.2.second_other, f32[2,32,64]{2,1,0:T(8,128)S(1)} %get-tuple-element.51.near_ranks, ...), custom_call_target="tpu_custom_call" | custom-call | flops 188743680 | bytes 5111808 | tf_op jit(solution)/shard_map/pallas_call | solution.py:576
  39.3 8.5 %all_to_all.22.third = bf16[16,8,768]{2,1,0:T(8,128)(2,1)S(1)} all-to-all(bf16[16,8,768]{2,1,0:T(8,128)(2,1)S(1)} %get-tuple-element.53), channel_id=1, replica_groups=mesh['dp'=2,'half'=2,'chip'=4,'core'=2] {'dp','chip','core'}, dimensions={0} | all-to-all | bytes 393216 | tf_op jit(solution)/shard_map/all_to_all | solution.py:688
  47.8 1.2 %collective-permute-start.3 = (bf16[8,768]{1,0:T(8,128)(2,1)S(1)}, bf16[8,768]{1,0:T(8,128)(2,1)S(1)}, u32[]{:S(2)}, u32[]{:S(2)}) collective-permute-start(bf16[8,768]{1,0:T(8,128)(2,1)S(1)} %get-tuple-element.58), channel_id=1, source_target_pairs={{0,8},{8,0},{1,9},{9,1},{2,10},{10,2},{3,11},{11,3},{4,12},{12,4},... | collective-permute-start | bytes 36872 | tf_op jit(solution)/shard_map/ppermute | solution.py:557
  49.0 2.5 %shard_map.146 = (bf16[32,64,320]{2,1,0:T(8,128)(2,1)}, bf16[32,64,320]{2,1,0:T(8,128)(2,1)}) custom-call(f32[2,64,64]{2,1,0:T(8,128)S(1)} %get-tuple-element.59.left_rows, f32[2,64,320]{2,1,0:T(8,128)S(1)} %get-tuple-element.60.right_rows), custom_call_target="tpu_custom_call" | custom-call | flops 20971520 | bytes 2818048 | tf_op jit(solution)/shard_map/pallas_call | solution.py:576
  51.5 0.0 collective-permute-done.3.other
  51.5 0.3 shard_map.147
  51.8 9.8 %all_to_all.23.fourth = bf16[16,4,768]{2,1,0:T(4,128)(2,1)S(1)} all-to-all(bf16[16,4,768]{2,1,0:T(4,128)(2,1)S(1)} %get-tuple-element.66), channel_id=1, replica_groups=mesh['dp'=2,'half'=2,'chip'=4,'core'=2] {'dp','half','chip'}, dimensions={0} | all-to-all | bytes 196608 | tf_op jit(solution)/shard_map/all_to_all | solution.py:712
  61.6 2.6 %collective-permute-start.4 = (bf16[16,4,768]{2,1,0:T(4,128)(2,1)S(1)}, bf16[16,4,768]{2,1,0:T(4,128)(2,1)S(1)}, u32[]{:S(2)}, u32[]{:S(2)}) collective-permute-start(bf16[16,4,768]{2,1,0:T(4,128)(2,1)S(1)} %all_to_all.23.fourth), channel_id=1, source_target_pairs={{0,1},{1,0},{2,3},{3,2},{4,5},{5,4},{6,7},{7,6},{8,9},{9,8},{10,11... | collective-permute-start | bytes 294920 | tf_op jit(solution)/shard_map/ppermute | solution.py:557
  64.2 0.4 shard_map.148
  64.6 0.5 collective-permute-done.4.fourth_other
  65.1 1.7 %shard_map.149 = (bf16[256,1280]{1,0:T(8,128)(2,1)}, bf16[4,64,640]{2,1,0:T(8,128)(2,1)}, bf16[4,64,640]{2,1,0:T(8,128)(2,1)}) custom-call(bf16[16,4,768]{2,1,0:T(4,128)(2,1)S(1)} %all_to_all.23.fourth, bf16[16,4,768]{2,1,0:T(4,128)(2,1)S(1)} %collective-permute-done.4.fourth_other, bf16[256,1280]{1,0:T(8,128)(2,1)S(1)} %bitcast.17, ...), custom_call_target="tpu_custom_call" | custom-call | flops 125829120 | bytes 3112960 | tf_op jit(solution)/shard_map/pallas_call | solution.py:576
  (3 shorter events, 0.0 us)
Async XLA Ops:
  0.6 0.9 %copy-start.8 = (bf16[1280,64]{0,1:T(8,128)(2,1)S(1)}, bf16[1280,64]{0,1:T(8,128)(2,1)}, u32[]{:S(2)}) copy-start(bf16[1280,64]{0,1:T(8,128)(2,1)} %param.12) | copy-start | bytes 491524
  0.6 1.2 %copy-start.6 = (bf16[1,256,1280]{2,1,0:T(8,128)(2,1)S(1)}, bf16[1,256,1280]{2,1,0:T(8,128)(2,1)}, u32[]{:S(2)}) copy-start(bf16[1,256,1280]{2,1,0:T(8,128)(2,1)} %param.11) | copy-start | bytes 1966084
  0.7 1.4 %copy-start.5 = (bf16[1,256,1280]{2,1,0:T(8,128)(2,1)S(1)}, bf16[1,256,1280]{2,1,0:T(8,128)(2,1)}, u32[]{:S(2)}) copy-start(bf16[1,256,1280]{2,1,0:T(8,128)(2,1)} %param.10) | copy-start | bytes 1966084
  3.0 1.5 %collective-permute-start = (bf16[16,4,1408]{2,1,0:T(4,128)(2,1)S(1)}, bf16[16,4,1408]{2,1,0:T(4,128)(2,1)S(1)}, u32[]{:S(2)}, u32[]{:S(2)}) collective-permute-start(bf16[16,4,1408]{2,1,0:T(4,128)(2,1)S(1)} %get-tuple-element.45), channel_id=1, source_target_pairs={{0,1},{1,0},{2,3},{3,2},{4,5},{5,4},{6,7},{7,6},{8,9},{9,8},{10,11... | collective-permute-start | bytes 540680 | tf_op jit(solution)/shard_map/ppermute | solution.py:557
  4.5 14.8 %copy-start.2 = (bf16[4,640,64]{1,2,0:T(8,128)(2,1)S(1)}, bf16[4,640,64]{1,2,0:T(8,128)(2,1)}, u32[]{:S(2)}) copy-start(bf16[4,640,64]{1,2,0:T(8,128)(2,1)} %param.16) | copy-start | bytes 983044
  4.5 14.8 %copy-start.7 = (bf16[4,64,640]{2,1,0:T(8,128)(2,1)S(1)}, bf16[4,64,640]{2,1,0:T(8,128)(2,1)}, u32[]{:S(2)}) copy-start(bf16[4,64,640]{2,1,0:T(8,128)(2,1)} %out_right.1) | copy-start | bytes 983044
  4.5 16.9 %copy-start.9 = (bf16[1,64,1280]{2,1,0:T(8,128)(2,1)S(1)}, bf16[1,64,1280]{2,1,0:T(8,128)(2,1)}, u32[]{:S(2)}) copy-start(bf16[1,64,1280]{2,1,0:T(8,128)(2,1)} %param.13) | copy-start | bytes 491524
  19.9 3.6 %collective-permute-start.1 = (bf16[8,1408]{1,0:T(8,128)(2,1)S(1)}, bf16[8,1408]{1,0:T(8,128)(2,1)S(1)}, u32[]{:S(2)}, u32[]{:S(2)}) collective-permute-start(bf16[8,1408]{1,0:T(8,128)(2,1)S(1)} %get-tuple-element.48.own), channel_id=1, source_target_pairs={{0,8},{8,0},{1,9},{9,1},{2,10},{10,2},{3,11},{11,3},{4,12},{12,4},... | collective-permute-start | bytes 67592 | tf_op jit(solution)/shard_map/ppermute | solution.py:557
  21.8 14.0 %copy-start = (bf16[32,64,320]{2,1,0:T(8,128)(2,1)S(1)}, bf16[32,64,320]{2,1,0:T(8,128)(2,1)}, u32[]{:S(2)}) copy-start(bf16[32,64,320]{2,1,0:T(8,128)(2,1)} %in_right.3) | copy-start | bytes 3932164
  21.8 14.0 %copy-start.1 = (bf16[32,320,64]{1,2,0:T(8,128)(2,1)S(1)}, bf16[32,320,64]{1,2,0:T(8,128)(2,1)}, u32[]{:S(2)}) copy-start(bf16[32,320,64]{1,2,0:T(8,128)(2,1)} %param.18) | copy-start | bytes 3932164
  31.4 5.4 %collective-permute-start.2 = (bf16[8,8,1408]{2,1,0:T(8,128)(2,1)S(1)}, bf16[8,8,1408]{2,1,0:T(8,128)(2,1)S(1)}, u32[]{:S(2)}, u32[]{:S(2)}) collective-permute-start(bf16[8,8,1408]{2,1,0:T(8,128)(2,1)S(1)} %all_to_all.21.second), channel_id=1, source_target_pairs={{0,1},{1,0},{2,3},{3,2},{4,5},{5,4},{6,7},{7,6},{8,9},{9,8},{10,11... | collective-permute-start | bytes 540680 | tf_op jit(solution)/shard_map/ppermute | solution.py:557
  35.8 1.1 %copy-start.3 = (bf16[1280,320]{0,1:T(8,128)(2,1)S(1)}, bf16[1280,320]{0,1:T(8,128)(2,1)}, u32[]{:S(2)}) copy-start(bf16[1280,320]{0,1:T(8,128)(2,1)} %param.14) | copy-start | bytes 2457604
  35.8 1.4 %copy-start.4 = (bf16[320,1280]{1,0:T(8,128)(2,1)S(1)}, bf16[320,1280]{1,0:T(8,128)(2,1)}, u32[]{:S(2)}) copy-start(bf16[320,1280]{1,0:T(8,128)(2,1)} %base_out.1) | copy-start | bytes 2457604
  47.8 3.7 %collective-permute-start.3 = (bf16[8,768]{1,0:T(8,128)(2,1)S(1)}, bf16[8,768]{1,0:T(8,128)(2,1)S(1)}, u32[]{:S(2)}, u32[]{:S(2)}) collective-permute-start(bf16[8,768]{1,0:T(8,128)(2,1)S(1)} %get-tuple-element.58), channel_id=1, source_target_pairs={{0,8},{8,0},{1,9},{9,1},{2,10},{10,2},{3,11},{11,3},{4,12},{12,4},... | collective-permute-start | bytes 36872 | tf_op jit(solution)/shard_map/ppermute | solution.py:557
  61.6 3.6 %collective-permute-start.4 = (bf16[16,4,768]{2,1,0:T(4,128)(2,1)S(1)}, bf16[16,4,768]{2,1,0:T(4,128)(2,1)S(1)}, u32[]{:S(2)}, u32[]{:S(2)}) collective-permute-start(bf16[16,4,768]{2,1,0:T(4,128)(2,1)S(1)} %all_to_all.23.fourth), channel_id=1, source_target_pairs={{0,1},{1,0},{2,3},{3,2},{4,5},{5,4},{6,7},{7,6},{8,9},{9,8},{10,11... | collective-permute-start | bytes 294920 | tf_op jit(solution)/shard_map/ppermute | solution.py:557

commit v19 on v18

--- a/solution.py
+++ b/solution.py
@@ -360,7 +360,7 @@
     return out
 
 
-def near_kernel(second, in_right, out_left, ranks_out, products_out):
+def near_kernel(second, in_right, out_left, _, __, ranks_out, products_out):
     found = factor_products(second, in_right, out_left, lax.axis_index("core"))
     for number, (value, product) in enumerate(found):
         ranks_out[number] = value
@@ -662,7 +662,7 @@
     near_ranks, near_products = call(
         near_kernel,
         [array(full, 2, total_rows // 2, rank), array(full, 2, total_rows // 2, hidden)],
-        [second, in_right, out_left],
+        [second, in_right, out_left, base_in, base_out],
         2 * total_rows * owned * rank * hidden,
         size=0,
     )

time: 67.4 us -> 67.4 us (level)
  no operation moved by 1% of the time
where the time goes in v19:
time: 67.4 us; the launch traced here: 66.8 us
  blocking collectives  41 us (61%)
  starting transfers between devices  9.81 us (15%)
  Pallas kernels  9.65 us (14%)
  waiting for transfers between devices  4.18 us (6%)
  local copies, waits for them, and re-layouts  1.38 us (2%)
  between operations  0.75 us (1%)
    all_to_all x1, blocking collectives, local(): first = lax.all_to_all(first, SAME_CORE, 0, 0, tiled=True)  14.5 us
    ppermute x5, starting transfers between devices, swap(): return lax.ppermute(blocks, axis, [(0, 1), (1, 0)])  9.81 us
    all_to_all x1, blocking collectives, local(): fourth = lax.all_to_all(fourth, SAME_CORE, 0, 0, tiled=True)  9.76 us
    pallas_call x13, Pallas kernels, call(): pl.pallas_call(kernel, out_shape=outs, in_specs=[pl.BlockSpec(memory_spac...  9.65 us
    all_to_all x1, blocking collectives, local(): third = lax.all_to_all(third, HALF, 0, 0, tiled=True)  8.82 us
    all_to_all x1, blocking collectives, to_group(): blocks = lax.all_to_all(blocks, HALF_CORE, 0, 0, tiled=True)  7.93 us
    ppermute x5, waiting for transfers between devices, swap(): return lax.ppermute(blocks, axis, [(0, 1), (1, 0)])  4.18 us
    unnamed x20, local copies, waits for them, and re-layouts  1.38 us
  transfers between devices with their start and end apart: 5, of which 4 were waited for; matrix products, arithmetic and copies ran while one was open for 0% of the time, Pallas kernels for 5%

profile of v19, /device:TPU:1, one launch (start us, length us, event | category | flops | bytes accessed | tf_op | source)
XLA Modules:
  0.0 66.8 jit_solution(2765044769846365512)
XLA Ops:
  0.6 0.0 copy-start.8
  0.6 0.0 copy-start.6
  0.7 0.0 copy-start.5
  0.7 0.9 %copy-done.8 = bf16[1280,64]{0,1:T(8,128)(2,1)S(1)} copy-done((bf16[1280,64]{0,1:T(8,128)(2,1)S(1)}, bf16[1280,64]{0,1:T(8,128)(2,1)}, u32[]{:S(2)}) %copy-start.8) | copy-done | bytes 163864
  1.5 0.3 copy-done.6
  1.8 0.2 copy-done.5
  2.0 1.0 %shard_map.138 = (bf16[16,4,1408]{2,1,0:T(4,128)(2,1)S(1)}, bf16[16,4,1408]{2,1,0:T(4,128)(2,1)S(1)}, f32[64,256]{1,0:T(8,128)S(1)}, f32[64,256]{1,0:T(8,128)S(1)}) custom-call(f32[8,128]{1,0:T(8,128)S(1)} %shard_map.137._, bf16[256,1280]{1,0:T(8,128)(2,1)S(1)} %bitcast.17, bf16[256,1280]{1,0:T(8,128)(2,1)S(1)} %bitcast.19, bf16[64,1280]{1,0:T(8,128)(2,1)S(1)} %bitcast.22), custom_call_target="tpu_custom_call" | custom-call | flops 10125829120 | bytes 1970176 | tf_op jit(solution)/shard_map/pallas_call | solution.py:576
  3.0 0.1 collective-permute-start
  3.2 1.4 %collective-permute-done.other = bf16[16,4,1408]{2,1,0:T(4,128)(2,1)S(1)} collective-permute-done((bf16[16,4,1408]{2,1,0:T(4,128)(2,1)S(1)}, bf16[16,4,1408]{2,1,0:T(4,128)(2,1)S(1)}, u32[]{:S(2)}, u32[]{:S(2)}) %collective-permute-start) | collective-permute-done | bytes 180256 | tf_op jit(solution)/shard_map/ppermute | solution.py:557
  4.5 0.0 copy-start.4
  4.5 0.0 copy-start.7
  4.5 0.0 copy-start.9
  4.5 0.3 shard_map.139
  4.8 14.5 %all_to_all.20.first = bf16[16,4,1408]{2,1,0:T(4,128)(2,1)S(1)} all-to-all(bf16[16,4,1408]{2,1,0:T(4,128)(2,1)S(1)} %shard_map.139), channel_id=1, replica_groups=mesh['dp'=2,'half'=2,'chip'=4,'core'=2] {'dp','half','chip'}, dimensions={0} | all-to-all | bytes 360448 | tf_op jit(solution)/shard_map/all_to_all | solution.py:639
  19.4 0.0 copy-done.4
  19.4 0.0 copy-done.7
  19.4 0.5 shard_map.140
  19.9 1.5 %collective-permute-start.1 = (bf16[8,1408]{1,0:T(8,128)(2,1)S(1)}, bf16[8,1408]{1,0:T(8,128)(2,1)S(1)}, u32[]{:S(2)}, u32[]{:S(2)}) collective-permute-start(bf16[8,1408]{1,0:T(8,128)(2,1)S(1)} %get-tuple-element.48.own), channel_id=1, source_target_pairs={{0,8},{8,0},{1,9},{9,1},{2,10},{10,2},{3,11},{11,3},{4,12},{12,4},... | collective-permute-start | bytes 67592 | tf_op jit(solution)/shard_map/ppermute | solution.py:557
  21.4 0.0 copy-done.9
  21.4 0.4 shard_map.141.mixing
  21.8 0.0 copy-start
  21.8 0.0 copy-start.1
  21.8 0.0 copy-start.2
  21.9 0.0 copy-start.3
  21.9 1.6 %collective-permute-done.1.beside = bf16[8,1408]{1,0:T(8,128)(2,1)S(1)} collective-permute-done((bf16[8,1408]{1,0:T(8,128)(2,1)S(1)}, bf16[8,1408]{1,0:T(8,128)(2,1)S(1)}, u32[]{:S(2)}, u32[]{:S(2)}) %collective-permute-start.1) | collective-permute-done | bytes 22560 | tf_op jit(solution)/shard_map/ppermute | solution.py:557
  23.5 7.9 %all_to_all.21.second = bf16[8,8,1408]{2,1,0:T(8,128)(2,1)S(1)} all-to-all(bf16[8,8,1408]{2,1,0:T(8,128)(2,1)S(1)} %bitcast.21), channel_id=1, replica_groups=mesh['dp'=2,'half'=2,'chip'=4,'core'=2] {'dp','chip'}, dimensions={0} | all-to-all | bytes 360448 | tf_op jit(solution)/shard_map/all_to_all | solution.py:569
  31.4 4.3 %collective-permute-start.2 = (bf16[8,8,1408]{2,1,0:T(8,128)(2,1)S(1)}, bf16[8,8,1408]{2,1,0:T(8,128)(2,1)S(1)}, u32[]{:S(2)}, u32[]{:S(2)}) collective-permute-start(bf16[8,8,1408]{2,1,0:T(8,128)(2,1)S(1)} %all_to_all.21.second), channel_id=1, source_target_pairs={{0,1},{1,0},{2,3},{3,2},{4,5},{5,4},{6,7},{7,6},{8,9},{9,8},{10,11... | collective-permute-start | bytes 540680 | tf_op jit(solution)/shard_map/ppermute | solution.py:557
  35.8 0.0 copy-done
  35.8 0.0 copy-done.1
  35.8 0.0 copy-done.2
  35.8 0.0 copy-done.3
  35.8 0.4 shard_map.143
  36.2 0.7 %collective-permute-done.2.second_other = bf16[8,8,1408]{2,1,0:T(8,128)(2,1)S(1)} collective-permute-done((bf16[8,8,1408]{2,1,0:T(8,128)(2,1)S(1)}, bf16[8,8,1408]{2,1,0:T(8,128)(2,1)S(1)}, u32[]{:S(2)}, u32[]{:S(2)}) %collective-permute-start.2) | collective-permute-done | bytes 180256 | tf_op jit(solution)/shard_map/ppermute | solution.py:557
  36.8 2.1 %shard_map.144 = (bf16[16,8,768]{2,1,0:T(8,128)(2,1)S(1)}, f32[2,64,320]{2,1,0:T(8,128)S(1)}, f32[2,64,64]{2,1,0:T(8,128)S(1)}) custom-call(bf16[8,8,1408]{2,1,0:T(8,128)(2,1)S(1)} %all_to_all.21.second, bf16[8,8,1408]{2,1,0:T(8,128)(2,1)S(1)} %collective-permute-done.2.second_other, f32[2,32,64]{2,1,0:T(8,128)S(1)} %get-tuple-element.51.near_ranks, ...), custom_call_target="tpu_custom_call" | custom-call | flops 188743680 | bytes 5111808 | tf_op jit(solution)/shard_map/pallas_call | solution.py:576
  38.9 8.8 %all_to_all.22.third = bf16[16,8,768]{2,1,0:T(8,128)(2,1)S(1)} all-to-all(bf16[16,8,768]{2,1,0:T(8,128)(2,1)S(1)} %get-tuple-element.53), channel_id=1, replica_groups=mesh['dp'=2,'half'=2,'chip'=4,'core'=2] {'dp','chip','core'}, dimensions={0} | all-to-all | bytes 393216 | tf_op jit(solution)/shard_map/all_to_all | solution.py:688
  47.8 1.2 %collective-permute-start.3 = (bf16[8,768]{1,0:T(8,128)(2,1)S(1)}, bf16[8,768]{1,0:T(8,128)(2,1)S(1)}, u32[]{:S(2)}, u32[]{:S(2)}) collective-permute-start(bf16[8,768]{1,0:T(8,128)(2,1)S(1)} %get-tuple-element.58), channel_id=1, source_target_pairs={{0,8},{8,0},{1,9},{9,1},{2,10},{10,2},{3,11},{11,3},{4,12},{12,4},... | collective-permute-start | bytes 36872 | tf_op jit(solution)/shard_map/ppermute | solution.py:557
  49.0 2.5 %shard_map.146 = (bf16[32,64,320]{2,1,0:T(8,128)(2,1)}, bf16[32,64,320]{2,1,0:T(8,128)(2,1)}) custom-call(f32[2,64,64]{2,1,0:T(8,128)S(1)} %get-tuple-element.59.left_rows, f32[2,64,320]{2,1,0:T(8,128)S(1)} %get-tuple-element.60.right_rows), custom_call_target="tpu_custom_call" | custom-call | flops 20971520 | bytes 2818048 | tf_op jit(solution)/shard_map/pallas_call | solution.py:576
  51.5 0.0 collective-permute-done.3.other
  51.5 0.3 shard_map.147
  51.8 9.8 %all_to_all.23.fourth = bf16[16,4,768]{2,1,0:T(4,128)(2,1)S(1)} all-to-all(bf16[16,4,768]{2,1,0:T(4,128)(2,1)S(1)} %get-tuple-element.66), channel_id=1, replica_groups=mesh['dp'=2,'half'=2,'chip'=4,'core'=2] {'dp','half','chip'}, dimensions={0} | all-to-all | bytes 196608 | tf_op jit(solution)/shard_map/all_to_all | solution.py:712
  61.6 2.6 %collective-permute-start.4 = (bf16[16,4,768]{2,1,0:T(4,128)(2,1)S(1)}, bf16[16,4,768]{2,1,0:T(4,128)(2,1)S(1)}, u32[]{:S(2)}, u32[]{:S(2)}) collective-permute-start(bf16[16,4,768]{2,1,0:T(4,128)(2,1)S(1)} %all_to_all.23.fourth), channel_id=1, source_target_pairs={{0,1},{1,0},{2,3},{3,2},{4,5},{5,4},{6,7},{7,6},{8,9},{9,8},{10,11... | collective-permute-start | bytes 294920 | tf_op jit(solution)/shard_map/ppermute | solution.py:557
  64.2 0.4 shard_map.148
  64.6 0.5 collective-permute-done.4.fourth_other
  65.1 1.7 %shard_map.149 = (bf16[256,1280]{1,0:T(8,128)(2,1)}, bf16[4,64,640]{2,1,0:T(8,128)(2,1)}, bf16[4,64,640]{2,1,0:T(8,128)(2,1)}) custom-call(bf16[16,4,768]{2,1,0:T(4,128)(2,1)S(1)} %all_to_all.23.fourth, bf16[16,4,768]{2,1,0:T(4,128)(2,1)S(1)} %collective-permute-done.4.fourth_other, bf16[256,1280]{1,0:T(8,128)(2,1)S(1)} %bitcast.18, ...), custom_call_target="tpu_custom_call" | custom-call | flops 125829120 | bytes 3112960 | tf_op jit(solution)/shard_map/pallas_call | solution.py:576
  (3 shorter events, 0.0 us)
Async XLA Ops:
  0.6 0.9 %copy-start.8 = (bf16[1280,64]{0,1:T(8,128)(2,1)S(1)}, bf16[1280,64]{0,1:T(8,128)(2,1)}, u32[]{:S(2)}) copy-start(bf16[1280,64]{0,1:T(8,128)(2,1)} %param.12) | copy-start | bytes 491524
  0.6 1.2 %copy-start.6 = (bf16[1,256,1280]{2,1,0:T(8,128)(2,1)S(1)}, bf16[1,256,1280]{2,1,0:T(8,128)(2,1)}, u32[]{:S(2)}) copy-start(bf16[1,256,1280]{2,1,0:T(8,128)(2,1)} %param.11) | copy-start | bytes 1966084
  0.7 1.4 %copy-start.5 = (bf16[1,256,1280]{2,1,0:T(8,128)(2,1)S(1)}, bf16[1,256,1280]{2,1,0:T(8,128)(2,1)}, u32[]{:S(2)}) copy-start(bf16[1,256,1280]{2,1,0:T(8,128)(2,1)} %param.10) | copy-start | bytes 1966084
  3.0 1.5 %collective-permute-start = (bf16[16,4,1408]{2,1,0:T(4,128)(2,1)S(1)}, bf16[16,4,1408]{2,1,0:T(4,128)(2,1)S(1)}, u32[]{:S(2)}, u32[]{:S(2)}) collective-permute-start(bf16[16,4,1408]{2,1,0:T(4,128)(2,1)S(1)} %get-tuple-element.45), channel_id=1, source_target_pairs={{0,1},{1,0},{2,3},{3,2},{4,5},{5,4},{6,7},{7,6},{8,9},{9,8},{10,11... | collective-permute-start | bytes 540680 | tf_op jit(solution)/shard_map/ppermute | solution.py:557
  4.5 14.8 %copy-start.4 = (bf16[4,640,64]{1,2,0:T(8,128)(2,1)S(1)}, bf16[4,640,64]{1,2,0:T(8,128)(2,1)}, u32[]{:S(2)}) copy-start(bf16[4,640,64]{1,2,0:T(8,128)(2,1)} %param.16) | copy-start | bytes 983044
  4.5 14.8 %copy-start.7 = (bf16[4,64,640]{2,1,0:T(8,128)(2,1)S(1)}, bf16[4,64,640]{2,1,0:T(8,128)(2,1)}, u32[]{:S(2)}) copy-start(bf16[4,64,640]{2,1,0:T(8,128)(2,1)} %out_right.1) | copy-start | bytes 983044
  4.5 16.9 %copy-start.9 = (bf16[1,64,1280]{2,1,0:T(8,128)(2,1)S(1)}, bf16[1,64,1280]{2,1,0:T(8,128)(2,1)}, u32[]{:S(2)}) copy-start(bf16[1,64,1280]{2,1,0:T(8,128)(2,1)} %param.13) | copy-start | bytes 491524
  19.9 3.6 %collective-permute-start.1 = (bf16[8,1408]{1,0:T(8,128)(2,1)S(1)}, bf16[8,1408]{1,0:T(8,128)(2,1)S(1)}, u32[]{:S(2)}, u32[]{:S(2)}) collective-permute-start(bf16[8,1408]{1,0:T(8,128)(2,1)S(1)} %get-tuple-element.48.own), channel_id=1, source_target_pairs={{0,8},{8,0},{1,9},{9,1},{2,10},{10,2},{3,11},{11,3},{4,12},{12,4},... | collective-permute-start | bytes 67592 | tf_op jit(solution)/shard_map/ppermute | solution.py:557
  21.8 14.0 %copy-start = (bf16[32,64,320]{2,1,0:T(8,128)(2,1)S(1)}, bf16[32,64,320]{2,1,0:T(8,128)(2,1)}, u32[]{:S(2)}) copy-start(bf16[32,64,320]{2,1,0:T(8,128)(2,1)} %in_right.3) | copy-start | bytes 3932164
  21.8 14.0 %copy-start.1 = (bf16[32,320,64]{1,2,0:T(8,128)(2,1)S(1)}, bf16[32,320,64]{1,2,0:T(8,128)(2,1)}, u32[]{:S(2)}) copy-start(bf16[32,320,64]{1,2,0:T(8,128)(2,1)} %param.18) | copy-start | bytes 3932164
  21.8 13.9 %copy-start.2 = (bf16[1280,320]{0,1:T(8,128)(2,1)S(1)}, bf16[1280,320]{0,1:T(8,128)(2,1)}, u32[]{:S(2)}) copy-start(bf16[1280,320]{0,1:T(8,128)(2,1)} %param.14) | copy-start | bytes 2457604
  21.9 13.9 %copy-start.3 = (bf16[320,1280]{1,0:T(8,128)(2,1)S(1)}, bf16[320,1280]{1,0:T(8,128)(2,1)}, u32[]{:S(2)}) copy-start(bf16[320,1280]{1,0:T(8,128)(2,1)} %base_out.1) | copy-start | bytes 2457604
  31.4 5.4 %collective-permute-start.2 = (bf16[8,8,1408]{2,1,0:T(8,128)(2,1)S(1)}, bf16[8,8,1408]{2,1,0:T(8,128)(2,1)S(1)}, u32[]{:S(2)}, u32[]{:S(2)}) collective-permute-start(bf16[8,8,1408]{2,1,0:T(8,128)(2,1)S(1)} %all_to_all.21.second), channel_id=1, source_target_pairs={{0,1},{1,0},{2,3},{3,2},{4,5},{5,4},{6,7},{7,6},{8,9},{9,8},{10,11... | collective-permute-start | bytes 540680 | tf_op jit(solution)/shard_map/ppermute | solution.py:557
  47.8 3.7 %collective-permute-start.3 = (bf16[8,768]{1,0:T(8,128)(2,1)S(1)}, bf16[8,768]{1,0:T(8,128)(2,1)S(1)}, u32[]{:S(2)}, u32[]{:S(2)}) collective-permute-start(bf16[8,768]{1,0:T(8,128)(2,1)S(1)} %get-tuple-element.58), channel_id=1, source_target_pairs={{0,8},{8,0},{1,9},{9,1},{2,10},{10,2},{3,11},{11,3},{4,12},{12,4},... | collective-permute-start | bytes 36872 | tf_op jit(solution)/shard_map/ppermute | solution.py:557
  61.6 3.6 %collective-permute-start.4 = (bf16[16,4,768]{2,1,0:T(4,128)(2,1)S(1)}, bf16[16,4,768]{2,1,0:T(4,128)(2,1)S(1)}, u32[]{:S(2)}, u32[]{:S(2)}) collective-permute-start(bf16[16,4,768]{2,1,0:T(4,128)(2,1)S(1)} %all_to_all.23.fourth), channel_id=1, source_target_pairs={{0,1},{1,0},{2,3},{3,2},{4,5},{5,4},{6,7},{7,6},{8,9},{9,8},{10,11... | collective-permute-start | bytes 294920 | tf_op jit(solution)/shard_map/ppermute | solution.py:557

commit v20 on v19

--- a/solution.py
+++ b/solution.py
@@ -491,10 +491,45 @@
             fourth[group * (fourth.shape[0] // groups) + place] = rows
 
 
+def half_tokens(blocks, tokens, logits, mixing, core):
+    number, owned, _ = blocks.shape
+    chips = number // 2
+    width = tokens.shape[1] // 2
+
+    def rows(half, columns):
+        taken = [blocks[half * chips + chip, :, columns] for chip in range(chips)]
+        return jnp.concatenate([part.astype(jnp.float32) for part in taken], axis=0)
+
+    def chosen(values):
+        taken = []
+        for chip in range(chips):
+            even = values[2 * chip * owned : (2 * chip + 1) * owned]
+            odd = values[(2 * chip + 1) * owned : (2 * chip + 2) * owned]
+            taken.append(jnp.where(core == 0, even, odd))
+        return jnp.concatenate(taken, axis=0)
+
+    grads = jnp.concatenate([rows(half, slice(0, width)) for half in range(2)], axis=1)
+    grads = grads.astype(jnp.bfloat16)
+    stats = [rows(half, slice(width, width + STATS)) for half in range(2)]
+    peak = stats[0][:, 0:1] + stats[0][:, 1:2]
+    total = stats[0][:, 2:3] + stats[0][:, 3:4]
+    shift = functools.reduce(jnp.add, [part[:, 4:5] + part[:, 5:6] for part in stats])
+    dispatch = jnp.exp(chosen(logits[...]) - peak) / total
+    weight_grad = dot_last(grads, tokens[...])
+    logit_grad = dispatch * (weight_grad - shift) + chosen(mixing[...])
+    return grads, dispatch, logit_grad
+
+
+def near_tokens_kernel(fourth, tokens, logits, mixing, grads, dispatch, logit_grad):
+    found = half_tokens(fourth, tokens, logits, mixing, lax.axis_index("core"))
+    grads[...], dispatch[...], logit_grad[...] = found
+
+
 def tokens_kernel(
-    groups,
-    fourth,
     fourth_other,
+    near_grads,
+    near_dispatch,
+    near_logit_grad,
     tokens,
     router,
     logits,
@@ -514,31 +549,16 @@
     ]
     for copy in copies:
         copy.start()
-    blocks, owned, _ = fourth.shape
-    chips = blocks // groups
-    width = tokens.shape[1] // groups
-    first_core = lax.axis_index("core") == 0
-
-    def rows(half, columns):
-        taken = []
-        for chip in range(chips):
-            own = fourth[half * chips + chip, :, columns].astype(jnp.float32)
-            other = fourth_other[half * chips + chip, :, columns].astype(jnp.float32)
-            taken.append(jnp.where(first_core, own, other))
-            taken.append(jnp.where(first_core, other, own))
-        return jnp.concatenate(taken, axis=0)
-
-    grads = jnp.concatenate([rows(half, slice(0, width)) for half in range(groups)], axis=1)
-    grads = grads.astype(jnp.bfloat16)
-    stats = [rows(half, slice(width, width + STATS)) for half in range(groups)]
-    peak = stats[0][:, 0:1] + stats[0][:, 1:2]
-    total = stats[0][:, 2:3] + stats[0][:, 3:4]
-    shift = functools.reduce(jnp.add, [part[:, 4:5] + part[:, 5:6] for part in stats])
-    dispatch = jnp.exp(logits[...] - peak) / total
-    weight_grad = dot_last(grads, tokens[...])
-    logit_grad = dispatch * (weight_grad - shift) + mixing[...]
-    left = jnp.concatenate([dispatch, logit_grad], axis=0).T.astype(jnp.bfloat16)
-    right = jnp.concatenate([grads, router[...]], axis=0)
+    core = lax.axis_index("core")
+    far = half_tokens(fourth_other, tokens, logits, mixing, 1 - core)
+    owned = fourth_other.shape[1]
+    ordered = []
+    for start in range(0, near_logit_grad.shape[0], owned):
+        own, other = near_logit_grad[start : start + owned], far[2][start : start + owned]
+        ordered.append(jnp.where(core == 0, own, other))
+        ordered.append(jnp.where(core == 0, other, own))
+    left = jnp.concatenate([near_dispatch[...], far[1], *ordered], axis=0).T.astype(jnp.bfloat16)
+    right = jnp.concatenate([near_grads[...], far[0], router[...]], axis=0)
     parts = sent.shape[0]
     size = out.shape[1] // parts
     for part in range(parts):
@@ -718,16 +738,27 @@
         [ranks, lows],
         4 * owned * rank * slice_width * rows,
     )
-    fourth_other, grad_in_left, grad_out_right = lax.optimization_barrier(
-        (fourth_other, grad_in_left, grad_out_right)
+    near = call(
+        near_tokens_kernel,
+        [
+            array(low, slots // 2, width),
+            array(full, slots // 2, count),
+            array(full, slots // 2, count),
+        ],
+        [fourth, image_rows, logits, mixing],
+        count * slots * width,
+        size=0,
+    )
+    fourth_other, grad_in_left, grad_out_right, *near = lax.optimization_barrier(
+        (fourth_other, grad_in_left, grad_out_right, *near)
     )
     parts = width // 256 if width % 256 == 0 else 1
     token_grad, grad_in_left, grad_out_right = call(
-        functools.partial(tokens_kernel, groups),
+        tokens_kernel,
         [array(low, count, width)] + [array(low, owned, rank, slice_width)] * 2,
         [
-            fourth,
             fourth_other,
+            *near,
             image_rows,
             router,
             logits,

time: 67.4 us -> 67.4 us (level)
    pallas_call x13 -> x14, Pallas kernels: 9.65 us -> 9.98 us  [call(): pl.pallas_call(kernel, out_shape=outs, in_specs=[pl.BlockSpec(memory_spac...]
  transfers between devices with their start and end apart: 5 -> 5, of which waited for: 4 -> 4; matrix products, arithmetic and copies ran while one was open for 0% -> 0% of each run, Pallas kernels for 5% -> 6%
where the time goes in v20:
time: 67.4 us; the launch traced here: 66.8 us
  blocking collectives  41 us (61%)
  Pallas kernels  9.98 us (15%)
  starting transfers between devices  9.81 us (15%)
  waiting for transfers between devices  3.84 us (6%)
  local copies, waits for them, and re-layouts  1.38 us (2%)
  between operations  0.75 us (1%)
    all_to_all x1, blocking collectives, local(): first = lax.all_to_all(first, SAME_CORE, 0, 0, tiled=True)  14.5 us
    pallas_call x14, Pallas kernels, call(): pl.pallas_call(kernel, out_shape=outs, in_specs=[pl.BlockSpec(memory_spac...  9.98 us
    ppermute x5, starting transfers between devices, swap(): return lax.ppermute(blocks, axis, [(0, 1), (1, 0)])  9.81 us
    all_to_all x1, blocking collectives, local(): fourth = lax.all_to_all(fourth, SAME_CORE, 0, 0, tiled=True)  9.75 us
    all_to_all x1, blocking collectives, local(): third = lax.all_to_all(third, HALF, 0, 0, tiled=True)  8.83 us
    all_to_all x1, blocking collectives, to_group(): blocks = lax.all_to_all(blocks, HALF_CORE, 0, 0, tiled=True)  7.93 us
    ppermute x5, waiting for transfers between devices, swap(): return lax.ppermute(blocks, axis, [(0, 1), (1, 0)])  3.84 us
    unnamed x20, local copies, waits for them, and re-layouts  1.38 us
  transfers between devices with their start and end apart: 5, of which 4 were waited for; matrix products, arithmetic and copies ran while one was open for 0% of the time, Pallas kernels for 6%

profile of v20, /device:TPU:1, one launch (start us, length us, event | category | flops | bytes accessed | tf_op | source)
XLA Modules:
  0.0 66.8 jit_solution(17528471489857094977)
XLA Ops:
  0.6 0.0 copy-start.8
  0.6 0.0 copy-start.6
  0.7 0.0 copy-start.4
  0.7 0.9 %copy-done.8 = bf16[1280,64]{0,1:T(8,128)(2,1)S(1)} copy-done((bf16[1280,64]{0,1:T(8,128)(2,1)S(1)}, bf16[1280,64]{0,1:T(8,128)(2,1)}, u32[]{:S(2)}) %copy-start.8) | copy-done | bytes 163864
  1.5 0.3 copy-done.6
  1.8 0.2 copy-done.4
  2.0 1.0 %shard_map.138 = (bf16[16,4,1408]{2,1,0:T(4,128)(2,1)S(1)}, bf16[16,4,1408]{2,1,0:T(4,128)(2,1)S(1)}, f32[64,256]{1,0:T(8,128)S(1)}, f32[64,256]{1,0:T(8,128)S(1)}) custom-call(f32[8,128]{1,0:T(8,128)S(1)} %shard_map.137._, bf16[256,1280]{1,0:T(8,128)(2,1)S(1)} %bitcast.15, bf16[256,1280]{1,0:T(8,128)(2,1)S(1)} %bitcast.20, bf16[64,1280]{1,0:T(8,128)(2,1)S(1)} %bitcast.23), custom_call_target="tpu_custom_call" | custom-call | flops 10125829120 | bytes 1970176 | tf_op jit(solution)/shard_map/pallas_call | solution.py:596
  3.0 0.1 collective-permute-start
  3.2 1.4 %collective-permute-done.other = bf16[16,4,1408]{2,1,0:T(4,128)(2,1)S(1)} collective-permute-done((bf16[16,4,1408]{2,1,0:T(4,128)(2,1)S(1)}, bf16[16,4,1408]{2,1,0:T(4,128)(2,1)S(1)}, u32[]{:S(2)}, u32[]{:S(2)}) %collective-permute-start) | collective-permute-done | bytes 180256 | tf_op jit(solution)/shard_map/ppermute | solution.py:577
  4.5 0.0 copy-start.5
  4.5 0.0 copy-start.7
  4.5 0.0 copy-start.9
  4.5 0.3 shard_map.139
  4.8 14.5 %all_to_all.20.first = bf16[16,4,1408]{2,1,0:T(4,128)(2,1)S(1)} all-to-all(bf16[16,4,1408]{2,1,0:T(4,128)(2,1)S(1)} %shard_map.139), channel_id=1, replica_groups=mesh['dp'=2,'half'=2,'chip'=4,'core'=2] {'dp','half','chip'}, dimensions={0} | all-to-all | bytes 360448 | tf_op jit(solution)/shard_map/all_to_all | solution.py:659
  19.4 0.0 copy-done.5
  19.4 0.0 copy-done.7
  19.4 0.5 shard_map.140
  19.9 1.5 %collective-permute-start.1 = (bf16[8,1408]{1,0:T(8,128)(2,1)S(1)}, bf16[8,1408]{1,0:T(8,128)(2,1)S(1)}, u32[]{:S(2)}, u32[]{:S(2)}) collective-permute-start(bf16[8,1408]{1,0:T(8,128)(2,1)S(1)} %get-tuple-element.54.own), channel_id=1, source_target_pairs={{0,8},{8,0},{1,9},{9,1},{2,10},{10,2},{3,11},{11,3},{4,12},{12,4},... | collective-permute-start | bytes 67592 | tf_op jit(solution)/shard_map/ppermute | solution.py:577
  21.4 0.0 copy-done.9
  21.4 0.4 shard_map.141.mixing
  21.8 0.0 copy-start
  21.8 0.0 copy-start.1
  21.8 0.0 copy-start.2
  21.9 0.0 copy-start.3
  21.9 1.6 %collective-permute-done.1.beside = bf16[8,1408]{1,0:T(8,128)(2,1)S(1)} collective-permute-done((bf16[8,1408]{1,0:T(8,128)(2,1)S(1)}, bf16[8,1408]{1,0:T(8,128)(2,1)S(1)}, u32[]{:S(2)}, u32[]{:S(2)}) %collective-permute-start.1) | collective-permute-done | bytes 22560 | tf_op jit(solution)/shard_map/ppermute | solution.py:577
  23.5 7.9 %all_to_all.21.second = bf16[8,8,1408]{2,1,0:T(8,128)(2,1)S(1)} all-to-all(bf16[8,8,1408]{2,1,0:T(8,128)(2,1)S(1)} %bitcast.22), channel_id=1, replica_groups=mesh['dp'=2,'half'=2,'chip'=4,'core'=2] {'dp','chip'}, dimensions={0} | all-to-all | bytes 360448 | tf_op jit(solution)/shard_map/all_to_all | solution.py:589
  31.4 4.3 %collective-permute-start.2 = (bf16[8,8,1408]{2,1,0:T(8,128)(2,1)S(1)}, bf16[8,8,1408]{2,1,0:T(8,128)(2,1)S(1)}, u32[]{:S(2)}, u32[]{:S(2)}) collective-permute-start(bf16[8,8,1408]{2,1,0:T(8,128)(2,1)S(1)} %all_to_all.21.second), channel_id=1, source_target_pairs={{0,1},{1,0},{2,3},{3,2},{4,5},{5,4},{6,7},{7,6},{8,9},{9,8},{10,11... | collective-permute-start | bytes 540680 | tf_op jit(solution)/shard_map/ppermute | solution.py:577
  35.8 0.0 copy-done
  35.8 0.0 copy-done.1
  35.8 0.0 copy-done.2
  35.8 0.0 copy-done.3
  35.8 0.4 shard_map.143
  36.1 0.7 %collective-permute-done.2.second_other = bf16[8,8,1408]{2,1,0:T(8,128)(2,1)S(1)} collective-permute-done((bf16[8,8,1408]{2,1,0:T(8,128)(2,1)S(1)}, bf16[8,8,1408]{2,1,0:T(8,128)(2,1)S(1)}, u32[]{:S(2)}, u32[]{:S(2)}) %collective-permute-start.2) | collective-permute-done | bytes 180256 | tf_op jit(solution)/shard_map/ppermute | solution.py:577
  36.8 2.1 %shard_map.144 = (bf16[16,8,768]{2,1,0:T(8,128)(2,1)S(1)}, f32[2,64,320]{2,1,0:T(8,128)S(1)}, f32[2,64,64]{2,1,0:T(8,128)S(1)}) custom-call(bf16[8,8,1408]{2,1,0:T(8,128)(2,1)S(1)} %all_to_all.21.second, bf16[8,8,1408]{2,1,0:T(8,128)(2,1)S(1)} %collective-permute-done.2.second_other, f32[2,32,64]{2,1,0:T(8,128)S(1)} %get-tuple-element.57.near_ranks, ...), custom_call_target="tpu_custom_call" | custom-call | flops 188743680 | bytes 5111808 | tf_op jit(solution)/shard_map/pallas_call | solution.py:596
  38.9 8.8 %all_to_all.22.third = bf16[16,8,768]{2,1,0:T(8,128)(2,1)S(1)} all-to-all(bf16[16,8,768]{2,1,0:T(8,128)(2,1)S(1)} %get-tuple-element.59), channel_id=1, replica_groups=mesh['dp'=2,'half'=2,'chip'=4,'core'=2] {'dp','chip','core'}, dimensions={0} | all-to-all | bytes 393216 | tf_op jit(solution)/shard_map/all_to_all | solution.py:708
  47.8 1.2 %collective-permute-start.3 = (bf16[8,768]{1,0:T(8,128)(2,1)S(1)}, bf16[8,768]{1,0:T(8,128)(2,1)S(1)}, u32[]{:S(2)}, u32[]{:S(2)}) collective-permute-start(bf16[8,768]{1,0:T(8,128)(2,1)S(1)} %get-tuple-element.64), channel_id=1, source_target_pairs={{0,8},{8,0},{1,9},{9,1},{2,10},{10,2},{3,11},{11,3},{4,12},{12,4},... | collective-permute-start | bytes 36872 | tf_op jit(solution)/shard_map/ppermute | solution.py:577
  49.0 2.5 %shard_map.146 = (bf16[32,64,320]{2,1,0:T(8,128)(2,1)}, bf16[32,64,320]{2,1,0:T(8,128)(2,1)}) custom-call(f32[2,64,64]{2,1,0:T(8,128)S(1)} %get-tuple-element.65.left_rows, f32[2,64,320]{2,1,0:T(8,128)S(1)} %get-tuple-element.66.right_rows), custom_call_target="tpu_custom_call" | custom-call | flops 20971520 | bytes 2818048 | tf_op jit(solution)/shard_map/pallas_call | solution.py:596
  51.5 0.0 collective-permute-done.3.other
  51.5 0.3 shard_map.147
  51.8 9.8 %all_to_all.23.fourth = bf16[16,4,768]{2,1,0:T(4,128)(2,1)S(1)} all-to-all(bf16[16,4,768]{2,1,0:T(4,128)(2,1)S(1)} %get-tuple-element.72), channel_id=1, replica_groups=mesh['dp'=2,'half'=2,'chip'=4,'core'=2] {'dp','half','chip'}, dimensions={0} | all-to-all | bytes 196608 | tf_op jit(solution)/shard_map/all_to_all | solution.py:732
  61.6 2.6 %collective-permute-start.4 = (bf16[16,4,768]{2,1,0:T(4,128)(2,1)S(1)}, bf16[16,4,768]{2,1,0:T(4,128)(2,1)S(1)}, u32[]{:S(2)}, u32[]{:S(2)}) collective-permute-start(bf16[16,4,768]{2,1,0:T(4,128)(2,1)S(1)} %all_to_all.23.fourth), channel_id=1, source_target_pairs={{0,1},{1,0},{2,3},{3,2},{4,5},{5,4},{6,7},{7,6},{8,9},{9,8},{10,11... | collective-permute-start | bytes 294920 | tf_op jit(solution)/shard_map/ppermute | solution.py:577
  64.2 0.4 shard_map.148
  64.6 0.3 shard_map.149
  64.9 0.2 collective-permute-done.4.fourth_other
  65.1 1.7 %shard_map.150 = (bf16[256,1280]{1,0:T(8,128)(2,1)}, bf16[4,64,640]{2,1,0:T(8,128)(2,1)}, bf16[4,64,640]{2,1,0:T(8,128)(2,1)}) custom-call(bf16[16,4,768]{2,1,0:T(4,128)(2,1)S(1)} %collective-permute-done.4.fourth_other, bf16[32,1280]{1,0:T(8,128)(2,1)S(1)} %get-tuple-element.85.near_grads, f32[32,256]{1,0:T(8,128)S(1)} %get-tuple-element.86.near_dispatch, ...), custom_call_target="tpu_custom_call" | custom-call | flops 125829120 | bytes 3162112 | tf_op jit(solution)/shard_map/pallas_call | solution.py:596
  (3 shorter events, 0.0 us)
Async XLA Ops:
  0.6 0.9 %copy-start.8 = (bf16[1280,64]{0,1:T(8,128)(2,1)S(1)}, bf16[1280,64]{0,1:T(8,128)(2,1)}, u32[]{:S(2)}) copy-start(bf16[1280,64]{0,1:T(8,128)(2,1)} %param.12) | copy-start | bytes 491524
  0.6 1.2 %copy-start.6 = (bf16[1,256,1280]{2,1,0:T(8,128)(2,1)S(1)}, bf16[1,256,1280]{2,1,0:T(8,128)(2,1)}, u32[]{:S(2)}) copy-start(bf16[1,256,1280]{2,1,0:T(8,128)(2,1)} %param.11) | copy-start | bytes 1966084
  0.7 1.4 %copy-start.4 = (bf16[1,256,1280]{2,1,0:T(8,128)(2,1)S(1)}, bf16[1,256,1280]{2,1,0:T(8,128)(2,1)}, u32[]{:S(2)}) copy-start(bf16[1,256,1280]{2,1,0:T(8,128)(2,1)} %param.10) | copy-start | bytes 1966084
  3.0 1.5 %collective-permute-start = (bf16[16,4,1408]{2,1,0:T(4,128)(2,1)S(1)}, bf16[16,4,1408]{2,1,0:T(4,128)(2,1)S(1)}, u32[]{:S(2)}, u32[]{:S(2)}) collective-permute-start(bf16[16,4,1408]{2,1,0:T(4,128)(2,1)S(1)} %get-tuple-element.51), channel_id=1, source_target_pairs={{0,1},{1,0},{2,3},{3,2},{4,5},{5,4},{6,7},{7,6},{8,9},{9,8},{10,11... | collective-permute-start | bytes 540680 | tf_op jit(solution)/shard_map/ppermute | solution.py:577
  4.5 14.8 %copy-start.5 = (bf16[4,640,64]{1,2,0:T(8,128)(2,1)S(1)}, bf16[4,640,64]{1,2,0:T(8,128)(2,1)}, u32[]{:S(2)}) copy-start(bf16[4,640,64]{1,2,0:T(8,128)(2,1)} %param.16) | copy-start | bytes 983044
  4.5 14.8 %copy-start.7 = (bf16[4,64,640]{2,1,0:T(8,128)(2,1)S(1)}, bf16[4,64,640]{2,1,0:T(8,128)(2,1)}, u32[]{:S(2)}) copy-start(bf16[4,64,640]{2,1,0:T(8,128)(2,1)} %out_right.1) | copy-start | bytes 983044
  4.5 16.9 %copy-start.9 = (bf16[1,64,1280]{2,1,0:T(8,128)(2,1)S(1)}, bf16[1,64,1280]{2,1,0:T(8,128)(2,1)}, u32[]{:S(2)}) copy-start(bf16[1,64,1280]{2,1,0:T(8,128)(2,1)} %param.13) | copy-start | bytes 491524
  19.9 3.6 %collective-permute-start.1 = (bf16[8,1408]{1,0:T(8,128)(2,1)S(1)}, bf16[8,1408]{1,0:T(8,128)(2,1)S(1)}, u32[]{:S(2)}, u32[]{:S(2)}) collective-permute-start(bf16[8,1408]{1,0:T(8,128)(2,1)S(1)} %get-tuple-element.54.own), channel_id=1, source_target_pairs={{0,8},{8,0},{1,9},{9,1},{2,10},{10,2},{3,11},{11,3},{4,12},{12,4},... | collective-permute-start | bytes 67592 | tf_op jit(solution)/shard_map/ppermute | solution.py:577
  21.8 14.0 %copy-start = (bf16[32,64,320]{2,1,0:T(8,128)(2,1)S(1)}, bf16[32,64,320]{2,1,0:T(8,128)(2,1)}, u32[]{:S(2)}) copy-start(bf16[32,64,320]{2,1,0:T(8,128)(2,1)} %in_right.3) | copy-start | bytes 3932164
  21.8 14.0 %copy-start.1 = (bf16[32,320,64]{1,2,0:T(8,128)(2,1)S(1)}, bf16[32,320,64]{1,2,0:T(8,128)(2,1)}, u32[]{:S(2)}) copy-start(bf16[32,320,64]{1,2,0:T(8,128)(2,1)} %param.18) | copy-start | bytes 3932164
  21.8 13.9 %copy-start.2 = (bf16[1280,320]{0,1:T(8,128)(2,1)S(1)}, bf16[1280,320]{0,1:T(8,128)(2,1)}, u32[]{:S(2)}) copy-start(bf16[1280,320]{0,1:T(8,128)(2,1)} %param.14) | copy-start | bytes 2457604
  21.9 13.9 %copy-start.3 = (bf16[320,1280]{1,0:T(8,128)(2,1)S(1)}, bf16[320,1280]{1,0:T(8,128)(2,1)}, u32[]{:S(2)}) copy-start(bf16[320,1280]{1,0:T(8,128)(2,1)} %base_out.1) | copy-start | bytes 2457604
  31.4 5.4 %collective-permute-start.2 = (bf16[8,8,1408]{2,1,0:T(8,128)(2,1)S(1)}, bf16[8,8,1408]{2,1,0:T(8,128)(2,1)S(1)}, u32[]{:S(2)}, u32[]{:S(2)}) collective-permute-start(bf16[8,8,1408]{2,1,0:T(8,128)(2,1)S(1)} %all_to_all.21.second), channel_id=1, source_target_pairs={{0,1},{1,0},{2,3},{3,2},{4,5},{5,4},{6,7},{7,6},{8,9},{9,8},{10,11... | collective-permute-start | bytes 540680 | tf_op jit(solution)/shard_map/ppermute | solution.py:577
  47.8 3.7 %collective-permute-start.3 = (bf16[8,768]{1,0:T(8,128)(2,1)S(1)}, bf16[8,768]{1,0:T(8,128)(2,1)S(1)}, u32[]{:S(2)}, u32[]{:S(2)}) collective-permute-start(bf16[8,768]{1,0:T(8,128)(2,1)S(1)} %get-tuple-element.64), channel_id=1, source_target_pairs={{0,8},{8,0},{1,9},{9,1},{2,10},{10,2},{3,11},{11,3},{4,12},{12,4},... | collective-permute-start | bytes 36872 | tf_op jit(solution)/shard_map/ppermute | solution.py:577
  61.6 3.6 %collective-permute-start.4 = (bf16[16,4,768]{2,1,0:T(4,128)(2,1)S(1)}, bf16[16,4,768]{2,1,0:T(4,128)(2,1)S(1)}, u32[]{:S(2)}, u32[]{:S(2)}) collective-permute-start(bf16[16,4,768]{2,1,0:T(4,128)(2,1)S(1)} %all_to_all.23.fourth), channel_id=1, source_target_pairs={{0,1},{1,0},{2,3},{3,2},{4,5},{5,4},{6,7},{7,6},{8,9},{9,8},{10,11... | collective-permute-start | bytes 294920 | tf_op jit(solution)/shard_map/ppermute | solution.py:577

commit v21 on v19

--- a/solution.py
+++ b/solution.py
@@ -721,7 +721,7 @@
     fourth_other, grad_in_left, grad_out_right = lax.optimization_barrier(
         (fourth_other, grad_in_left, grad_out_right)
     )
-    parts = width // 256 if width % 256 == 0 else 1
+    parts = 2 if width % 256 == 0 else 1
     token_grad, grad_in_left, grad_out_right = call(
         functools.partial(tokens_kernel, groups),
         [array(low, count, width)] + [array(low, owned, rank, slice_width)] * 2,

time: 67.4 us -> 67.4 us (level)
  no operation moved by 1% of the time
where the time goes in v21:
time: 67.4 us; the launch traced here: 66.9 us
  blocking collectives  41 us (61%)
  starting transfers between devices  9.81 us (15%)
  Pallas kernels  9.7 us (14%)
  waiting for transfers between devices  4.18 us (6%)
  local copies, waits for them, and re-layouts  1.38 us (2%)
  between operations  0.75 us (1%)
    all_to_all x1, blocking collectives, local(): first = lax.all_to_all(first, SAME_CORE, 0, 0, tiled=True)  14.5 us
    ppermute x5, starting transfers between devices, swap(): return lax.ppermute(blocks, axis, [(0, 1), (1, 0)])  9.81 us
    all_to_all x1, blocking collectives, local(): fourth = lax.all_to_all(fourth, SAME_CORE, 0, 0, tiled=True)  9.76 us
    pallas_call x13, Pallas kernels, call(): pl.pallas_call(kernel, out_shape=outs, in_specs=[pl.BlockSpec(memory_spac...  9.7 us
    all_to_all x1, blocking collectives, local(): third = lax.all_to_all(third, HALF, 0, 0, tiled=True)  8.82 us
    all_to_all x1, blocking collectives, to_group(): blocks = lax.all_to_all(blocks, HALF_CORE, 0, 0, tiled=True)  7.93 us
    ppermute x5, waiting for transfers between devices, swap(): return lax.ppermute(blocks, axis, [(0, 1), (1, 0)])  4.18 us
    unnamed x20, local copies, waits for them, and re-layouts  1.38 us
  transfers between devices with their start and end apart: 5, of which 4 were waited for; matrix products, arithmetic and copies ran while one was open for 0% of the time, Pallas kernels for 5%

profile of v21, /device:TPU:1, one launch (start us, length us, event | category | flops | bytes accessed | tf_op | source)
XLA Modules:
  0.0 66.9 jit_solution(9600021545073548335)
XLA Ops:
  0.6 0.0 copy-start.8
  0.6 0.0 copy-start.6
  0.7 0.0 copy-start.5
  0.7 0.9 %copy-done.8 = bf16[1280,64]{0,1:T(8,128)(2,1)S(1)} copy-done((bf16[1280,64]{0,1:T(8,128)(2,1)S(1)}, bf16[1280,64]{0,1:T(8,128)(2,1)}, u32[]{:S(2)}) %copy-start.8) | copy-done | bytes 163864
  1.5 0.3 copy-done.6
  1.8 0.2 copy-done.5
  2.0 1.0 %shard_map.138 = (bf16[16,4,1408]{2,1,0:T(4,128)(2,1)S(1)}, bf16[16,4,1408]{2,1,0:T(4,128)(2,1)S(1)}, f32[64,256]{1,0:T(8,128)S(1)}, f32[64,256]{1,0:T(8,128)S(1)}) custom-call(f32[8,128]{1,0:T(8,128)S(1)} %shard_map.137._, bf16[256,1280]{1,0:T(8,128)(2,1)S(1)} %bitcast.17, bf16[256,1280]{1,0:T(8,128)(2,1)S(1)} %bitcast.19, bf16[64,1280]{1,0:T(8,128)(2,1)S(1)} %bitcast.22), custom_call_target="tpu_custom_call" | custom-call | flops 10125829120 | bytes 1970176 | tf_op jit(solution)/shard_map/pallas_call | solution.py:576
  3.0 0.1 collective-permute-start
  3.2 1.4 %collective-permute-done.other = bf16[16,4,1408]{2,1,0:T(4,128)(2,1)S(1)} collective-permute-done((bf16[16,4,1408]{2,1,0:T(4,128)(2,1)S(1)}, bf16[16,4,1408]{2,1,0:T(4,128)(2,1)S(1)}, u32[]{:S(2)}, u32[]{:S(2)}) %collective-permute-start) | collective-permute-done | bytes 180256 | tf_op jit(solution)/shard_map/ppermute | solution.py:557
  4.5 0.0 copy-start.4
  4.5 0.0 copy-start.7
  4.5 0.0 copy-start.9
  4.5 0.3 shard_map.139
  4.8 14.5 %all_to_all.20.first = bf16[16,4,1408]{2,1,0:T(4,128)(2,1)S(1)} all-to-all(bf16[16,4,1408]{2,1,0:T(4,128)(2,1)S(1)} %shard_map.139), channel_id=1, replica_groups=mesh['dp'=2,'half'=2,'chip'=4,'core'=2] {'dp','half','chip'}, dimensions={0} | all-to-all | bytes 360448 | tf_op jit(solution)/shard_map/all_to_all | solution.py:639
  19.4 0.0 copy-done.4
  19.4 0.0 copy-done.7
  19.4 0.5 shard_map.140
  19.9 1.5 %collective-permute-start.1 = (bf16[8,1408]{1,0:T(8,128)(2,1)S(1)}, bf16[8,1408]{1,0:T(8,128)(2,1)S(1)}, u32[]{:S(2)}, u32[]{:S(2)}) collective-permute-start(bf16[8,1408]{1,0:T(8,128)(2,1)S(1)} %get-tuple-element.48.own), channel_id=1, source_target_pairs={{0,8},{8,0},{1,9},{9,1},{2,10},{10,2},{3,11},{11,3},{4,12},{12,4},... | collective-permute-start | bytes 67592 | tf_op jit(solution)/shard_map/ppermute | solution.py:557
  21.4 0.0 copy-done.9
  21.4 0.4 shard_map.141.mixing
  21.8 0.0 copy-start
  21.8 0.0 copy-start.1
  21.8 0.0 copy-start.2
  21.9 0.0 copy-start.3
  21.9 1.6 %collective-permute-done.1.beside = bf16[8,1408]{1,0:T(8,128)(2,1)S(1)} collective-permute-done((bf16[8,1408]{1,0:T(8,128)(2,1)S(1)}, bf16[8,1408]{1,0:T(8,128)(2,1)S(1)}, u32[]{:S(2)}, u32[]{:S(2)}) %collective-permute-start.1) | collective-permute-done | bytes 22560 | tf_op jit(solution)/shard_map/ppermute | solution.py:557
  23.5 7.9 %all_to_all.21.second = bf16[8,8,1408]{2,1,0:T(8,128)(2,1)S(1)} all-to-all(bf16[8,8,1408]{2,1,0:T(8,128)(2,1)S(1)} %bitcast.21), channel_id=1, replica_groups=mesh['dp'=2,'half'=2,'chip'=4,'core'=2] {'dp','chip'}, dimensions={0} | all-to-all | bytes 360448 | tf_op jit(solution)/shard_map/all_to_all | solution.py:569
  31.4 4.3 %collective-permute-start.2 = (bf16[8,8,1408]{2,1,0:T(8,128)(2,1)S(1)}, bf16[8,8,1408]{2,1,0:T(8,128)(2,1)S(1)}, u32[]{:S(2)}, u32[]{:S(2)}) collective-permute-start(bf16[8,8,1408]{2,1,0:T(8,128)(2,1)S(1)} %all_to_all.21.second), channel_id=1, source_target_pairs={{0,1},{1,0},{2,3},{3,2},{4,5},{5,4},{6,7},{7,6},{8,9},{9,8},{10,11... | collective-permute-start | bytes 540680 | tf_op jit(solution)/shard_map/ppermute | solution.py:557
  35.8 0.0 copy-done
  35.8 0.0 copy-done.1
  35.8 0.0 copy-done.2
  35.8 0.0 copy-done.3
  35.8 0.4 shard_map.143
  36.2 0.7 %collective-permute-done.2.second_other = bf16[8,8,1408]{2,1,0:T(8,128)(2,1)S(1)} collective-permute-done((bf16[8,8,1408]{2,1,0:T(8,128)(2,1)S(1)}, bf16[8,8,1408]{2,1,0:T(8,128)(2,1)S(1)}, u32[]{:S(2)}, u32[]{:S(2)}) %collective-permute-start.2) | collective-permute-done | bytes 180256 | tf_op jit(solution)/shard_map/ppermute | solution.py:557
  36.8 2.1 %shard_map.144 = (bf16[16,8,768]{2,1,0:T(8,128)(2,1)S(1)}, f32[2,64,320]{2,1,0:T(8,128)S(1)}, f32[2,64,64]{2,1,0:T(8,128)S(1)}) custom-call(bf16[8,8,1408]{2,1,0:T(8,128)(2,1)S(1)} %all_to_all.21.second, bf16[8,8,1408]{2,1,0:T(8,128)(2,1)S(1)} %collective-permute-done.2.second_other, f32[2,32,64]{2,1,0:T(8,128)S(1)} %get-tuple-element.51.near_ranks, ...), custom_call_target="tpu_custom_call" | custom-call | flops 188743680 | bytes 5111808 | tf_op jit(solution)/shard_map/pallas_call | solution.py:576
  38.9 8.8 %all_to_all.22.third = bf16[16,8,768]{2,1,0:T(8,128)(2,1)S(1)} all-to-all(bf16[16,8,768]{2,1,0:T(8,128)(2,1)S(1)} %get-tuple-element.53), channel_id=1, replica_groups=mesh['dp'=2,'half'=2,'chip'=4,'core'=2] {'dp','chip','core'}, dimensions={0} | all-to-all | bytes 393216 | tf_op jit(solution)/shard_map/all_to_all | solution.py:688
  47.8 1.2 %collective-permute-start.3 = (bf16[8,768]{1,0:T(8,128)(2,1)S(1)}, bf16[8,768]{1,0:T(8,128)(2,1)S(1)}, u32[]{:S(2)}, u32[]{:S(2)}) collective-permute-start(bf16[8,768]{1,0:T(8,128)(2,1)S(1)} %get-tuple-element.58), channel_id=1, source_target_pairs={{0,8},{8,0},{1,9},{9,1},{2,10},{10,2},{3,11},{11,3},{4,12},{12,4},... | collective-permute-start | bytes 36872 | tf_op jit(solution)/shard_map/ppermute | solution.py:557
  49.0 2.5 %shard_map.146 = (bf16[32,64,320]{2,1,0:T(8,128)(2,1)}, bf16[32,64,320]{2,1,0:T(8,128)(2,1)}) custom-call(f32[2,64,64]{2,1,0:T(8,128)S(1)} %get-tuple-element.59.left_rows, f32[2,64,320]{2,1,0:T(8,128)S(1)} %get-tuple-element.60.right_rows), custom_call_target="tpu_custom_call" | custom-call | flops 20971520 | bytes 2818048 | tf_op jit(solution)/shard_map/pallas_call | solution.py:576
  51.5 0.0 collective-permute-done.3.other
  51.5 0.3 shard_map.147
  51.8 9.8 %all_to_all.23.fourth = bf16[16,4,768]{2,1,0:T(4,128)(2,1)S(1)} all-to-all(bf16[16,4,768]{2,1,0:T(4,128)(2,1)S(1)} %get-tuple-element.66), channel_id=1, replica_groups=mesh['dp'=2,'half'=2,'chip'=4,'core'=2] {'dp','half','chip'}, dimensions={0} | all-to-all | bytes 196608 | tf_op jit(solution)/shard_map/all_to_all | solution.py:712
  61.6 2.6 %collective-permute-start.4 = (bf16[16,4,768]{2,1,0:T(4,128)(2,1)S(1)}, bf16[16,4,768]{2,1,0:T(4,128)(2,1)S(1)}, u32[]{:S(2)}, u32[]{:S(2)}) collective-permute-start(bf16[16,4,768]{2,1,0:T(4,128)(2,1)S(1)} %all_to_all.23.fourth), channel_id=1, source_target_pairs={{0,1},{1,0},{2,3},{3,2},{4,5},{5,4},{6,7},{7,6},{8,9},{9,8},{10,11... | collective-permute-start | bytes 294920 | tf_op jit(solution)/shard_map/ppermute | solution.py:557
  64.2 0.4 shard_map.148
  64.6 0.5 collective-permute-done.4.fourth_other
  65.1 1.7 %shard_map.149 = (bf16[256,1280]{1,0:T(8,128)(2,1)}, bf16[4,64,640]{2,1,0:T(8,128)(2,1)}, bf16[4,64,640]{2,1,0:T(8,128)(2,1)}) custom-call(bf16[16,4,768]{2,1,0:T(4,128)(2,1)S(1)} %all_to_all.23.fourth, bf16[16,4,768]{2,1,0:T(4,128)(2,1)S(1)} %collective-permute-done.4.fourth_other, bf16[256,1280]{1,0:T(8,128)(2,1)S(1)} %bitcast.18, ...), custom_call_target="tpu_custom_call" | custom-call | flops 125829120 | bytes 3112960 | tf_op jit(solution)/shard_map/pallas_call | solution.py:576
  (3 shorter events, 0.0 us)
Async XLA Ops:
  0.6 0.9 %copy-start.8 = (bf16[1280,64]{0,1:T(8,128)(2,1)S(1)}, bf16[1280,64]{0,1:T(8,128)(2,1)}, u32[]{:S(2)}) copy-start(bf16[1280,64]{0,1:T(8,128)(2,1)} %param.12) | copy-start | bytes 491524
  0.6 1.2 %copy-start.6 = (bf16[1,256,1280]{2,1,0:T(8,128)(2,1)S(1)}, bf16[1,256,1280]{2,1,0:T(8,128)(2,1)}, u32[]{:S(2)}) copy-start(bf16[1,256,1280]{2,1,0:T(8,128)(2,1)} %param.11) | copy-start | bytes 1966084
  0.7 1.4 %copy-start.5 = (bf16[1,256,1280]{2,1,0:T(8,128)(2,1)S(1)}, bf16[1,256,1280]{2,1,0:T(8,128)(2,1)}, u32[]{:S(2)}) copy-start(bf16[1,256,1280]{2,1,0:T(8,128)(2,1)} %param.10) | copy-start | bytes 1966084
  3.0 1.5 %collective-permute-start = (bf16[16,4,1408]{2,1,0:T(4,128)(2,1)S(1)}, bf16[16,4,1408]{2,1,0:T(4,128)(2,1)S(1)}, u32[]{:S(2)}, u32[]{:S(2)}) collective-permute-start(bf16[16,4,1408]{2,1,0:T(4,128)(2,1)S(1)} %get-tuple-element.45), channel_id=1, source_target_pairs={{0,1},{1,0},{2,3},{3,2},{4,5},{5,4},{6,7},{7,6},{8,9},{9,8},{10,11... | collective-permute-start | bytes 540680 | tf_op jit(solution)/shard_map/ppermute | solution.py:557
  4.5 14.8 %copy-start.4 = (bf16[4,640,64]{1,2,0:T(8,128)(2,1)S(1)}, bf16[4,640,64]{1,2,0:T(8,128)(2,1)}, u32[]{:S(2)}) copy-start(bf16[4,640,64]{1,2,0:T(8,128)(2,1)} %param.16) | copy-start | bytes 983044
  4.5 14.8 %copy-start.7 = (bf16[4,64,640]{2,1,0:T(8,128)(2,1)S(1)}, bf16[4,64,640]{2,1,0:T(8,128)(2,1)}, u32[]{:S(2)}) copy-start(bf16[4,64,640]{2,1,0:T(8,128)(2,1)} %out_right.1) | copy-start | bytes 983044
  4.5 16.9 %copy-start.9 = (bf16[1,64,1280]{2,1,0:T(8,128)(2,1)S(1)}, bf16[1,64,1280]{2,1,0:T(8,128)(2,1)}, u32[]{:S(2)}) copy-start(bf16[1,64,1280]{2,1,0:T(8,128)(2,1)} %param.13) | copy-start | bytes 491524
  19.9 3.6 %collective-permute-start.1 = (bf16[8,1408]{1,0:T(8,128)(2,1)S(1)}, bf16[8,1408]{1,0:T(8,128)(2,1)S(1)}, u32[]{:S(2)}, u32[]{:S(2)}) collective-permute-start(bf16[8,1408]{1,0:T(8,128)(2,1)S(1)} %get-tuple-element.48.own), channel_id=1, source_target_pairs={{0,8},{8,0},{1,9},{9,1},{2,10},{10,2},{3,11},{11,3},{4,12},{12,4},... | collective-permute-start | bytes 67592 | tf_op jit(solution)/shard_map/ppermute | solution.py:557
  21.8 14.0 %copy-start = (bf16[32,64,320]{2,1,0:T(8,128)(2,1)S(1)}, bf16[32,64,320]{2,1,0:T(8,128)(2,1)}, u32[]{:S(2)}) copy-start(bf16[32,64,320]{2,1,0:T(8,128)(2,1)} %in_right.3) | copy-start | bytes 3932164
  21.8 14.0 %copy-start.1 = (bf16[32,320,64]{1,2,0:T(8,128)(2,1)S(1)}, bf16[32,320,64]{1,2,0:T(8,128)(2,1)}, u32[]{:S(2)}) copy-start(bf16[32,320,64]{1,2,0:T(8,128)(2,1)} %param.18) | copy-start | bytes 3932164
  21.8 13.9 %copy-start.2 = (bf16[1280,320]{0,1:T(8,128)(2,1)S(1)}, bf16[1280,320]{0,1:T(8,128)(2,1)}, u32[]{:S(2)}) copy-start(bf16[1280,320]{0,1:T(8,128)(2,1)} %param.14) | copy-start | bytes 2457604
  21.9 13.9 %copy-start.3 = (bf16[320,1280]{1,0:T(8,128)(2,1)S(1)}, bf16[320,1280]{1,0:T(8,128)(2,1)}, u32[]{:S(2)}) copy-start(bf16[320,1280]{1,0:T(8,128)(2,1)} %base_out.1) | copy-start | bytes 2457604
  31.4 5.4 %collective-permute-start.2 = (bf16[8,8,1408]{2,1,0:T(8,128)(2,1)S(1)}, bf16[8,8,1408]{2,1,0:T(8,128)(2,1)S(1)}, u32[]{:S(2)}, u32[]{:S(2)}) collective-permute-start(bf16[8,8,1408]{2,1,0:T(8,128)(2,1)S(1)} %all_to_all.21.second), channel_id=1, source_target_pairs={{0,1},{1,0},{2,3},{3,2},{4,5},{5,4},{6,7},{7,6},{8,9},{9,8},{10,11... | collective-permute-start | bytes 540680 | tf_op jit(solution)/shard_map/ppermute | solution.py:557
  47.8 3.7 %collective-permute-start.3 = (bf16[8,768]{1,0:T(8,128)(2,1)S(1)}, bf16[8,768]{1,0:T(8,128)(2,1)S(1)}, u32[]{:S(2)}, u32[]{:S(2)}) collective-permute-start(bf16[8,768]{1,0:T(8,128)(2,1)S(1)} %get-tuple-element.58), channel_id=1, source_target_pairs={{0,8},{8,0},{1,9},{9,1},{2,10},{10,2},{3,11},{11,3},{4,12},{12,4},... | collective-permute-start | bytes 36872 | tf_op jit(solution)/shard_map/ppermute | solution.py:557
  61.6 3.6 %collective-permute-start.4 = (bf16[16,4,768]{2,1,0:T(4,128)(2,1)S(1)}, bf16[16,4,768]{2,1,0:T(4,128)(2,1)S(1)}, u32[]{:S(2)}, u32[]{:S(2)}) collective-permute-start(bf16[16,4,768]{2,1,0:T(4,128)(2,1)S(1)} %all_to_all.23.fourth), channel_id=1, source_target_pairs={{0,1},{1,0},{2,3},{3,2},{4,5},{5,4},{6,7},{7,6},{8,9},{9,8},{10,11... | collective-permute-start | bytes 294920 | tf_op jit(solution)/shard_map/ppermute | solution.py:557
